TPU v7x, 32 devices: a whole 2x2x4 slice. The times are simulated.
32 devices in a mesh: groups: 2 (over x), frame: 8 (over z, y), space: 2 (over core).
Axes of the slice: x: 2, y: 2, z: 4, core: 2. Of those that a mesh axis runs over, the one named last changes fastest.
Arguments:
- queries: bfloat16 [16, 12, 80, 2240], P(('groups', 'frame'), 'space'), parts along dimension 0, may hold values from -6 to 6
- keys: bfloat16 [16, 12, 80, 2240], P(('groups', 'frame'), 'space'), parts along dimension 0, may hold values from -6 to 6
- values: bfloat16 [16, 12, 80, 2240], P(('groups', 'frame'), 'space'), parts along dimension 0, may hold values from -6 to 6
- residual: bfloat16 [16, 12, 80, 2240], P(('groups', 'frame'), 'space'), parts along dimension 0, may hold values from -6 to 6
- attn_gain: float32 [2240], replicated, may hold values from 0.5 to 1.5
- value_taps: float32 [9, 2240], replicated, may hold values from -2 to 2
- gate_taps: float32 [9, 2240], replicated, may hold values from -2 to 2
Outputs:
- block_out: bfloat16 [16, 12, 80, 2240], P(('groups', 'frame'), 'space'), parts along dimension 0
There are 2 independent parts, one for each index of `groups`. A program takes and returns all parts, laid end to end along the dimension named above; an argument that names none is the same for every part. Nothing has to cross between parts.
All inputs are finite; a program needn't handle non-finite values.
Results may differ from a plain program's by a relative error of at most 0.008.
Values may be sent and summed in bfloat16 or wider, within the bound.
No kernel may reach another device: no remote copies, remote signals or barrier semaphores. Data moves between devices by JAX's collectives and lax.ppermute only.
A program may use at most 128 MiB of HBM per device.

v0:
```python
import jax
import jax.numpy as jnp
from jax import lax
from jax.sharding import PartitionSpec as P

HEAD_DIM = 112


def entering(value, axis, combine, identity):
    devices, here = (lax.axis_size(axis), lax.axis_index(axis))
    everything = lax.all_gather(value.astype(jnp.bfloat16), axis)
    start = jnp.broadcast_to(jnp.asarray(identity, value.dtype), value.shape)

    def step(k, before):
        reached = k < here
        new = combine(before, everything[k].astype(value.dtype))
        return jnp.where(reached, new, before)

    return lax.fori_loop(0, devices, step, start)


def with_halo(value, sides, width):
    for axis, dim in sides:
        devices, length = (lax.axis_size(axis), value.shape[dim])
        up = [(i, (i + 1) % devices) for i in range(devices - 1)]
        down = [(j, i) for i, j in up]
        last = lax.slice_in_dim(value, length - width, length, axis=dim)
        initial = lax.slice_in_dim(value, 0, width, axis=dim)
        before = lax.ppermute(last, axis, up)
        after = lax.ppermute(initial, axis, down)
        value = jnp.concatenate([before, value, after], axis=dim)
    return value


def add_states(earlier, later):
    return earlier + later


def on_device(queries, keys, values, residual, attn_gain, value_taps, gate_taps):
    frames, rows, width, dim = queries.shape
    heads = dim // HEAD_DIM
    tokens = frames * rows * width
    feature_keys = jnp.maximum(keys, 0).reshape(tokens, heads, HEAD_DIM)
    value_rows = values.reshape(tokens, heads, HEAD_DIM)
    partial_value_state = jnp.einsum(
        "rag,rap->agp", feature_keys, value_rows, preferred_element_type=jnp.float32
    )
    share = lax.psum_scatter(
        partial_value_state.astype(jnp.bfloat16), "space", scatter_dimension=0, tiled=True
    ).astype(jnp.float32)
    prev_share = entering(share, "frame", add_states, jnp.zeros_like(share))
    previous_frame_pass, local_frame_pass = (
        lax.all_gather(prev_share.astype(jnp.bfloat16), "space", axis=0, tiled=True),
        lax.all_gather(share.astype(jnp.bfloat16), "space", axis=0, tiled=True),
    )
    feature_queries = jnp.maximum(queries, 0).reshape(tokens, heads, HEAD_DIM)
    numerator_sum = jnp.einsum(
        "ubq,bql->ubl", feature_queries, local_frame_pass, preferred_element_type=jnp.float32
    )
    numerator_sum = numerator_sum + jnp.einsum(
        "ubq,bql->ubl", feature_queries, previous_frame_pass, preferred_element_type=jnp.float32
    )
    scale = lax.rsqrt(jnp.mean(numerator_sum * numerator_sum, axis=-1, keepdims=True) + 1e-06)
    normed = (numerator_sum * scale).reshape(rows, width, dim)
    mixed = (residual.reshape(rows, width, dim).astype(jnp.float32) + normed * attn_gain).astype(
        jnp.bfloat16
    )
    extended = with_halo(mixed, (("space", 0),), 1)
    padded = jnp.pad(extended.astype(jnp.float32), ((0, 0), (1, 1), (0, 0)))
    conv_v = jnp.zeros((rows, width, dim), jnp.float32)
    conv_g = jnp.zeros((rows, width, dim), jnp.float32)
    for tap_row in range(3):
        for tap_col in range(3):
            window = padded[tap_row : tap_row + rows, tap_col : tap_col + width, :]
            conv_v = conv_v + value_taps[3 * tap_row + tap_col] * window
            conv_g = conv_g + gate_taps[3 * tap_row + tap_col] * window
    block_out = mixed.astype(jnp.float32) + conv_v * jax.nn.silu(conv_g)
    return block_out.astype(jnp.bfloat16).reshape(frames, rows, width, dim)


def solution(mesh):
    placed = (
        P(("groups", "frame"), "space", None, None),
        P(("groups", "frame"), "space", None, None),
        P(("groups", "frame"), "space", None, None),
        P(("groups", "frame"), "space", None, None),
        P(),
        P(),
        P(),
    )
    return jax.shard_map(
        on_device,
        mesh=mesh,
        in_specs=placed,
        out_specs=P(("groups", "frame"), "space", None, None),
        check_vma=False,
    )
```

profile of v0, /device:TPU:0, one launch (start us, length us, event | category | flops | bytes accessed | tf_op | source)
XLA Modules:
  0.0 145.8 jit_solution(8434362103516767503)
XLA Ops:
  6.5 1.8 %broadcast_maximum_fusion.1 = bf16[1,6,80,2240]{3,2,1,0:T(8,128)(2,1)S(1)} fusion(bf16[1,6,80,2240]{3,2,1,0:T(8,128)(2,1)} %param.10), kind=kLoop, calls=%fused_computation.21 | loop fusion | flops 1075200 | bytes 4300800 | tf_op jit(solution)/shard_map/max | solution.py:43
  8.3 4.1 %reshape.47 = bf16[480,20,112]{2,1,0:T(8,128)(2,1)} reshape(bf16[1,6,80,2240]{3,2,1,0:T(8,128)(2,1)S(1)} %broadcast_maximum_fusion.1) | data formatting | bytes 4300800 | tf_op jit(solution)/shard_map/reshape | solution.py:43
  12.4 6.3 %reshape.48 = bf16[480,20,112]{2,1,0:T(8,128)(2,1)} reshape(bf16[1,6,80,2240]{3,2,1,0:T(8,128)(2,1)} %param.11) | data formatting | bytes 4300800 | tf_op jit(solution)/shard_map/reshape | solution.py:44
  18.8 3.8 %fusion.6 = bf16[20,112,112]{2,1,0:T(8,128)(2,1)} fusion(bf16[480,20,112]{2,1,0:T(8,128)(2,1)} %reshape.48, bf16[480,20,112]{2,1,0:T(8,128)(2,1)S(1)} %copy-done), kind=kOutput, calls=%fused_computation.19 | convolution fusion | flops 241095680 | bytes 4802560 | tf_op jit(solution)/shard_map/rag,rap->agp/dot_general | solution.py:45
  22.6 10.8 %reduce-scatter.2.cloned.1.call-done = bf16[10,112,112]{2,1,0:T(8,128)(2,1)} async-done(((bf16[20,112,112]{2,1,0:T(8,128)(2,1)}), bf16[10,112,112]{2,1,0:T(8,128)(2,1)}) %reduce-scatter.2.cloned.1.call-update) | async-done | bytes 250896 | tf_op jit(solution)/shard_map/reduce_scatter | solution.py:48
  33.5 1.8 %broadcast_maximum_fusion = bf16[1,6,80,2240]{3,2,1,0:T(8,128)(2,1)S(1)} fusion(bf16[1,6,80,2240]{3,2,1,0:T(8,128)(2,1)} %param.9), kind=kLoop, calls=%fused_computation.20 | loop fusion | flops 1075200 | bytes 4300800 | tf_op jit(solution)/shard_map/max | solution.py:56
  35.3 4.1 %reshape.49 = bf16[480,20,112]{2,1,0:T(8,128)(2,1)} reshape(bf16[1,6,80,2240]{3,2,1,0:T(8,128)(2,1)S(1)} %broadcast_maximum_fusion) | data formatting | bytes 4300800 | tf_op jit(solution)/shard_map/reshape | solution.py:56
  39.4 3.6 %copy.25 = bf16[480,20,112]{0,2,1:T(8,128)(2,1)S(1)} copy(bf16[480,20,112]{2,1,0:T(8,128)(2,1)} %reshape.49) | data formatting | bytes 4300800 | tf_op jit(solution)/shard_map/reshape | solution.py:56
  43.0 2.2 %all_gather.12 = bf16[20,112,112]{2,1,0:T(8,128)(2,1)S(1)} all-gather(bf16[10,112,112]{2,1,0:T(8,128)(2,1)S(1)} %copy-done.2), channel_id=1, replica_groups=mesh['groups'=2,'frame'=8,'space'=2] {'space'}, dimensions={0}, use_global_device_ids=true | all-gather | bytes 752640 | tf_op jit(solution)/shard_map/all_gather | solution.py:54
  45.2 2.9 %fusion.12 = f32[20,112,480]{2,1,0:T(8,128)} fusion(bf16[20,112,112]{2,1,0:T(8,128)(2,1)S(1)} %all_gather.12, bf16[480,20,112]{0,2,1:T(8,128)(2,1)S(1)} %copy.25), kind=kOutput, calls=%fused_computation.42 | convolution fusion | flops 240844800 | bytes 6952960 | tf_op jit(solution)/shard_map/ubq,bql->ubl/dot_general | solution.py:57
  48.0 40.3 %all-gather.3.cloned.1.call-done = bf16[80,112,112]{2,1,0:T(8,128)(2,1)} async-done(((bf16[10,112,112]{2,1,0:T(8,128)(2,1)}), bf16[80,112,112]{2,1,0:T(8,128)(2,1)}) %all-gather.3.cloned.1.call-update) | async-done | bytes 2007056 | tf_op jit(solution)/shard_map/all_gather | solution.py:11
  88.3 10.1 %while.14 = (s32[]{:T(128)}, f32[10,112,112]{2,1,0:T(8,128)S(1)}, s32[]{:T(128)}, bf16[8,10,112,112]{3,2,1,0:T(8,128)(2,1)}, s32[]{:T(128)}, /*index=5*/s32[]{:T(128)}) while((s32[]{:T(128)}, f32[10,112,112]{2,1,0:T(8,128)S(1)}, s32[]{:T(128)}, bf16[8,10,112,112]{3,2,1,0:T(8,128)(2,1)}, s32[]{:T(128)}, /*index=5*/s32[]{:T(128)}) %tuple.66), condition=%wide.region_2.3_spmd.clone, body=%wide.region_1.2_spmd.clone.sunk | while | flops 501764 | bytes 1254493 | solution.py:19
  89.6 1.2 add_select_fusion.2
  90.9 1.2 add_select_fusion.2
  98.5 2.2 %all_gather.15 = bf16[20,112,112]{2,1,0:T(8,128)(2,1)S(1)} all-gather(bf16[10,112,112]{2,1,0:T(8,128)(2,1)S(1)} %convert_element_type.42), channel_id=1, replica_groups=mesh['groups'=2,'frame'=8,'space'=2] {'space'}, dimensions={0}, use_global_device_ids=true | all-gather | bytes 752640 | tf_op jit(solution)/shard_map/all_gather | solution.py:53
  100.7 3.2 %fusion = (f32[480,20]{0,1:T(8,128)S(1)}, f32[20,112,480]{2,1,0:T(8,128)S(1)}) fusion(f32[20,112,480]{2,1,0:T(8,128)} %fusion.12, bf16[20,112,112]{2,1,0:T(8,128)(2,1)S(1)} %all_gather.15, bf16[480,20,112]{0,2,1:T(8,128)(2,1)S(1)} %copy.25), kind=kOutput, calls=%fused_computation.9 | convolution fusion | flops 244060800 | bytes 11292160 | tf_op jit(solution)/shard_map/ubq,bql->ubl/dot_general | solution.py:60
  104.0 2.9 %bitcast_multiply_fusion = f32[480,20,112]{0,2,1:T(8,128)} fusion(f32[20,112,480]{2,1,0:T(8,128)S(1)} %get-tuple-element.129, f32[480,20]{0,1:T(8,128)S(1)} %add_rsqrt_fusion), kind=kLoop, calls=%fused_computation.7 | loop fusion | flops 1075200 | bytes 8640000 | tf_op jit(solution)/shard_map/mul | solution.py:64
  106.9 6.1 %copy.28 = f32[480,20,112]{2,1,0:T(8,128)} copy(f32[480,20,112]{0,2,1:T(8,128)} %bitcast_multiply_fusion) | data formatting | bytes 8601600 | tf_op jit(solution)/shard_map/mul | solution.py:64
  113.0 7.0 %reshape.50 = f32[6,80,2240]{2,1,0:T(8,128)} reshape(f32[480,20,112]{2,1,0:T(8,128)} %copy.28) | data formatting | bytes 8601600 | tf_op jit(solution)/shard_map/reshape | solution.py:64
  120.0 2.8 %fusion.1 = bf16[6,80,2240]{2,1,0:T(8,128)(2,1)S(1)} fusion(f32[6,80,2240]{2,1,0:T(8,128)} %reshape.50, bf16[1,6,80,2240]{3,2,1,0:T(8,128)(2,1)S(1)} %copy-done.1, f32[2240]{0:T(1024)S(1)} %copy-done.5), kind=kLoop, calls=%fused_computation.11 | loop fusion | flops 4300800 | bytes 8610560 | tf_op jit(solution)/shard_map/convert_element_type | solution.py:65
  122.9 2.1 %collective-permute-start = (bf16[1,80,2240]{2,1,0:T(8,128)(2,1)S(1)}, bf16[1,80,2240]{2,1,0:T(8,128)(2,1)S(1)}, u32[]{:S(2)}, u32[]{:S(2)}) collective-permute-start(bf16[1,80,2240]{2,1,0:T(8,128)(2,1)S(1)} %get-tuple-element.126), channel_id=1, source_target_pairs={{0,1},{2,3},{4,5},{6,7},{8,9},{10,11},{12,13},{14,15},{16,17},{18,... | collective-permute-start | bytes 1075208 | tf_op jit(solution)/shard_map/ppermute | solution.py:29
  124.9 1.5 %collective-permute-start.1 = (bf16[1,80,2240]{2,1,0:T(8,128)(2,1)S(1)}, bf16[1,80,2240]{2,1,0:T(8,128)(2,1)S(1)}, u32[]{:S(2)}, u32[]{:S(2)}) collective-permute-start(bf16[1,80,2240]{2,1,0:T(8,128)(2,1)S(1)} %get-tuple-element.127), channel_id=1, source_target_pairs={{1,0},{3,2},{5,4},{7,6},{9,8},{11,10},{13,12},{15,14},{17,16},{19,... | collective-permute-start | bytes 1075208 | tf_op jit(solution)/shard_map/ppermute | solution.py:30
  126.9 1.6 %collective-permute-done.1 = bf16[1,80,2240]{2,1,0:T(8,128)(2,1)S(1)} collective-permute-done((bf16[1,80,2240]{2,1,0:T(8,128)(2,1)S(1)}, bf16[1,80,2240]{2,1,0:T(8,128)(2,1)S(1)}, u32[]{:S(2)}, u32[]{:S(2)}) %collective-permute-start.1) | collective-permute-done | bytes 358432 | tf_op jit(solution)/shard_map/ppermute | solution.py:30
  129.0 10.0 %fusion.5 = bf16[1,6,80,2240]{3,2,1,0:T(8,128)(2,1)} fusion(f32[2240]{0:T(1024)S(1)} %get-tuple-element.116, f32[2240]{0:T(1024)S(1)} %get-tuple-element.117, f32[2240]{0:T(1024)S(1)} %get-tuple-element.110, f32[2240]{0:T(1024)S(1)} %get-tuple-element.111, f32[2240]{0:T(1024)S(1)} %get-tuple-element.112, f32[2240]{0:T(1024)S(1)} %get-tuple-element.113, ...), kind=kLoop, calls=%fused_computation.18 | loop fusion | flops 45158400 | bytes 23752704 | tf_op jit(solution)/shard_map/reshape | solution.py:78
  (29 shorter events, 8.6 us)
Async XLA Ops:
  6.5 26.9 %reduce-scatter.2.cloned.1.call-start = ((), (), s32[]{:S(2)}) async-start(), calls=%async_computation.1 | async-start | bytes 860160 | tf_op jit(solution)/shard_map/reduce_scatter | solution.py:48
  12.4 6.3 %copy-start = (bf16[480,20,112]{2,1,0:T(8,128)(2,1)S(1)}, bf16[480,20,112]{2,1,0:T(8,128)(2,1)}, u32[]{:S(2)}) copy-start(bf16[480,20,112]{2,1,0:T(8,128)(2,1)} %reshape.47) | copy-start | bytes 6451204
  22.6 65.8 %all-gather.3.cloned.1.call-start = ((), (), s32[]{:S(2)}) async-start(), calls=%async_computation.2 | async-start | bytes 2580480 | tf_op jit(solution)/shard_map/all_gather | solution.py:11
  35.2 7.7 %copy-start.2 = (bf16[10,112,112]{2,1,0:T(8,128)(2,1)S(1)}, bf16[10,112,112]{2,1,0:T(8,128)(2,1)}, u32[]{:S(2)}) copy-start(bf16[10,112,112]{2,1,0:T(8,128)(2,1)} %reduce-scatter.2.cloned.1.call-done) | copy-start | bytes 752644
  113.0 7.0 %copy-start.1 = (bf16[1,6,80,2240]{3,2,1,0:T(8,128)(2,1)S(1)}, bf16[1,6,80,2240]{3,2,1,0:T(8,128)(2,1)}, u32[]{:S(2)}) copy-start(bf16[1,6,80,2240]{3,2,1,0:T(8,128)(2,1)} %param.12) | copy-start | bytes 6451204
  113.0 7.0 %copy-start.5 = (f32[2240]{0:T(1024)S(1)}, f32[2240]{0:T(1024)}, u32[]{:S(2)}) copy-start(f32[2240]{0:T(1024)} %param.13) | copy-start | bytes 26884
  120.0 6.4 %copy-start.3 = (f32[9,2240]{1,0:T(8,128)S(1)}, f32[9,2240]{1,0:T(8,128)}, u32[]{:S(2)}) copy-start(f32[9,2240]{1,0:T(8,128)} %param.15) | copy-start | bytes 241924
  120.0 6.4 %copy-start.4 = (f32[9,2240]{1,0:T(8,128)S(1)}, f32[9,2240]{1,0:T(8,128)}, u32[]{:S(2)}) copy-start(f32[9,2240]{1,0:T(8,128)} %param.14) | copy-start | bytes 241924
  122.9 4.0 %collective-permute-start = (bf16[1,80,2240]{2,1,0:T(8,128)(2,1)S(1)}, bf16[1,80,2240]{2,1,0:T(8,128)(2,1)S(1)}, u32[]{:S(2)}, u32[]{:S(2)}) collective-permute-start(bf16[1,80,2240]{2,1,0:T(8,128)(2,1)S(1)} %get-tuple-element.126), channel_id=1, source_target_pairs={{0,1},{2,3},{4,5},{6,7},{8,9},{10,11},{12,13},{14,15},{16,17},{18,... | collective-permute-start | bytes 1075208 | tf_op jit(solution)/shard_map/ppermute | solution.py:29
  124.9 3.6 %collective-permute-start.1 = (bf16[1,80,2240]{2,1,0:T(8,128)(2,1)S(1)}, bf16[1,80,2240]{2,1,0:T(8,128)(2,1)S(1)}, u32[]{:S(2)}, u32[]{:S(2)}) collective-permute-start(bf16[1,80,2240]{2,1,0:T(8,128)(2,1)S(1)} %get-tuple-element.127), channel_id=1, source_target_pairs={{1,0},{3,2},{5,4},{7,6},{9,8},{11,10},{13,12},{15,14},{17,16},{19,... | collective-permute-start | bytes 1075208 | tf_op jit(solution)/shard_map/ppermute | solution.py:30
Sparse Core Ops, SparseCore 0:
  22.7 10.7 reduce-scatter.1
  35.8 52.4 all-gather.2
where the time goes:
time: 147 us; the launch traced here: 146 us
  waiting for transfers between devices  52.8 us (36%)
  local copies, waits for them, and re-layouts  31.7 us (22%)
  other arithmetic  29.8 us (20%)
  between operations  13.6 us (9%)
  matrix products  9.84 us (7%)
  blocking collectives  4.43 us (3%)
  starting transfers between devices  3.58 us (2%)
    all_gather x1, waiting for transfers between devices, entering(): everything = lax.all_gather(value.astype(jnp.bfloat16), axis)  40.3 us
    reduce_scatter x1, waiting for transfers between devices, on_device(): lax.psum_scatter(partial_value_state.astype(jnp.bfloat16), 'space', scatt...  10.8 us
    reshape x1, other arithmetic, on_device(): return block_out.astype(jnp.bfloat16).reshape(frames, rows, width, dim)  9.99 us
    select_n x8, other arithmetic, step(): return jnp.where(reached, new, before)  9.97 us
    reshape x2, local copies, waits for them, and re-layouts, on_device(): feature_queries = jnp.maximum(queries, 0).reshape(tokens, heads, HEAD_DIM)  7.69 us
    reshape x1, local copies, waits for them, and re-layouts, on_device(): normed = (numerator_sum * scale).reshape(rows, width, dim)  6.99 us
    reshape x1, local copies, waits for them, and re-layouts, on_device(): value_rows = values.reshape(tokens, heads, HEAD_DIM)  6.32 us
    mul x1, local copies, waits for them, and re-layouts, on_device(): normed = (numerator_sum * scale).reshape(rows, width, dim)  6.09 us
  transfers between devices with their start and end apart: 4, of which 3 were waited for; matrix products, arithmetic and copies ran while one was open for 9% of the time, Pallas kernels for 0%

commit v1 on v0

v1 whole, which is shorter than its diff:
```python
import functools
import math

import jax
import jax.numpy as jnp
from jax import lax
from jax.experimental import pallas as pl
from jax.experimental.pallas import tpu as pltpu
from jax.sharding import PartitionSpec as P

HEAD_DIM = 112
LANES = 128
GROUP = math.lcm(HEAD_DIM, LANES)
TILES = GROUP // LANES
VMEM_LIMIT = 48 * 2**20


def cdiv(a, b):
    return -(-a // b)


def lane_iota(shape):
    return lax.broadcasted_iota(jnp.int32, shape, len(shape) - 1)


def tile_heads(j):
    lo, hi = j * LANES, (j + 1) * LANES
    heads = range(lo // HEAD_DIM, cdiv(hi, HEAD_DIM))
    return [(h, max(h * HEAD_DIM - lo, 0), min((h + 1) * HEAD_DIM - lo, LANES)) for h in heads]


def spans():
    result = []
    for j in range(0, TILES, 2):
        tiles = list(range(j, min(j + 2, TILES)))
        first = tile_heads(tiles[0])[0][0] * HEAD_DIM // LANES
        last = cdiv((tile_heads(tiles[-1])[-1][0] + 1) * HEAD_DIM, LANES)
        result.append((tiles, first, last))
    return result


def state_kernel(dim, keys_ref, values_ref, state_ref, turned):
    g = pl.program_id(0)
    left = dim - g * GROUP
    turned[...] = jnp.maximum(keys_ref[...], 0).T
    for j in range(TILES):

        def tile(j=j):
            heads = tile_heads(j)
            start = heads[0][0] * HEAD_DIM
            stop = (heads[-1][0] + 1) * HEAD_DIM
            product = jnp.dot(
                turned[start:stop, :],
                values_ref[:, j * LANES : (j + 1) * LANES],
                preferred_element_type=jnp.float32,
            )
            lane = lane_iota((HEAD_DIM, LANES))
            total = jnp.zeros((HEAD_DIM, LANES), jnp.float32)
            for place, (_, lo, hi) in enumerate(heads):
                part = product[place * HEAD_DIM : (place + 1) * HEAD_DIM]
                total = jnp.where((lane >= lo) & (lane < hi), part, total)
            total = jnp.where(lane + j * LANES < left, total, 0.0)
            state_ref[j * HEAD_DIM : (j + 1) * HEAD_DIM, :] = total.astype(jnp.bfloat16)

        pl.when(j * LANES < left)(tile)

        @pl.when(j * LANES >= left)
        def _(j=j):
            state_ref[j * HEAD_DIM : (j + 1) * HEAD_DIM, :] = jnp.zeros(
                (HEAD_DIM, LANES), jnp.bfloat16
            )


def frame_states(keys, values, rows):
    tokens, dim = keys.shape
    return pl.pallas_call(
        functools.partial(state_kernel, dim),
        out_shape=jax.ShapeDtypeStruct((rows, LANES), jnp.bfloat16),
        grid=(cdiv(dim, GROUP),),
        in_specs=[pl.BlockSpec((tokens, GROUP), lambda g: (0, g))] * 2,
        out_specs=pl.BlockSpec((TILES * HEAD_DIM, LANES), lambda g: (g, 0)),
        scratch_shapes=[pltpu.VMEM((GROUP, tokens), jnp.bfloat16)],
        compiler_params=pltpu.CompilerParams(vmem_limit_bytes=VMEM_LIMIT),
        cost_estimate=pl.CostEstimate(
            flops=2 * tokens * dim * HEAD_DIM, bytes_accessed=4 * tokens * dim, transcendentals=0
        ),
        name="frame_states",
    )(keys, values)


def mix_kernel(
    dim, rows, width, edges,
    place_ref, queries_ref, residual_ref, edge_ref, state_ref, gain_ref, vtaps_ref, gtaps_ref,
    out_ref,
    features, weights, same, numer, shifted,
):
    g = pl.program_id(0)
    left = dim - g * GROUP
    tokens = rows * width
    total = tokens + edges * width

    @pl.when(g == 0)
    def _():
        weights[...] = jnp.zeros_like(weights)
        same[...] = jnp.zeros_like(same)
        ones = jnp.ones((HEAD_DIM, LANES), jnp.float32)
        lane = lane_iota((HEAD_DIM, LANES))
        for number, (tiles, first, _) in enumerate(spans()):
            for side, j in enumerate(tiles):
                for h, lo, hi in tile_heads(j):
                    start = h * HEAD_DIM - first * LANES
                    block = jnp.where((lane >= lo) & (lane < hi), ones, 0.0)
                    same[
                        number, start : start + HEAD_DIM, side * LANES : (side + 1) * LANES
                    ] = block.astype(jnp.bfloat16)
        for row in range(rows + 2):
            if edges == 2 and row in (0, rows + 1):
                continue
            shifted[:, row] = jnp.zeros((3, width, LANES), jnp.float32)

    inside = lane_iota((1, GROUP)) < left
    zero = jnp.zeros((), jnp.bfloat16)
    features[:tokens] = jnp.where(inside, jnp.maximum(queries_ref[...], zero), zero)
    for e in range(edges):
        features[tokens + e * width : tokens + (e + 1) * width] = jnp.where(
            inside, jnp.maximum(edge_ref[0, e], zero), zero
        )

    for number, (tiles, first, last) in enumerate(spans()):

        def numerators(number=number, tiles=tiles, first=first, last=last):
            for side, j in enumerate(tiles):
                state = state_ref[j * HEAD_DIM : (j + 1) * HEAD_DIM, :].astype(jnp.float32)
                lane = lane_iota((HEAD_DIM, LANES))
                for h, lo, hi in tile_heads(j):
                    start = h * HEAD_DIM - first * LANES
                    block = jnp.where((lane >= lo) & (lane < hi), state, 0.0)
                    weights[
                        number, start : start + HEAD_DIM, side * LANES : (side + 1) * LANES
                    ] = block.astype(jnp.bfloat16)
            depth, wide = (last - first) * LANES, len(tiles) * LANES
            numer[:, tiles[0] * LANES : tiles[0] * LANES + wide] = jnp.dot(
                features[:, first * LANES : last * LANES],
                weights[number, :depth, :wide],
                preferred_element_type=jnp.float32,
            )

        pl.when(tiles[0] * LANES < left)(numerators)

        @pl.when(tiles[0] * LANES >= left)
        def _(tiles=tiles):
            numer[:, tiles[0] * LANES : (tiles[-1] + 1) * LANES] = jnp.zeros(
                (total, len(tiles) * LANES), jnp.float32
            )

    column = lax.broadcasted_iota(jnp.int32, (width, LANES), 0)
    for number, (tiles, first, last) in enumerate(spans()):
        for side, j in enumerate(tiles):

            def tile(number=number, side=side, first=first, last=last, j=j):
                lanes = slice(j * LANES, (j + 1) * LANES)
                gain = gain_ref[:, lanes]

                def mixed_row(source, residual, row):
                    here = numer[pl.ds(source, width), first * LANES : last * LANES]
                    squares = (here * here).astype(jnp.bfloat16)
                    mean = jnp.dot(
                        squares,
                        same[
                            number, : (last - first) * LANES, side * LANES : (side + 1) * LANES
                        ],
                        preferred_element_type=jnp.float32,
                    ) * (1.0 / HEAD_DIM)
                    value = numer[pl.ds(source, width), lanes] * lax.rsqrt(mean + 1e-06)
                    mixed = residual.astype(jnp.float32) + value * gain
                    mixed = mixed.astype(jnp.bfloat16).astype(jnp.float32)
                    shifted[1, row] = mixed
                    shifted[0, row] = jnp.where(column == 0, 0.0, pltpu.roll(mixed, 1, 0))
                    shifted[2, row] = jnp.where(
                        column == width - 1, 0.0, pltpu.roll(mixed, width - 1, 0)
                    )

                def mix(row, carry):
                    source = pl.multiple_of(row * width, width)
                    mixed_row(source, residual_ref[pl.ds(source, width), lanes], row + 1)
                    return carry

                lax.fori_loop(0, rows, mix, 0)
                for e in range(edges):
                    mixed_row(tokens + e * width, edge_ref[1, e, :, lanes], place_ref[e])

                def convolve(row, carry):
                    conv_v = jnp.zeros((width, LANES), jnp.float32)
                    conv_g = jnp.zeros((width, LANES), jnp.float32)
                    for tap_row in range(3):
                        for tap_col in range(3):
                            window = shifted[tap_col, row + tap_row]
                            tap = 3 * tap_row + tap_col
                            conv_v = conv_v + vtaps_ref[tap : tap + 1, lanes] * window
                            conv_g = conv_g + gtaps_ref[tap : tap + 1, lanes] * window
                    gate = conv_g / (1.0 + jnp.exp(-conv_g))
                    result = shifted[1, row + 1] + conv_v * gate
                    out_ref[pl.ds(pl.multiple_of(row * width, width), width), lanes] = (
                        result.astype(jnp.bfloat16)
                    )
                    return carry

                lax.fori_loop(0, rows, convolve, 0)

            pl.when(j * LANES < left)(tile)


def mix(place, queries, residual, edge, state, gain, value_taps, gate_taps, rows, width):
    tokens, dim = queries.shape
    edges = edge.shape[1]
    total = tokens + edges * width
    depth = max(last - first for _, first, last in spans()) * LANES
    block = pl.BlockSpec((tokens, GROUP), lambda g: (0, g))
    taps = pl.BlockSpec((value_taps.shape[0], GROUP), lambda g: (0, g))
    return pl.pallas_call(
        functools.partial(mix_kernel, dim, rows, width, edges),
        out_shape=jax.ShapeDtypeStruct((tokens, dim), jnp.bfloat16),
        grid=(cdiv(dim, GROUP),),
        in_specs=[
            pl.BlockSpec(memory_space=pltpu.SMEM),
            block,
            block,
            pl.BlockSpec((2, edges, width, GROUP), lambda g: (0, 0, 0, g)),
            pl.BlockSpec((TILES * HEAD_DIM, LANES), lambda g: (g, 0)),
            pl.BlockSpec((1, GROUP), lambda g: (0, g)),
            taps,
            taps,
        ],
        out_specs=block,
        scratch_shapes=[
            pltpu.VMEM((total, GROUP), jnp.bfloat16),
            pltpu.VMEM((len(spans()), depth, 2 * LANES), jnp.bfloat16),
            pltpu.VMEM((len(spans()), depth, 2 * LANES), jnp.bfloat16),
            pltpu.VMEM((total, GROUP), jnp.float32),
            pltpu.VMEM((3, rows + 2, width, LANES), jnp.float32),
        ],
        compiler_params=pltpu.CompilerParams(vmem_limit_bytes=VMEM_LIMIT),
        cost_estimate=pl.CostEstimate(
            flops=60 * tokens * dim, bytes_accessed=6 * tokens * dim, transcendentals=2 * tokens * dim
        ),
        name="mix",
    )(place, queries, residual, edge, state, gain, value_taps, gate_taps)


def edge_rows(queries, residual, rows, width):
    devices, here = lax.axis_size("space"), lax.axis_index("space")
    dim = queries.shape[-1]
    both = [a.reshape(rows, width, dim) for a in (queries, residual)]
    if devices == 2:
        mine = jnp.stack([jnp.where(here == 0, a[rows - 1 :], a[:1]) for a in both])
        edge = lax.ppermute(mine, "space", [(0, 1), (1, 0)])
        place = jnp.where(here == 0, rows + 1, 0).astype(jnp.int32)[None]
        return edge, place
    up = [(i, i + 1) for i in range(devices - 1)]
    down = [(j, i) for i, j in up]
    before = lax.ppermute(jnp.stack([a[rows - 1 :] for a in both]), "space", up)
    after = lax.ppermute(jnp.stack([a[:1] for a in both]), "space", down)
    return jnp.concatenate([before, after], axis=1), jnp.array([0, rows + 1], jnp.int32)


def share_of_sum(state):
    devices, here = lax.axis_size("space"), lax.axis_index("space")
    if devices != 2:
        return lax.psum_scatter(state, "space", scatter_dimension=0, tiled=True)
    half = state.shape[0] // 2
    halves = state.reshape(2, half, LANES)
    sent = jnp.where(here == 0, halves[1], halves[0])
    kept = jnp.where(here == 0, halves[0], halves[1])
    got = lax.ppermute(sent, "space", [(0, 1), (1, 0)])
    return (kept.astype(jnp.float32) + got.astype(jnp.float32)).astype(jnp.bfloat16)


def prefix_sum(share):
    frames = lax.axis_size("frame")
    pieces = share.reshape(frames, share.shape[0] // frames, LANES)
    pieces = lax.all_to_all(pieces, "frame", split_axis=0, concat_axis=0, tiled=True)
    running = [pieces[0].astype(jnp.float32)]
    for f in range(1, frames):
        running.append(running[-1] + pieces[f].astype(jnp.float32))
    sums = jnp.stack(running).astype(jnp.bfloat16)
    sums = lax.all_to_all(sums, "frame", split_axis=0, concat_axis=0, tiled=True)
    return sums.reshape(share.shape)


def on_device(queries, keys, values, residual, attn_gain, value_taps, gate_taps):
    frames, rows, width, dim = queries.shape
    tokens = frames * rows * width
    flat = lambda a: a.reshape(tokens, dim)
    unit = 16 * lax.axis_size("space") * lax.axis_size("frame")
    state_rows = cdiv(cdiv(dim, LANES) * HEAD_DIM, unit) * unit
    edge, place = edge_rows(queries, residual, rows, width)
    state = frame_states(flat(keys), flat(values), state_rows)
    share = prefix_sum(share_of_sum(state))
    state = lax.all_gather(share, "space", axis=0, tiled=True)
    out = mix(
        place, flat(queries), flat(residual), edge, state, attn_gain[None], value_taps, gate_taps,
        rows, width,
    )
    return out.reshape(frames, rows, width, dim)


def solution(mesh):
    placed = P(("groups", "frame"), "space", None, None)
    return jax.shard_map(
        on_device,
        mesh=mesh,
        in_specs=(placed, placed, placed, placed, P(), P(), P()),
        out_specs=placed,
        check_vma=False,
    )
```

time: 147 us -> 86 us (0.59)
  Pallas kernels: 0 us -> 42.4 us
  waiting for transfers between devices: 52.8 us -> 16.8 us
  local copies, waits for them, and re-layouts: 31.7 us -> 5.51 us
  other arithmetic: 29.8 us -> 7.35 us
  between operations: 13.6 us -> 0.09 us
  matrix products: 9.84 us -> 0 us
  starting transfers between devices: 3.58 us -> 11.3 us
  blocking collectives: 4.43 us -> 2.17 us
    pallas_call x0 -> x2, Pallas kernels: none -> 42.4 us  [the longest x1 36.3 us: mix(): pl.pallas_call(functools.partial(mix_kernel, dim, rows, width, edges), ou...]
    all_gather x1 -> x0, waiting for transfers between devices: 40.3 us -> none  [entering(): everything = lax.all_gather(value.astype(jnp.bfloat16), axis)]
    reshape x5 -> x0, local copies, waits for them, and re-layouts: 25.1 us -> none  [the longest x2 7.69 us: on_device(): feature_queries = jnp.maximum(queries, 0).reshape(tokens, heads, HEAD_DIM)]
    all_to_all x0 -> x2, waiting for transfers between devices: none -> 15.6 us  [the longest x1 8.54 us: prefix_sum(): lax.all_to_all(sums, 'frame', split_axis=0, concat_axis=0, tiled=True)]
    reduce_scatter x1 -> x0, waiting for transfers between devices: 10.8 us -> none  [on_device(): lax.psum_scatter(partial_value_state.astype(jnp.bfloat16), 'space', scatt...]
    all_to_all x0 -> x2, starting transfers between devices: none -> 10.8 us  [the longest x1 7.2 us: prefix_sum(): lax.all_to_all(pieces, 'frame', split_axis=0, concat_axis=0, tiled=True)]
    reshape x1 -> x0, other arithmetic: 9.99 us -> none  [on_device(): return block_out.astype(jnp.bfloat16).reshape(frames, rows, width, dim)]
    dot_general x3 -> x0, matrix products: 9.84 us -> none  [the longest x1 3.78 us: on_device(): jnp.einsum('rag,rap->agp', feature_keys, value_rows, preferred_element_ty...]
  transfers between devices with their start and end apart: 4 -> 4, of which waited for: 3 -> 3; matrix products, arithmetic and copies ran while one was open for 9% -> 8% of each run, Pallas kernels for 0% -> 0%
where the time goes in v1:
time: 86 us; the launch traced here: 85.5 us
  Pallas kernels  42.4 us (49%)
  waiting for transfers between devices  16.8 us (20%)
  starting transfers between devices  11.3 us (13%)
  other arithmetic  7.35 us (9%)
  local copies, waits for them, and re-layouts  5.51 us (6%)
  blocking collectives  2.17 us (3%)
    pallas_call x1, Pallas kernels, mix(): pl.pallas_call(functools.partial(mix_kernel, dim, rows, width, edges), ou...  36.3 us
    all_to_all x1, waiting for transfers between devices, prefix_sum(): lax.all_to_all(sums, 'frame', split_axis=0, concat_axis=0, tiled=True)  8.54 us
    all_to_all x1, starting transfers between devices, prefix_sum(): lax.all_to_all(pieces, 'frame', split_axis=0, concat_axis=0, tiled=True)  7.2 us
    all_to_all x1, waiting for transfers between devices, prefix_sum(): lax.all_to_all(pieces, 'frame', split_axis=0, concat_axis=0, tiled=True)  7.06 us
    pallas_call x1, Pallas kernels, frame_states(): pl.pallas_call(functools.partial(state_kernel, dim), out_shape=jax.ShapeD...  6.03 us
    unnamed x15, local copies, waits for them, and re-layouts  5.5 us
    unnamed x6, other arithmetic  3.77 us
    all_to_all x1, starting transfers between devices, prefix_sum(): lax.all_to_all(sums, 'frame', split_axis=0, concat_axis=0, tiled=True)  3.59 us
  transfers between devices with their start and end apart: 4, of which 3 were waited for; matrix products, arithmetic and copies ran while one was open for 8% of the time, Pallas kernels for 0%

profile of v1, /device:TPU:0, one launch (start us, length us, event | category | flops | bytes accessed | tf_op | source)
XLA Modules:
  0.0 85.5 jit_solution(2548029139907325485)
XLA Ops:
  0.0 1.6 %copy-done.2 = bf16[1,6,80,2240]{3,2,1,0:T(8,128)(2,1)S(1)} copy-done((bf16[1,6,80,2240]{3,2,1,0:T(8,128)(2,1)S(1)}, bf16[1,6,80,2240]{3,2,1,0:T(8,128)(2,1)}, u32[]{:S(2)}) %copy-start.2) | copy-done | bytes 2150424
  1.6 1.6 %copy-done.3 = bf16[1,6,80,2240]{3,2,1,0:T(8,128)(2,1)S(1)} copy-done((bf16[1,6,80,2240]{3,2,1,0:T(8,128)(2,1)S(1)}, bf16[1,6,80,2240]{3,2,1,0:T(8,128)(2,1)}, u32[]{:S(2)}) %copy-start.3) | copy-done | bytes 2150424
  3.2 6.0 %frame_states.1 = bf16[2048,128]{1,0:T(8,128)(2,1)S(1)} custom-call(bf16[480,2240]{1,0:T(8,128)(2,1)S(1)} %bitcast.10, bf16[480,2240]{1,0:T(8,128)(2,1)S(1)} %bitcast.11), custom_call_target="tpu_custom_call" | custom-call | flops 240844800 | bytes 4300800 | tf_op jit(solution)/shard_map/frame_states/pallas_call | solution.py:76
  9.3 0.0 copy-start
  9.3 0.5 collective-permute-start.1
  9.9 1.2 %collective-permute-done.1 = bf16[1024,128]{1,0:T(8,128)(2,1)S(1)} collective-permute-done((bf16[1024,128]{1,0:T(8,128)(2,1)S(1)}, bf16[1024,128]{1,0:T(8,128)(2,1)S(1)}, u32[]{:S(2)}, u32[]{:S(2)}) %collective-permute-start.1) | collective-permute-done | bytes 262176 | tf_op jit(solution)/shard_map/ppermute | solution.py:274
  11.0 0.8 add_convert_fusion
  11.8 7.2 %all-to-all-start = ((bf16[8,128,128]{2,1,0:T(8,128)(2,1)}), bf16[8,128,128]{2,1,0:T(8,128)(2,1)S(1)}, u32[]{:S(2)}, u32[]{:S(2)}) async-start(bf16[8,128,128]{2,1,0:T(8,128)(2,1)} %bitcast.5), calls=%async_computation | async-start | bytes 524288 | tf_op jit(solution)/shard_map/all_to_all | solution.py:281
  19.0 1.2 %slice_select_fusion = (bf16[1,1,80,2240]{3,2,1,0:T(8,128)(2,1)S(1)}, bf16[1,1,80,2240]{3,2,1,0:T(8,128)(2,1)S(1)}) fusion(bf16[1,6,80,2240]{3,2,1,0:T(8,128)(2,1)} %param.10, pred[]{:T(512)S(6)} %eq.2, bf16[1,6,80,2240]{3,2,1,0:T(8,128)(2,1)S(1)} %copy-done), kind=kLoop, calls=%fused_computation.2 | loop fusion | flops 358400 | bytes 2150401 | tf_op jit(solution)/shard_map/jit(_where)/select_n | solution.py:255
  20.3 0.9 %pad_maximum_fusion = bf16[2,1,80,2240]{3,2,1,0:T(8,128)(2,1)} fusion(bf16[1,1,80,2240]{3,2,1,0:T(8,128)(2,1)S(1)} %get-tuple-element.7, bf16[1,1,80,2240]{3,2,1,0:T(8,128)(2,1)S(1)} %get-tuple-element.8), kind=kLoop, calls=%fused_computation | loop fusion | flops 358400 | bytes 1433600 | tf_op jit(solution)/shard_map/stack | solution.py:255
  21.2 7.1 %all-to-all-done = bf16[8,128,128]{2,1,0:T(8,128)(2,1)S(1)} async-done(((bf16[8,128,128]{2,1,0:T(8,128)(2,1)}), bf16[8,128,128]{2,1,0:T(8,128)(2,1)S(1)}, u32[]{:S(2)}, u32[]{:S(2)}) %all-to-all-start) | async-done | bytes 262176 | tf_op jit(solution)/shard_map/all_to_all | solution.py:281
  28.3 0.6 slice_dynamic-update-slice_fusion
  28.9 0.6 fusion.5
  29.5 0.6 convert_dynamic-update-slice_fusion.2
  30.1 0.6 fusion.4
  30.7 0.6 convert_dynamic-update-slice_fusion.1
  31.4 0.6 fusion.3
  32.0 0.6 convert_dynamic-update-slice_fusion
  32.6 0.6 fusion.6
  33.3 3.6 %all-to-all-start.1 = ((bf16[8,128,128]{2,1,0:T(8,128)(2,1)}), bf16[8,128,128]{2,1,0:T(8,128)(2,1)S(1)}, u32[]{:S(2)}, u32[]{:S(2)}) async-start(bf16[8,128,128]{2,1,0:T(8,128)(2,1)} %fusion.6), calls=%async_computation.1 | async-start | bytes 524288 | tf_op jit(solution)/shard_map/all_to_all | solution.py:286
  36.9 8.5 %all-to-all-done.1 = bf16[8,128,128]{2,1,0:T(8,128)(2,1)S(1)} async-done(((bf16[8,128,128]{2,1,0:T(8,128)(2,1)}), bf16[8,128,128]{2,1,0:T(8,128)(2,1)S(1)}, u32[]{:S(2)}, u32[]{:S(2)}) %all-to-all-start.1) | async-done | bytes 262176 | tf_op jit(solution)/shard_map/all_to_all | solution.py:286
  45.4 2.2 %all_gather.3.state_ref = bf16[2048,128]{1,0:T(8,128)(2,1)S(1)} all-gather(bf16[1024,128]{1,0:T(8,128)(2,1)S(1)} %bitcast.12), channel_id=1, replica_groups=mesh['groups'=2,'frame'=8,'space'=2] {'space'}, dimensions={0}, use_global_device_ids=true | all-gather | bytes 786432 | tf_op jit(solution)/shard_map/all_gather | solution.py:299
  47.6 1.6 %copy-done.1 = bf16[1,6,80,2240]{3,2,1,0:T(8,128)(2,1)S(1)} copy-done((bf16[1,6,80,2240]{3,2,1,0:T(8,128)(2,1)S(1)}, bf16[1,6,80,2240]{3,2,1,0:T(8,128)(2,1)}, u32[]{:S(2)}) %copy-start.1) | copy-done | bytes 2150424
  49.2 36.3 %mix.1 = bf16[480,2240]{1,0:T(8,128)(2,1)} custom-call(s32[1]{0:T(128)} %bitcast.place_ref, bf16[480,2240]{1,0:T(8,128)(2,1)S(1)} %bitcast.8, bf16[480,2240]{1,0:T(8,128)(2,1)S(1)} %bitcast.9, bf16[2,1,80,2240]{3,2,1,0:T(8,128)(2,1)S(1)} %collective-permute-done.edge_ref, bf16[2048,128]{1,0:T(8,128)(2,1)S(1)} %all_gather.3.state_ref, ...), custom_call_target="tpu_custom_call" | custom-call | flops 64512000 | bytes 6451200 | tf_op jit(solution)/shard_map/mix/pallas_call | solution.py:220
  (14 shorter events, 0.1 us)
Async XLA Ops:
  0.0 1.6 %copy-start.2 = (bf16[1,6,80,2240]{3,2,1,0:T(8,128)(2,1)S(1)}, bf16[1,6,80,2240]{3,2,1,0:T(8,128)(2,1)}, u32[]{:S(2)}) copy-start(bf16[1,6,80,2240]{3,2,1,0:T(8,128)(2,1)} %param.8) | copy-start | bytes 6451204
  1.6 1.6 %copy-start.3 = (bf16[1,6,80,2240]{3,2,1,0:T(8,128)(2,1)S(1)}, bf16[1,6,80,2240]{3,2,1,0:T(8,128)(2,1)}, u32[]{:S(2)}) copy-start(bf16[1,6,80,2240]{3,2,1,0:T(8,128)(2,1)} %param.9) | copy-start | bytes 6451204
  9.3 9.7 %copy-start = (bf16[1,6,80,2240]{3,2,1,0:T(8,128)(2,1)S(1)}, bf16[1,6,80,2240]{3,2,1,0:T(8,128)(2,1)}, u32[]{:S(2)}) copy-start(bf16[1,6,80,2240]{3,2,1,0:T(8,128)(2,1)} %param.7) | copy-start | bytes 6451204
  9.3 1.7 %collective-permute-start.1 = (bf16[1024,128]{1,0:T(8,128)(2,1)S(1)}, bf16[1024,128]{1,0:T(8,128)(2,1)S(1)}, u32[]{:S(2)}, u32[]{:S(2)}) collective-permute-start(bf16[1024,128]{1,0:T(8,128)(2,1)S(1)} %broadcast_select_fusion), channel_id=1, source_target_pairs={{0,1},{1,0},{2,3},{3,2},{4,5},{5,4},{6,7},{7,6},{8,9},{9,8},{10,11... | collective-permute-start | bytes 786440 | tf_op jit(solution)/shard_map/ppermute | solution.py:274
  11.8 16.4 %all-to-all-start = ((bf16[8,128,128]{2,1,0:T(8,128)(2,1)}), bf16[8,128,128]{2,1,0:T(8,128)(2,1)S(1)}, u32[]{:S(2)}, u32[]{:S(2)}) async-start(bf16[8,128,128]{2,1,0:T(8,128)(2,1)} %bitcast.5), calls=%async_computation | async-start | bytes 524288 | tf_op jit(solution)/shard_map/all_to_all | solution.py:281
  19.0 17.8 %copy-start.6 = (f32[2240]{0:T(1024)S(1)}, f32[2240]{0:T(1024)}, u32[]{:S(2)}) copy-start(f32[2240]{0:T(1024)} %param.11) | copy-start | bytes 26884
  20.2 27.4 %copy-start.4 = (f32[9,2240]{1,0:T(8,128)S(1)}, f32[9,2240]{1,0:T(8,128)}, u32[]{:S(2)}) copy-start(f32[9,2240]{1,0:T(8,128)} %vtaps_ref.1) | copy-start | bytes 241924
  20.2 27.4 %copy-start.5 = (f32[9,2240]{1,0:T(8,128)S(1)}, f32[9,2240]{1,0:T(8,128)}, u32[]{:S(2)}) copy-start(f32[9,2240]{1,0:T(8,128)} %gtaps_ref.1) | copy-start | bytes 241924
  21.2 26.4 %collective-permute-start = (bf16[2,1,80,2240]{3,2,1,0:T(8,128)(2,1)}, bf16[2,1,80,2240]{3,2,1,0:T(8,128)(2,1)S(1)}, u32[]{:S(2)}, u32[]{:S(2)}) collective-permute-start(bf16[2,1,80,2240]{3,2,1,0:T(8,128)(2,1)} %pad_maximum_fusion), channel_id=1, source_target_pairs={{0,1},{1,0},{2,3},{3,2},{4,5},{5,4},{6,7},{7,6},{8,9},{9,8},{10,11... | collective-permute-start | bytes 2150408 | tf_op jit(solution)/shard_map/ppermute | solution.py:256
  33.3 12.2 %all-to-all-start.1 = ((bf16[8,128,128]{2,1,0:T(8,128)(2,1)}), bf16[8,128,128]{2,1,0:T(8,128)(2,1)S(1)}, u32[]{:S(2)}, u32[]{:S(2)}) async-start(bf16[8,128,128]{2,1,0:T(8,128)(2,1)} %fusion.6), calls=%async_computation.1 | async-start | bytes 524288 | tf_op jit(solution)/shard_map/all_to_all | solution.py:286
  47.6 1.6 %copy-start.1 = (bf16[1,6,80,2240]{3,2,1,0:T(8,128)(2,1)S(1)}, bf16[1,6,80,2240]{3,2,1,0:T(8,128)(2,1)}, u32[]{:S(2)}) copy-start(bf16[1,6,80,2240]{3,2,1,0:T(8,128)(2,1)} %param.10) | copy-start | bytes 6451204

commit v2 on v1

v2 whole, which is shorter than its diff:
```python
import functools
import math

import jax
import jax.numpy as jnp
from jax import lax
from jax.experimental import pallas as pl
from jax.experimental.pallas import tpu as pltpu
from jax.sharding import PartitionSpec as P

HEAD_DIM = 112
LANES = 128
GROUP = math.lcm(HEAD_DIM, LANES)
TILES = GROUP // LANES
VMEM_LIMIT = 60 * 2**20


def cdiv(a, b):
    return -(-a // b)


def lane_iota(shape):
    return lax.broadcasted_iota(jnp.int32, shape, len(shape) - 1)


def tile_heads(j, lanes):
    lo, hi = j * LANES, min((j + 1) * LANES, lanes)
    heads = range(lo // HEAD_DIM, cdiv(hi, HEAD_DIM))
    return [(h, max(h * HEAD_DIM - lo, 0), min((h + 1) * HEAD_DIM - lo, LANES)) for h in heads]


def spans(lanes):
    count = cdiv(lanes, LANES)
    result = []
    for j in range(0, count, 2):
        tiles = list(range(j, min(j + 2, count)))
        first = tile_heads(tiles[0], lanes)[0][0] * HEAD_DIM // LANES
        last = cdiv((tile_heads(tiles[-1], lanes)[-1][0] + 1) * HEAD_DIM, LANES)
        result.append((tiles, first, last))
    return result


def by_group(dim, body):
    full, rest = divmod(dim, GROUP)
    if full:
        pl.when(pl.program_id(0) < full)(lambda: body(GROUP))
    if rest:
        pl.when(pl.program_id(0) >= full)(lambda: body(rest))


def state_kernel(dim, keys_ref, values_ref, state_ref, turned):
    def body(lanes):
        turned[...] = jnp.maximum(keys_ref[...], 0).T
        lane = lane_iota((HEAD_DIM, LANES))
        for tiles, _, _ in spans(lanes):
            begin = tile_heads(tiles[0], lanes)[0][0]
            end = tile_heads(tiles[-1], lanes)[-1][0] + 1
            product = jnp.dot(
                turned[begin * HEAD_DIM : end * HEAD_DIM, :],
                values_ref[:, tiles[0] * LANES : (tiles[-1] + 1) * LANES],
                preferred_element_type=jnp.float32,
            )
            for side, j in enumerate(tiles):
                total = jnp.zeros((HEAD_DIM, LANES), jnp.float32)
                for h, lo, hi in tile_heads(j, lanes):
                    part = product[
                        (h - begin) * HEAD_DIM : (h - begin + 1) * HEAD_DIM,
                        side * LANES : (side + 1) * LANES,
                    ]
                    total = jnp.where((lane >= lo) & (lane < hi), part, total)
                state_ref[j * HEAD_DIM : (j + 1) * HEAD_DIM, :] = total.astype(jnp.bfloat16)
        unused = (TILES - cdiv(lanes, LANES)) * HEAD_DIM
        if unused:
            state_ref[TILES * HEAD_DIM - unused :, :] = jnp.zeros((unused, LANES), jnp.bfloat16)

    by_group(dim, body)


def frame_states(keys, values, rows):
    tokens, dim = keys.shape
    return pl.pallas_call(
        functools.partial(state_kernel, dim),
        out_shape=jax.ShapeDtypeStruct((rows, LANES), jnp.bfloat16),
        grid=(cdiv(dim, GROUP),),
        in_specs=[pl.BlockSpec((tokens, GROUP), lambda g: (0, g))] * 2,
        out_specs=pl.BlockSpec((TILES * HEAD_DIM, LANES), lambda g: (g, 0)),
        scratch_shapes=[pltpu.VMEM((GROUP, tokens), jnp.bfloat16)],
        compiler_params=pltpu.CompilerParams(vmem_limit_bytes=VMEM_LIMIT),
        cost_estimate=pl.CostEstimate(
            flops=2 * tokens * dim * HEAD_DIM, bytes_accessed=4 * tokens * dim, transcendentals=0
        ),
        name="frame_states",
    )(keys, values)


def mix_kernel(
    dim, rows, width, edges,
    place_ref, queries_ref, residual_ref, edge_ref, state_ref, gain_ref, vtaps_ref, gtaps_ref,
    out_ref,
    features, weights, same, numer, squares, shifted,
):
    tokens = rows * width
    total = tokens + edges * width

    @pl.when(pl.program_id(0) == 0)
    def _():
        weights[...] = jnp.zeros_like(weights)
        same[...] = jnp.zeros_like(same)
        lane = lane_iota((HEAD_DIM, LANES))
        for number, (tiles, first, _) in enumerate(spans(min(GROUP, dim))):
            for side, j in enumerate(tiles):
                for h, lo, hi in tile_heads(j, GROUP):
                    start = h * HEAD_DIM - first * LANES
                    block = jnp.where((lane >= lo) & (lane < hi), 1.0, 0.0)
                    same[
                        number, start : start + HEAD_DIM, side * LANES : (side + 1) * LANES
                    ] = block.astype(jnp.bfloat16)
        for row in (0, rows + 1):
            shifted[:, row] = jnp.zeros((3, width, LANES), jnp.float32)

    zero = jnp.zeros((), jnp.bfloat16)
    column = lax.broadcasted_iota(jnp.int32, (width, LANES), 0)
    lane = lane_iota((HEAD_DIM, LANES))

    def store_shifted(mixed, row):
        mixed = mixed.astype(jnp.bfloat16).astype(jnp.float32)
        shifted[1, row] = mixed
        shifted[0, row] = jnp.where(column == 0, 0.0, pltpu.roll(mixed, 1, 0))
        shifted[2, row] = jnp.where(column == width - 1, 0.0, pltpu.roll(mixed, width - 1, 0))

    def body(lanes):
        count = cdiv(lanes, LANES)
        end = count * LANES
        inside = lane_iota((1, end)) < lanes

        def feature(queries):
            queries = jnp.maximum(queries, zero)
            return queries if lanes == end else jnp.where(inside, queries, zero)

        features[:tokens, :end] = feature(queries_ref[:, :end])
        for e in range(edges):
            features[tokens + e * width : tokens + (e + 1) * width, :end] = feature(
                edge_ref[0, e, :, :end]
            )
        for number, (tiles, first, last) in enumerate(spans(lanes)):
            for side, j in enumerate(tiles):
                state = state_ref[j * HEAD_DIM : (j + 1) * HEAD_DIM, :].astype(jnp.float32)
                for h, lo, hi in tile_heads(j, lanes):
                    start = h * HEAD_DIM - first * LANES
                    block = jnp.where((lane >= lo) & (lane < hi), state, 0.0)
                    weights[
                        number, start : start + HEAD_DIM, side * LANES : (side + 1) * LANES
                    ] = block.astype(jnp.bfloat16)
            depth, wide = (last - first) * LANES, len(tiles) * LANES
            product = jnp.dot(
                features[:, first * LANES : last * LANES],
                weights[number, :depth, :wide],
                preferred_element_type=jnp.float32,
            )
            here = slice(tiles[0] * LANES, tiles[0] * LANES + wide)
            numer[:, here] = product
            squares[:, here] = (product * product).astype(jnp.bfloat16)

        for number, (tiles, first, last) in enumerate(spans(lanes)):
            depth, wide = (last - first) * LANES, len(tiles) * LANES
            sums = jnp.dot(
                squares[:, first * LANES : last * LANES],
                same[number, :depth, :wide],
                preferred_element_type=jnp.float32,
            )
            here = slice(tiles[0] * LANES, tiles[0] * LANES + wide)
            scale = lax.rsqrt(sums * (1.0 / HEAD_DIM) + 1e-06)
            numer[:, here] = numer[:, here] * scale * gain_ref[:, here]

        for j in range(count):
            here = slice(j * LANES, (j + 1) * LANES)
            for row in range(rows):
                source = slice(row * width, (row + 1) * width)
                store_shifted(
                    residual_ref[source, here].astype(jnp.float32) + numer[source, here], row + 1
                )
            for e in range(edges):
                source = slice(tokens + e * width, tokens + (e + 1) * width)
                store_shifted(
                    edge_ref[1, e, :, here].astype(jnp.float32) + numer[source, here], place_ref[e]
                )

            def convolve(row, carry, here=here):
                conv_v = jnp.zeros((width, LANES), jnp.float32)
                half_g = jnp.zeros((width, LANES), jnp.float32)
                for tap_row in range(3):
                    for tap_col in range(3):
                        window = shifted[tap_col, row + tap_row]
                        tap = 3 * tap_row + tap_col
                        conv_v = conv_v + vtaps_ref[tap : tap + 1, here] * window
                        half_g = half_g + (0.5 * gtaps_ref[tap : tap + 1, here]) * window
                gate = half_g + half_g * jnp.tanh(half_g)
                result = shifted[1, row + 1] + conv_v * gate
                out_ref[pl.ds(pl.multiple_of(row * width, width), width), here] = result.astype(
                    jnp.bfloat16
                )
                return carry

            lax.fori_loop(0, rows, convolve, 0)

    by_group(dim, body)


def mix(place, queries, residual, edge, state, gain, value_taps, gate_taps, rows, width):
    tokens, dim = queries.shape
    edges = edge.shape[1]
    total = tokens + edges * width
    pairs = spans(min(GROUP, dim))
    depth = max(last - first for _, first, last in pairs) * LANES
    block = pl.BlockSpec((tokens, GROUP), lambda g: (0, g))
    taps = pl.BlockSpec((value_taps.shape[0], GROUP), lambda g: (0, g))
    return pl.pallas_call(
        functools.partial(mix_kernel, dim, rows, width, edges),
        out_shape=jax.ShapeDtypeStruct((tokens, dim), jnp.bfloat16),
        grid=(cdiv(dim, GROUP),),
        in_specs=[
            pl.BlockSpec(memory_space=pltpu.SMEM),
            block,
            block,
            pl.BlockSpec((2, edges, width, GROUP), lambda g: (0, 0, 0, g)),
            pl.BlockSpec((TILES * HEAD_DIM, LANES), lambda g: (g, 0)),
            pl.BlockSpec((1, GROUP), lambda g: (0, g)),
            taps,
            taps,
        ],
        out_specs=block,
        scratch_shapes=[
            pltpu.VMEM((total, GROUP), jnp.bfloat16),
            pltpu.VMEM((len(pairs), depth, 2 * LANES), jnp.bfloat16),
            pltpu.VMEM((len(pairs), depth, 2 * LANES), jnp.bfloat16),
            pltpu.VMEM((total, GROUP), jnp.float32),
            pltpu.VMEM((total, GROUP), jnp.bfloat16),
            pltpu.VMEM((3, rows + 2, width, LANES), jnp.float32),
        ],
        compiler_params=pltpu.CompilerParams(vmem_limit_bytes=VMEM_LIMIT),
        cost_estimate=pl.CostEstimate(
            flops=60 * tokens * dim, bytes_accessed=6 * tokens * dim, transcendentals=2 * tokens * dim
        ),
        name="mix",
    )(place, queries, residual, edge, state, gain, value_taps, gate_taps)


def edge_rows(queries, residual, rows, width):
    devices, here = lax.axis_size("space"), lax.axis_index("space")
    dim = queries.shape[-1]
    both = [a.reshape(rows, width, dim) for a in (queries, residual)]
    if devices == 2:
        mine = jnp.stack([jnp.where(here == 0, a[rows - 1 :], a[:1]) for a in both])
        edge = lax.ppermute(mine, "space", [(0, 1), (1, 0)])
        place = jnp.where(here == 0, rows + 1, 0).astype(jnp.int32)[None]
        return edge, place
    up = [(i, i + 1) for i in range(devices - 1)]
    down = [(j, i) for i, j in up]
    before = lax.ppermute(jnp.stack([a[rows - 1 :] for a in both]), "space", up)
    after = lax.ppermute(jnp.stack([a[:1] for a in both]), "space", down)
    return jnp.concatenate([before, after], axis=1), jnp.array([0, rows + 1], jnp.int32)


def share_of_sum(state):
    devices, here = lax.axis_size("space"), lax.axis_index("space")
    if devices != 2:
        return lax.psum_scatter(state, "space", scatter_dimension=0, tiled=True)
    half = state.shape[0] // 2
    halves = state.reshape(2, half, LANES)
    sent = jnp.where(here == 0, halves[1], halves[0])
    kept = jnp.where(here == 0, halves[0], halves[1])
    got = lax.ppermute(sent, "space", [(0, 1), (1, 0)])
    return (kept.astype(jnp.float32) + got.astype(jnp.float32)).astype(jnp.bfloat16)


def running_sum_kernel(pieces_ref, sums_ref):
    running = jnp.zeros(pieces_ref.shape[1:], jnp.float32)
    for f in range(pieces_ref.shape[0]):
        running = running + pieces_ref[f].astype(jnp.float32)
        sums_ref[f] = running.astype(jnp.bfloat16)


def prefix_sum(share):
    frames = lax.axis_size("frame")
    pieces = share.reshape(frames, share.shape[0] // frames, LANES)
    pieces = lax.all_to_all(pieces, "frame", split_axis=0, concat_axis=0, tiled=True)
    sums = pl.pallas_call(
        running_sum_kernel,
        out_shape=jax.ShapeDtypeStruct(pieces.shape, jnp.bfloat16),
        name="running_sum",
    )(pieces)
    sums = lax.all_to_all(sums, "frame", split_axis=0, concat_axis=0, tiled=True)
    return sums.reshape(share.shape)


def on_device(queries, keys, values, residual, attn_gain, value_taps, gate_taps):
    frames, rows, width, dim = queries.shape
    tokens = frames * rows * width
    flat = lambda a: a.reshape(tokens, dim)
    unit = 16 * lax.axis_size("space") * lax.axis_size("frame")
    state_rows = cdiv(cdiv(dim, LANES) * HEAD_DIM, unit) * unit
    edge, place = edge_rows(queries, residual, rows, width)
    state = frame_states(flat(keys), flat(values), state_rows)
    share = prefix_sum(share_of_sum(state))
    state = lax.all_gather(share, "space", axis=0, tiled=True)
    out = mix(
        place, flat(queries), flat(residual), edge, state, attn_gain[None], value_taps, gate_taps,
        rows, width,
    )
    return out.reshape(frames, rows, width, dim)


def solution(mesh):
    placed = P(("groups", "frame"), "space", None, None)
    return jax.shard_map(
        on_device,
        mesh=mesh,
        in_specs=(placed, placed, placed, placed, P(), P(), P()),
        out_specs=placed,
        check_vma=False,
    )
```

time: 86 us -> 58.1 us (0.68)
  Pallas kernels: 42.4 us -> 20.7 us
  other arithmetic: 7.35 us -> 3.39 us
  local copies, waits for them, and re-layouts: 5.51 us -> 2.18 us
  waiting for transfers between devices: 16.8 us -> 17.7 us
    pallas_call x1, Pallas kernels: 36.3 us -> 14.7 us  [mix(): pl.pallas_call(functools.partial(mix_kernel, dim, rows, width, edges), ou...]
    unnamed x15 -> x8, local copies, waits for them, and re-layouts: 5.5 us -> 1.58 us
    unnamed x6 -> x0, other arithmetic: 3.77 us -> none
    all_to_all x1, waiting for transfers between devices: 7.06 us -> 9.22 us  [prefix_sum(): lax.all_to_all(pieces, 'frame', split_axis=0, concat_axis=0, tiled=True)]
    pallas_call x1, Pallas kernels: 6.03 us -> 4.31 us  [frame_states(): pl.pallas_call(functools.partial(state_kernel, dim), out_shape=jax.ShapeD...]
    pallas_call x0 -> x1, Pallas kernels: none -> 1.7 us  [prefix_sum(): pl.pallas_call(running_sum_kernel, out_shape=jax.ShapeDtypeStruct(pieces....]
    ppermute x1, waiting for transfers between devices: 1.16 us -> 0.01 us  [share_of_sum(): got = lax.ppermute(sent, 'space', [(0, 1), (1, 0)])]
    select_n x1, other arithmetic: 0.03 us -> 1.12 us  [share_of_sum(): sent = jnp.where(here == 0, halves[1], halves[0])]
  transfers between devices with their start and end apart: 4 -> 4, of which waited for: 3 -> 2; matrix products, arithmetic and copies ran while one was open for 8% -> 4% of each run, Pallas kernels for 0% -> 3%
where the time goes in v2:
time: 58.1 us; the launch traced here: 57.6 us
  Pallas kernels  20.7 us (36%)
  waiting for transfers between devices  17.7 us (30%)
  starting transfers between devices  11.3 us (19%)
  other arithmetic  3.39 us (6%)
  blocking collectives  2.3 us (4%)
  local copies, waits for them, and re-layouts  2.18 us (4%)
    pallas_call x1, Pallas kernels, mix(): pl.pallas_call(functools.partial(mix_kernel, dim, rows, width, edges), ou...  14.7 us
    all_to_all x1, waiting for transfers between devices, prefix_sum(): lax.all_to_all(pieces, 'frame', split_axis=0, concat_axis=0, tiled=True)  9.22 us
    all_to_all x1, waiting for transfers between devices, prefix_sum(): lax.all_to_all(sums, 'frame', split_axis=0, concat_axis=0, tiled=True)  8.47 us
    all_to_all x1, starting transfers between devices, prefix_sum(): lax.all_to_all(pieces, 'frame', split_axis=0, concat_axis=0, tiled=True)  6.94 us
    pallas_call x1, Pallas kernels, frame_states(): pl.pallas_call(functools.partial(state_kernel, dim), out_shape=jax.ShapeD...  4.31 us
    all_to_all x1, starting transfers between devices, prefix_sum(): lax.all_to_all(sums, 'frame', split_axis=0, concat_axis=0, tiled=True)  3.59 us
    all_gather x1, blocking collectives, on_device(): state = lax.all_gather(share, 'space', axis=0, tiled=True)  2.3 us
    pallas_call x1, Pallas kernels, prefix_sum(): pl.pallas_call(running_sum_kernel, out_shape=jax.ShapeDtypeStruct(pieces....  1.7 us
  transfers between devices with their start and end apart: 4, of which 2 were waited for; matrix products, arithmetic and copies ran while one was open for 4% of the time, Pallas kernels for 3%

profile of v2, /device:TPU:0, one launch (start us, length us, event | category | flops | bytes accessed | tf_op | source)
XLA Modules:
  0.0 57.6 jit_solution(6689392513277397682)
XLA Ops:
  0.0 4.3 %frame_states.1 = bf16[2048,128]{1,0:T(8,128)(2,1)} custom-call(bf16[480,2240]{1,0:T(8,128)(2,1)} %bitcast.10, bf16[480,2240]{1,0:T(8,128)(2,1)} %bitcast.11), custom_call_target="tpu_custom_call" | custom-call | flops 240844800 | bytes 4300800 | tf_op jit(solution)/shard_map/frame_states/pallas_call | solution.py:81
  4.3 0.0 copy-start
  4.3 1.1 %broadcast_select_fusion = bf16[1024,128]{1,0:T(8,128)(2,1)S(1)} fusion(pred[]{:T(512)S(6)} %eq.2, bf16[2048,128]{1,0:T(8,128)(2,1)} %frame_states.1), kind=kLoop, calls=%fused_computation.4 | loop fusion | flops 131072 | bytes 786433 | tf_op jit(solution)/shard_map/jit(_where)/select_n | solution.py:270
  5.4 0.5 collective-permute-start.1
  6.0 1.4 %slice_select_fusion = (bf16[1,1,80,2240]{3,2,1,0:T(8,128)(2,1)S(1)}, bf16[1,1,80,2240]{3,2,1,0:T(8,128)(2,1)S(1)}) fusion(bf16[1,6,80,2240]{3,2,1,0:T(8,128)(2,1)} %param.10, pred[]{:T(512)S(6)} %eq.2, bf16[1,6,80,2240]{3,2,1,0:T(8,128)(2,1)} %param.7), kind=kLoop, calls=%fused_computation.2 | loop fusion | flops 358400 | bytes 2150401 | tf_op jit(solution)/shard_map/jit(_where)/select_n | solution.py:253
  7.4 0.0 copy-start.3
  7.4 0.0 collective-permute-done.1
  7.4 0.0 copy-done
  7.4 0.8 %add_convert_fusion = bf16[1024,128]{1,0:T(8,128)(2,1)} fusion(bf16[1024,128]{1,0:T(8,128)(2,1)S(1)} %collective-permute-done.1, pred[]{:T(512)S(6)} %eq.2, bf16[2048,128]{1,0:T(8,128)(2,1)S(1)} %copy-done), kind=kLoop, calls=%fused_computation.1 | loop fusion | flops 655360 | bytes 1048577 | tf_op jit(solution)/shard_map/convert_element_type | solution.py:273
  8.2 6.9 %all-to-all-start = ((bf16[8,128,128]{2,1,0:T(8,128)(2,1)}), bf16[8,128,128]{2,1,0:T(8,128)(2,1)S(1)}, u32[]{:S(2)}, u32[]{:S(2)}) async-start(bf16[8,128,128]{2,1,0:T(8,128)(2,1)} %bitcast.5), calls=%async_computation | async-start | bytes 524288 | tf_op jit(solution)/shard_map/all_to_all | solution.py:286
  15.1 0.1 pad_maximum_fusion
  15.2 0.2 collective-permute-start
  15.4 9.2 %all-to-all-done.pieces_ref = bf16[8,128,128]{2,1,0:T(8,128)(2,1)S(1)} async-done(((bf16[8,128,128]{2,1,0:T(8,128)(2,1)}), bf16[8,128,128]{2,1,0:T(8,128)(2,1)S(1)}, u32[]{:S(2)}, u32[]{:S(2)}) %all-to-all-start) | async-done | bytes 262176 | tf_op jit(solution)/shard_map/all_to_all | solution.py:286
  24.6 0.0 copy-start.1
  24.6 0.7 %copy-done.1 = bf16[8,128,128]{2,1,0:T(8,128)(2,1)} copy-done((bf16[8,128,128]{2,1,0:T(8,128)(2,1)}, bf16[8,128,128]{2,1,0:T(8,128)(2,1)S(1)}, u32[]{:S(2)}) %copy-start.1) | copy-done | bytes 262168
  25.3 1.7 %running_sum.1 = bf16[8,128,128]{2,1,0:T(8,128)(2,1)} custom-call(bf16[8,128,128]{2,1,0:T(8,128)(2,1)} %copy-done.1), custom_call_target="tpu_custom_call" | custom-call | tf_op jit(solution)/shard_map/running_sum/pallas_call | solution.py:287
  27.1 3.6 %all-to-all-start.1 = ((bf16[8,128,128]{2,1,0:T(8,128)(2,1)}), bf16[8,128,128]{2,1,0:T(8,128)(2,1)S(1)}, u32[]{:S(2)}, u32[]{:S(2)}) async-start(bf16[8,128,128]{2,1,0:T(8,128)(2,1)} %running_sum.1), calls=%async_computation.1 | async-start | bytes 524288 | tf_op jit(solution)/shard_map/all_to_all | solution.py:292
  30.6 0.0 copy-done.3
  30.6 0.6 %broadcast_in_dim.7.gain_ref = f32[1,2240]{1,0:T(1,128)} reshape(f32[2240]{0:T(1024)S(1)} %copy-done.3) | data formatting | bytes 17920 | tf_op jit(solution)/shard_map/broadcast_in_dim | solution.py:307
  31.2 8.5 %all-to-all-done.1 = bf16[8,128,128]{2,1,0:T(8,128)(2,1)S(1)} async-done(((bf16[8,128,128]{2,1,0:T(8,128)(2,1)}), bf16[8,128,128]{2,1,0:T(8,128)(2,1)S(1)}, u32[]{:S(2)}, u32[]{:S(2)}) %all-to-all-start.1) | async-done | bytes 262176 | tf_op jit(solution)/shard_map/all_to_all | solution.py:292
  39.7 2.3 %all_gather.3.state_ref = bf16[2048,128]{1,0:T(8,128)(2,1)} all-gather(bf16[1024,128]{1,0:T(8,128)(2,1)S(1)} %bitcast.12), channel_id=1, replica_groups=mesh['groups'=2,'frame'=8,'space'=2] {'space'}, dimensions={0}, use_global_device_ids=true | all-gather | bytes 786432 | tf_op jit(solution)/shard_map/all_gather | solution.py:305
  42.0 0.0 collective-permute-done.edge_ref
  42.0 0.9 %copy-done.2 = bf16[2,1,80,2240]{3,2,1,0:T(8,128)(2,1)} copy-done((bf16[2,1,80,2240]{3,2,1,0:T(8,128)(2,1)}, bf16[2,1,80,2240]{3,2,1,0:T(8,128)(2,1)S(1)}, u32[]{:S(2)}) %copy-start.2) | copy-done | bytes 716824
  42.9 14.7 %mix.1 = bf16[480,2240]{1,0:T(8,128)(2,1)} custom-call(s32[1]{0:T(128)} %bitcast.place_ref, bf16[480,2240]{1,0:T(8,128)(2,1)} %bitcast.8, bf16[480,2240]{1,0:T(8,128)(2,1)} %bitcast.9, bf16[2,1,80,2240]{3,2,1,0:T(8,128)(2,1)} %copy-done.2, bf16[2048,128]{1,0:T(8,128)(2,1)} %all_gather.3.state_ref, f32[1,2240]{1,0:T(1,128)} %broadcast_in_dim.7.gain_ref, ...), custom_call_target="tpu_custom_call" | custom-call | flops 64512000 | bytes 6451200 | tf_op jit(solution)/shard_map/mix/pallas_call | solution.py:217
  (1 shorter events, 0.0 us)
Async XLA Ops:
  4.3 3.1 %copy-start = (bf16[2048,128]{1,0:T(8,128)(2,1)S(1)}, bf16[2048,128]{1,0:T(8,128)(2,1)}, u32[]{:S(2)}) copy-start(bf16[2048,128]{1,0:T(8,128)(2,1)} %frame_states.1) | copy-start | bytes 1572868
  5.4 1.9 %collective-permute-start.1 = (bf16[1024,128]{1,0:T(8,128)(2,1)S(1)}, bf16[1024,128]{1,0:T(8,128)(2,1)S(1)}, u32[]{:S(2)}, u32[]{:S(2)}) collective-permute-start(bf16[1024,128]{1,0:T(8,128)(2,1)S(1)} %broadcast_select_fusion), channel_id=1, source_target_pairs={{0,1},{1,0},{2,3},{3,2},{4,5},{5,4},{6,7},{7,6},{8,9},{9,8},{10,11... | collective-permute-start | bytes 786440 | tf_op jit(solution)/shard_map/ppermute | solution.py:272
  7.4 23.3 %copy-start.3 = (f32[2240]{0:T(1024)S(1)}, f32[2240]{0:T(1024)}, u32[]{:S(2)}) copy-start(f32[2240]{0:T(1024)} %param.11) | copy-start | bytes 26884
  8.2 16.4 %all-to-all-start = ((bf16[8,128,128]{2,1,0:T(8,128)(2,1)}), bf16[8,128,128]{2,1,0:T(8,128)(2,1)S(1)}, u32[]{:S(2)}, u32[]{:S(2)}) async-start(bf16[8,128,128]{2,1,0:T(8,128)(2,1)} %bitcast.5), calls=%async_computation | async-start | bytes 524288 | tf_op jit(solution)/shard_map/all_to_all | solution.py:286
  15.2 26.8 %collective-permute-start = (bf16[2,1,80,2240]{3,2,1,0:T(8,128)(2,1)S(1)}, bf16[2,1,80,2240]{3,2,1,0:T(8,128)(2,1)S(1)}, u32[]{:S(2)}, u32[]{:S(2)}) collective-permute-start(bf16[2,1,80,2240]{3,2,1,0:T(8,128)(2,1)S(1)} %pad_maximum_fusion), channel_id=1, source_target_pairs={{0,1},{1,0},{2,3},{3,2},{4,5},{5,4},{6,7},{7,6},{8,9},{9,8},{10,11... | collective-permute-start | bytes 2150408 | tf_op jit(solution)/shard_map/ppermute | solution.py:254
  24.6 0.7 %copy-start.1 = (bf16[8,128,128]{2,1,0:T(8,128)(2,1)}, bf16[8,128,128]{2,1,0:T(8,128)(2,1)S(1)}, u32[]{:S(2)}) copy-start(bf16[8,128,128]{2,1,0:T(8,128)(2,1)S(1)} %all-to-all-done.pieces_ref) | copy-start | bytes 786436
  27.1 12.7 %all-to-all-start.1 = ((bf16[8,128,128]{2,1,0:T(8,128)(2,1)}), bf16[8,128,128]{2,1,0:T(8,128)(2,1)S(1)}, u32[]{:S(2)}, u32[]{:S(2)}) async-start(bf16[8,128,128]{2,1,0:T(8,128)(2,1)} %running_sum.1), calls=%async_computation.1 | async-start | bytes 524288 | tf_op jit(solution)/shard_map/all_to_all | solution.py:292
  42.0 0.9 %copy-start.2 = (bf16[2,1,80,2240]{3,2,1,0:T(8,128)(2,1)}, bf16[2,1,80,2240]{3,2,1,0:T(8,128)(2,1)S(1)}, u32[]{:S(2)}) copy-start(bf16[2,1,80,2240]{3,2,1,0:T(8,128)(2,1)S(1)} %collective-permute-done.edge_ref) | copy-start | bytes 2150404

commit v3 on v2

--- a/solution.py
+++ b/solution.py
@@ -12,7 +12,6 @@
 LANES = 128
 GROUP = math.lcm(HEAD_DIM, LANES)
 TILES = GROUP // LANES
-VMEM_LIMIT = 60 * 2**20
 
 
 def cdiv(a, b):
@@ -48,7 +47,10 @@
         pl.when(pl.program_id(0) >= full)(lambda: body(rest))
 
 
-def state_kernel(dim, keys_ref, values_ref, state_ref, turned):
+def state_kernel(dim, spot_ref, keys_ref, values_ref, *refs):
+    *parts, turned, whole = refs
+    step = pl.program_id(0)
+
     def body(lanes):
         turned[...] = jnp.maximum(keys_ref[...], 0).T
         lane = lane_iota((HEAD_DIM, LANES))
@@ -68,37 +70,50 @@
                         side * LANES : (side + 1) * LANES,
                     ]
                     total = jnp.where((lane >= lo) & (lane < hi), part, total)
-                state_ref[j * HEAD_DIM : (j + 1) * HEAD_DIM, :] = total.astype(jnp.bfloat16)
-        unused = (TILES - cdiv(lanes, LANES)) * HEAD_DIM
-        if unused:
-            state_ref[TILES * HEAD_DIM - unused :, :] = jnp.zeros((unused, LANES), jnp.bfloat16)
+                row = pl.multiple_of((step * TILES + j) * HEAD_DIM, 16)
+                whole[pl.ds(row, HEAD_DIM), :] = total.astype(jnp.bfloat16)
 
     by_group(dim, body)
 
-
-def frame_states(keys, values, rows):
+    @pl.when(step == pl.num_programs(0) - 1)
+    def _():
+        used = cdiv(dim, LANES) * HEAD_DIM
+        if used < whole.shape[0]:
+            whole[used:, :] = jnp.zeros((whole.shape[0] - used, LANES), jnp.bfloat16)
+        for k, part in enumerate(parts):
+            size = part.shape[0]
+            row = pl.multiple_of(lax.rem(spot_ref[0] + k, len(parts)) * size, 16)
+            part[...] = whole[pl.ds(row, size), :]
+
+
+def frame_states(spot, keys, values, rows, parts):
     tokens, dim = keys.shape
+    part = (rows // parts, LANES)
+    block = pl.BlockSpec((tokens, GROUP), lambda g: (0, g))
     return pl.pallas_call(
         functools.partial(state_kernel, dim),
-        out_shape=jax.ShapeDtypeStruct((rows, LANES), jnp.bfloat16),
+        out_shape=[jax.ShapeDtypeStruct(part, jnp.bfloat16)] * parts,
         grid=(cdiv(dim, GROUP),),
-        in_specs=[pl.BlockSpec((tokens, GROUP), lambda g: (0, g))] * 2,
-        out_specs=pl.BlockSpec((TILES * HEAD_DIM, LANES), lambda g: (g, 0)),
-        scratch_shapes=[pltpu.VMEM((GROUP, tokens), jnp.bfloat16)],
-        compiler_params=pltpu.CompilerParams(vmem_limit_bytes=VMEM_LIMIT),
+        in_specs=[pl.BlockSpec(memory_space=pltpu.SMEM), block, block],
+        out_specs=[pl.BlockSpec(part, lambda g: (0, 0))] * parts,
+        scratch_shapes=[
+            pltpu.VMEM((GROUP, tokens), jnp.bfloat16),
+            pltpu.VMEM((rows, LANES), jnp.bfloat16),
+        ],
+        compiler_params=pltpu.CompilerParams(vmem_limit_bytes=60 * 2**20),
         cost_estimate=pl.CostEstimate(
             flops=2 * tokens * dim * HEAD_DIM, bytes_accessed=4 * tokens * dim, transcendentals=0
         ),
         name="frame_states",
-    )(keys, values)
+    )(spot, keys, values)
 
 
 def mix_kernel(
     dim, rows, width, edges,
-    place_ref, queries_ref, residual_ref, edge_ref, state_ref, gain_ref, vtaps_ref, gtaps_ref,
-    out_ref,
-    features, weights, same, numer, squares, shifted,
+    place_ref, spots_ref, queries_ref, residual_ref, edge_ref, gain_ref, vtaps_ref, gtaps_ref, *refs,
 ):
+    *pieces, out_ref, states, features, weights, same, numer, squares, shifted = refs
+    step = pl.program_id(0)
     tokens = rows * width
     total = tokens + edges * width
 
@@ -117,6 +132,9 @@
                     ] = block.astype(jnp.bfloat16)
         for row in (0, rows + 1):
             shifted[:, row] = jnp.zeros((3, width, LANES), jnp.float32)
+        for k, piece in enumerate(pieces):
+            size = piece.shape[0]
+            states[pl.ds(pl.multiple_of(spots_ref[k] * size, 16), size), :] = piece[...]
 
     zero = jnp.zeros((), jnp.bfloat16)
     column = lax.broadcasted_iota(jnp.int32, (width, LANES), 0)
@@ -144,7 +162,8 @@
             )
         for number, (tiles, first, last) in enumerate(spans(lanes)):
             for side, j in enumerate(tiles):
-                state = state_ref[j * HEAD_DIM : (j + 1) * HEAD_DIM, :].astype(jnp.float32)
+                row = pl.multiple_of((step * TILES + j) * HEAD_DIM, 16)
+                state = states[pl.ds(row, HEAD_DIM), :].astype(jnp.float32)
                 for h, lo, hi in tile_heads(j, lanes):
                     start = h * HEAD_DIM - first * LANES
                     block = jnp.where((lane >= lo) & (lane < hi), state, 0.0)
@@ -206,7 +225,7 @@
     by_group(dim, body)
 
 
-def mix(place, queries, residual, edge, state, gain, value_taps, gate_taps, rows, width):
+def mix(place, spots, queries, residual, edge, gain, value_taps, gate_taps, pieces, rows, width):
     tokens, dim = queries.shape
     edges = edge.shape[1]
     total = tokens + edges * width
@@ -220,16 +239,18 @@
         grid=(cdiv(dim, GROUP),),
         in_specs=[
             pl.BlockSpec(memory_space=pltpu.SMEM),
+            pl.BlockSpec(memory_space=pltpu.SMEM),
             block,
             block,
             pl.BlockSpec((2, edges, width, GROUP), lambda g: (0, 0, 0, g)),
-            pl.BlockSpec((TILES * HEAD_DIM, LANES), lambda g: (g, 0)),
             pl.BlockSpec((1, GROUP), lambda g: (0, g)),
             taps,
             taps,
-        ],
+        ]
+        + [pl.BlockSpec(piece.shape, lambda g: (0, 0)) for piece in pieces],
         out_specs=block,
         scratch_shapes=[
+            pltpu.VMEM((sum(piece.shape[0] for piece in pieces), LANES), jnp.bfloat16),
             pltpu.VMEM((total, GROUP), jnp.bfloat16),
             pltpu.VMEM((len(pairs), depth, 2 * LANES), jnp.bfloat16),
             pltpu.VMEM((len(pairs), depth, 2 * LANES), jnp.bfloat16),
@@ -237,12 +258,12 @@
             pltpu.VMEM((total, GROUP), jnp.bfloat16),
             pltpu.VMEM((3, rows + 2, width, LANES), jnp.float32),
         ],
-        compiler_params=pltpu.CompilerParams(vmem_limit_bytes=VMEM_LIMIT),
+        compiler_params=pltpu.CompilerParams(vmem_limit_bytes=36 * 2**20),
         cost_estimate=pl.CostEstimate(
             flops=60 * tokens * dim, bytes_accessed=6 * tokens * dim, transcendentals=2 * tokens * dim
         ),
         name="mix",
-    )(place, queries, residual, edge, state, gain, value_taps, gate_taps)
+    )(place, spots, queries, residual, edge, gain, value_taps, gate_taps, *pieces)
 
 
 def edge_rows(queries, residual, rows, width):
@@ -261,51 +282,93 @@
     return jnp.concatenate([before, after], axis=1), jnp.array([0, rows + 1], jnp.int32)
 
 
-def share_of_sum(state):
-    devices, here = lax.axis_size("space"), lax.axis_index("space")
-    if devices != 2:
-        return lax.psum_scatter(state, "space", scatter_dimension=0, tiled=True)
-    half = state.shape[0] // 2
-    halves = state.reshape(2, half, LANES)
-    sent = jnp.where(here == 0, halves[1], halves[0])
-    kept = jnp.where(here == 0, halves[0], halves[1])
-    got = lax.ppermute(sent, "space", [(0, 1), (1, 0)])
-    return (kept.astype(jnp.float32) + got.astype(jnp.float32)).astype(jnp.bfloat16)
-
-
-def running_sum_kernel(pieces_ref, sums_ref):
-    running = jnp.zeros(pieces_ref.shape[1:], jnp.float32)
-    for f in range(pieces_ref.shape[0]):
-        running = running + pieces_ref[f].astype(jnp.float32)
-        sums_ref[f] = running.astype(jnp.bfloat16)
-
-
-def prefix_sum(share):
-    frames = lax.axis_size("frame")
-    pieces = share.reshape(frames, share.shape[0] // frames, LANES)
-    pieces = lax.all_to_all(pieces, "frame", split_axis=0, concat_axis=0, tiled=True)
-    sums = pl.pallas_call(
-        running_sum_kernel,
-        out_shape=jax.ShapeDtypeStruct(pieces.shape, jnp.bfloat16),
-        name="running_sum",
-    )(pieces)
-    sums = lax.all_to_all(sums, "frame", split_axis=0, concat_axis=0, tiled=True)
-    return sums.reshape(share.shape)
+def small_kernel(body, name, outs, scalars, *arrays):
+    return pl.pallas_call(
+        body,
+        out_shape=[jax.ShapeDtypeStruct(shape, jnp.bfloat16) for shape in outs],
+        in_specs=[pl.BlockSpec(memory_space=pltpu.SMEM)]
+        + [pl.BlockSpec(memory_space=pltpu.VMEM)] * len(arrays),
+        out_specs=[pl.BlockSpec(memory_space=pltpu.VMEM)] * len(outs),
+        name=name,
+    )(scalars, *arrays)
+
+
+def add(*values):
+    total = values[0].astype(jnp.float32)
+    for value in values[1:]:
+        total = total + value.astype(jnp.float32)
+    return total
+
+
+def split_sum_body(spot_ref, kept_ref, got_ref, mine_ref, theirs_ref):
+    size = mine_ref.shape[0]
+    for ref, side in ((theirs_ref, 1 - spot_ref[0]), (mine_ref, spot_ref[0])):
+        rows = pl.ds(pl.multiple_of(side * size, 16), size)
+        ref[...] = add(kept_ref[rows, :], got_ref[rows, :]).astype(jnp.bfloat16)
+
+
+def sum_body(_, *refs):
+    *terms, out_ref = refs
+    out_ref[...] = add(*[term[...] for term in terms]).astype(jnp.bfloat16)
+
+
+def pair_sums_body(spot_ref, own_ref, partner_ref, *refs):
+    *earlier, mine_ref, theirs_ref = refs
+    before = add(*[ref[...] for ref in earlier])
+    own, partner = add(own_ref[...]), add(partner_ref[...])
+    first = spot_ref[0] == 0
+    both = before + (own + partner)
+    mine_ref[...] = jnp.where(first, before + own, both).astype(jnp.bfloat16)
+    theirs_ref[...] = jnp.where(first, both, before + partner).astype(jnp.bfloat16)
+
+
+def running_states(keys, values, rows):
+    devices, frames = lax.axis_size("space"), lax.axis_size("frame")
+    core, frame = lax.axis_index("space"), lax.axis_index("frame")
+    if devices != 2 or frames % 2 or frames < 4:
+        (state,) = frame_states(jnp.zeros((1,), jnp.int32), keys, values, rows, 1)
+        state = lax.psum(state.astype(jnp.float32), "space").astype(jnp.bfloat16)
+        every = lax.all_gather(state, "frame").astype(jnp.float32)
+        reached = (jnp.arange(frames) <= frame)[:, None, None]
+        total = jnp.sum(jnp.where(reached, every, 0.0), axis=0).astype(jnp.bfloat16)
+        return [total], jnp.zeros((1,), jnp.int32)
+    parity = lax.rem(frame, 2)
+    swap = [(0, 1), (1, 0)]
+    partners = [(f, f ^ 1) for f in range(frames)]
+    spot = parity.astype(jnp.int32)[None]
+    kept, sent = frame_states(core.astype(jnp.int32)[None], keys, values, rows, 2)
+    got = lax.ppermute(sent, "space", swap)
+    quarter = (rows // 4, LANES)
+    own, sent = small_kernel(split_sum_body, "split_sum", [quarter] * 2, spot, kept, got)
+    partner = lax.ppermute(sent, "frame", partners)
+    (total,) = small_kernel(sum_body, "pair_sum", [quarter], spot, own, partner)
+    earlier = []
+    stride = 2
+    while stride < frames:
+        got = lax.ppermute(total, "frame", [(f, f + stride) for f in range(frames - stride)])
+        earlier.append(got)
+        stride *= 2
+        if stride < frames:
+            (total,) = small_kernel(sum_body, "stride_sum", [quarter], spot, total, got)
+    mine, theirs = small_kernel(
+        pair_sums_body, "pair_sums", [quarter] * 2, spot, own, partner, *earlier
+    )
+    other = lax.ppermute(theirs, "frame", partners)
+    pieces = [mine, other, lax.ppermute(mine, "space", swap), lax.ppermute(other, "space", swap)]
+    spots = [2 * c + p for c in (core, 1 - core) for p in (parity, 1 - parity)]
+    return pieces, jnp.stack(spots).astype(jnp.int32)
 
 
 def on_device(queries, keys, values, residual, attn_gain, value_taps, gate_taps):
     frames, rows, width, dim = queries.shape
     tokens = frames * rows * width
     flat = lambda a: a.reshape(tokens, dim)
-    unit = 16 * lax.axis_size("space") * lax.axis_size("frame")
-    state_rows = cdiv(cdiv(dim, LANES) * HEAD_DIM, unit) * unit
+    state_rows = cdiv(cdiv(dim, LANES) * HEAD_DIM, 64) * 64
     edge, place = edge_rows(queries, residual, rows, width)
-    state = frame_states(flat(keys), flat(values), state_rows)
-    share = prefix_sum(share_of_sum(state))
-    state = lax.all_gather(share, "space", axis=0, tiled=True)
+    pieces, spots = running_states(flat(keys), flat(values), state_rows)
     out = mix(
-        place, flat(queries), flat(residual), edge, state, attn_gain[None], value_taps, gate_taps,
-        rows, width,
+        place, spots, flat(queries), flat(residual), edge, attn_gain[None], value_taps, gate_taps,
+        pieces, rows, width,
     )
     return out.reshape(frames, rows, width, dim)
 

time: 58.1 us -> 63.5 us (1.093); the launches traced: 57.6 us -> 62.3 us
  Pallas kernels: 20.7 us -> 26.4 us
  waiting for transfers between devices: 17.7 us -> 14.5 us
  local copies, waits for them, and re-layouts: 2.18 us -> 5.18 us
  starting transfers between devices: 11.3 us -> 14 us
  blocking collectives: 2.3 us -> 0 us
  other arithmetic: 3.39 us -> 2.19 us
    all_to_all x2 -> x0, waiting for transfers between devices: 17.7 us -> none  [the longest x1 9.22 us: prefix_sum(): lax.all_to_all(pieces, 'frame', split_axis=0, concat_axis=0, tiled=True)]
    ppermute x1 -> x7, waiting for transfers between devices: 0.01 us -> 14.5 us  [the longest x2 5.62 us: running_states(): lax.ppermute(total, 'frame', [(f, f + stride) for f in range(frames - str...]
    ppermute x1 -> x7, starting transfers between devices: 0.52 us -> 13.9 us  [the longest x2 8.95 us: running_states(): lax.ppermute(total, 'frame', [(f, f + stride) for f in range(frames - str...]
    all_to_all x2 -> x0, starting transfers between devices: 10.5 us -> none  [the longest x1 6.94 us: prefix_sum(): lax.all_to_all(pieces, 'frame', split_axis=0, concat_axis=0, tiled=True)]
    pallas_call x2 -> x5, Pallas kernels: 6.02 us -> 11.5 us  [the longest x4 6.92 us: small_kernel(): pl.pallas_call(body, out_shape=[jax.ShapeDtypeStruct(shape, jnp.bfloat16)...]
    unnamed x8 -> x20, local copies, waits for them, and re-layouts: 1.58 us -> 5.18 us
    all_gather x1 -> x0, blocking collectives: 2.3 us -> none  [on_device(): state = lax.all_gather(share, 'space', axis=0, tiled=True)]
    select_n x1 -> x0, other arithmetic: 1.12 us -> none  [share_of_sum(): sent = jnp.where(here == 0, halves[1], halves[0])]
  transfers between devices with their start and end apart: 4 -> 8, of which waited for: 2 -> 5; matrix products, arithmetic and copies ran while one was open for 4% -> 4% of each run, Pallas kernels for 3% -> 11%
where the time goes in v3:
time: 63.5 us; the launch traced here: 62.3 us
  Pallas kernels  26.4 us (42%)
  waiting for transfers between devices  14.5 us (23%)
  starting transfers between devices  14 us (22%)
  local copies, waits for them, and re-layouts  5.18 us (8%)
  other arithmetic  2.19 us (3%)
    pallas_call x1, Pallas kernels, mix(): pl.pallas_call(functools.partial(mix_kernel, dim, rows, width, edges), ou...  14.9 us
    ppermute x2, starting transfers between devices, running_states(): lax.ppermute(total, 'frame', [(f, f + stride) for f in range(frames - str...  8.95 us
    pallas_call x4, Pallas kernels, small_kernel(): pl.pallas_call(body, out_shape=[jax.ShapeDtypeStruct(shape, jnp.bfloat16)...  6.92 us
    ppermute x2, waiting for transfers between devices, running_states(): lax.ppermute(total, 'frame', [(f, f + stride) for f in range(frames - str...  5.62 us
    unnamed x20, local copies, waits for them, and re-layouts  5.18 us
    pallas_call x1, Pallas kernels, frame_states(): pl.pallas_call(functools.partial(state_kernel, dim), out_shape=[jax.Shape...  4.57 us
    ppermute x1, waiting for transfers between devices, running_states(): partner = lax.ppermute(sent, 'frame', partners)  3.88 us
    ppermute x1, waiting for transfers between devices, running_states(): other = lax.ppermute(theirs, 'frame', partners)  3.66 us
  transfers between devices with their start and end apart: 8, of which 5 were waited for; matrix products, arithmetic and copies ran while one was open for 4% of the time, Pallas kernels for 11%

profile of v3, /device:TPU:0, one launch (start us, length us, event | category | flops | bytes accessed | tf_op | source)
XLA Modules:
  0.0 62.3 jit_solution(17161753185800016913)
XLA Ops:
  0.0 4.6 %frame_states.1 = (bf16[1024,128]{1,0:T(8,128)(2,1)}, bf16[1024,128]{1,0:T(8,128)(2,1)}) custom-call(s32[1]{0:T(128)} %bitcast.8.spot_ref, bf16[480,2240]{1,0:T(8,128)(2,1)} %bitcast.14, bf16[480,2240]{1,0:T(8,128)(2,1)} %bitcast.15), custom_call_target="tpu_custom_call" | custom-call | flops 240844800 | bytes 4300800 | tf_op jit(solution)/shard_map/frame_states/pallas_call | solution.py:93
  4.6 0.5 collective-permute-start.1
  5.0 1.2 %slice_select_fusion = (bf16[1,1,80,2240]{3,2,1,0:T(8,128)(2,1)S(1)}, bf16[1,1,80,2240]{3,2,1,0:T(8,128)(2,1)S(1)}) fusion(bf16[1,6,80,2240]{3,2,1,0:T(8,128)(2,1)} %param.10, pred[]{:T(512)S(6)} %eq.2, bf16[1,6,80,2240]{3,2,1,0:T(8,128)(2,1)S(1)} %copy-done), kind=kLoop, calls=%fused_computation.1 | loop fusion | flops 358400 | bytes 2150401 | tf_op jit(solution)/shard_map/jit(_where)/select_n | solution.py:274
  6.2 0.9 %pad_maximum_fusion = bf16[2,1,80,2240]{3,2,1,0:T(8,128)(2,1)} fusion(bf16[1,1,80,2240]{3,2,1,0:T(8,128)(2,1)S(1)} %get-tuple-element.17, bf16[1,1,80,2240]{3,2,1,0:T(8,128)(2,1)S(1)} %get-tuple-element.18), kind=kLoop, calls=%fused_computation | loop fusion | flops 358400 | bytes 1433600 | tf_op jit(solution)/shard_map/stack | solution.py:274
  7.2 0.7 %copy-done.7 = bf16[1024,128]{1,0:T(8,128)(2,1)} copy-done((bf16[1024,128]{1,0:T(8,128)(2,1)}, bf16[1024,128]{1,0:T(8,128)(2,1)S(1)}, u32[]{:S(2)}) %copy-start.7) | copy-done | bytes 262168
  7.9 1.8 %split_sum.1 = (bf16[512,128]{1,0:T(8,128)(2,1)}, bf16[512,128]{1,0:T(8,128)(2,1)}) custom-call(s32[1]{0:T(128)} %bitcast.7.spot_ref._, bf16[1024,128]{1,0:T(8,128)(2,1)} %get-tuple-element.11.kept_ref, bf16[1024,128]{1,0:T(8,128)(2,1)} %copy-done.7), custom_call_target="tpu_custom_call" | custom-call | tf_op jit(solution)/shard_map/split_sum/pallas_call | solution.py:286
  9.7 3.0 %collective-permute-start.2 = (bf16[512,128]{1,0:T(8,128)(2,1)}, bf16[512,128]{1,0:T(8,128)(2,1)S(1)}, u32[]{:S(2)}, u32[]{:S(2)}) collective-permute-start(bf16[512,128]{1,0:T(8,128)(2,1)} %get-tuple-element.14), channel_id=1, source_target_pairs={{0,2},{2,0},{4,6},{6,4},{8,10},{10,8},{12,14},{14,12},{1,3},{3,1},... | collective-permute-start | bytes 393224 | tf_op jit(solution)/shard_map/ppermute | solution.py:343
  12.7 3.9 %collective-permute-done.2.refs_1_.partner_ref = bf16[512,128]{1,0:T(8,128)(2,1)S(1)} collective-permute-done((bf16[512,128]{1,0:T(8,128)(2,1)}, bf16[512,128]{1,0:T(8,128)(2,1)S(1)}, u32[]{:S(2)}, u32[]{:S(2)}) %collective-permute-start.2) | collective-permute-done | bytes 131104 | tf_op jit(solution)/shard_map/ppermute | solution.py:343
  16.5 0.6 %copy-done.5 = bf16[512,128]{1,0:T(8,128)(2,1)} copy-done((bf16[512,128]{1,0:T(8,128)(2,1)}, bf16[512,128]{1,0:T(8,128)(2,1)S(1)}, u32[]{:S(2)}) %copy-start.5) | copy-done | bytes 131096
  17.2 1.6 %pair_sum.1.refs_0_ = bf16[512,128]{1,0:T(8,128)(2,1)} custom-call(s32[1]{0:T(128)} %bitcast.7.spot_ref._, bf16[512,128]{1,0:T(8,128)(2,1)} %get-tuple-element.13.refs_0_.own_ref, bf16[512,128]{1,0:T(8,128)(2,1)} %copy-done.5), custom_call_target="tpu_custom_call" | custom-call | tf_op jit(solution)/shard_map/pair_sum/pallas_call | solution.py:286
  18.8 3.7 %collective-permute-start.3 = (bf16[512,128]{1,0:T(8,128)(2,1)}, bf16[512,128]{1,0:T(8,128)(2,1)S(1)}, u32[]{:S(2)}, u32[]{:S(2)}) collective-permute-start(bf16[512,128]{1,0:T(8,128)(2,1)} %pair_sum.1.refs_0_), channel_id=1, source_target_pairs={{0,4},{2,6},{4,8},{6,10},{8,12},{10,14},{1,5},{3,7},{5,9},{7,11},{... | collective-permute-start | bytes 393224 | tf_op jit(solution)/shard_map/ppermute | solution.py:348
  22.5 2.8 %collective-permute-done.3.refs_1_.refs_0_ = bf16[512,128]{1,0:T(8,128)(2,1)S(1)} collective-permute-done((bf16[512,128]{1,0:T(8,128)(2,1)}, bf16[512,128]{1,0:T(8,128)(2,1)S(1)}, u32[]{:S(2)}, u32[]{:S(2)}) %collective-permute-start.3) | collective-permute-done | bytes 131104 | tf_op jit(solution)/shard_map/ppermute | solution.py:348
  25.3 0.6 %copy-done.6 = bf16[512,128]{1,0:T(8,128)(2,1)} copy-done((bf16[512,128]{1,0:T(8,128)(2,1)}, bf16[512,128]{1,0:T(8,128)(2,1)S(1)}, u32[]{:S(2)}) %copy-start.6) | copy-done | bytes 131096
  26.0 1.6 %stride_sum.1 = bf16[512,128]{1,0:T(8,128)(2,1)} custom-call(s32[1]{0:T(128)} %bitcast.7.spot_ref._, bf16[512,128]{1,0:T(8,128)(2,1)} %pair_sum.1.refs_0_, bf16[512,128]{1,0:T(8,128)(2,1)} %copy-done.6), custom_call_target="tpu_custom_call" | custom-call | tf_op jit(solution)/shard_map/stride_sum/pallas_call | solution.py:286
  27.6 5.3 %collective-permute-start.4 = (bf16[512,128]{1,0:T(8,128)(2,1)}, bf16[512,128]{1,0:T(8,128)(2,1)S(1)}, u32[]{:S(2)}, u32[]{:S(2)}) collective-permute-start(bf16[512,128]{1,0:T(8,128)(2,1)} %stride_sum.1), channel_id=1, source_target_pairs={{0,8},{2,10},{4,12},{6,14},{1,9},{3,11},{5,13},{7,15},{16,24},{18,... | collective-permute-start | bytes 393224 | tf_op jit(solution)/shard_map/ppermute | solution.py:348
  32.9 2.8 %collective-permute-done.4.refs_1_ = bf16[512,128]{1,0:T(8,128)(2,1)S(1)} collective-permute-done((bf16[512,128]{1,0:T(8,128)(2,1)}, bf16[512,128]{1,0:T(8,128)(2,1)S(1)}, u32[]{:S(2)}, u32[]{:S(2)}) %collective-permute-start.4) | collective-permute-done | bytes 131104 | tf_op jit(solution)/shard_map/ppermute | solution.py:348
  35.7 0.6 %copy-done.8 = bf16[512,128]{1,0:T(8,128)(2,1)} copy-done((bf16[512,128]{1,0:T(8,128)(2,1)}, bf16[512,128]{1,0:T(8,128)(2,1)S(1)}, u32[]{:S(2)}) %copy-start.8) | copy-done | bytes 131096
  36.3 1.9 %pair_sums.1 = (bf16[512,128]{1,0:T(8,128)(2,1)}, bf16[512,128]{1,0:T(8,128)(2,1)}) custom-call(s32[1]{0:T(128)} %bitcast.7.spot_ref._, bf16[512,128]{1,0:T(8,128)(2,1)} %get-tuple-element.13.refs_0_.own_ref, bf16[512,128]{1,0:T(8,128)(2,1)} %copy-done.5, bf16[512,128]{1,0:T(8,128)(2,1)} %copy-done.6, bf16[512,128]{1,0:T(8,128)(2,1)} %copy-done.8), custom_call_target="tpu_custom_call" | custom-call | tf_op jit(solution)/shard_map/pair_sums/pallas_call | solution.py:286
  38.2 1.5 %collective-permute-start.5 = (bf16[512,128]{1,0:T(8,128)(2,1)}, bf16[512,128]{1,0:T(8,128)(2,1)S(1)}, u32[]{:S(2)}, u32[]{:S(2)}) collective-permute-start(bf16[512,128]{1,0:T(8,128)(2,1)} %get-tuple-element.16), channel_id=1, source_target_pairs={{0,2},{2,0},{4,6},{6,4},{8,10},{10,8},{12,14},{14,12},{1,3},{3,1},... | collective-permute-start | bytes 393224 | tf_op jit(solution)/shard_map/ppermute | solution.py:356
  39.8 3.7 %collective-permute-done.5.refs_1_ = bf16[512,128]{1,0:T(8,128)(2,1)S(1)} collective-permute-done((bf16[512,128]{1,0:T(8,128)(2,1)}, bf16[512,128]{1,0:T(8,128)(2,1)S(1)}, u32[]{:S(2)}, u32[]{:S(2)}) %collective-permute-start.5) | collective-permute-done | bytes 131104 | tf_op jit(solution)/shard_map/ppermute | solution.py:356
  43.5 1.4 %collective-permute-done.7.refs_3_ = bf16[512,128]{1,0:T(8,128)(2,1)} collective-permute-done((bf16[512,128]{1,0:T(8,128)(2,1)S(1)}, bf16[512,128]{1,0:T(8,128)(2,1)}, u32[]{:S(2)}, u32[]{:S(2)}) %collective-permute-start.7) | collective-permute-done | bytes 131104 | tf_op jit(solution)/shard_map/ppermute | solution.py:357
  44.9 1.6 %copy-done.1 = bf16[1,6,80,2240]{3,2,1,0:T(8,128)(2,1)S(1)} copy-done((bf16[1,6,80,2240]{3,2,1,0:T(8,128)(2,1)S(1)}, bf16[1,6,80,2240]{3,2,1,0:T(8,128)(2,1)}, u32[]{:S(2)}) %copy-start.1) | copy-done | bytes 2150424
  46.5 0.9 %copy-done.4 = bf16[512,128]{1,0:T(8,128)(2,1)S(1)} copy-done((bf16[512,128]{1,0:T(8,128)(2,1)S(1)}, bf16[512,128]{1,0:T(8,128)(2,1)}, u32[]{:S(2)}) %copy-start.4) | copy-done | bytes 131096
  47.4 14.9 %mix.1 = bf16[480,2240]{1,0:T(8,128)(2,1)} custom-call(s32[1]{0:T(128)} %bitcast.place_ref, s32[4]{0:T(128)S(1)} %pad_add_fusion.spots_ref, bf16[480,2240]{1,0:T(8,128)(2,1)S(1)} %bitcast.12, bf16[480,2240]{1,0:T(8,128)(2,1)S(1)} %bitcast.13, bf16[2,1,80,2240]{3,2,1,0:T(8,128)(2,1)S(1)} %collective-permute-done.edge_ref, ...), custom_call_target="tpu_custom_call" | custom-call | flops 64512000 | bytes 6451200 | tf_op jit(solution)/shard_map/mix/pallas_call | solution.py:236
  (22 shorter events, 0.2 us)
Async XLA Ops:
  0.0 5.0 %copy-start = (bf16[1,6,80,2240]{3,2,1,0:T(8,128)(2,1)S(1)}, bf16[1,6,80,2240]{3,2,1,0:T(8,128)(2,1)}, u32[]{:S(2)}) copy-start(bf16[1,6,80,2240]{3,2,1,0:T(8,128)(2,1)} %param.7) | copy-start | bytes 6451204
  4.6 2.7 %collective-permute-start.1 = (bf16[1024,128]{1,0:T(8,128)(2,1)}, bf16[1024,128]{1,0:T(8,128)(2,1)S(1)}, u32[]{:S(2)}, u32[]{:S(2)}) collective-permute-start(bf16[1024,128]{1,0:T(8,128)(2,1)} %get-tuple-element.12), channel_id=1, source_target_pairs={{0,1},{1,0},{2,3},{3,2},{4,5},{5,4},{6,7},{7,6},{8,9},{9,8},{10,11... | collective-permute-start | bytes 786440 | tf_op jit(solution)/shard_map/ppermute | solution.py:340
  6.2 37.2 %copy-start.9 = (f32[2240]{0:T(1024)S(1)}, f32[2240]{0:T(1024)}, u32[]{:S(2)}) copy-start(f32[2240]{0:T(1024)} %param.11) | copy-start | bytes 26884
  6.2 38.7 %copy-start.2 = (f32[9,2240]{1,0:T(8,128)S(1)}, f32[9,2240]{1,0:T(8,128)}, u32[]{:S(2)}) copy-start(f32[9,2240]{1,0:T(8,128)} %vtaps_ref.1) | copy-start | bytes 241924
  6.2 38.7 %copy-start.3 = (f32[9,2240]{1,0:T(8,128)S(1)}, f32[9,2240]{1,0:T(8,128)}, u32[]{:S(2)}) copy-start(f32[9,2240]{1,0:T(8,128)} %gtaps_ref.1) | copy-start | bytes 241924
  7.2 36.3 %collective-permute-start = (bf16[2,1,80,2240]{3,2,1,0:T(8,128)(2,1)}, bf16[2,1,80,2240]{3,2,1,0:T(8,128)(2,1)S(1)}, u32[]{:S(2)}, u32[]{:S(2)}) collective-permute-start(bf16[2,1,80,2240]{3,2,1,0:T(8,128)(2,1)} %pad_maximum_fusion), channel_id=1, source_target_pairs={{0,1},{1,0},{2,3},{3,2},{4,5},{5,4},{6,7},{7,6},{8,9},{9,8},{10,11... | collective-permute-start | bytes 2150408 | tf_op jit(solution)/shard_map/ppermute | solution.py:275
  7.2 0.7 %copy-start.7 = (bf16[1024,128]{1,0:T(8,128)(2,1)}, bf16[1024,128]{1,0:T(8,128)(2,1)S(1)}, u32[]{:S(2)}) copy-start(bf16[1024,128]{1,0:T(8,128)(2,1)S(1)} %collective-permute-done.1.got_ref) | copy-start | bytes 786436
  9.7 6.9 %collective-permute-start.2 = (bf16[512,128]{1,0:T(8,128)(2,1)}, bf16[512,128]{1,0:T(8,128)(2,1)S(1)}, u32[]{:S(2)}, u32[]{:S(2)}) collective-permute-start(bf16[512,128]{1,0:T(8,128)(2,1)} %get-tuple-element.14), channel_id=1, source_target_pairs={{0,2},{2,0},{4,6},{6,4},{8,10},{10,8},{12,14},{14,12},{1,3},{3,1},... | collective-permute-start | bytes 393224 | tf_op jit(solution)/shard_map/ppermute | solution.py:343
  16.5 0.7 %copy-start.5 = (bf16[512,128]{1,0:T(8,128)(2,1)}, bf16[512,128]{1,0:T(8,128)(2,1)S(1)}, u32[]{:S(2)}) copy-start(bf16[512,128]{1,0:T(8,128)(2,1)S(1)} %collective-permute-done.2.refs_1_.partner_ref) | copy-start | bytes 393220
  18.8 6.5 %collective-permute-start.3 = (bf16[512,128]{1,0:T(8,128)(2,1)}, bf16[512,128]{1,0:T(8,128)(2,1)S(1)}, u32[]{:S(2)}, u32[]{:S(2)}) collective-permute-start(bf16[512,128]{1,0:T(8,128)(2,1)} %pair_sum.1.refs_0_), channel_id=1, source_target_pairs={{0,4},{2,6},{4,8},{6,10},{8,12},{10,14},{1,5},{3,7},{5,9},{7,11},{... | collective-permute-start | bytes 393224 | tf_op jit(solution)/shard_map/ppermute | solution.py:348
  25.3 0.6 %copy-start.6 = (bf16[512,128]{1,0:T(8,128)(2,1)}, bf16[512,128]{1,0:T(8,128)(2,1)S(1)}, u32[]{:S(2)}) copy-start(bf16[512,128]{1,0:T(8,128)(2,1)S(1)} %collective-permute-done.3.refs_1_.refs_0_) | copy-start | bytes 393220
  27.6 8.1 %collective-permute-start.4 = (bf16[512,128]{1,0:T(8,128)(2,1)}, bf16[512,128]{1,0:T(8,128)(2,1)S(1)}, u32[]{:S(2)}, u32[]{:S(2)}) collective-permute-start(bf16[512,128]{1,0:T(8,128)(2,1)} %stride_sum.1), channel_id=1, source_target_pairs={{0,8},{2,10},{4,12},{6,14},{1,9},{3,11},{5,13},{7,15},{16,24},{18,... | collective-permute-start | bytes 393224 | tf_op jit(solution)/shard_map/ppermute | solution.py:348
  35.7 0.6 %copy-start.8 = (bf16[512,128]{1,0:T(8,128)(2,1)}, bf16[512,128]{1,0:T(8,128)(2,1)S(1)}, u32[]{:S(2)}) copy-start(bf16[512,128]{1,0:T(8,128)(2,1)S(1)} %collective-permute-done.4.refs_1_) | copy-start | bytes 393220
  38.2 5.2 %collective-permute-start.5 = (bf16[512,128]{1,0:T(8,128)(2,1)}, bf16[512,128]{1,0:T(8,128)(2,1)S(1)}, u32[]{:S(2)}, u32[]{:S(2)}) collective-permute-start(bf16[512,128]{1,0:T(8,128)(2,1)} %get-tuple-element.16), channel_id=1, source_target_pairs={{0,2},{2,0},{4,6},{6,4},{8,10},{10,8},{12,14},{14,12},{1,3},{3,1},... | collective-permute-start | bytes 393224 | tf_op jit(solution)/shard_map/ppermute | solution.py:356
  39.7 3.8 %collective-permute-start.6 = (bf16[512,128]{1,0:T(8,128)(2,1)}, bf16[512,128]{1,0:T(8,128)(2,1)S(1)}, u32[]{:S(2)}, u32[]{:S(2)}) collective-permute-start(bf16[512,128]{1,0:T(8,128)(2,1)} %get-tuple-element.15.refs_0_), channel_id=1, source_target_pairs={{0,1},{1,0},{2,3},{3,2},{4,5},{5,4},{6,7},{7,6},{8,9},{9,8},{10,11... | collective-permute-start | bytes 393224 | tf_op jit(solution)/shard_map/ppermute | solution.py:357
  43.4 1.5 %collective-permute-start.7 = (bf16[512,128]{1,0:T(8,128)(2,1)S(1)}, bf16[512,128]{1,0:T(8,128)(2,1)}, u32[]{:S(2)}, u32[]{:S(2)}) collective-permute-start(bf16[512,128]{1,0:T(8,128)(2,1)S(1)} %collective-permute-done.5.refs_1_), channel_id=1, source_target_pairs={{0,1},{1,0},{2,3},{3,2},{4,5},{5,4},{6,7},{7,6},{8,9},{9,8},{10,11... | collective-permute-start | bytes 393224 | tf_op jit(solution)/shard_map/ppermute | solution.py:357
  44.9 1.6 %copy-start.1 = (bf16[1,6,80,2240]{3,2,1,0:T(8,128)(2,1)S(1)}, bf16[1,6,80,2240]{3,2,1,0:T(8,128)(2,1)}, u32[]{:S(2)}) copy-start(bf16[1,6,80,2240]{3,2,1,0:T(8,128)(2,1)} %param.10) | copy-start | bytes 6451204
  46.5 0.9 %copy-start.4 = (bf16[512,128]{1,0:T(8,128)(2,1)S(1)}, bf16[512,128]{1,0:T(8,128)(2,1)}, u32[]{:S(2)}) copy-start(bf16[512,128]{1,0:T(8,128)(2,1)} %get-tuple-element.15.refs_0_) | copy-start | bytes 393220

commit v4 on v3

--- a/solution.py
+++ b/solution.py
@@ -16,6 +16,10 @@
 
 def cdiv(a, b):
     return -(-a // b)
+
+
+def in_hbm(array):
+    return pltpu.with_memory_space_constraint(array, pltpu.HBM)
 
 
 def lane_iota(shape):
@@ -47,9 +51,25 @@
         pl.when(pl.program_id(0) >= full)(lambda: body(rest))
 
 
-def state_kernel(dim, spot_ref, keys_ref, values_ref, *refs):
-    *parts, turned, whole = refs
+def state_kernel(dim, with_edge, spot_ref, keys_ref, values_ref, *refs):
     step = pl.program_id(0)
+    *refs, turned, whole, semaphores = refs
+    if with_edge:
+        *sources, edge_ref = refs[:2] + refs[-1:]
+        parts = refs[2:-1]
+        row = (sources[0].shape[0] - 1) * (1 - lax.axis_index("space"))
+        copies = [
+            pltpu.make_async_copy(source.at[row], edge_ref.at[k, 0], semaphores.at[k])
+            for k, source in enumerate(sources)
+        ]
+
+        @pl.when(step == 0)
+        def _():
+            for copy in copies:
+                copy.start()
+
+    else:
+        parts = refs
 
     def body(lanes):
         turned[...] = jnp.maximum(keys_ref[...], 0).T
@@ -84,28 +104,35 @@
             size = part.shape[0]
             row = pl.multiple_of(lax.rem(spot_ref[0] + k, len(parts)) * size, 16)
             part[...] = whole[pl.ds(row, size), :]
-
-
-def frame_states(spot, keys, values, rows, parts):
+        if with_edge:
+            for copy in copies:
+                copy.wait()
+
+
+def frame_states(spot, keys, values, rows, parts, edged=()):
     tokens, dim = keys.shape
     part = (rows // parts, LANES)
     block = pl.BlockSpec((tokens, GROUP), lambda g: (0, g))
     return pl.pallas_call(
-        functools.partial(state_kernel, dim),
-        out_shape=[jax.ShapeDtypeStruct(part, jnp.bfloat16)] * parts,
+        functools.partial(state_kernel, dim, bool(edged)),
+        out_shape=[pltpu.VMEM(part, jnp.bfloat16)] * parts
+        + [pltpu.VMEM((len(edged), 1, *edged[0].shape[1:]), jnp.bfloat16) for _ in edged[:1]],
         grid=(cdiv(dim, GROUP),),
-        in_specs=[pl.BlockSpec(memory_space=pltpu.SMEM), block, block],
-        out_specs=[pl.BlockSpec(part, lambda g: (0, 0))] * parts,
+        in_specs=[pl.BlockSpec(memory_space=pltpu.SMEM), block, block]
+        + [pl.BlockSpec(memory_space=pl.ANY)] * len(edged),
+        out_specs=[pl.BlockSpec(part, lambda g: (0, 0))] * parts
+        + [pl.BlockSpec(memory_space=pl.ANY) for _ in edged[:1]],
         scratch_shapes=[
             pltpu.VMEM((GROUP, tokens), jnp.bfloat16),
             pltpu.VMEM((rows, LANES), jnp.bfloat16),
+            pltpu.SemaphoreType.DMA((2,)),
         ],
         compiler_params=pltpu.CompilerParams(vmem_limit_bytes=60 * 2**20),
         cost_estimate=pl.CostEstimate(
             flops=2 * tokens * dim * HEAD_DIM, bytes_accessed=4 * tokens * dim, transcendentals=0
         ),
         name="frame_states",
-    )(spot, keys, values)
+    )(spot, in_hbm(keys), in_hbm(values), *[in_hbm(array) for array in edged])
 
 
 def mix_kernel(
@@ -263,32 +290,27 @@
             flops=60 * tokens * dim, bytes_accessed=6 * tokens * dim, transcendentals=2 * tokens * dim
         ),
         name="mix",
-    )(place, spots, queries, residual, edge, gain, value_taps, gate_taps, *pieces)
-
-
-def edge_rows(queries, residual, rows, width):
-    devices, here = lax.axis_size("space"), lax.axis_index("space")
-    dim = queries.shape[-1]
-    both = [a.reshape(rows, width, dim) for a in (queries, residual)]
-    if devices == 2:
-        mine = jnp.stack([jnp.where(here == 0, a[rows - 1 :], a[:1]) for a in both])
-        edge = lax.ppermute(mine, "space", [(0, 1), (1, 0)])
-        place = jnp.where(here == 0, rows + 1, 0).astype(jnp.int32)[None]
-        return edge, place
+    )(place, spots, in_hbm(queries), in_hbm(residual), edge, gain, value_taps, gate_taps, *pieces)
+
+
+def edge_rows(queries, residual):
+    devices, rows = lax.axis_size("space"), queries.shape[0]
     up = [(i, i + 1) for i in range(devices - 1)]
     down = [(j, i) for i, j in up]
-    before = lax.ppermute(jnp.stack([a[rows - 1 :] for a in both]), "space", up)
-    after = lax.ppermute(jnp.stack([a[:1] for a in both]), "space", down)
+    both = jnp.stack([queries, residual])
+    before = lax.ppermute(both[:, rows - 1 :], "space", up)
+    after = lax.ppermute(both[:, :1], "space", down)
     return jnp.concatenate([before, after], axis=1), jnp.array([0, rows + 1], jnp.int32)
 
 
 def small_kernel(body, name, outs, scalars, *arrays):
     return pl.pallas_call(
         body,
-        out_shape=[jax.ShapeDtypeStruct(shape, jnp.bfloat16) for shape in outs],
+        out_shape=[pltpu.VMEM(shape, jnp.bfloat16) for shape in outs],
         in_specs=[pl.BlockSpec(memory_space=pltpu.SMEM)]
         + [pl.BlockSpec(memory_space=pltpu.VMEM)] * len(arrays),
         out_specs=[pl.BlockSpec(memory_space=pltpu.VMEM)] * len(outs),
+        compiler_params=pltpu.CompilerParams(vmem_limit_bytes=4 * 2**20),
         name=name,
     )(scalars, *arrays)
 
@@ -314,7 +336,10 @@
 
 def pair_sums_body(spot_ref, own_ref, partner_ref, *refs):
     *earlier, mine_ref, theirs_ref = refs
-    before = add(*[ref[...] for ref in earlier])
+    before = jnp.zeros(own_ref.shape, jnp.float32)
+    for k, ref in enumerate(earlier):
+        from_before = lax.rem(spot_ref[1] // (2 << k), 2) == 1
+        before = before + jnp.where(from_before, add(ref[...]), 0.0)
     own, partner = add(own_ref[...]), add(partner_ref[...])
     first = spot_ref[0] == 0
     both = before + (own + partner)
@@ -322,30 +347,33 @@
     theirs_ref[...] = jnp.where(first, both, before + partner).astype(jnp.bfloat16)
 
 
-def running_states(keys, values, rows):
+def running_states(keys, values, queries, residual, rows):
     devices, frames = lax.axis_size("space"), lax.axis_size("frame")
     core, frame = lax.axis_index("space"), lax.axis_index("frame")
-    if devices != 2 or frames % 2 or frames < 4:
+    if devices != 2 or frames < 2 or frames & (frames - 1):
         (state,) = frame_states(jnp.zeros((1,), jnp.int32), keys, values, rows, 1)
         state = lax.psum(state.astype(jnp.float32), "space").astype(jnp.bfloat16)
         every = lax.all_gather(state, "frame").astype(jnp.float32)
         reached = (jnp.arange(frames) <= frame)[:, None, None]
         total = jnp.sum(jnp.where(reached, every, 0.0), axis=0).astype(jnp.bfloat16)
-        return [total], jnp.zeros((1,), jnp.int32)
-    parity = lax.rem(frame, 2)
+        return [total], jnp.zeros((1,), jnp.int32), edge_rows(queries, residual)
     swap = [(0, 1), (1, 0)]
-    partners = [(f, f ^ 1) for f in range(frames)]
-    spot = parity.astype(jnp.int32)[None]
-    kept, sent = frame_states(core.astype(jnp.int32)[None], keys, values, rows, 2)
+    spot = jnp.stack([lax.rem(frame, 2), frame]).astype(jnp.int32)
+    kept, sent, edge = frame_states(
+        core.astype(jnp.int32)[None], keys, values, rows, 2, (queries, residual)
+    )
     got = lax.ppermute(sent, "space", swap)
     quarter = (rows // 4, LANES)
     own, sent = small_kernel(split_sum_body, "split_sum", [quarter] * 2, spot, kept, got)
-    partner = lax.ppermute(sent, "frame", partners)
+    edge, sent = lax.optimization_barrier((edge, sent))
+    edge = lax.ppermute(edge, "space", swap)
+    place = jnp.where(core == 0, queries.shape[0] + 1, 0).astype(jnp.int32)[None]
+    partner = lax.ppermute(sent, "frame", [(f, f ^ 1) for f in range(frames)])
     (total,) = small_kernel(sum_body, "pair_sum", [quarter], spot, own, partner)
     earlier = []
     stride = 2
     while stride < frames:
-        got = lax.ppermute(total, "frame", [(f, f + stride) for f in range(frames - stride)])
+        got = lax.ppermute(total, "frame", [(f, f ^ stride) for f in range(frames)])
         earlier.append(got)
         stride *= 2
         if stride < frames:
@@ -353,10 +381,10 @@
     mine, theirs = small_kernel(
         pair_sums_body, "pair_sums", [quarter] * 2, spot, own, partner, *earlier
     )
-    other = lax.ppermute(theirs, "frame", partners)
+    other = lax.ppermute(theirs, "frame", [(f, f ^ 1) for f in range(frames)])
     pieces = [mine, other, lax.ppermute(mine, "space", swap), lax.ppermute(other, "space", swap)]
-    spots = [2 * c + p for c in (core, 1 - core) for p in (parity, 1 - parity)]
-    return pieces, jnp.stack(spots).astype(jnp.int32)
+    spots = [2 * c + p for c in (core, 1 - core) for p in (spot[0], 1 - spot[0])]
+    return pieces, jnp.stack(spots).astype(jnp.int32), (edge, place)
 
 
 def on_device(queries, keys, values, residual, attn_gain, value_taps, gate_taps):
@@ -364,8 +392,13 @@
     tokens = frames * rows * width
     flat = lambda a: a.reshape(tokens, dim)
     state_rows = cdiv(cdiv(dim, LANES) * HEAD_DIM, 64) * 64
-    edge, place = edge_rows(queries, residual, rows, width)
-    pieces, spots = running_states(flat(keys), flat(values), state_rows)
+    pieces, spots, (edge, place) = running_states(
+        flat(keys),
+        flat(values),
+        queries.reshape(rows, width, dim),
+        residual.reshape(rows, width, dim),
+        state_rows,
+    )
     out = mix(
         place, spots, flat(queries), flat(residual), edge, attn_gain[None], value_taps, gate_taps,
         pieces, rows, width,

time: 63.5 us -> 49.7 us (0.78); the launches traced: 62.3 us -> 49.5 us
  Pallas kernels: 26.4 us -> 20.9 us
  local copies, waits for them, and re-layouts: 5.18 us -> 0.02 us
  starting transfers between devices: 14 us -> 9.22 us
  waiting for transfers between devices: 14.5 us -> 19.2 us
  other arithmetic: 2.19 us -> 0.16 us
    pallas_call x5, Pallas kernels: 11.5 us -> 6.18 us  [the longest x1 3.75 us: frame_states(): pl.pallas_call(functools.partial(state_kernel, dim, bool(edged)), out_sha...]
    unnamed x20 -> x6, local copies, waits for them, and re-layouts: 5.18 us -> 0.01 us
    ppermute x5, starting transfers between devices: 13.5 us -> 8.68 us  [the longest x2 4.51 us: running_states(): got = lax.ppermute(total, 'frame', [(f, f ^ stride) for f in range(frames)])]
    ppermute x5, waiting for transfers between devices: 13.2 us -> 16.8 us  [the longest x2 8.85 us: running_states(): got = lax.ppermute(total, 'frame', [(f, f ^ stride) for f in range(frames)])]
    select_n x1 -> x0, other arithmetic: 1.17 us -> none  [edge_rows(): mine = jnp.stack([jnp.where(here == 0, a[rows - 1:], a[:1]) for a in both])]
    ppermute x1, waiting for transfers between devices: 0.01 us -> 1.09 us  [running_states(): got = lax.ppermute(sent, 'space', swap)]
    another operation x2, other arithmetic: 1.02 us -> 0.16 us  [the longest x1 0.08 us: running_states(): return (pieces, jnp.stack(spots).astype(jnp.int32), (edge, place))]
  transfers between devices with their start and end apart: 8 -> 8, of which waited for: 5 -> 6; matrix products, arithmetic and copies ran while one was open for 4% -> 0% of each run, Pallas kernels for 11% -> 4%
where the time goes in v4:
time: 49.7 us; the launch traced here: 49.5 us
  Pallas kernels  20.9 us (42%)
  waiting for transfers between devices  19.2 us (39%)
  starting transfers between devices  9.22 us (19%)
    pallas_call x1, Pallas kernels, mix(): pl.pallas_call(functools.partial(mix_kernel, dim, rows, width, edges), ou...  14.7 us
    ppermute x2, waiting for transfers between devices, running_states(): got = lax.ppermute(total, 'frame', [(f, f ^ stride) for f in range(frames)])  8.85 us
    ppermute x2, starting transfers between devices, running_states(): got = lax.ppermute(total, 'frame', [(f, f ^ stride) for f in range(frames)])  4.51 us
    ppermute x1, waiting for transfers between devices, running_states(): partner = lax.ppermute(sent, 'frame', [(f, f ^ 1) for f in range(frames)])  4.02 us
    ppermute x1, waiting for transfers between devices, running_states(): other = lax.ppermute(theirs, 'frame', [(f, f ^ 1) for f in range(frames)])  3.97 us
    pallas_call x1, Pallas kernels, frame_states(): pl.pallas_call(functools.partial(state_kernel, dim, bool(edged)), out_sha...  3.75 us
    ppermute x1, starting transfers between devices, running_states(): partner = lax.ppermute(sent, 'frame', [(f, f ^ 1) for f in range(frames)])  2.67 us
    pallas_call x4, Pallas kernels, small_kernel(): pl.pallas_call(body, out_shape=[pltpu.VMEM(shape, jnp.bfloat16) for shape...  2.43 us
  transfers between devices with their start and end apart: 8, of which 6 were waited for; matrix products, arithmetic and copies ran while one was open for 0% of the time, Pallas kernels for 4%

profile of v4, /device:TPU:0, one launch (start us, length us, event | category | flops | bytes accessed | tf_op | source)
XLA Modules:
  0.0 49.5 jit_solution(5457528526407806734)
XLA Ops:
  0.0 3.8 %frame_states.1 = (bf16[1024,128]{1,0:T(8,128)(2,1)S(1)}, bf16[1024,128]{1,0:T(8,128)(2,1)S(1)}, bf16[2,1,80,2240]{3,2,1,0:T(8,128)(2,1)S(1)}) custom-call(s32[1]{0:T(128)} %bitcast.7.spot_ref, bf16[480,2240]{1,0:T(8,128)(2,1)} %bitcast.19, bf16[480,2240]{1,0:T(8,128)(2,1)} %bitcast.20, bf16[6,80,2240]{2,1,0:T(8,128)(2,1)} %bitcast.15, ...), custom_call_target="tpu_custom_call" | custom-call | flops 240844800 | bytes 4300800 | tf_op jit(solution)/shard_map/frame_states/pallas_call | solution.py:116
  3.8 0.5 %collective-permute-start = (bf16[1024,128]{1,0:T(8,128)(2,1)S(1)}, bf16[1024,128]{1,0:T(8,128)(2,1)S(1)}, u32[]{:S(2)}, u32[]{:S(2)}) collective-permute-start(bf16[1024,128]{1,0:T(8,128)(2,1)S(1)} %get-tuple-element.16), channel_id=1, source_target_pairs={{0,1},{1,0},{2,3},{3,2},{4,5},{5,4},{6,7},{7,6},{8,9},{9,8},{10,11... | collective-permute-start | bytes 786440 | tf_op jit(solution)/shard_map/ppermute | solution.py:365
  4.3 0.1 pad_add_fusion.1.spot_ref._
  4.4 1.1 %collective-permute-done.got_ref = bf16[1024,128]{1,0:T(8,128)(2,1)S(1)} collective-permute-done((bf16[1024,128]{1,0:T(8,128)(2,1)S(1)}, bf16[1024,128]{1,0:T(8,128)(2,1)S(1)}, u32[]{:S(2)}, u32[]{:S(2)}) %collective-permute-start) | collective-permute-done | bytes 262176 | tf_op jit(solution)/shard_map/ppermute | solution.py:365
  5.5 0.6 %split_sum.1 = (bf16[512,128]{1,0:T(8,128)(2,1)S(1)}, bf16[512,128]{1,0:T(8,128)(2,1)S(1)}) custom-call(s32[2]{0:T(128)S(1)} %pad_add_fusion.1.spot_ref._, bf16[1024,128]{1,0:T(8,128)(2,1)S(1)} %get-tuple-element.15.kept_ref, bf16[1024,128]{1,0:T(8,128)(2,1)S(1)} %collective-permute-done.got_ref), custom_call_target="tpu_custom_call" | custom-call | tf_op jit(solution)/shard_map/split_sum/pallas_call | solution.py:307
  6.1 0.4 collective-permute-start.1
  6.5 2.7 %collective-permute-start.2 = (bf16[512,128]{1,0:T(8,128)(2,1)S(1)}, bf16[512,128]{1,0:T(8,128)(2,1)S(1)}, u32[]{:S(2)}, u32[]{:S(2)}) collective-permute-start(bf16[512,128]{1,0:T(8,128)(2,1)S(1)} %get-tuple-element.20), channel_id=1, source_target_pairs={{0,2},{2,0},{4,6},{6,4},{8,10},{10,8},{12,14},{14,12},{1,3},{3,1},... | collective-permute-start | bytes 393224 | tf_op jit(solution)/shard_map/ppermute | solution.py:371
  9.2 4.0 %collective-permute-done.2.refs_1_.partner_ref = bf16[512,128]{1,0:T(8,128)(2,1)S(1)} collective-permute-done((bf16[512,128]{1,0:T(8,128)(2,1)S(1)}, bf16[512,128]{1,0:T(8,128)(2,1)S(1)}, u32[]{:S(2)}, u32[]{:S(2)}) %collective-permute-start.2) | collective-permute-done | bytes 131104 | tf_op jit(solution)/shard_map/ppermute | solution.py:371
  13.2 0.6 %pair_sum.1.refs_0_ = bf16[512,128]{1,0:T(8,128)(2,1)S(1)} custom-call(s32[2]{0:T(128)S(1)} %pad_add_fusion.1.spot_ref._, bf16[512,128]{1,0:T(8,128)(2,1)S(1)} %get-tuple-element.19.refs_0_.own_ref, bf16[512,128]{1,0:T(8,128)(2,1)S(1)} %collective-permute-done.2.refs_1_.partner_ref), custom_call_target="tpu_custom_call" | custom-call | tf_op jit(solution)/shard_map/pair_sum/pallas_call | solution.py:307
  13.8 1.9 %collective-permute-start.3 = (bf16[512,128]{1,0:T(8,128)(2,1)S(1)}, bf16[512,128]{1,0:T(8,128)(2,1)S(1)}, u32[]{:S(2)}, u32[]{:S(2)}) collective-permute-start(bf16[512,128]{1,0:T(8,128)(2,1)S(1)} %pair_sum.1.refs_0_), channel_id=1, source_target_pairs={{0,4},{2,6},{4,0},{6,2},{8,12},{10,14},{12,8},{14,10},{1,5},{3,7},... | collective-permute-start | bytes 393224 | tf_op jit(solution)/shard_map/ppermute | solution.py:376
  15.6 3.4 %collective-permute-done.3.refs_1_.refs_0_ = bf16[512,128]{1,0:T(8,128)(2,1)S(1)} collective-permute-done((bf16[512,128]{1,0:T(8,128)(2,1)S(1)}, bf16[512,128]{1,0:T(8,128)(2,1)S(1)}, u32[]{:S(2)}, u32[]{:S(2)}) %collective-permute-start.3) | collective-permute-done | bytes 131104 | tf_op jit(solution)/shard_map/ppermute | solution.py:376
  19.0 0.6 %stride_sum.1 = bf16[512,128]{1,0:T(8,128)(2,1)S(1)} custom-call(s32[2]{0:T(128)S(1)} %pad_add_fusion.1.spot_ref._, bf16[512,128]{1,0:T(8,128)(2,1)S(1)} %pair_sum.1.refs_0_, bf16[512,128]{1,0:T(8,128)(2,1)S(1)} %collective-permute-done.3.refs_1_.refs_0_), custom_call_target="tpu_custom_call" | custom-call | tf_op jit(solution)/shard_map/stride_sum/pallas_call | solution.py:307
  19.6 2.6 %collective-permute-start.4 = (bf16[512,128]{1,0:T(8,128)(2,1)S(1)}, bf16[512,128]{1,0:T(8,128)(2,1)S(1)}, u32[]{:S(2)}, u32[]{:S(2)}) collective-permute-start(bf16[512,128]{1,0:T(8,128)(2,1)S(1)} %stride_sum.1), channel_id=1, source_target_pairs={{0,8},{2,10},{4,12},{6,14},{8,0},{10,2},{12,4},{14,6},{1,9},{3,11}... | collective-permute-start | bytes 393224 | tf_op jit(solution)/shard_map/ppermute | solution.py:376
  22.3 5.4 %collective-permute-done.4.refs_1_ = bf16[512,128]{1,0:T(8,128)(2,1)S(1)} collective-permute-done((bf16[512,128]{1,0:T(8,128)(2,1)S(1)}, bf16[512,128]{1,0:T(8,128)(2,1)S(1)}, u32[]{:S(2)}, u32[]{:S(2)}) %collective-permute-start.4) | collective-permute-done | bytes 131104 | tf_op jit(solution)/shard_map/ppermute | solution.py:376
  27.7 0.7 %pair_sums.1 = (bf16[512,128]{1,0:T(8,128)(2,1)S(1)}, bf16[512,128]{1,0:T(8,128)(2,1)S(1)}) custom-call(s32[2]{0:T(128)S(1)} %pad_add_fusion.1.spot_ref._, bf16[512,128]{1,0:T(8,128)(2,1)S(1)} %get-tuple-element.19.refs_0_.own_ref, bf16[512,128]{1,0:T(8,128)(2,1)S(1)} %collective-permute-done.2.refs_1_.partner_ref, ...), custom_call_target="tpu_custom_call" | custom-call | tf_op jit(solution)/shard_map/pair_sums/pallas_call | solution.py:307
  28.4 1.1 %collective-permute-start.5 = (bf16[512,128]{1,0:T(8,128)(2,1)S(1)}, bf16[512,128]{1,0:T(8,128)(2,1)S(1)}, u32[]{:S(2)}, u32[]{:S(2)}) collective-permute-start(bf16[512,128]{1,0:T(8,128)(2,1)S(1)} %get-tuple-element.22), channel_id=1, source_target_pairs={{0,2},{2,0},{4,6},{6,4},{8,10},{10,8},{12,14},{14,12},{1,3},{3,1},... | collective-permute-start | bytes 393224 | tf_op jit(solution)/shard_map/ppermute | solution.py:384
  29.5 0.0 collective-permute-start.6
  29.5 4.0 %collective-permute-done.5.refs_1_ = bf16[512,128]{1,0:T(8,128)(2,1)S(1)} collective-permute-done((bf16[512,128]{1,0:T(8,128)(2,1)S(1)}, bf16[512,128]{1,0:T(8,128)(2,1)S(1)}, u32[]{:S(2)}, u32[]{:S(2)}) %collective-permute-start.5) | collective-permute-done | bytes 131104 | tf_op jit(solution)/shard_map/ppermute | solution.py:384
  33.4 0.0 collective-permute-start.7
  33.5 0.1 pad_add_fusion.spots_ref
  33.5 0.0 collective-permute-done.6.refs_2_
  33.5 1.2 %collective-permute-done.7.refs_3_ = bf16[512,128]{1,0:T(8,128)(2,1)S(1)} collective-permute-done((bf16[512,128]{1,0:T(8,128)(2,1)S(1)}, bf16[512,128]{1,0:T(8,128)(2,1)S(1)}, u32[]{:S(2)}, u32[]{:S(2)}) %collective-permute-start.7) | collective-permute-done | bytes 131104 | tf_op jit(solution)/shard_map/ppermute | solution.py:385
  34.8 0.0 collective-permute-done.1.edge_ref
  34.8 14.7 %mix.1 = bf16[480,2240]{1,0:T(8,128)(2,1)} custom-call(s32[1]{0:T(128)} %bitcast.place_ref, s32[4]{0:T(128)S(1)} %pad_add_fusion.spots_ref, bf16[480,2240]{1,0:T(8,128)(2,1)} %bitcast.16, bf16[480,2240]{1,0:T(8,128)(2,1)} %bitcast.18, bf16[2,1,80,2240]{3,2,1,0:T(8,128)(2,1)S(1)} %collective-permute-done.1.edge_ref, f32[1,2240]{1,0:T(1,128)S(1)} %broadcast_in_dim.11.gain_ref, ...), custom_call_target="tpu_custom_call" | custom-call | flops 64512000 | bytes 6451200 | tf_op jit(solution)/shard_map/mix/pallas_call | solution.py:263
  (7 shorter events, 0.0 us)
Async XLA Ops:
  0.0 33.4 %copy-start.2 = (f32[2240]{0:T(1024)S(1)}, f32[2240]{0:T(1024)}, u32[]{:S(2)}) copy-start(f32[2240]{0:T(1024)} %param.11) | copy-start | bytes 26884
  0.0 34.8 %copy-start = (f32[9,2240]{1,0:T(8,128)S(1)}, f32[9,2240]{1,0:T(8,128)}, u32[]{:S(2)}) copy-start(f32[9,2240]{1,0:T(8,128)} %vtaps_ref.1) | copy-start | bytes 241924
  0.0 34.8 %copy-start.1 = (f32[9,2240]{1,0:T(8,128)S(1)}, f32[9,2240]{1,0:T(8,128)}, u32[]{:S(2)}) copy-start(f32[9,2240]{1,0:T(8,128)} %gtaps_ref.1) | copy-start | bytes 241924
  3.8 1.7 %collective-permute-start = (bf16[1024,128]{1,0:T(8,128)(2,1)S(1)}, bf16[1024,128]{1,0:T(8,128)(2,1)S(1)}, u32[]{:S(2)}, u32[]{:S(2)}) collective-permute-start(bf16[1024,128]{1,0:T(8,128)(2,1)S(1)} %get-tuple-element.16), channel_id=1, source_target_pairs={{0,1},{1,0},{2,3},{3,2},{4,5},{5,4},{6,7},{7,6},{8,9},{9,8},{10,11... | collective-permute-start | bytes 786440 | tf_op jit(solution)/shard_map/ppermute | solution.py:365
  6.1 28.7 %collective-permute-start.1 = (bf16[2,1,80,2240]{3,2,1,0:T(8,128)(2,1)S(1)}, bf16[2,1,80,2240]{3,2,1,0:T(8,128)(2,1)S(1)}, u32[]{:S(2)}, u32[]{:S(2)}) collective-permute-start(bf16[2,1,80,2240]{3,2,1,0:T(8,128)(2,1)S(1)} %get-tuple-element.18), channel_id=1, source_target_pairs={{0,1},{1,0},{2,3},{3,2},{4,5},{5,4},{6,7},{7,6},{8,9},{9,8},{10,11... | collective-permute-start | bytes 2150408 | tf_op jit(solution)/shard_map/ppermute | solution.py:369
  6.5 6.7 %collective-permute-start.2 = (bf16[512,128]{1,0:T(8,128)(2,1)S(1)}, bf16[512,128]{1,0:T(8,128)(2,1)S(1)}, u32[]{:S(2)}, u32[]{:S(2)}) collective-permute-start(bf16[512,128]{1,0:T(8,128)(2,1)S(1)} %get-tuple-element.20), channel_id=1, source_target_pairs={{0,2},{2,0},{4,6},{6,4},{8,10},{10,8},{12,14},{14,12},{1,3},{3,1},... | collective-permute-start | bytes 393224 | tf_op jit(solution)/shard_map/ppermute | solution.py:371
  13.8 5.3 %collective-permute-start.3 = (bf16[512,128]{1,0:T(8,128)(2,1)S(1)}, bf16[512,128]{1,0:T(8,128)(2,1)S(1)}, u32[]{:S(2)}, u32[]{:S(2)}) collective-permute-start(bf16[512,128]{1,0:T(8,128)(2,1)S(1)} %pair_sum.1.refs_0_), channel_id=1, source_target_pairs={{0,4},{2,6},{4,0},{6,2},{8,12},{10,14},{12,8},{14,10},{1,5},{3,7},... | collective-permute-start | bytes 393224 | tf_op jit(solution)/shard_map/ppermute | solution.py:376
  19.6 8.1 %collective-permute-start.4 = (bf16[512,128]{1,0:T(8,128)(2,1)S(1)}, bf16[512,128]{1,0:T(8,128)(2,1)S(1)}, u32[]{:S(2)}, u32[]{:S(2)}) collective-permute-start(bf16[512,128]{1,0:T(8,128)(2,1)S(1)} %stride_sum.1), channel_id=1, source_target_pairs={{0,8},{2,10},{4,12},{6,14},{8,0},{10,2},{12,4},{14,6},{1,9},{3,11}... | collective-permute-start | bytes 393224 | tf_op jit(solution)/shard_map/ppermute | solution.py:376
  28.4 5.0 %collective-permute-start.5 = (bf16[512,128]{1,0:T(8,128)(2,1)S(1)}, bf16[512,128]{1,0:T(8,128)(2,1)S(1)}, u32[]{:S(2)}, u32[]{:S(2)}) collective-permute-start(bf16[512,128]{1,0:T(8,128)(2,1)S(1)} %get-tuple-element.22), channel_id=1, source_target_pairs={{0,2},{2,0},{4,6},{6,4},{8,10},{10,8},{12,14},{14,12},{1,3},{3,1},... | collective-permute-start | bytes 393224 | tf_op jit(solution)/shard_map/ppermute | solution.py:384
  29.5 4.1 %collective-permute-start.6 = (bf16[512,128]{1,0:T(8,128)(2,1)S(1)}, bf16[512,128]{1,0:T(8,128)(2,1)S(1)}, u32[]{:S(2)}, u32[]{:S(2)}) collective-permute-start(bf16[512,128]{1,0:T(8,128)(2,1)S(1)} %get-tuple-element.21.refs_0_), channel_id=1, source_target_pairs={{0,1},{1,0},{2,3},{3,2},{4,5},{5,4},{6,7},{7,6},{8,9},{9,8},{10,11... | collective-permute-start | bytes 393224 | tf_op jit(solution)/shard_map/ppermute | solution.py:385
  33.4 1.3 %collective-permute-start.7 = (bf16[512,128]{1,0:T(8,128)(2,1)S(1)}, bf16[512,128]{1,0:T(8,128)(2,1)S(1)}, u32[]{:S(2)}, u32[]{:S(2)}) collective-permute-start(bf16[512,128]{1,0:T(8,128)(2,1)S(1)} %collective-permute-done.5.refs_1_), channel_id=1, source_target_pairs={{0,1},{1,0},{2,3},{3,2},{4,5},{5,4},{6,7},{7,6},{8,9},{9,8},{10,11... | collective-permute-start | bytes 393224 | tf_op jit(solution)/shard_map/ppermute | solution.py:385

commit v5 on v4

--- a/solution.py
+++ b/solution.py
@@ -10,6 +10,7 @@
 
 HEAD_DIM = 112
 LANES = 128
+PACK = 16
 GROUP = math.lcm(HEAD_DIM, LANES)
 TILES = GROUP // LANES
 
@@ -139,7 +140,7 @@
     dim, rows, width, edges,
     place_ref, spots_ref, queries_ref, residual_ref, edge_ref, gain_ref, vtaps_ref, gtaps_ref, *refs,
 ):
-    *pieces, out_ref, states, features, weights, same, numer, squares, shifted = refs
+    *pieces, out_ref, states, features, weights, same, numer, squares, shifted, taps = refs
     step = pl.program_id(0)
     tokens = rows * width
     total = tokens + edges * width
@@ -158,7 +159,7 @@
                         number, start : start + HEAD_DIM, side * LANES : (side + 1) * LANES
                     ] = block.astype(jnp.bfloat16)
         for row in (0, rows + 1):
-            shifted[:, row] = jnp.zeros((3, width, LANES), jnp.float32)
+            shifted[:, row] = jnp.zeros(shifted.shape[:1] + shifted.shape[2:], jnp.bfloat16)
         for k, piece in enumerate(pieces):
             size = piece.shape[0]
             states[pl.ds(pl.multiple_of(spots_ref[k] * size, 16), size), :] = piece[...]
@@ -168,10 +169,12 @@
     lane = lane_iota((HEAD_DIM, LANES))
 
     def store_shifted(mixed, row):
-        mixed = mixed.astype(jnp.bfloat16).astype(jnp.float32)
-        shifted[1, row] = mixed
-        shifted[0, row] = jnp.where(column == 0, 0.0, pltpu.roll(mixed, 1, 0))
-        shifted[2, row] = jnp.where(column == width - 1, 0.0, pltpu.roll(mixed, width - 1, 0))
+        packed = lambda a: a.astype(jnp.bfloat16).reshape(width // PACK, PACK, LANES)
+        shifted[1, row] = packed(mixed)
+        shifted[0, row] = packed(jnp.where(column == 0, 0.0, pltpu.roll(mixed, 1, 0)))
+        shifted[2, row] = packed(
+            jnp.where(column == width - 1, 0.0, pltpu.roll(mixed, width - 1, 0))
+        )
 
     def body(lanes):
         count = cdiv(lanes, LANES)
@@ -214,40 +217,43 @@
                 same[number, :depth, :wide],
                 preferred_element_type=jnp.float32,
             )
-            here = slice(tiles[0] * LANES, tiles[0] * LANES + wide)
             scale = lax.rsqrt(sums * (1.0 / HEAD_DIM) + 1e-06)
-            numer[:, here] = numer[:, here] * scale * gain_ref[:, here]
-
-        for j in range(count):
-            here = slice(j * LANES, (j + 1) * LANES)
-            for row in range(rows):
-                source = slice(row * width, (row + 1) * width)
-                store_shifted(
-                    residual_ref[source, here].astype(jnp.float32) + numer[source, here], row + 1
-                )
-            for e in range(edges):
-                source = slice(tokens + e * width, tokens + (e + 1) * width)
-                store_shifted(
-                    edge_ref[1, e, :, here].astype(jnp.float32) + numer[source, here], place_ref[e]
-                )
-
-            def convolve(row, carry, here=here):
-                conv_v = jnp.zeros((width, LANES), jnp.float32)
-                half_g = jnp.zeros((width, LANES), jnp.float32)
-                for tap_row in range(3):
-                    for tap_col in range(3):
-                        window = shifted[tap_col, row + tap_row]
-                        tap = 3 * tap_row + tap_col
-                        conv_v = conv_v + vtaps_ref[tap : tap + 1, here] * window
-                        half_g = half_g + (0.5 * gtaps_ref[tap : tap + 1, here]) * window
-                gate = half_g + half_g * jnp.tanh(half_g)
-                result = shifted[1, row + 1] + conv_v * gate
-                out_ref[pl.ds(pl.multiple_of(row * width, width), width), here] = result.astype(
-                    jnp.bfloat16
-                )
-                return carry
-
-            lax.fori_loop(0, rows, convolve, 0)
+            for side, j in enumerate(tiles):
+                here = slice(j * LANES, (j + 1) * LANES)
+                gain = gain_ref[:, here]
+
+                def mixed(source, residual, side=side, here=here, gain=gain):
+                    normed = numer[source, here] * scale[source, side * LANES : (side + 1) * LANES]
+                    return residual.astype(jnp.float32) + normed * gain
+
+                for row in range(rows):
+                    source = slice(row * width, (row + 1) * width)
+                    store_shifted(mixed(source, residual_ref[source, here]), row + 1)
+                for e in range(edges):
+                    source = slice(tokens + e * width, tokens + (e + 1) * width)
+                    store_shifted(mixed(source, edge_ref[1, e, :, here]), place_ref[e])
+                for tap in range(9):
+                    for k, (ref, factor) in enumerate(((vtaps_ref, 1.0), (gtaps_ref, 0.5))):
+                        row = ref[tap : tap + 1, here] * factor
+                        taps[k, tap] = jnp.broadcast_to(row, (PACK, LANES)).astype(jnp.bfloat16)
+
+                def convolve(row, carry, here=here):
+                    sums = []
+                    for tap_row in range(3):
+                        windows = [shifted[i, row + tap_row] for i in range(3)]
+                        for k in range(2):
+                            terms = [taps[k, 3 * tap_row + i] * windows[i] for i in range(3)]
+                            sums.append(terms[0] + terms[1] + terms[2])
+                    conv_v = (sums[0] + sums[2] + sums[4]).astype(jnp.float32)
+                    half_g = (sums[1] + sums[3] + sums[5]).astype(jnp.float32)
+                    gate = half_g + half_g * jnp.tanh(half_g)
+                    result = shifted[1, row + 1].astype(jnp.float32) + conv_v * gate
+                    out_ref[pl.ds(pl.multiple_of(row * width, width), width), here] = (
+                        result.astype(jnp.bfloat16).reshape(width, LANES)
+                    )
+                    return carry
+
+                lax.fori_loop(0, rows, convolve, 0)
 
     by_group(dim, body)
 
@@ -283,7 +289,8 @@
             pltpu.VMEM((len(pairs), depth, 2 * LANES), jnp.bfloat16),
             pltpu.VMEM((total, GROUP), jnp.float32),
             pltpu.VMEM((total, GROUP), jnp.bfloat16),
-            pltpu.VMEM((3, rows + 2, width, LANES), jnp.float32),
+            pltpu.VMEM((3, rows + 2, width // PACK, PACK, LANES), jnp.bfloat16),
+            pltpu.VMEM((2, 9, PACK, LANES), jnp.bfloat16),
         ],
         compiler_params=pltpu.CompilerParams(vmem_limit_bytes=36 * 2**20),
         cost_estimate=pl.CostEstimate(

time: 49.7 us -> 52.3 us (1.052)
  Pallas kernels: 20.9 us -> 23.6 us
    pallas_call x1, Pallas kernels: 14.7 us -> 17.4 us  [mix(): pl.pallas_call(functools.partial(mix_kernel, dim, rows, width, edges), ou...]
  transfers between devices with their start and end apart: 8 -> 8, of which waited for: 6 -> 6; matrix products, arithmetic and copies ran while one was open for 0% -> 0% of each run, Pallas kernels for 4% -> 3%
where the time goes in v5:
time: 52.3 us; the launch traced here: 52.2 us
  Pallas kernels  23.6 us (45%)
  waiting for transfers between devices  19.2 us (37%)
  starting transfers between devices  9.22 us (18%)
    pallas_call x1, Pallas kernels, mix(): pl.pallas_call(functools.partial(mix_kernel, dim, rows, width, edges), ou...  17.4 us
    ppermute x2, waiting for transfers between devices, running_states(): got = lax.ppermute(total, 'frame', [(f, f ^ stride) for f in range(frames)])  8.85 us
    ppermute x2, starting transfers between devices, running_states(): got = lax.ppermute(total, 'frame', [(f, f ^ stride) for f in range(frames)])  4.51 us
    ppermute x1, waiting for transfers between devices, running_states(): partner = lax.ppermute(sent, 'frame', [(f, f ^ 1) for f in range(frames)])  4.02 us
    ppermute x1, waiting for transfers between devices, running_states(): other = lax.ppermute(theirs, 'frame', [(f, f ^ 1) for f in range(frames)])  3.97 us
    pallas_call x1, Pallas kernels, frame_states(): pl.pallas_call(functools.partial(state_kernel, dim, bool(edged)), out_sha...  3.75 us
    ppermute x1, starting transfers between devices, running_states(): partner = lax.ppermute(sent, 'frame', [(f, f ^ 1) for f in range(frames)])  2.67 us
    pallas_call x4, Pallas kernels, small_kernel(): pl.pallas_call(body, out_shape=[pltpu.VMEM(shape, jnp.bfloat16) for shape...  2.43 us
  transfers between devices with their start and end apart: 8, of which 6 were waited for; matrix products, arithmetic and copies ran while one was open for 0% of the time, Pallas kernels for 3%

profile of v5, /device:TPU:0, one launch (start us, length us, event | category | flops | bytes accessed | tf_op | source)
XLA Modules:
  0.0 52.2 jit_solution(13456625869581256210)
XLA Ops:
  0.0 3.8 %frame_states.1 = (bf16[1024,128]{1,0:T(8,128)(2,1)S(1)}, bf16[1024,128]{1,0:T(8,128)(2,1)S(1)}, bf16[2,1,80,2240]{3,2,1,0:T(8,128)(2,1)S(1)}) custom-call(s32[1]{0:T(128)} %bitcast.7.spot_ref, bf16[480,2240]{1,0:T(8,128)(2,1)} %bitcast.19, bf16[480,2240]{1,0:T(8,128)(2,1)} %bitcast.20, bf16[6,80,2240]{2,1,0:T(8,128)(2,1)} %bitcast.15, ...), custom_call_target="tpu_custom_call" | custom-call | flops 240844800 | bytes 4300800 | tf_op jit(solution)/shard_map/frame_states/pallas_call | solution.py:117
  3.8 0.5 %collective-permute-start = (bf16[1024,128]{1,0:T(8,128)(2,1)S(1)}, bf16[1024,128]{1,0:T(8,128)(2,1)S(1)}, u32[]{:S(2)}, u32[]{:S(2)}) collective-permute-start(bf16[1024,128]{1,0:T(8,128)(2,1)S(1)} %get-tuple-element.16), channel_id=1, source_target_pairs={{0,1},{1,0},{2,3},{3,2},{4,5},{5,4},{6,7},{7,6},{8,9},{9,8},{10,11... | collective-permute-start | bytes 786440 | tf_op jit(solution)/shard_map/ppermute | solution.py:372
  4.3 0.1 pad_add_fusion.1.spot_ref._
  4.4 1.1 %collective-permute-done.got_ref = bf16[1024,128]{1,0:T(8,128)(2,1)S(1)} collective-permute-done((bf16[1024,128]{1,0:T(8,128)(2,1)S(1)}, bf16[1024,128]{1,0:T(8,128)(2,1)S(1)}, u32[]{:S(2)}, u32[]{:S(2)}) %collective-permute-start) | collective-permute-done | bytes 262176 | tf_op jit(solution)/shard_map/ppermute | solution.py:372
  5.5 0.6 %split_sum.1 = (bf16[512,128]{1,0:T(8,128)(2,1)S(1)}, bf16[512,128]{1,0:T(8,128)(2,1)S(1)}) custom-call(s32[2]{0:T(128)S(1)} %pad_add_fusion.1.spot_ref._, bf16[1024,128]{1,0:T(8,128)(2,1)S(1)} %get-tuple-element.15.kept_ref, bf16[1024,128]{1,0:T(8,128)(2,1)S(1)} %collective-permute-done.got_ref), custom_call_target="tpu_custom_call" | custom-call | tf_op jit(solution)/shard_map/split_sum/pallas_call | solution.py:314
  6.1 0.4 collective-permute-start.1
  6.5 2.7 %collective-permute-start.2 = (bf16[512,128]{1,0:T(8,128)(2,1)S(1)}, bf16[512,128]{1,0:T(8,128)(2,1)S(1)}, u32[]{:S(2)}, u32[]{:S(2)}) collective-permute-start(bf16[512,128]{1,0:T(8,128)(2,1)S(1)} %get-tuple-element.20), channel_id=1, source_target_pairs={{0,2},{2,0},{4,6},{6,4},{8,10},{10,8},{12,14},{14,12},{1,3},{3,1},... | collective-permute-start | bytes 393224 | tf_op jit(solution)/shard_map/ppermute | solution.py:378
  9.2 4.0 %collective-permute-done.2.refs_1_.partner_ref = bf16[512,128]{1,0:T(8,128)(2,1)S(1)} collective-permute-done((bf16[512,128]{1,0:T(8,128)(2,1)S(1)}, bf16[512,128]{1,0:T(8,128)(2,1)S(1)}, u32[]{:S(2)}, u32[]{:S(2)}) %collective-permute-start.2) | collective-permute-done | bytes 131104 | tf_op jit(solution)/shard_map/ppermute | solution.py:378
  13.2 0.6 %pair_sum.1.refs_0_ = bf16[512,128]{1,0:T(8,128)(2,1)S(1)} custom-call(s32[2]{0:T(128)S(1)} %pad_add_fusion.1.spot_ref._, bf16[512,128]{1,0:T(8,128)(2,1)S(1)} %get-tuple-element.19.refs_0_.own_ref, bf16[512,128]{1,0:T(8,128)(2,1)S(1)} %collective-permute-done.2.refs_1_.partner_ref), custom_call_target="tpu_custom_call" | custom-call | tf_op jit(solution)/shard_map/pair_sum/pallas_call | solution.py:314
  13.8 1.9 %collective-permute-start.3 = (bf16[512,128]{1,0:T(8,128)(2,1)S(1)}, bf16[512,128]{1,0:T(8,128)(2,1)S(1)}, u32[]{:S(2)}, u32[]{:S(2)}) collective-permute-start(bf16[512,128]{1,0:T(8,128)(2,1)S(1)} %pair_sum.1.refs_0_), channel_id=1, source_target_pairs={{0,4},{2,6},{4,0},{6,2},{8,12},{10,14},{12,8},{14,10},{1,5},{3,7},... | collective-permute-start | bytes 393224 | tf_op jit(solution)/shard_map/ppermute | solution.py:383
  15.6 3.4 %collective-permute-done.3.refs_1_.refs_0_ = bf16[512,128]{1,0:T(8,128)(2,1)S(1)} collective-permute-done((bf16[512,128]{1,0:T(8,128)(2,1)S(1)}, bf16[512,128]{1,0:T(8,128)(2,1)S(1)}, u32[]{:S(2)}, u32[]{:S(2)}) %collective-permute-start.3) | collective-permute-done | bytes 131104 | tf_op jit(solution)/shard_map/ppermute | solution.py:383
  19.0 0.6 %stride_sum.1 = bf16[512,128]{1,0:T(8,128)(2,1)S(1)} custom-call(s32[2]{0:T(128)S(1)} %pad_add_fusion.1.spot_ref._, bf16[512,128]{1,0:T(8,128)(2,1)S(1)} %pair_sum.1.refs_0_, bf16[512,128]{1,0:T(8,128)(2,1)S(1)} %collective-permute-done.3.refs_1_.refs_0_), custom_call_target="tpu_custom_call" | custom-call | tf_op jit(solution)/shard_map/stride_sum/pallas_call | solution.py:314
  19.6 2.6 %collective-permute-start.4 = (bf16[512,128]{1,0:T(8,128)(2,1)S(1)}, bf16[512,128]{1,0:T(8,128)(2,1)S(1)}, u32[]{:S(2)}, u32[]{:S(2)}) collective-permute-start(bf16[512,128]{1,0:T(8,128)(2,1)S(1)} %stride_sum.1), channel_id=1, source_target_pairs={{0,8},{2,10},{4,12},{6,14},{8,0},{10,2},{12,4},{14,6},{1,9},{3,11}... | collective-permute-start | bytes 393224 | tf_op jit(solution)/shard_map/ppermute | solution.py:383
  22.3 5.4 %collective-permute-done.4.refs_1_ = bf16[512,128]{1,0:T(8,128)(2,1)S(1)} collective-permute-done((bf16[512,128]{1,0:T(8,128)(2,1)S(1)}, bf16[512,128]{1,0:T(8,128)(2,1)S(1)}, u32[]{:S(2)}, u32[]{:S(2)}) %collective-permute-start.4) | collective-permute-done | bytes 131104 | tf_op jit(solution)/shard_map/ppermute | solution.py:383
  27.7 0.7 %pair_sums.1 = (bf16[512,128]{1,0:T(8,128)(2,1)S(1)}, bf16[512,128]{1,0:T(8,128)(2,1)S(1)}) custom-call(s32[2]{0:T(128)S(1)} %pad_add_fusion.1.spot_ref._, bf16[512,128]{1,0:T(8,128)(2,1)S(1)} %get-tuple-element.19.refs_0_.own_ref, bf16[512,128]{1,0:T(8,128)(2,1)S(1)} %collective-permute-done.2.refs_1_.partner_ref, ...), custom_call_target="tpu_custom_call" | custom-call | tf_op jit(solution)/shard_map/pair_sums/pallas_call | solution.py:314
  28.4 1.1 %collective-permute-start.5 = (bf16[512,128]{1,0:T(8,128)(2,1)S(1)}, bf16[512,128]{1,0:T(8,128)(2,1)S(1)}, u32[]{:S(2)}, u32[]{:S(2)}) collective-permute-start(bf16[512,128]{1,0:T(8,128)(2,1)S(1)} %get-tuple-element.22), channel_id=1, source_target_pairs={{0,2},{2,0},{4,6},{6,4},{8,10},{10,8},{12,14},{14,12},{1,3},{3,1},... | collective-permute-start | bytes 393224 | tf_op jit(solution)/shard_map/ppermute | solution.py:391
  29.5 0.0 collective-permute-start.6
  29.5 4.0 %collective-permute-done.5.refs_1_ = bf16[512,128]{1,0:T(8,128)(2,1)S(1)} collective-permute-done((bf16[512,128]{1,0:T(8,128)(2,1)S(1)}, bf16[512,128]{1,0:T(8,128)(2,1)S(1)}, u32[]{:S(2)}, u32[]{:S(2)}) %collective-permute-start.5) | collective-permute-done | bytes 131104 | tf_op jit(solution)/shard_map/ppermute | solution.py:391
  33.4 0.0 collective-permute-start.7
  33.5 0.1 pad_add_fusion.spots_ref
  33.5 0.0 collective-permute-done.6.refs_2_
  33.5 1.2 %collective-permute-done.7.refs_3_ = bf16[512,128]{1,0:T(8,128)(2,1)S(1)} collective-permute-done((bf16[512,128]{1,0:T(8,128)(2,1)S(1)}, bf16[512,128]{1,0:T(8,128)(2,1)S(1)}, u32[]{:S(2)}, u32[]{:S(2)}) %collective-permute-start.7) | collective-permute-done | bytes 131104 | tf_op jit(solution)/shard_map/ppermute | solution.py:392
  34.8 0.0 collective-permute-done.1.edge_ref
  34.8 17.4 %mix.1 = bf16[480,2240]{1,0:T(8,128)(2,1)} custom-call(s32[1]{0:T(128)} %bitcast.place_ref, s32[4]{0:T(128)S(1)} %pad_add_fusion.spots_ref, bf16[480,2240]{1,0:T(8,128)(2,1)} %bitcast.16, bf16[480,2240]{1,0:T(8,128)(2,1)} %bitcast.18, bf16[2,1,80,2240]{3,2,1,0:T(8,128)(2,1)S(1)} %collective-permute-done.1.edge_ref, f32[1,2240]{1,0:T(1,128)S(1)} %broadcast_in_dim.11.gain_ref, ...), custom_call_target="tpu_custom_call" | custom-call | flops 64512000 | bytes 6451200 | tf_op jit(solution)/shard_map/mix/pallas_call | solution.py:269
  (7 shorter events, 0.0 us)
Async XLA Ops:
  0.0 33.4 %copy-start.2 = (f32[2240]{0:T(1024)S(1)}, f32[2240]{0:T(1024)}, u32[]{:S(2)}) copy-start(f32[2240]{0:T(1024)} %param.11) | copy-start | bytes 26884
  0.0 34.8 %copy-start = (f32[9,2240]{1,0:T(8,128)S(1)}, f32[9,2240]{1,0:T(8,128)}, u32[]{:S(2)}) copy-start(f32[9,2240]{1,0:T(8,128)} %vtaps_ref.1) | copy-start | bytes 241924
  0.0 34.8 %copy-start.1 = (f32[9,2240]{1,0:T(8,128)S(1)}, f32[9,2240]{1,0:T(8,128)}, u32[]{:S(2)}) copy-start(f32[9,2240]{1,0:T(8,128)} %gtaps_ref.1) | copy-start | bytes 241924
  3.8 1.7 %collective-permute-start = (bf16[1024,128]{1,0:T(8,128)(2,1)S(1)}, bf16[1024,128]{1,0:T(8,128)(2,1)S(1)}, u32[]{:S(2)}, u32[]{:S(2)}) collective-permute-start(bf16[1024,128]{1,0:T(8,128)(2,1)S(1)} %get-tuple-element.16), channel_id=1, source_target_pairs={{0,1},{1,0},{2,3},{3,2},{4,5},{5,4},{6,7},{7,6},{8,9},{9,8},{10,11... | collective-permute-start | bytes 786440 | tf_op jit(solution)/shard_map/ppermute | solution.py:372
  6.1 28.7 %collective-permute-start.1 = (bf16[2,1,80,2240]{3,2,1,0:T(8,128)(2,1)S(1)}, bf16[2,1,80,2240]{3,2,1,0:T(8,128)(2,1)S(1)}, u32[]{:S(2)}, u32[]{:S(2)}) collective-permute-start(bf16[2,1,80,2240]{3,2,1,0:T(8,128)(2,1)S(1)} %get-tuple-element.18), channel_id=1, source_target_pairs={{0,1},{1,0},{2,3},{3,2},{4,5},{5,4},{6,7},{7,6},{8,9},{9,8},{10,11... | collective-permute-start | bytes 2150408 | tf_op jit(solution)/shard_map/ppermute | solution.py:376
  6.5 6.7 %collective-permute-start.2 = (bf16[512,128]{1,0:T(8,128)(2,1)S(1)}, bf16[512,128]{1,0:T(8,128)(2,1)S(1)}, u32[]{:S(2)}, u32[]{:S(2)}) collective-permute-start(bf16[512,128]{1,0:T(8,128)(2,1)S(1)} %get-tuple-element.20), channel_id=1, source_target_pairs={{0,2},{2,0},{4,6},{6,4},{8,10},{10,8},{12,14},{14,12},{1,3},{3,1},... | collective-permute-start | bytes 393224 | tf_op jit(solution)/shard_map/ppermute | solution.py:378
  13.8 5.3 %collective-permute-start.3 = (bf16[512,128]{1,0:T(8,128)(2,1)S(1)}, bf16[512,128]{1,0:T(8,128)(2,1)S(1)}, u32[]{:S(2)}, u32[]{:S(2)}) collective-permute-start(bf16[512,128]{1,0:T(8,128)(2,1)S(1)} %pair_sum.1.refs_0_), channel_id=1, source_target_pairs={{0,4},{2,6},{4,0},{6,2},{8,12},{10,14},{12,8},{14,10},{1,5},{3,7},... | collective-permute-start | bytes 393224 | tf_op jit(solution)/shard_map/ppermute | solution.py:383
  19.6 8.1 %collective-permute-start.4 = (bf16[512,128]{1,0:T(8,128)(2,1)S(1)}, bf16[512,128]{1,0:T(8,128)(2,1)S(1)}, u32[]{:S(2)}, u32[]{:S(2)}) collective-permute-start(bf16[512,128]{1,0:T(8,128)(2,1)S(1)} %stride_sum.1), channel_id=1, source_target_pairs={{0,8},{2,10},{4,12},{6,14},{8,0},{10,2},{12,4},{14,6},{1,9},{3,11}... | collective-permute-start | bytes 393224 | tf_op jit(solution)/shard_map/ppermute | solution.py:383
  28.4 5.0 %collective-permute-start.5 = (bf16[512,128]{1,0:T(8,128)(2,1)S(1)}, bf16[512,128]{1,0:T(8,128)(2,1)S(1)}, u32[]{:S(2)}, u32[]{:S(2)}) collective-permute-start(bf16[512,128]{1,0:T(8,128)(2,1)S(1)} %get-tuple-element.22), channel_id=1, source_target_pairs={{0,2},{2,0},{4,6},{6,4},{8,10},{10,8},{12,14},{14,12},{1,3},{3,1},... | collective-permute-start | bytes 393224 | tf_op jit(solution)/shard_map/ppermute | solution.py:391
  29.5 4.1 %collective-permute-start.6 = (bf16[512,128]{1,0:T(8,128)(2,1)S(1)}, bf16[512,128]{1,0:T(8,128)(2,1)S(1)}, u32[]{:S(2)}, u32[]{:S(2)}) collective-permute-start(bf16[512,128]{1,0:T(8,128)(2,1)S(1)} %get-tuple-element.21.refs_0_), channel_id=1, source_target_pairs={{0,1},{1,0},{2,3},{3,2},{4,5},{5,4},{6,7},{7,6},{8,9},{9,8},{10,11... | collective-permute-start | bytes 393224 | tf_op jit(solution)/shard_map/ppermute | solution.py:392
  33.4 1.3 %collective-permute-start.7 = (bf16[512,128]{1,0:T(8,128)(2,1)S(1)}, bf16[512,128]{1,0:T(8,128)(2,1)S(1)}, u32[]{:S(2)}, u32[]{:S(2)}) collective-permute-start(bf16[512,128]{1,0:T(8,128)(2,1)S(1)} %collective-permute-done.5.refs_1_), channel_id=1, source_target_pairs={{0,1},{1,0},{2,3},{3,2},{4,5},{5,4},{6,7},{7,6},{8,9},{9,8},{10,11... | collective-permute-start | bytes 393224 | tf_op jit(solution)/shard_map/ppermute | solution.py:392

commit v6 on v5

--- a/solution.py
+++ b/solution.py
@@ -10,7 +10,6 @@
 
 HEAD_DIM = 112
 LANES = 128
-PACK = 16
 GROUP = math.lcm(HEAD_DIM, LANES)
 TILES = GROUP // LANES
 
@@ -140,7 +139,7 @@
     dim, rows, width, edges,
     place_ref, spots_ref, queries_ref, residual_ref, edge_ref, gain_ref, vtaps_ref, gtaps_ref, *refs,
 ):
-    *pieces, out_ref, states, features, weights, same, numer, squares, shifted, taps = refs
+    *pieces, out_ref, states, features, weights, same, numer, squares, windows, diagonals = refs
     step = pl.program_id(0)
     tokens = rows * width
     total = tokens + edges * width
@@ -158,8 +157,7 @@
                     same[
                         number, start : start + HEAD_DIM, side * LANES : (side + 1) * LANES
                     ] = block.astype(jnp.bfloat16)
-        for row in (0, rows + 1):
-            shifted[:, row] = jnp.zeros(shifted.shape[:1] + shifted.shape[2:], jnp.bfloat16)
+        diagonals[...] = jnp.zeros_like(diagonals)
         for k, piece in enumerate(pieces):
             size = piece.shape[0]
             states[pl.ds(pl.multiple_of(spots_ref[k] * size, 16), size), :] = piece[...]
@@ -168,13 +166,14 @@
     column = lax.broadcasted_iota(jnp.int32, (width, LANES), 0)
     lane = lane_iota((HEAD_DIM, LANES))
 
-    def store_shifted(mixed, row):
-        packed = lambda a: a.astype(jnp.bfloat16).reshape(width // PACK, PACK, LANES)
-        shifted[1, row] = packed(mixed)
-        shifted[0, row] = packed(jnp.where(column == 0, 0.0, pltpu.roll(mixed, 1, 0)))
-        shifted[2, row] = packed(
-            jnp.where(column == width - 1, 0.0, pltpu.roll(mixed, width - 1, 0))
-        )
+    diagonal = lax.broadcasted_iota(jnp.int32, (LANES, LANES), 0) == lane_iota((LANES, LANES))
+
+    def store_windows(mixed, row, slot):
+        here = slice(row * width, (row + 1) * width)
+        before = jnp.where(column == 0, 0.0, pltpu.roll(mixed, 1, 0))
+        after = jnp.where(column == width - 1, 0.0, pltpu.roll(mixed, width - 1, 0))
+        for i, window in enumerate((before, mixed, after)):
+            windows[slot, here, i * LANES : (i + 1) * LANES] = window.astype(jnp.bfloat16)
 
     def body(lanes):
         count = cdiv(lanes, LANES)
@@ -224,36 +223,41 @@
 
                 def mixed(source, residual, side=side, here=here, gain=gain):
                     normed = numer[source, here] * scale[source, side * LANES : (side + 1) * LANES]
-                    return residual.astype(jnp.float32) + normed * gain
-
+                    value = residual.astype(jnp.float32) + normed * gain
+                    if lanes < here.stop:
+                        value = jnp.where(lane_iota(value.shape) < lanes - here.start, value, 0.0)
+                    return value
+
+                slot = j % 2
                 for row in range(rows):
                     source = slice(row * width, (row + 1) * width)
-                    store_shifted(mixed(source, residual_ref[source, here]), row + 1)
+                    store_windows(mixed(source, residual_ref[source, here]), row + 1, slot)
+                outside = [None, None]
                 for e in range(edges):
                     source = slice(tokens + e * width, tokens + (e + 1) * width)
-                    store_shifted(mixed(source, edge_ref[1, e, :, here]), place_ref[e])
+                    value = mixed(source, edge_ref[1, e, :, here])
+                    for k, row in enumerate((0, rows + 1)):
+                        part = jnp.where(place_ref[e] == row, value, 0.0)
+                        outside[k] = part if outside[k] is None else outside[k] + part
+                for k, row in enumerate((0, rows + 1)):
+                    store_windows(outside[k], row, slot)
                 for tap in range(9):
                     for k, (ref, factor) in enumerate(((vtaps_ref, 1.0), (gtaps_ref, 0.5))):
-                        row = ref[tap : tap + 1, here] * factor
-                        taps[k, tap] = jnp.broadcast_to(row, (PACK, LANES)).astype(jnp.bfloat16)
-
-                def convolve(row, carry, here=here):
-                    sums = []
-                    for tap_row in range(3):
-                        windows = [shifted[i, row + tap_row] for i in range(3)]
-                        for k in range(2):
-                            terms = [taps[k, 3 * tap_row + i] * windows[i] for i in range(3)]
-                            sums.append(terms[0] + terms[1] + terms[2])
-                    conv_v = (sums[0] + sums[2] + sums[4]).astype(jnp.float32)
-                    half_g = (sums[1] + sums[3] + sums[5]).astype(jnp.float32)
-                    gate = half_g + half_g * jnp.tanh(half_g)
-                    result = shifted[1, row + 1].astype(jnp.float32) + conv_v * gate
-                    out_ref[pl.ds(pl.multiple_of(row * width, width), width), here] = (
-                        result.astype(jnp.bfloat16).reshape(width, LANES)
+                        block = jnp.where(diagonal, ref[tap : tap + 1, here] * factor, 0.0)
+                        diagonals[
+                            slot, tap * LANES : (tap + 1) * LANES, k * LANES : (k + 1) * LANES
+                        ] = block.astype(jnp.bfloat16)
+                conv = jnp.zeros((tokens, 2 * LANES), jnp.float32)
+                for i in range(3):
+                    conv = conv + jnp.dot(
+                        windows[slot, i * width : i * width + tokens, :],
+                        diagonals[slot, 3 * i * LANES : 3 * (i + 1) * LANES, :],
+                        preferred_element_type=jnp.float32,
                     )
-                    return carry
-
-                lax.fori_loop(0, rows, convolve, 0)
+                conv_v, half_g = conv[:, :LANES], conv[:, LANES:]
+                gate = half_g + half_g * jnp.tanh(half_g)
+                center = windows[slot, width : width + tokens, LANES : 2 * LANES]
+                out_ref[:, here] = (center.astype(jnp.float32) + conv_v * gate).astype(jnp.bfloat16)
 
     by_group(dim, body)
 
@@ -289,8 +293,8 @@
             pltpu.VMEM((len(pairs), depth, 2 * LANES), jnp.bfloat16),
             pltpu.VMEM((total, GROUP), jnp.float32),
             pltpu.VMEM((total, GROUP), jnp.bfloat16),
-            pltpu.VMEM((3, rows + 2, width // PACK, PACK, LANES), jnp.bfloat16),
-            pltpu.VMEM((2, 9, PACK, LANES), jnp.bfloat16),
+            pltpu.VMEM((2, (rows + 2) * width, 3 * LANES), jnp.bfloat16),
+            pltpu.VMEM((2, 9 * LANES, 2 * LANES), jnp.bfloat16),
         ],
         compiler_params=pltpu.CompilerParams(vmem_limit_bytes=36 * 2**20),
         cost_estimate=pl.CostEstimate(

time: 52.3 us -> 53.3 us (1.019)
  Pallas kernels: 23.6 us -> 24.6 us
    pallas_call x1, Pallas kernels: 17.4 us -> 18.4 us  [mix(): pl.pallas_call(functools.partial(mix_kernel, dim, rows, width, edges), ou...]
where the time goes in v6:
time: 53.3 us; the launch traced here: 53.2 us
  Pallas kernels  24.6 us (46%)
  waiting for transfers between devices  19.2 us (36%)
  starting transfers between devices  9.22 us (17%)
    pallas_call x1, Pallas kernels, mix(): pl.pallas_call(functools.partial(mix_kernel, dim, rows, width, edges), ou...  18.4 us
    ppermute x2, waiting for transfers between devices, running_states(): got = lax.ppermute(total, 'frame', [(f, f ^ stride) for f in range(frames)])  8.85 us
    ppermute x2, starting transfers between devices, running_states(): got = lax.ppermute(total, 'frame', [(f, f ^ stride) for f in range(frames)])  4.51 us
    ppermute x1, waiting for transfers between devices, running_states(): partner = lax.ppermute(sent, 'frame', [(f, f ^ 1) for f in range(frames)])  4.02 us
    ppermute x1, waiting for transfers between devices, running_states(): other = lax.ppermute(theirs, 'frame', [(f, f ^ 1) for f in range(frames)])  3.97 us
    pallas_call x1, Pallas kernels, frame_states(): pl.pallas_call(functools.partial(state_kernel, dim, bool(edged)), out_sha...  3.75 us
    ppermute x1, starting transfers between devices, running_states(): partner = lax.ppermute(sent, 'frame', [(f, f ^ 1) for f in range(frames)])  2.67 us
    pallas_call x4, Pallas kernels, small_kernel(): pl.pallas_call(body, out_shape=[pltpu.VMEM(shape, jnp.bfloat16) for shape...  2.43 us
  transfers between devices with their start and end apart: 8, of which 6 were waited for; matrix products, arithmetic and copies ran while one was open for 0% of the time, Pallas kernels for 3%

profile of v6, /device:TPU:0, one launch (start us, length us, event | category | flops | bytes accessed | tf_op | source)
XLA Modules:
  0.0 53.2 jit_solution(2491867072209413467)
XLA Ops:
  0.0 3.8 %frame_states.1 = (bf16[1024,128]{1,0:T(8,128)(2,1)S(1)}, bf16[1024,128]{1,0:T(8,128)(2,1)S(1)}, bf16[2,1,80,2240]{3,2,1,0:T(8,128)(2,1)S(1)}) custom-call(s32[1]{0:T(128)} %bitcast.7.spot_ref, bf16[480,2240]{1,0:T(8,128)(2,1)} %bitcast.19, bf16[480,2240]{1,0:T(8,128)(2,1)} %bitcast.20, bf16[6,80,2240]{2,1,0:T(8,128)(2,1)} %bitcast.15, ...), custom_call_target="tpu_custom_call" | custom-call | flops 240844800 | bytes 4300800 | tf_op jit(solution)/shard_map/frame_states/pallas_call | solution.py:116
  3.8 0.5 %collective-permute-start = (bf16[1024,128]{1,0:T(8,128)(2,1)S(1)}, bf16[1024,128]{1,0:T(8,128)(2,1)S(1)}, u32[]{:S(2)}, u32[]{:S(2)}) collective-permute-start(bf16[1024,128]{1,0:T(8,128)(2,1)S(1)} %get-tuple-element.16), channel_id=1, source_target_pairs={{0,1},{1,0},{2,3},{3,2},{4,5},{5,4},{6,7},{7,6},{8,9},{9,8},{10,11... | collective-permute-start | bytes 786440 | tf_op jit(solution)/shard_map/ppermute | solution.py:376
  4.3 0.1 pad_add_fusion.1.spot_ref._
  4.4 1.1 %collective-permute-done.got_ref = bf16[1024,128]{1,0:T(8,128)(2,1)S(1)} collective-permute-done((bf16[1024,128]{1,0:T(8,128)(2,1)S(1)}, bf16[1024,128]{1,0:T(8,128)(2,1)S(1)}, u32[]{:S(2)}, u32[]{:S(2)}) %collective-permute-start) | collective-permute-done | bytes 262176 | tf_op jit(solution)/shard_map/ppermute | solution.py:376
  5.5 0.6 %split_sum.1 = (bf16[512,128]{1,0:T(8,128)(2,1)S(1)}, bf16[512,128]{1,0:T(8,128)(2,1)S(1)}) custom-call(s32[2]{0:T(128)S(1)} %pad_add_fusion.1.spot_ref._, bf16[1024,128]{1,0:T(8,128)(2,1)S(1)} %get-tuple-element.15.kept_ref, bf16[1024,128]{1,0:T(8,128)(2,1)S(1)} %collective-permute-done.got_ref), custom_call_target="tpu_custom_call" | custom-call | tf_op jit(solution)/shard_map/split_sum/pallas_call | solution.py:318
  6.1 0.4 collective-permute-start.1
  6.5 2.7 %collective-permute-start.2 = (bf16[512,128]{1,0:T(8,128)(2,1)S(1)}, bf16[512,128]{1,0:T(8,128)(2,1)S(1)}, u32[]{:S(2)}, u32[]{:S(2)}) collective-permute-start(bf16[512,128]{1,0:T(8,128)(2,1)S(1)} %get-tuple-element.20), channel_id=1, source_target_pairs={{0,2},{2,0},{4,6},{6,4},{8,10},{10,8},{12,14},{14,12},{1,3},{3,1},... | collective-permute-start | bytes 393224 | tf_op jit(solution)/shard_map/ppermute | solution.py:382
  9.2 4.0 %collective-permute-done.2.refs_1_.partner_ref = bf16[512,128]{1,0:T(8,128)(2,1)S(1)} collective-permute-done((bf16[512,128]{1,0:T(8,128)(2,1)S(1)}, bf16[512,128]{1,0:T(8,128)(2,1)S(1)}, u32[]{:S(2)}, u32[]{:S(2)}) %collective-permute-start.2) | collective-permute-done | bytes 131104 | tf_op jit(solution)/shard_map/ppermute | solution.py:382
  13.2 0.6 %pair_sum.1.refs_0_ = bf16[512,128]{1,0:T(8,128)(2,1)S(1)} custom-call(s32[2]{0:T(128)S(1)} %pad_add_fusion.1.spot_ref._, bf16[512,128]{1,0:T(8,128)(2,1)S(1)} %get-tuple-element.19.refs_0_.own_ref, bf16[512,128]{1,0:T(8,128)(2,1)S(1)} %collective-permute-done.2.refs_1_.partner_ref), custom_call_target="tpu_custom_call" | custom-call | tf_op jit(solution)/shard_map/pair_sum/pallas_call | solution.py:318
  13.8 1.9 %collective-permute-start.3 = (bf16[512,128]{1,0:T(8,128)(2,1)S(1)}, bf16[512,128]{1,0:T(8,128)(2,1)S(1)}, u32[]{:S(2)}, u32[]{:S(2)}) collective-permute-start(bf16[512,128]{1,0:T(8,128)(2,1)S(1)} %pair_sum.1.refs_0_), channel_id=1, source_target_pairs={{0,4},{2,6},{4,0},{6,2},{8,12},{10,14},{12,8},{14,10},{1,5},{3,7},... | collective-permute-start | bytes 393224 | tf_op jit(solution)/shard_map/ppermute | solution.py:387
  15.6 3.4 %collective-permute-done.3.refs_1_.refs_0_ = bf16[512,128]{1,0:T(8,128)(2,1)S(1)} collective-permute-done((bf16[512,128]{1,0:T(8,128)(2,1)S(1)}, bf16[512,128]{1,0:T(8,128)(2,1)S(1)}, u32[]{:S(2)}, u32[]{:S(2)}) %collective-permute-start.3) | collective-permute-done | bytes 131104 | tf_op jit(solution)/shard_map/ppermute | solution.py:387
  19.0 0.6 %stride_sum.1 = bf16[512,128]{1,0:T(8,128)(2,1)S(1)} custom-call(s32[2]{0:T(128)S(1)} %pad_add_fusion.1.spot_ref._, bf16[512,128]{1,0:T(8,128)(2,1)S(1)} %pair_sum.1.refs_0_, bf16[512,128]{1,0:T(8,128)(2,1)S(1)} %collective-permute-done.3.refs_1_.refs_0_), custom_call_target="tpu_custom_call" | custom-call | tf_op jit(solution)/shard_map/stride_sum/pallas_call | solution.py:318
  19.6 2.6 %collective-permute-start.4 = (bf16[512,128]{1,0:T(8,128)(2,1)S(1)}, bf16[512,128]{1,0:T(8,128)(2,1)S(1)}, u32[]{:S(2)}, u32[]{:S(2)}) collective-permute-start(bf16[512,128]{1,0:T(8,128)(2,1)S(1)} %stride_sum.1), channel_id=1, source_target_pairs={{0,8},{2,10},{4,12},{6,14},{8,0},{10,2},{12,4},{14,6},{1,9},{3,11}... | collective-permute-start | bytes 393224 | tf_op jit(solution)/shard_map/ppermute | solution.py:387
  22.3 5.4 %collective-permute-done.4.refs_1_ = bf16[512,128]{1,0:T(8,128)(2,1)S(1)} collective-permute-done((bf16[512,128]{1,0:T(8,128)(2,1)S(1)}, bf16[512,128]{1,0:T(8,128)(2,1)S(1)}, u32[]{:S(2)}, u32[]{:S(2)}) %collective-permute-start.4) | collective-permute-done | bytes 131104 | tf_op jit(solution)/shard_map/ppermute | solution.py:387
  27.7 0.7 %pair_sums.1 = (bf16[512,128]{1,0:T(8,128)(2,1)S(1)}, bf16[512,128]{1,0:T(8,128)(2,1)S(1)}) custom-call(s32[2]{0:T(128)S(1)} %pad_add_fusion.1.spot_ref._, bf16[512,128]{1,0:T(8,128)(2,1)S(1)} %get-tuple-element.19.refs_0_.own_ref, bf16[512,128]{1,0:T(8,128)(2,1)S(1)} %collective-permute-done.2.refs_1_.partner_ref, ...), custom_call_target="tpu_custom_call" | custom-call | tf_op jit(solution)/shard_map/pair_sums/pallas_call | solution.py:318
  28.4 1.1 %collective-permute-start.5 = (bf16[512,128]{1,0:T(8,128)(2,1)S(1)}, bf16[512,128]{1,0:T(8,128)(2,1)S(1)}, u32[]{:S(2)}, u32[]{:S(2)}) collective-permute-start(bf16[512,128]{1,0:T(8,128)(2,1)S(1)} %get-tuple-element.22), channel_id=1, source_target_pairs={{0,2},{2,0},{4,6},{6,4},{8,10},{10,8},{12,14},{14,12},{1,3},{3,1},... | collective-permute-start | bytes 393224 | tf_op jit(solution)/shard_map/ppermute | solution.py:395
  29.5 0.0 collective-permute-start.6
  29.5 4.0 %collective-permute-done.5.refs_1_ = bf16[512,128]{1,0:T(8,128)(2,1)S(1)} collective-permute-done((bf16[512,128]{1,0:T(8,128)(2,1)S(1)}, bf16[512,128]{1,0:T(8,128)(2,1)S(1)}, u32[]{:S(2)}, u32[]{:S(2)}) %collective-permute-start.5) | collective-permute-done | bytes 131104 | tf_op jit(solution)/shard_map/ppermute | solution.py:395
  33.4 0.0 collective-permute-start.7
  33.5 0.1 pad_add_fusion.spots_ref
  33.5 0.0 collective-permute-done.6.refs_2_
  33.5 1.2 %collective-permute-done.7.refs_3_ = bf16[512,128]{1,0:T(8,128)(2,1)S(1)} collective-permute-done((bf16[512,128]{1,0:T(8,128)(2,1)S(1)}, bf16[512,128]{1,0:T(8,128)(2,1)S(1)}, u32[]{:S(2)}, u32[]{:S(2)}) %collective-permute-start.7) | collective-permute-done | bytes 131104 | tf_op jit(solution)/shard_map/ppermute | solution.py:396
  34.8 0.0 collective-permute-done.1.edge_ref
  34.8 18.4 %mix.1 = bf16[480,2240]{1,0:T(8,128)(2,1)} custom-call(s32[1]{0:T(128)} %bitcast.place_ref, s32[4]{0:T(128)S(1)} %pad_add_fusion.spots_ref, bf16[480,2240]{1,0:T(8,128)(2,1)} %bitcast.16, bf16[480,2240]{1,0:T(8,128)(2,1)} %bitcast.18, bf16[2,1,80,2240]{3,2,1,0:T(8,128)(2,1)S(1)} %collective-permute-done.1.edge_ref, f32[1,2240]{1,0:T(1,128)S(1)} %broadcast_in_dim.11.gain_ref, ...), custom_call_target="tpu_custom_call" | custom-call | flops 64512000 | bytes 6451200 | tf_op jit(solution)/shard_map/mix/pallas_call | solution.py:273
  (7 shorter events, 0.0 us)
Async XLA Ops:
  0.0 33.4 %copy-start.2 = (f32[2240]{0:T(1024)S(1)}, f32[2240]{0:T(1024)}, u32[]{:S(2)}) copy-start(f32[2240]{0:T(1024)} %param.11) | copy-start | bytes 26884
  0.0 34.8 %copy-start = (f32[9,2240]{1,0:T(8,128)S(1)}, f32[9,2240]{1,0:T(8,128)}, u32[]{:S(2)}) copy-start(f32[9,2240]{1,0:T(8,128)} %vtaps_ref.1) | copy-start | bytes 241924
  0.0 34.8 %copy-start.1 = (f32[9,2240]{1,0:T(8,128)S(1)}, f32[9,2240]{1,0:T(8,128)}, u32[]{:S(2)}) copy-start(f32[9,2240]{1,0:T(8,128)} %gtaps_ref.1) | copy-start | bytes 241924
  3.8 1.7 %collective-permute-start = (bf16[1024,128]{1,0:T(8,128)(2,1)S(1)}, bf16[1024,128]{1,0:T(8,128)(2,1)S(1)}, u32[]{:S(2)}, u32[]{:S(2)}) collective-permute-start(bf16[1024,128]{1,0:T(8,128)(2,1)S(1)} %get-tuple-element.16), channel_id=1, source_target_pairs={{0,1},{1,0},{2,3},{3,2},{4,5},{5,4},{6,7},{7,6},{8,9},{9,8},{10,11... | collective-permute-start | bytes 786440 | tf_op jit(solution)/shard_map/ppermute | solution.py:376
  6.1 28.7 %collective-permute-start.1 = (bf16[2,1,80,2240]{3,2,1,0:T(8,128)(2,1)S(1)}, bf16[2,1,80,2240]{3,2,1,0:T(8,128)(2,1)S(1)}, u32[]{:S(2)}, u32[]{:S(2)}) collective-permute-start(bf16[2,1,80,2240]{3,2,1,0:T(8,128)(2,1)S(1)} %get-tuple-element.18), channel_id=1, source_target_pairs={{0,1},{1,0},{2,3},{3,2},{4,5},{5,4},{6,7},{7,6},{8,9},{9,8},{10,11... | collective-permute-start | bytes 2150408 | tf_op jit(solution)/shard_map/ppermute | solution.py:380
  6.5 6.7 %collective-permute-start.2 = (bf16[512,128]{1,0:T(8,128)(2,1)S(1)}, bf16[512,128]{1,0:T(8,128)(2,1)S(1)}, u32[]{:S(2)}, u32[]{:S(2)}) collective-permute-start(bf16[512,128]{1,0:T(8,128)(2,1)S(1)} %get-tuple-element.20), channel_id=1, source_target_pairs={{0,2},{2,0},{4,6},{6,4},{8,10},{10,8},{12,14},{14,12},{1,3},{3,1},... | collective-permute-start | bytes 393224 | tf_op jit(solution)/shard_map/ppermute | solution.py:382
  13.8 5.3 %collective-permute-start.3 = (bf16[512,128]{1,0:T(8,128)(2,1)S(1)}, bf16[512,128]{1,0:T(8,128)(2,1)S(1)}, u32[]{:S(2)}, u32[]{:S(2)}) collective-permute-start(bf16[512,128]{1,0:T(8,128)(2,1)S(1)} %pair_sum.1.refs_0_), channel_id=1, source_target_pairs={{0,4},{2,6},{4,0},{6,2},{8,12},{10,14},{12,8},{14,10},{1,5},{3,7},... | collective-permute-start | bytes 393224 | tf_op jit(solution)/shard_map/ppermute | solution.py:387
  19.6 8.1 %collective-permute-start.4 = (bf16[512,128]{1,0:T(8,128)(2,1)S(1)}, bf16[512,128]{1,0:T(8,128)(2,1)S(1)}, u32[]{:S(2)}, u32[]{:S(2)}) collective-permute-start(bf16[512,128]{1,0:T(8,128)(2,1)S(1)} %stride_sum.1), channel_id=1, source_target_pairs={{0,8},{2,10},{4,12},{6,14},{8,0},{10,2},{12,4},{14,6},{1,9},{3,11}... | collective-permute-start | bytes 393224 | tf_op jit(solution)/shard_map/ppermute | solution.py:387
  28.4 5.0 %collective-permute-start.5 = (bf16[512,128]{1,0:T(8,128)(2,1)S(1)}, bf16[512,128]{1,0:T(8,128)(2,1)S(1)}, u32[]{:S(2)}, u32[]{:S(2)}) collective-permute-start(bf16[512,128]{1,0:T(8,128)(2,1)S(1)} %get-tuple-element.22), channel_id=1, source_target_pairs={{0,2},{2,0},{4,6},{6,4},{8,10},{10,8},{12,14},{14,12},{1,3},{3,1},... | collective-permute-start | bytes 393224 | tf_op jit(solution)/shard_map/ppermute | solution.py:395
  29.5 4.1 %collective-permute-start.6 = (bf16[512,128]{1,0:T(8,128)(2,1)S(1)}, bf16[512,128]{1,0:T(8,128)(2,1)S(1)}, u32[]{:S(2)}, u32[]{:S(2)}) collective-permute-start(bf16[512,128]{1,0:T(8,128)(2,1)S(1)} %get-tuple-element.21.refs_0_), channel_id=1, source_target_pairs={{0,1},{1,0},{2,3},{3,2},{4,5},{5,4},{6,7},{7,6},{8,9},{9,8},{10,11... | collective-permute-start | bytes 393224 | tf_op jit(solution)/shard_map/ppermute | solution.py:396
  33.4 1.3 %collective-permute-start.7 = (bf16[512,128]{1,0:T(8,128)(2,1)S(1)}, bf16[512,128]{1,0:T(8,128)(2,1)S(1)}, u32[]{:S(2)}, u32[]{:S(2)}) collective-permute-start(bf16[512,128]{1,0:T(8,128)(2,1)S(1)} %collective-permute-done.5.refs_1_), channel_id=1, source_target_pairs={{0,1},{1,0},{2,3},{3,2},{4,5},{5,4},{6,7},{7,6},{8,9},{9,8},{10,11... | collective-permute-start | bytes 393224 | tf_op jit(solution)/shard_map/ppermute | solution.py:396

commit v7 on v4

--- a/solution.py
+++ b/solution.py
@@ -43,15 +43,26 @@
     return result
 
 
-def by_group(dim, body):
+def by_group(dim, groups, body):
     full, rest = divmod(dim, GROUP)
-    if full:
-        pl.when(pl.program_id(0) < full)(lambda: body(GROUP))
-    if rest:
-        pl.when(pl.program_id(0) >= full)(lambda: body(rest))
-
-
-def state_kernel(dim, with_edge, spot_ref, keys_ref, values_ref, *refs):
+    group = pl.program_id(0) + groups[0]
+    if groups[0] < full:
+        pl.when(group < full)(lambda: body(GROUP))
+    if rest and groups[-1] == full:
+        pl.when(group == full)(lambda: body(rest))
+
+
+def chunks(dim):
+    count = cdiv(dim, GROUP)
+    return [range(0, 1), range(1, count)] if count > 1 else [range(0, 1)]
+
+
+def state_rows(dim, groups):
+    lanes = min(dim, (groups[-1] + 1) * GROUP) - groups[0] * GROUP
+    return cdiv(lanes, LANES) * HEAD_DIM
+
+
+def state_kernel(dim, groups, with_edge, spot_ref, keys_ref, values_ref, *refs):
     step = pl.program_id(0)
     *refs, turned, whole, semaphores = refs
     if with_edge:
@@ -93,11 +104,11 @@
                 row = pl.multiple_of((step * TILES + j) * HEAD_DIM, 16)
                 whole[pl.ds(row, HEAD_DIM), :] = total.astype(jnp.bfloat16)
 
-    by_group(dim, body)
+    by_group(dim, groups, body)
 
     @pl.when(step == pl.num_programs(0) - 1)
     def _():
-        used = cdiv(dim, LANES) * HEAD_DIM
+        used = state_rows(dim, groups)
         if used < whole.shape[0]:
             whole[used:, :] = jnp.zeros((whole.shape[0] - used, LANES), jnp.bfloat16)
         for k, part in enumerate(parts):
@@ -109,15 +120,16 @@
                 copy.wait()
 
 
-def frame_states(spot, keys, values, rows, parts, edged=()):
+def frame_states(groups, spot, keys, values, parts, edged=()):
     tokens, dim = keys.shape
+    rows = cdiv(state_rows(dim, groups), 64) * 64
     part = (rows // parts, LANES)
-    block = pl.BlockSpec((tokens, GROUP), lambda g: (0, g))
+    block = pl.BlockSpec((tokens, GROUP), lambda g: (0, g + groups[0]))
     return pl.pallas_call(
-        functools.partial(state_kernel, dim, bool(edged)),
+        functools.partial(state_kernel, dim, groups, bool(edged)),
         out_shape=[pltpu.VMEM(part, jnp.bfloat16)] * parts
         + [pltpu.VMEM((len(edged), 1, *edged[0].shape[1:]), jnp.bfloat16) for _ in edged[:1]],
-        grid=(cdiv(dim, GROUP),),
+        grid=(len(groups),),
         in_specs=[pl.BlockSpec(memory_space=pltpu.SMEM), block, block]
         + [pl.BlockSpec(memory_space=pl.ANY)] * len(edged),
         out_specs=[pl.BlockSpec(part, lambda g: (0, 0))] * parts
@@ -129,17 +141,20 @@
         ],
         compiler_params=pltpu.CompilerParams(vmem_limit_bytes=60 * 2**20),
         cost_estimate=pl.CostEstimate(
-            flops=2 * tokens * dim * HEAD_DIM, bytes_accessed=4 * tokens * dim, transcendentals=0
+            flops=2 * tokens * len(groups) * GROUP * HEAD_DIM,
+            bytes_accessed=4 * tokens * len(groups) * GROUP,
+            transcendentals=0,
         ),
         name="frame_states",
     )(spot, in_hbm(keys), in_hbm(values), *[in_hbm(array) for array in edged])
 
 
 def mix_kernel(
-    dim, rows, width, edges,
+    dim, groups, rows, width, edges, earlier,
     place_ref, spots_ref, queries_ref, residual_ref, edge_ref, gain_ref, vtaps_ref, gtaps_ref, *refs,
 ):
     *pieces, out_ref, states, features, weights, same, numer, squares, shifted = refs
+    pieces = pieces[: len(pieces) - earlier]
     step = pl.program_id(0)
     tokens = rows * width
     total = tokens + edges * width
@@ -249,32 +264,36 @@
 
             lax.fori_loop(0, rows, convolve, 0)
 
-    by_group(dim, body)
-
-
-def mix(place, spots, queries, residual, edge, gain, value_taps, gate_taps, pieces, rows, width):
+    by_group(dim, groups, body)
+
+
+def mix(groups, out, place, spots, queries, residual, edge, gain, value_taps, gate_taps, pieces, rows, width):
     tokens, dim = queries.shape
     edges = edge.shape[1]
     total = tokens + edges * width
     pairs = spans(min(GROUP, dim))
     depth = max(last - first for _, first, last in pairs) * LANES
-    block = pl.BlockSpec((tokens, GROUP), lambda g: (0, g))
-    taps = pl.BlockSpec((value_taps.shape[0], GROUP), lambda g: (0, g))
+    block = pl.BlockSpec((tokens, GROUP), lambda g: (0, g + groups[0]))
+    taps = pl.BlockSpec((value_taps.shape[0], GROUP), lambda g: (0, g + groups[0]))
+    here = tokens * len(groups) * GROUP
+    first = [] if out is None else [out]
     return pl.pallas_call(
-        functools.partial(mix_kernel, dim, rows, width, edges),
+        functools.partial(mix_kernel, dim, groups, rows, width, edges, len(first)),
         out_shape=jax.ShapeDtypeStruct((tokens, dim), jnp.bfloat16),
-        grid=(cdiv(dim, GROUP),),
+        grid=(len(groups),),
         in_specs=[
             pl.BlockSpec(memory_space=pltpu.SMEM),
             pl.BlockSpec(memory_space=pltpu.SMEM),
             block,
             block,
-            pl.BlockSpec((2, edges, width, GROUP), lambda g: (0, 0, 0, g)),
-            pl.BlockSpec((1, GROUP), lambda g: (0, g)),
+            pl.BlockSpec((2, edges, width, GROUP), lambda g: (0, 0, 0, g + groups[0])),
+            pl.BlockSpec((1, GROUP), lambda g: (0, g + groups[0])),
             taps,
             taps,
         ]
-        + [pl.BlockSpec(piece.shape, lambda g: (0, 0)) for piece in pieces],
+        + [pl.BlockSpec(piece.shape, lambda g: (0, 0)) for piece in pieces]
+        + [pl.BlockSpec(memory_space=pl.ANY)] * len(first),
+        input_output_aliases={8 + len(pieces): 0} if first else {},
         out_specs=block,
         scratch_shapes=[
             pltpu.VMEM((sum(piece.shape[0] for piece in pieces), LANES), jnp.bfloat16),
@@ -287,10 +306,10 @@
         ],
         compiler_params=pltpu.CompilerParams(vmem_limit_bytes=36 * 2**20),
         cost_estimate=pl.CostEstimate(
-            flops=60 * tokens * dim, bytes_accessed=6 * tokens * dim, transcendentals=2 * tokens * dim
+            flops=1000 * here, bytes_accessed=6 * here, transcendentals=2 * here
         ),
         name="mix",
-    )(place, spots, in_hbm(queries), in_hbm(residual), edge, gain, value_taps, gate_taps, *pieces)
+    )(place, spots, in_hbm(queries), in_hbm(residual), edge, gain, value_taps, gate_taps, *pieces, *first)
 
 
 def edge_rows(queries, residual):
@@ -347,62 +366,88 @@
     theirs_ref[...] = jnp.where(first, both, before + partner).astype(jnp.bfloat16)
 
 
-def running_states(keys, values, queries, residual, rows):
+def running_states(keys, values, queries, residual):
     devices, frames = lax.axis_size("space"), lax.axis_size("frame")
     core, frame = lax.axis_index("space"), lax.axis_index("frame")
+    ranges = chunks(keys.shape[-1])
     if devices != 2 or frames < 2 or frames & (frames - 1):
-        (state,) = frame_states(jnp.zeros((1,), jnp.int32), keys, values, rows, 1)
-        state = lax.psum(state.astype(jnp.float32), "space").astype(jnp.bfloat16)
-        every = lax.all_gather(state, "frame").astype(jnp.float32)
         reached = (jnp.arange(frames) <= frame)[:, None, None]
-        total = jnp.sum(jnp.where(reached, every, 0.0), axis=0).astype(jnp.bfloat16)
-        return [total], jnp.zeros((1,), jnp.int32), edge_rows(queries, residual)
+        results = []
+        for groups in ranges:
+            (state,) = frame_states(groups, jnp.zeros((1,), jnp.int32), keys, values, 1)
+            state = lax.psum(state.astype(jnp.float32), "space").astype(jnp.bfloat16)
+            every = lax.all_gather(state, "frame").astype(jnp.float32)
+            total = jnp.sum(jnp.where(reached, every, 0.0), axis=0).astype(jnp.bfloat16)
+            results.append([total])
+        return results, jnp.zeros((1,), jnp.int32), edge_rows(queries, residual)
     swap = [(0, 1), (1, 0)]
+    exchange = lambda array, stride: lax.ppermute(
+        array, "frame", [(f, f ^ stride) for f in range(frames)]
+    )
     spot = jnp.stack([lax.rem(frame, 2), frame]).astype(jnp.int32)
-    kept, sent, edge = frame_states(
-        core.astype(jnp.int32)[None], keys, values, rows, 2, (queries, residual)
-    )
-    got = lax.ppermute(sent, "space", swap)
-    quarter = (rows // 4, LANES)
-    own, sent = small_kernel(split_sum_body, "split_sum", [quarter] * 2, spot, kept, got)
-    edge, sent = lax.optimization_barrier((edge, sent))
-    edge = lax.ppermute(edge, "space", swap)
-    place = jnp.where(core == 0, queries.shape[0] + 1, 0).astype(jnp.int32)[None]
-    partner = lax.ppermute(sent, "frame", [(f, f ^ 1) for f in range(frames)])
-    (total,) = small_kernel(sum_body, "pair_sum", [quarter], spot, own, partner)
-    earlier = []
+    kept, own, partner, total, earlier, results = {}, {}, {}, {}, {}, []
+    for c, groups in enumerate(ranges):
+        kept[c], sent, *edge = frame_states(
+            groups, core.astype(jnp.int32)[None], keys, values, 2, (queries, residual) if c == 0 else ()
+        )
+        if c == 0:
+            (edges,) = edge
+        got = lax.ppermute(sent, "space", swap)
+        quarter = (got.shape[0] // 2, LANES)
+        own[c], sent = small_kernel(
+            split_sum_body, "split_sum", [quarter] * 2, spot, kept[c], got
+        )
+        if c == 0:
+            edges, sent = lax.optimization_barrier((edges, sent))
+            edges = lax.ppermute(edges, "space", swap)
+        partner[c] = exchange(sent, 1)
+        earlier[c] = []
+    for c in own:
+        (total[c],) = small_kernel(sum_body, "pair_sum", [own[c].shape], spot, own[c], partner[c])
     stride = 2
     while stride < frames:
-        got = lax.ppermute(total, "frame", [(f, f ^ stride) for f in range(frames)])
-        earlier.append(got)
+        for c in own:
+            got = exchange(total[c], stride)
+            earlier[c].append(got)
+            if stride * 2 < frames:
+                (total[c],) = small_kernel(
+                    sum_body, "stride_sum", [got.shape], spot, total[c], got
+                )
         stride *= 2
-        if stride < frames:
-            (total,) = small_kernel(sum_body, "stride_sum", [quarter], spot, total, got)
-    mine, theirs = small_kernel(
-        pair_sums_body, "pair_sums", [quarter] * 2, spot, own, partner, *earlier
-    )
-    other = lax.ppermute(theirs, "frame", [(f, f ^ 1) for f in range(frames)])
-    pieces = [mine, other, lax.ppermute(mine, "space", swap), lax.ppermute(other, "space", swap)]
-    spots = [2 * c + p for c in (core, 1 - core) for p in (spot[0], 1 - spot[0])]
-    return pieces, jnp.stack(spots).astype(jnp.int32), (edge, place)
+    across = [
+        (2 * f + c, 2 * (f ^ 1) + (1 - c)) for f in range(frames) for c in range(2)
+    ]
+    for c in own:
+        mine, theirs = small_kernel(
+            pair_sums_body, "pair_sums", [own[c].shape] * 2, spot, own[c], partner[c], *earlier[c]
+        )
+        results.append(
+            [
+                mine,
+                lax.ppermute(mine, "space", swap),
+                exchange(theirs, 1),
+                lax.ppermute(theirs, ("frame", "space"), across),
+            ]
+        )
+    parity = spot[0]
+    spots = [2 * core + parity, 2 * (1 - core) + parity, 2 * core + 1 - parity, 3 - 2 * core - parity]
+    place = jnp.where(core == 0, queries.shape[0] + 1, 0).astype(jnp.int32)[None]
+    return results, jnp.stack(spots).astype(jnp.int32), (edges, place)
 
 
 def on_device(queries, keys, values, residual, attn_gain, value_taps, gate_taps):
     frames, rows, width, dim = queries.shape
     tokens = frames * rows * width
     flat = lambda a: a.reshape(tokens, dim)
-    state_rows = cdiv(cdiv(dim, LANES) * HEAD_DIM, 64) * 64
-    pieces, spots, (edge, place) = running_states(
-        flat(keys),
-        flat(values),
-        queries.reshape(rows, width, dim),
-        residual.reshape(rows, width, dim),
-        state_rows,
+    results, spots, (edge, place) = running_states(
+        flat(keys), flat(values), queries.reshape(rows, width, dim), residual.reshape(rows, width, dim)
     )
-    out = mix(
-        place, spots, flat(queries), flat(residual), edge, attn_gain[None], value_taps, gate_taps,
-        pieces, rows, width,
-    )
+    out = None
+    for groups, pieces in zip(chunks(dim), results):
+        out = mix(
+            groups, out, place, spots, flat(queries), flat(residual), edge, attn_gain[None],
+            value_taps, gate_taps, pieces, rows, width,
+        )
     return out.reshape(frames, rows, width, dim)
 
 

time: 49.7 us -> 54.2 us (1.091)
  Pallas kernels: 20.9 us -> 26.6 us
  waiting for transfers between devices: 19.2 us -> 13.6 us
  starting transfers between devices: 9.22 us -> 13.4 us
    ppermute x6 -> x11, waiting for transfers between devices: 18.1 us -> 11.4 us  [the longest x8 11.4 us: running_states(): lax.ppermute(array, 'frame', [(f, f ^ stride) for f in range(frames)])]
    ppermute x6 -> x11, starting transfers between devices: 8.68 us -> 12.4 us  [the longest x8 9.27 us: running_states(): lax.ppermute(array, 'frame', [(f, f ^ stride) for f in range(frames)])]
    pallas_call x2 -> x4, Pallas kernels: 18.5 us -> 22 us  [the longest x2 16.9 us: mix(): pl.pallas_call(functools.partial(mix_kernel, dim, groups, rows, width, ed...]
    pallas_call x4 -> x8, Pallas kernels: 2.43 us -> 4.63 us  [small_kernel(): pl.pallas_call(body, out_shape=[pltpu.VMEM(shape, jnp.bfloat16) for shape...]
    ppermute x1 -> x2, waiting for transfers between devices: 1.09 us -> 2.12 us  [running_states(): got = lax.ppermute(sent, 'space', swap)]
  transfers between devices with their start and end apart: 8 -> 15, of which waited for: 6 -> 6; matrix products, arithmetic and copies ran while one was open for 0% -> 0% of each run, Pallas kernels for 4% -> 25%
where the time goes in v7:
time: 54.2 us; the launch traced here: 53.9 us
  Pallas kernels  26.6 us (49%)
  waiting for transfers between devices  13.6 us (25%)
  starting transfers between devices  13.4 us (25%)
    pallas_call x2, Pallas kernels, mix(): pl.pallas_call(functools.partial(mix_kernel, dim, groups, rows, width, ed...  16.9 us
    ppermute x8, waiting for transfers between devices, running_states(): lax.ppermute(array, 'frame', [(f, f ^ stride) for f in range(frames)])  11.4 us
    ppermute x8, starting transfers between devices, running_states(): lax.ppermute(array, 'frame', [(f, f ^ stride) for f in range(frames)])  9.27 us
    pallas_call x2, Pallas kernels, frame_states(): pl.pallas_call(functools.partial(state_kernel, dim, groups, bool(edged)),...  5.06 us
    pallas_call x8, Pallas kernels, small_kernel(): pl.pallas_call(body, out_shape=[pltpu.VMEM(shape, jnp.bfloat16) for shape...  4.63 us
    ppermute x2, starting transfers between devices, running_states(): lax.ppermute(theirs, ('frame', 'space'), across)  2.72 us
    ppermute x2, waiting for transfers between devices, running_states(): got = lax.ppermute(sent, 'space', swap)  2.12 us
  transfers between devices with their start and end apart: 15, of which 6 were waited for; matrix products, arithmetic and copies ran while one was open for 0% of the time, Pallas kernels for 25%

profile of v7, /device:TPU:0, one launch (start us, length us, event | category | flops | bytes accessed | tf_op | source)
XLA Modules:
  0.0 53.9 jit_solution(4083589406686897360)
XLA Ops:
  0.0 2.6 %frame_states.2 = (bf16[416,128]{1,0:T(8,128)(2,1)S(1)}, bf16[416,128]{1,0:T(8,128)(2,1)S(1)}, bf16[2,1,80,2240]{3,2,1,0:T(8,128)(2,1)S(1)}) custom-call(s32[1]{0:T(128)} %bitcast.7.spot_ref, bf16[480,2240]{1,0:T(8,128)(2,1)} %bitcast.21, bf16[480,2240]{1,0:T(8,128)(2,1)} %bitcast.23, bf16[6,80,2240]{2,1,0:T(8,128)(2,1)} %bitcast.15, ...), custom_call_target="tpu_custom_call" | custom-call | flops 96337920 | bytes 1720320 | tf_op jit(solution)/shard_map/frame_states/pallas_call | solution.py:128
  3.2 0.9 %collective-permute-done.got_ref = bf16[416,128]{1,0:T(8,128)(2,1)S(1)} collective-permute-done((bf16[416,128]{1,0:T(8,128)(2,1)S(1)}, bf16[416,128]{1,0:T(8,128)(2,1)S(1)}, u32[]{:S(2)}, u32[]{:S(2)}) %collective-permute-start) | collective-permute-done | bytes 106528 | tf_op jit(solution)/shard_map/ppermute | solution.py:395
  4.1 0.6 %split_sum.2 = (bf16[208,128]{1,0:T(8,128)(2,1)S(1)}, bf16[208,128]{1,0:T(8,128)(2,1)S(1)}) custom-call(s32[2]{0:T(128)S(1)} %pad_add_fusion.1.spot_ref._, bf16[416,128]{1,0:T(8,128)(2,1)S(1)} %get-tuple-element.21.kept_ref, bf16[416,128]{1,0:T(8,128)(2,1)S(1)} %collective-permute-done.got_ref), custom_call_target="tpu_custom_call" | custom-call | tf_op jit(solution)/shard_map/split_sum/pallas_call | solution.py:326
  5.1 2.5 %frame_states.3 = (bf16[640,128]{1,0:T(8,128)(2,1)S(1)}, bf16[640,128]{1,0:T(8,128)(2,1)S(1)}) custom-call(s32[1]{0:T(128)} %bitcast.7.spot_ref, bf16[480,2240]{1,0:T(8,128)(2,1)} %bitcast.22, bf16[480,2240]{1,0:T(8,128)(2,1)} %bitcast.24), custom_call_target="tpu_custom_call" | custom-call | flops 192675840 | bytes 3440640 | tf_op jit(solution)/shard_map/frame_states/pallas_call | solution.py:128
  7.8 1.2 %collective-permute-done.2.got_ref = bf16[640,128]{1,0:T(8,128)(2,1)S(1)} collective-permute-done((bf16[640,128]{1,0:T(8,128)(2,1)S(1)}, bf16[640,128]{1,0:T(8,128)(2,1)S(1)}, u32[]{:S(2)}, u32[]{:S(2)}) %collective-permute-start.2) | collective-permute-done | bytes 163872 | tf_op jit(solution)/shard_map/ppermute | solution.py:395
  9.0 0.6 %split_sum.3 = (bf16[320,128]{1,0:T(8,128)(2,1)S(1)}, bf16[320,128]{1,0:T(8,128)(2,1)S(1)}) custom-call(s32[2]{0:T(128)S(1)} %pad_add_fusion.1.spot_ref._, bf16[640,128]{1,0:T(8,128)(2,1)S(1)} %get-tuple-element.25.kept_ref, bf16[640,128]{1,0:T(8,128)(2,1)S(1)} %collective-permute-done.2.got_ref), custom_call_target="tpu_custom_call" | custom-call | tf_op jit(solution)/shard_map/split_sum/pallas_call | solution.py:326
  9.6 2.7 %collective-permute-start.3 = (bf16[320,128]{1,0:T(8,128)(2,1)S(1)}, bf16[320,128]{1,0:T(8,128)(2,1)S(1)}, u32[]{:S(2)}, u32[]{:S(2)}) collective-permute-start(bf16[320,128]{1,0:T(8,128)(2,1)S(1)} %get-tuple-element.28), channel_id=1, source_target_pairs={{0,2},{2,0},{4,6},{6,4},{8,10},{10,8},{12,14},{14,12},{1,3},{3,1},... | collective-permute-start | bytes 245768 | tf_op jit(solution)/shard_map/ppermute | solution.py:384
  12.5 3.1 %collective-permute-done.3.refs_1_.partner_ref = bf16[320,128]{1,0:T(8,128)(2,1)S(1)} collective-permute-done((bf16[320,128]{1,0:T(8,128)(2,1)S(1)}, bf16[320,128]{1,0:T(8,128)(2,1)S(1)}, u32[]{:S(2)}, u32[]{:S(2)}) %collective-permute-start.3) | collective-permute-done | bytes 81952 | tf_op jit(solution)/shard_map/ppermute | solution.py:384
  15.6 0.6 %pair_sum.2.refs_0_ = bf16[320,128]{1,0:T(8,128)(2,1)S(1)} custom-call(s32[2]{0:T(128)S(1)} %pad_add_fusion.1.spot_ref._, bf16[320,128]{1,0:T(8,128)(2,1)S(1)} %get-tuple-element.27.refs_0_.own_ref, bf16[320,128]{1,0:T(8,128)(2,1)S(1)} %collective-permute-done.3.refs_1_.partner_ref), custom_call_target="tpu_custom_call" | custom-call | tf_op jit(solution)/shard_map/pair_sum/pallas_call | solution.py:326
  16.2 2.2 %collective-permute-start.4 = (bf16[320,128]{1,0:T(8,128)(2,1)S(1)}, bf16[320,128]{1,0:T(8,128)(2,1)S(1)}, u32[]{:S(2)}, u32[]{:S(2)}) collective-permute-start(bf16[320,128]{1,0:T(8,128)(2,1)S(1)} %pair_sum.2.refs_0_), channel_id=1, source_target_pairs={{0,4},{2,6},{4,0},{6,2},{8,12},{10,14},{12,8},{14,10},{1,5},{3,7},... | collective-permute-start | bytes 245768 | tf_op jit(solution)/shard_map/ppermute | solution.py:384
  18.3 0.6 %pair_sum.3.refs_0_ = bf16[208,128]{1,0:T(8,128)(2,1)S(1)} custom-call(s32[2]{0:T(128)S(1)} %pad_add_fusion.1.spot_ref._, bf16[208,128]{1,0:T(8,128)(2,1)S(1)} %get-tuple-element.31.refs_0_.own_ref, bf16[208,128]{1,0:T(8,128)(2,1)S(1)} %collective-permute-done.9.refs_1_.partner_ref), custom_call_target="tpu_custom_call" | custom-call | tf_op jit(solution)/shard_map/pair_sum/pallas_call | solution.py:326
  19.0 4.1 %collective-permute-done.10.refs_1_.refs_0_ = bf16[208,128]{1,0:T(8,128)(2,1)S(1)} collective-permute-done((bf16[208,128]{1,0:T(8,128)(2,1)S(1)}, bf16[208,128]{1,0:T(8,128)(2,1)S(1)}, u32[]{:S(2)}, u32[]{:S(2)}) %collective-permute-start.10) | collective-permute-done | bytes 53280 | tf_op jit(solution)/shard_map/ppermute | solution.py:384
  23.1 0.6 %stride_sum.3 = bf16[208,128]{1,0:T(8,128)(2,1)S(1)} custom-call(s32[2]{0:T(128)S(1)} %pad_add_fusion.1.spot_ref._, bf16[208,128]{1,0:T(8,128)(2,1)S(1)} %pair_sum.3.refs_0_, bf16[208,128]{1,0:T(8,128)(2,1)S(1)} %collective-permute-done.10.refs_1_.refs_0_), custom_call_target="tpu_custom_call" | custom-call | tf_op jit(solution)/shard_map/stride_sum/pallas_call | solution.py:326
  23.7 2.9 %collective-permute-start.11 = (bf16[208,128]{1,0:T(8,128)(2,1)S(1)}, bf16[208,128]{1,0:T(8,128)(2,1)S(1)}, u32[]{:S(2)}, u32[]{:S(2)}) collective-permute-start(bf16[208,128]{1,0:T(8,128)(2,1)S(1)} %stride_sum.3), channel_id=1, source_target_pairs={{0,8},{2,10},{4,12},{6,14},{8,0},{10,2},{12,4},{14,6},{1,9},{3,11}... | collective-permute-start | bytes 159752 | tf_op jit(solution)/shard_map/ppermute | solution.py:384
  26.6 0.6 %stride_sum.2 = bf16[320,128]{1,0:T(8,128)(2,1)S(1)} custom-call(s32[2]{0:T(128)S(1)} %pad_add_fusion.1.spot_ref._, bf16[320,128]{1,0:T(8,128)(2,1)S(1)} %pair_sum.2.refs_0_, bf16[320,128]{1,0:T(8,128)(2,1)S(1)} %collective-permute-done.4.refs_1_.refs_0_), custom_call_target="tpu_custom_call" | custom-call | tf_op jit(solution)/shard_map/stride_sum/pallas_call | solution.py:326
  27.3 3.1 %collective-permute-done.11.refs_1_ = bf16[208,128]{1,0:T(8,128)(2,1)S(1)} collective-permute-done((bf16[208,128]{1,0:T(8,128)(2,1)S(1)}, bf16[208,128]{1,0:T(8,128)(2,1)S(1)}, u32[]{:S(2)}, u32[]{:S(2)}) %collective-permute-start.11) | collective-permute-done | bytes 53280 | tf_op jit(solution)/shard_map/ppermute | solution.py:384
  30.4 0.6 %pair_sums.3 = (bf16[208,128]{1,0:T(8,128)(2,1)S(1)}, bf16[208,128]{1,0:T(8,128)(2,1)S(1)}) custom-call(s32[2]{0:T(128)S(1)} %pad_add_fusion.1.spot_ref._, bf16[208,128]{1,0:T(8,128)(2,1)S(1)} %get-tuple-element.31.refs_0_.own_ref, bf16[208,128]{1,0:T(8,128)(2,1)S(1)} %collective-permute-done.9.refs_1_.partner_ref, ...), custom_call_target="tpu_custom_call" | custom-call | tf_op jit(solution)/shard_map/pair_sums/pallas_call | solution.py:326
  31.1 1.7 %collective-permute-start.14 = (bf16[208,128]{1,0:T(8,128)(2,1)S(1)}, bf16[208,128]{1,0:T(8,128)(2,1)S(1)}, u32[]{:S(2)}, u32[]{:S(2)}) collective-permute-start(bf16[208,128]{1,0:T(8,128)(2,1)S(1)} %get-tuple-element.34), channel_id=1, source_target_pairs={{0,3},{1,2},{2,1},{3,0},{4,7},{5,6},{6,5},{7,4},{8,11},{9,10},{10,... | collective-permute-start | bytes 159752 | tf_op jit(solution)/shard_map/ppermute | solution.py:429
  33.3 0.6 %pair_sums.2 = (bf16[320,128]{1,0:T(8,128)(2,1)S(1)}, bf16[320,128]{1,0:T(8,128)(2,1)S(1)}) custom-call(s32[2]{0:T(128)S(1)} %pad_add_fusion.1.spot_ref._, bf16[320,128]{1,0:T(8,128)(2,1)S(1)} %get-tuple-element.27.refs_0_.own_ref, bf16[320,128]{1,0:T(8,128)(2,1)S(1)} %collective-permute-done.3.refs_1_.partner_ref, ...), custom_call_target="tpu_custom_call" | custom-call | tf_op jit(solution)/shard_map/pair_sums/pallas_call | solution.py:326
  33.9 1.0 %collective-permute-start.8 = (bf16[320,128]{1,0:T(8,128)(2,1)S(1)}, bf16[320,128]{1,0:T(8,128)(2,1)S(1)}, u32[]{:S(2)}, u32[]{:S(2)}) collective-permute-start(bf16[320,128]{1,0:T(8,128)(2,1)S(1)} %get-tuple-element.30), channel_id=1, source_target_pairs={{0,3},{1,2},{2,1},{3,0},{4,7},{5,6},{6,5},{7,4},{8,11},{9,10},{10,... | collective-permute-start | bytes 245768 | tf_op jit(solution)/shard_map/ppermute | solution.py:429
  34.9 0.7 %collective-permute-start.7 = (bf16[320,128]{1,0:T(8,128)(2,1)S(1)}, bf16[320,128]{1,0:T(8,128)(2,1)S(1)}, u32[]{:S(2)}, u32[]{:S(2)}) collective-permute-start(bf16[320,128]{1,0:T(8,128)(2,1)S(1)} %get-tuple-element.30), channel_id=1, source_target_pairs={{0,2},{2,0},{4,6},{6,4},{8,10},{10,8},{12,14},{14,12},{1,3},{3,1},... | collective-permute-start | bytes 245768 | tf_op jit(solution)/shard_map/ppermute | solution.py:384
  35.9 1.0 %collective-permute-done.13.refs_2_ = bf16[208,128]{1,0:T(8,128)(2,1)S(1)} collective-permute-done((bf16[208,128]{1,0:T(8,128)(2,1)S(1)}, bf16[208,128]{1,0:T(8,128)(2,1)S(1)}, u32[]{:S(2)}, u32[]{:S(2)}) %collective-permute-start.13) | collective-permute-done | bytes 53280 | tf_op jit(solution)/shard_map/ppermute | solution.py:384
  37.0 7.0 %mix.2.refs_4_ = bf16[480,2240]{1,0:T(8,128)(2,1)} custom-call(s32[1]{0:T(128)} %bitcast.place_ref, s32[4]{0:T(128)S(1)} %pad_add_fusion.spots_ref, bf16[480,2240]{1,0:T(8,128)(2,1)} %bitcast.16, bf16[480,2240]{1,0:T(8,128)(2,1)} %bitcast.19, bf16[2,1,80,2240]{3,2,1,0:T(8,128)(2,1)S(1)} %collective-permute-done.1.edge_ref, ...), custom_call_target="tpu_custom_call" | custom-call | flops 430080000 | bytes 2580480 | tf_op jit(solution)/shard_map/mix/pallas_call | solution.py:280
  44.0 9.9 %mix.3 = bf16[480,2240]{1,0:T(8,128)(2,1)} custom-call(s32[1]{0:T(128)} %bitcast.place_ref, s32[4]{0:T(128)S(1)} %pad_add_fusion.spots_ref, bf16[480,2240]{1,0:T(8,128)(2,1)} %bitcast.17, bf16[480,2240]{1,0:T(8,128)(2,1)} %bitcast.20, bf16[2,1,80,2240]{3,2,1,0:T(8,128)(2,1)S(1)} %collective-permute-done.1.edge_ref, ...), custom_call_target="tpu_custom_call", output_to_operand_aliasing={{}: (12, {})} | custom-call | flops 860160000 | bytes 5160960 | tf_op jit(solution)/shard_map/mix/pallas_call | solution.py:280
  (27 shorter events, 2.4 us)
Async XLA Ops:
  2.6 1.5 %collective-permute-start = (bf16[416,128]{1,0:T(8,128)(2,1)S(1)}, bf16[416,128]{1,0:T(8,128)(2,1)S(1)}, u32[]{:S(2)}, u32[]{:S(2)}) collective-permute-start(bf16[416,128]{1,0:T(8,128)(2,1)S(1)} %get-tuple-element.22), channel_id=1, source_target_pairs={{0,1},{1,0},{2,3},{3,2},{4,5},{5,4},{6,7},{7,6},{8,9},{9,8},{10,11... | collective-permute-start | bytes 319496 | tf_op jit(solution)/shard_map/ppermute | solution.py:395
  4.7 31.3 %copy-start.2 = (f32[2240]{0:T(1024)S(1)}, f32[2240]{0:T(1024)}, u32[]{:S(2)}) copy-start(f32[2240]{0:T(1024)} %param.11) | copy-start | bytes 26884
  4.7 32.3 %copy-start = (f32[9,2240]{1,0:T(8,128)S(1)}, f32[9,2240]{1,0:T(8,128)}, u32[]{:S(2)}) copy-start(f32[9,2240]{1,0:T(8,128)} %vtaps_ref.3) | copy-start | bytes 241924
  4.7 32.3 %copy-start.1 = (f32[9,2240]{1,0:T(8,128)S(1)}, f32[9,2240]{1,0:T(8,128)}, u32[]{:S(2)}) copy-start(f32[9,2240]{1,0:T(8,128)} %gtaps_ref.3) | copy-start | bytes 241924
  4.7 32.3 %collective-permute-start.1 = (bf16[2,1,80,2240]{3,2,1,0:T(8,128)(2,1)S(1)}, bf16[2,1,80,2240]{3,2,1,0:T(8,128)(2,1)S(1)}, u32[]{:S(2)}, u32[]{:S(2)}) collective-permute-start(bf16[2,1,80,2240]{3,2,1,0:T(8,128)(2,1)S(1)} %get-tuple-element.24), channel_id=1, source_target_pairs={{0,1},{1,0},{2,3},{3,2},{4,5},{5,4},{6,7},{7,6},{8,9},{9,8},{10,11... | collective-permute-start | bytes 2150408 | tf_op jit(solution)/shard_map/ppermute | solution.py:402
  7.6 1.5 %collective-permute-start.2 = (bf16[640,128]{1,0:T(8,128)(2,1)S(1)}, bf16[640,128]{1,0:T(8,128)(2,1)S(1)}, u32[]{:S(2)}, u32[]{:S(2)}) collective-permute-start(bf16[640,128]{1,0:T(8,128)(2,1)S(1)} %get-tuple-element.26), channel_id=1, source_target_pairs={{0,1},{1,0},{2,3},{3,2},{4,5},{5,4},{6,7},{7,6},{8,9},{9,8},{10,11... | collective-permute-start | bytes 491528 | tf_op jit(solution)/shard_map/ppermute | solution.py:395
  9.6 6.0 %collective-permute-start.3 = (bf16[320,128]{1,0:T(8,128)(2,1)S(1)}, bf16[320,128]{1,0:T(8,128)(2,1)S(1)}, u32[]{:S(2)}, u32[]{:S(2)}) collective-permute-start(bf16[320,128]{1,0:T(8,128)(2,1)S(1)} %get-tuple-element.28), channel_id=1, source_target_pairs={{0,2},{2,0},{4,6},{6,4},{8,10},{10,8},{12,14},{14,12},{1,3},{3,1},... | collective-permute-start | bytes 245768 | tf_op jit(solution)/shard_map/ppermute | solution.py:384
  12.4 6.0 %collective-permute-start.9 = (bf16[208,128]{1,0:T(8,128)(2,1)S(1)}, bf16[208,128]{1,0:T(8,128)(2,1)S(1)}, u32[]{:S(2)}, u32[]{:S(2)}) collective-permute-start(bf16[208,128]{1,0:T(8,128)(2,1)S(1)} %get-tuple-element.32), channel_id=1, source_target_pairs={{0,2},{2,0},{4,6},{6,4},{8,10},{10,8},{12,14},{14,12},{1,3},{3,1},... | collective-permute-start | bytes 159752 | tf_op jit(solution)/shard_map/ppermute | solution.py:384
  16.2 10.4 %collective-permute-start.4 = (bf16[320,128]{1,0:T(8,128)(2,1)S(1)}, bf16[320,128]{1,0:T(8,128)(2,1)S(1)}, u32[]{:S(2)}, u32[]{:S(2)}) collective-permute-start(bf16[320,128]{1,0:T(8,128)(2,1)S(1)} %pair_sum.2.refs_0_), channel_id=1, source_target_pairs={{0,4},{2,6},{4,0},{6,2},{8,12},{10,14},{12,8},{14,10},{1,5},{3,7},... | collective-permute-start | bytes 245768 | tf_op jit(solution)/shard_map/ppermute | solution.py:384
  18.9 4.2 %collective-permute-start.10 = (bf16[208,128]{1,0:T(8,128)(2,1)S(1)}, bf16[208,128]{1,0:T(8,128)(2,1)S(1)}, u32[]{:S(2)}, u32[]{:S(2)}) collective-permute-start(bf16[208,128]{1,0:T(8,128)(2,1)S(1)} %pair_sum.3.refs_0_), channel_id=1, source_target_pairs={{0,4},{2,6},{4,0},{6,2},{8,12},{10,14},{12,8},{14,10},{1,5},{3,7},... | collective-permute-start | bytes 159752 | tf_op jit(solution)/shard_map/ppermute | solution.py:384
  23.7 6.8 %collective-permute-start.11 = (bf16[208,128]{1,0:T(8,128)(2,1)S(1)}, bf16[208,128]{1,0:T(8,128)(2,1)S(1)}, u32[]{:S(2)}, u32[]{:S(2)}) collective-permute-start(bf16[208,128]{1,0:T(8,128)(2,1)S(1)} %stride_sum.3), channel_id=1, source_target_pairs={{0,8},{2,10},{4,12},{6,14},{8,0},{10,2},{12,4},{14,6},{1,9},{3,11}... | collective-permute-start | bytes 159752 | tf_op jit(solution)/shard_map/ppermute | solution.py:384
  27.1 6.2 %collective-permute-start.5 = (bf16[320,128]{1,0:T(8,128)(2,1)S(1)}, bf16[320,128]{1,0:T(8,128)(2,1)S(1)}, u32[]{:S(2)}, u32[]{:S(2)}) collective-permute-start(bf16[320,128]{1,0:T(8,128)(2,1)S(1)} %stride_sum.2), channel_id=1, source_target_pairs={{0,8},{2,10},{4,12},{6,14},{8,0},{10,2},{12,4},{14,6},{1,9},{3,11}... | collective-permute-start | bytes 245768 | tf_op jit(solution)/shard_map/ppermute | solution.py:384
  31.1 3.9 %collective-permute-start.12 = (bf16[208,128]{1,0:T(8,128)(2,1)S(1)}, bf16[208,128]{1,0:T(8,128)(2,1)S(1)}, u32[]{:S(2)}, u32[]{:S(2)}) collective-permute-start(bf16[208,128]{1,0:T(8,128)(2,1)S(1)} %get-tuple-element.33.refs_0_), channel_id=1, source_target_pairs={{0,1},{1,0},{2,3},{3,2},{4,5},{5,4},{6,7},{7,6},{8,9},{9,8},{10,11... | collective-permute-start | bytes 159752 | tf_op jit(solution)/shard_map/ppermute | solution.py:427
  31.1 4.5 %collective-permute-start.14 = (bf16[208,128]{1,0:T(8,128)(2,1)S(1)}, bf16[208,128]{1,0:T(8,128)(2,1)S(1)}, u32[]{:S(2)}, u32[]{:S(2)}) collective-permute-start(bf16[208,128]{1,0:T(8,128)(2,1)S(1)} %get-tuple-element.34), channel_id=1, source_target_pairs={{0,3},{1,2},{2,1},{3,0},{4,7},{5,6},{6,5},{7,4},{8,11},{9,10},{10,... | collective-permute-start | bytes 159752 | tf_op jit(solution)/shard_map/ppermute | solution.py:429
  32.8 4.1 %collective-permute-start.13 = (bf16[208,128]{1,0:T(8,128)(2,1)S(1)}, bf16[208,128]{1,0:T(8,128)(2,1)S(1)}, u32[]{:S(2)}, u32[]{:S(2)}) collective-permute-start(bf16[208,128]{1,0:T(8,128)(2,1)S(1)} %get-tuple-element.34), channel_id=1, source_target_pairs={{0,2},{2,0},{4,6},{6,4},{8,10},{10,8},{12,14},{14,12},{1,3},{3,1},... | collective-permute-start | bytes 159752 | tf_op jit(solution)/shard_map/ppermute | solution.py:384
  33.9 10.1 %collective-permute-start.8 = (bf16[320,128]{1,0:T(8,128)(2,1)S(1)}, bf16[320,128]{1,0:T(8,128)(2,1)S(1)}, u32[]{:S(2)}, u32[]{:S(2)}) collective-permute-start(bf16[320,128]{1,0:T(8,128)(2,1)S(1)} %get-tuple-element.30), channel_id=1, source_target_pairs={{0,3},{1,2},{2,1},{3,0},{4,7},{5,6},{6,5},{7,4},{8,11},{9,10},{10,... | collective-permute-start | bytes 245768 | tf_op jit(solution)/shard_map/ppermute | solution.py:429
  34.9 9.1 %collective-permute-start.7 = (bf16[320,128]{1,0:T(8,128)(2,1)S(1)}, bf16[320,128]{1,0:T(8,128)(2,1)S(1)}, u32[]{:S(2)}, u32[]{:S(2)}) collective-permute-start(bf16[320,128]{1,0:T(8,128)(2,1)S(1)} %get-tuple-element.30), channel_id=1, source_target_pairs={{0,2},{2,0},{4,6},{6,4},{8,10},{10,8},{12,14},{14,12},{1,3},{3,1},... | collective-permute-start | bytes 245768 | tf_op jit(solution)/shard_map/ppermute | solution.py:384
  35.6 8.4 %collective-permute-start.6 = (bf16[320,128]{1,0:T(8,128)(2,1)S(1)}, bf16[320,128]{1,0:T(8,128)(2,1)S(1)}, u32[]{:S(2)}, u32[]{:S(2)}) collective-permute-start(bf16[320,128]{1,0:T(8,128)(2,1)S(1)} %get-tuple-element.29.refs_0_), channel_id=1, source_target_pairs={{0,1},{1,0},{2,3},{3,2},{4,5},{5,4},{6,7},{7,6},{8,9},{9,8},{10,11... | collective-permute-start | bytes 245768 | tf_op jit(solution)/shard_map/ppermute | solution.py:427

commit v8 on v4

--- a/solution.py
+++ b/solution.py
@@ -139,12 +139,11 @@
     dim, rows, width, edges,
     place_ref, spots_ref, queries_ref, residual_ref, edge_ref, gain_ref, vtaps_ref, gtaps_ref, *refs,
 ):
-    *pieces, out_ref, states, features, weights, same, numer, squares, shifted = refs
+    *pieces, out_ref, states, features, weights, same, numer, squares, windows = refs
     step = pl.program_id(0)
     tokens = rows * width
-    total = tokens + edges * width
-
-    @pl.when(pl.program_id(0) == 0)
+
+    @pl.when(step == 0)
     def _():
         weights[...] = jnp.zeros_like(weights)
         same[...] = jnp.zeros_like(same)
@@ -157,26 +156,28 @@
                     same[
                         number, start : start + HEAD_DIM, side * LANES : (side + 1) * LANES
                     ] = block.astype(jnp.bfloat16)
-        for row in (0, rows + 1):
-            shifted[:, row] = jnp.zeros((3, width, LANES), jnp.float32)
         for k, piece in enumerate(pieces):
             size = piece.shape[0]
             states[pl.ds(pl.multiple_of(spots_ref[k] * size, 16), size), :] = piece[...]
 
     zero = jnp.zeros((), jnp.bfloat16)
-    column = lax.broadcasted_iota(jnp.int32, (width, LANES), 0)
     lane = lane_iota((HEAD_DIM, LANES))
-
-    def store_shifted(mixed, row):
+    sublane = lax.broadcasted_iota(jnp.int32, (8, LANES), 0)
+
+    def store_windows(mixed, row, slot):
         mixed = mixed.astype(jnp.bfloat16).astype(jnp.float32)
-        shifted[1, row] = mixed
-        shifted[0, row] = jnp.where(column == 0, 0.0, pltpu.roll(mixed, 1, 0))
-        shifted[2, row] = jnp.where(column == width - 1, 0.0, pltpu.roll(mixed, width - 1, 0))
+        windows[slot, 1, row] = mixed
+        before, after = pltpu.roll(mixed, 1, 0), pltpu.roll(mixed, width - 1, 0)
+        windows[slot, 0, row, :8] = jnp.where(sublane == 0, 0.0, before[:8])
+        windows[slot, 0, row, 8:] = before[8:]
+        windows[slot, 2, row, : width - 8] = after[: width - 8]
+        windows[slot, 2, row, width - 8 :] = jnp.where(sublane == 7, 0.0, after[width - 8 :])
 
     def body(lanes):
         count = cdiv(lanes, LANES)
         end = count * LANES
         inside = lane_iota((1, end)) < lanes
+        groups = spans(lanes)
 
         def feature(queries):
             queries = jnp.maximum(queries, zero)
@@ -187,7 +188,9 @@
             features[tokens + e * width : tokens + (e + 1) * width, :end] = feature(
                 edge_ref[0, e, :, :end]
             )
-        for number, (tiles, first, last) in enumerate(spans(lanes)):
+
+        def numerators(number):
+            tiles, first, last = groups[number]
             for side, j in enumerate(tiles):
                 row = pl.multiple_of((step * TILES + j) * HEAD_DIM, 16)
                 state = states[pl.ds(row, HEAD_DIM), :].astype(jnp.float32)
@@ -207,47 +210,54 @@
             numer[:, here] = product
             squares[:, here] = (product * product).astype(jnp.bfloat16)
 
-        for number, (tiles, first, last) in enumerate(spans(lanes)):
+        def head_sums(number):
+            tiles, first, last = groups[number]
             depth, wide = (last - first) * LANES, len(tiles) * LANES
-            sums = jnp.dot(
+            return jnp.dot(
                 squares[:, first * LANES : last * LANES],
                 same[number, :depth, :wide],
                 preferred_element_type=jnp.float32,
             )
-            here = slice(tiles[0] * LANES, tiles[0] * LANES + wide)
-            scale = lax.rsqrt(sums * (1.0 / HEAD_DIM) + 1e-06)
-            numer[:, here] = numer[:, here] * scale * gain_ref[:, here]
-
-        for j in range(count):
+
+        def mix_tile(j, sums):
             here = slice(j * LANES, (j + 1) * LANES)
+            slot = j % 2
+            gain = gain_ref[:, here] * math.sqrt(HEAD_DIM)
+
+            def mixed(source, residual):
+                normed = numer[source, here] * lax.rsqrt(sums[source] + HEAD_DIM * 1e-06)
+                return residual.astype(jnp.float32) + normed * gain
+
+            outside = [None, None]
+            for e in range(edges):
+                source = slice(tokens + e * width, tokens + (e + 1) * width)
+                value = mixed(source, edge_ref[1, e, :, here])
+                for k, row in enumerate((0, rows + 1)):
+                    part = jnp.where(place_ref[e] == row, value, 0.0)
+                    outside[k] = part if outside[k] is None else outside[k] + part
+            for k, row in enumerate((0, rows + 1)):
+                store_windows(outside[k], row, slot)
             for row in range(rows):
                 source = slice(row * width, (row + 1) * width)
-                store_shifted(
-                    residual_ref[source, here].astype(jnp.float32) + numer[source, here], row + 1
-                )
-            for e in range(edges):
-                source = slice(tokens + e * width, tokens + (e + 1) * width)
-                store_shifted(
-                    edge_ref[1, e, :, here].astype(jnp.float32) + numer[source, here], place_ref[e]
-                )
-
-            def convolve(row, carry, here=here):
-                conv_v = jnp.zeros((width, LANES), jnp.float32)
-                half_g = jnp.zeros((width, LANES), jnp.float32)
-                for tap_row in range(3):
-                    for tap_col in range(3):
-                        window = shifted[tap_col, row + tap_row]
-                        tap = 3 * tap_row + tap_col
-                        conv_v = conv_v + vtaps_ref[tap : tap + 1, here] * window
-                        half_g = half_g + (0.5 * gtaps_ref[tap : tap + 1, here]) * window
-                gate = half_g + half_g * jnp.tanh(half_g)
-                result = shifted[1, row + 1] + conv_v * gate
-                out_ref[pl.ds(pl.multiple_of(row * width, width), width), here] = result.astype(
-                    jnp.bfloat16
-                )
-                return carry
-
-            lax.fori_loop(0, rows, convolve, 0)
+                store_windows(mixed(source, residual_ref[source, here]), row + 1, slot)
+            for row in range(rows):
+                conv_v = half_g = None
+                for tap in range(9):
+                    window = windows[slot, tap % 3, row + tap // 3]
+                    value = vtaps_ref[tap : tap + 1, here] * window
+                    gate = (0.5 * gtaps_ref[tap : tap + 1, here]) * window
+                    conv_v = value if tap == 0 else conv_v + value
+                    half_g = gate if tap == 0 else half_g + gate
+                result = windows[slot, 1, row + 1] + conv_v * (half_g + half_g * jnp.tanh(half_g))
+                out_ref[row * width : (row + 1) * width, here] = result.astype(jnp.bfloat16)
+
+        numerators(0)
+        for number, (tiles, _, _) in enumerate(groups):
+            if number + 1 < len(groups):
+                numerators(number + 1)
+            sums = head_sums(number)
+            for side, j in enumerate(tiles):
+                mix_tile(j, sums[:, side * LANES : (side + 1) * LANES])
 
     by_group(dim, body)
 
@@ -283,7 +293,7 @@
             pltpu.VMEM((len(pairs), depth, 2 * LANES), jnp.bfloat16),
             pltpu.VMEM((total, GROUP), jnp.float32),
             pltpu.VMEM((total, GROUP), jnp.bfloat16),
-            pltpu.VMEM((3, rows + 2, width, LANES), jnp.float32),
+            pltpu.VMEM((2, 3, rows + 2, width, LANES), jnp.float32),
         ],
         compiler_params=pltpu.CompilerParams(vmem_limit_bytes=36 * 2**20),
         cost_estimate=pl.CostEstimate(

time: 49.7 us -> 49.7 us (level)
  no operation moved by 1% of the time
where the time goes in v8:
time: 49.7 us; the launch traced here: 49.6 us
  Pallas kernels  21 us (42%)
  waiting for transfers between devices  19.2 us (39%)
  starting transfers between devices  9.22 us (19%)
    pallas_call x1, Pallas kernels, mix(): pl.pallas_call(functools.partial(mix_kernel, dim, rows, width, edges), ou...  14.8 us
    ppermute x2, waiting for transfers between devices, running_states(): got = lax.ppermute(total, 'frame', [(f, f ^ stride) for f in range(frames)])  8.85 us
    ppermute x2, starting transfers between devices, running_states(): got = lax.ppermute(total, 'frame', [(f, f ^ stride) for f in range(frames)])  4.51 us
    ppermute x1, waiting for transfers between devices, running_states(): partner = lax.ppermute(sent, 'frame', [(f, f ^ 1) for f in range(frames)])  4.02 us
    ppermute x1, waiting for transfers between devices, running_states(): other = lax.ppermute(theirs, 'frame', [(f, f ^ 1) for f in range(frames)])  3.97 us
    pallas_call x1, Pallas kernels, frame_states(): pl.pallas_call(functools.partial(state_kernel, dim, bool(edged)), out_sha...  3.75 us
    ppermute x1, starting transfers between devices, running_states(): partner = lax.ppermute(sent, 'frame', [(f, f ^ 1) for f in range(frames)])  2.67 us
    pallas_call x4, Pallas kernels, small_kernel(): pl.pallas_call(body, out_shape=[pltpu.VMEM(shape, jnp.bfloat16) for shape...  2.43 us
  transfers between devices with their start and end apart: 8, of which 6 were waited for; matrix products, arithmetic and copies ran while one was open for 0% of the time, Pallas kernels for 4%

profile of v8, /device:TPU:0, one launch (start us, length us, event | category | flops | bytes accessed | tf_op | source)
XLA Modules:
  0.0 49.6 jit_solution(7518590192559310171)
XLA Ops:
  0.0 3.8 %frame_states.1 = (bf16[1024,128]{1,0:T(8,128)(2,1)S(1)}, bf16[1024,128]{1,0:T(8,128)(2,1)S(1)}, bf16[2,1,80,2240]{3,2,1,0:T(8,128)(2,1)S(1)}) custom-call(s32[1]{0:T(128)} %bitcast.7.spot_ref, bf16[480,2240]{1,0:T(8,128)(2,1)} %bitcast.19, bf16[480,2240]{1,0:T(8,128)(2,1)} %bitcast.20, bf16[6,80,2240]{2,1,0:T(8,128)(2,1)} %bitcast.15, ...), custom_call_target="tpu_custom_call" | custom-call | flops 240844800 | bytes 4300800 | tf_op jit(solution)/shard_map/frame_states/pallas_call | solution.py:116
  3.8 0.5 %collective-permute-start = (bf16[1024,128]{1,0:T(8,128)(2,1)S(1)}, bf16[1024,128]{1,0:T(8,128)(2,1)S(1)}, u32[]{:S(2)}, u32[]{:S(2)}) collective-permute-start(bf16[1024,128]{1,0:T(8,128)(2,1)S(1)} %get-tuple-element.16), channel_id=1, source_target_pairs={{0,1},{1,0},{2,3},{3,2},{4,5},{5,4},{6,7},{7,6},{8,9},{9,8},{10,11... | collective-permute-start | bytes 786440 | tf_op jit(solution)/shard_map/ppermute | solution.py:375
  4.3 0.1 pad_add_fusion.1.spot_ref._
  4.4 1.1 %collective-permute-done.got_ref = bf16[1024,128]{1,0:T(8,128)(2,1)S(1)} collective-permute-done((bf16[1024,128]{1,0:T(8,128)(2,1)S(1)}, bf16[1024,128]{1,0:T(8,128)(2,1)S(1)}, u32[]{:S(2)}, u32[]{:S(2)}) %collective-permute-start) | collective-permute-done | bytes 262176 | tf_op jit(solution)/shard_map/ppermute | solution.py:375
  5.5 0.6 %split_sum.1 = (bf16[512,128]{1,0:T(8,128)(2,1)S(1)}, bf16[512,128]{1,0:T(8,128)(2,1)S(1)}) custom-call(s32[2]{0:T(128)S(1)} %pad_add_fusion.1.spot_ref._, bf16[1024,128]{1,0:T(8,128)(2,1)S(1)} %get-tuple-element.15.kept_ref, bf16[1024,128]{1,0:T(8,128)(2,1)S(1)} %collective-permute-done.got_ref), custom_call_target="tpu_custom_call" | custom-call | tf_op jit(solution)/shard_map/split_sum/pallas_call | solution.py:317
  6.1 0.4 collective-permute-start.1
  6.5 2.7 %collective-permute-start.2 = (bf16[512,128]{1,0:T(8,128)(2,1)S(1)}, bf16[512,128]{1,0:T(8,128)(2,1)S(1)}, u32[]{:S(2)}, u32[]{:S(2)}) collective-permute-start(bf16[512,128]{1,0:T(8,128)(2,1)S(1)} %get-tuple-element.20), channel_id=1, source_target_pairs={{0,2},{2,0},{4,6},{6,4},{8,10},{10,8},{12,14},{14,12},{1,3},{3,1},... | collective-permute-start | bytes 393224 | tf_op jit(solution)/shard_map/ppermute | solution.py:381
  9.2 4.0 %collective-permute-done.2.refs_1_.partner_ref = bf16[512,128]{1,0:T(8,128)(2,1)S(1)} collective-permute-done((bf16[512,128]{1,0:T(8,128)(2,1)S(1)}, bf16[512,128]{1,0:T(8,128)(2,1)S(1)}, u32[]{:S(2)}, u32[]{:S(2)}) %collective-permute-start.2) | collective-permute-done | bytes 131104 | tf_op jit(solution)/shard_map/ppermute | solution.py:381
  13.2 0.6 %pair_sum.1.refs_0_ = bf16[512,128]{1,0:T(8,128)(2,1)S(1)} custom-call(s32[2]{0:T(128)S(1)} %pad_add_fusion.1.spot_ref._, bf16[512,128]{1,0:T(8,128)(2,1)S(1)} %get-tuple-element.19.refs_0_.own_ref, bf16[512,128]{1,0:T(8,128)(2,1)S(1)} %collective-permute-done.2.refs_1_.partner_ref), custom_call_target="tpu_custom_call" | custom-call | tf_op jit(solution)/shard_map/pair_sum/pallas_call | solution.py:317
  13.8 1.9 %collective-permute-start.3 = (bf16[512,128]{1,0:T(8,128)(2,1)S(1)}, bf16[512,128]{1,0:T(8,128)(2,1)S(1)}, u32[]{:S(2)}, u32[]{:S(2)}) collective-permute-start(bf16[512,128]{1,0:T(8,128)(2,1)S(1)} %pair_sum.1.refs_0_), channel_id=1, source_target_pairs={{0,4},{2,6},{4,0},{6,2},{8,12},{10,14},{12,8},{14,10},{1,5},{3,7},... | collective-permute-start | bytes 393224 | tf_op jit(solution)/shard_map/ppermute | solution.py:386
  15.6 3.4 %collective-permute-done.3.refs_1_.refs_0_ = bf16[512,128]{1,0:T(8,128)(2,1)S(1)} collective-permute-done((bf16[512,128]{1,0:T(8,128)(2,1)S(1)}, bf16[512,128]{1,0:T(8,128)(2,1)S(1)}, u32[]{:S(2)}, u32[]{:S(2)}) %collective-permute-start.3) | collective-permute-done | bytes 131104 | tf_op jit(solution)/shard_map/ppermute | solution.py:386
  19.0 0.6 %stride_sum.1 = bf16[512,128]{1,0:T(8,128)(2,1)S(1)} custom-call(s32[2]{0:T(128)S(1)} %pad_add_fusion.1.spot_ref._, bf16[512,128]{1,0:T(8,128)(2,1)S(1)} %pair_sum.1.refs_0_, bf16[512,128]{1,0:T(8,128)(2,1)S(1)} %collective-permute-done.3.refs_1_.refs_0_), custom_call_target="tpu_custom_call" | custom-call | tf_op jit(solution)/shard_map/stride_sum/pallas_call | solution.py:317
  19.6 2.6 %collective-permute-start.4 = (bf16[512,128]{1,0:T(8,128)(2,1)S(1)}, bf16[512,128]{1,0:T(8,128)(2,1)S(1)}, u32[]{:S(2)}, u32[]{:S(2)}) collective-permute-start(bf16[512,128]{1,0:T(8,128)(2,1)S(1)} %stride_sum.1), channel_id=1, source_target_pairs={{0,8},{2,10},{4,12},{6,14},{8,0},{10,2},{12,4},{14,6},{1,9},{3,11}... | collective-permute-start | bytes 393224 | tf_op jit(solution)/shard_map/ppermute | solution.py:386
  22.3 5.4 %collective-permute-done.4.refs_1_ = bf16[512,128]{1,0:T(8,128)(2,1)S(1)} collective-permute-done((bf16[512,128]{1,0:T(8,128)(2,1)S(1)}, bf16[512,128]{1,0:T(8,128)(2,1)S(1)}, u32[]{:S(2)}, u32[]{:S(2)}) %collective-permute-start.4) | collective-permute-done | bytes 131104 | tf_op jit(solution)/shard_map/ppermute | solution.py:386
  27.7 0.7 %pair_sums.1 = (bf16[512,128]{1,0:T(8,128)(2,1)S(1)}, bf16[512,128]{1,0:T(8,128)(2,1)S(1)}) custom-call(s32[2]{0:T(128)S(1)} %pad_add_fusion.1.spot_ref._, bf16[512,128]{1,0:T(8,128)(2,1)S(1)} %get-tuple-element.19.refs_0_.own_ref, bf16[512,128]{1,0:T(8,128)(2,1)S(1)} %collective-permute-done.2.refs_1_.partner_ref, ...), custom_call_target="tpu_custom_call" | custom-call | tf_op jit(solution)/shard_map/pair_sums/pallas_call | solution.py:317
  28.4 1.1 %collective-permute-start.5 = (bf16[512,128]{1,0:T(8,128)(2,1)S(1)}, bf16[512,128]{1,0:T(8,128)(2,1)S(1)}, u32[]{:S(2)}, u32[]{:S(2)}) collective-permute-start(bf16[512,128]{1,0:T(8,128)(2,1)S(1)} %get-tuple-element.22), channel_id=1, source_target_pairs={{0,2},{2,0},{4,6},{6,4},{8,10},{10,8},{12,14},{14,12},{1,3},{3,1},... | collective-permute-start | bytes 393224 | tf_op jit(solution)/shard_map/ppermute | solution.py:394
  29.5 0.0 collective-permute-start.6
  29.5 4.0 %collective-permute-done.5.refs_1_ = bf16[512,128]{1,0:T(8,128)(2,1)S(1)} collective-permute-done((bf16[512,128]{1,0:T(8,128)(2,1)S(1)}, bf16[512,128]{1,0:T(8,128)(2,1)S(1)}, u32[]{:S(2)}, u32[]{:S(2)}) %collective-permute-start.5) | collective-permute-done | bytes 131104 | tf_op jit(solution)/shard_map/ppermute | solution.py:394
  33.4 0.0 collective-permute-start.7
  33.5 0.1 pad_add_fusion.spots_ref
  33.5 0.0 collective-permute-done.6.refs_2_
  33.5 1.2 %collective-permute-done.7.refs_3_ = bf16[512,128]{1,0:T(8,128)(2,1)S(1)} collective-permute-done((bf16[512,128]{1,0:T(8,128)(2,1)S(1)}, bf16[512,128]{1,0:T(8,128)(2,1)S(1)}, u32[]{:S(2)}, u32[]{:S(2)}) %collective-permute-start.7) | collective-permute-done | bytes 131104 | tf_op jit(solution)/shard_map/ppermute | solution.py:395
  34.8 0.0 collective-permute-done.1.edge_ref
  34.8 14.8 %mix.1 = bf16[480,2240]{1,0:T(8,128)(2,1)} custom-call(s32[1]{0:T(128)} %bitcast.place_ref, s32[4]{0:T(128)S(1)} %pad_add_fusion.spots_ref, bf16[480,2240]{1,0:T(8,128)(2,1)} %bitcast.16, bf16[480,2240]{1,0:T(8,128)(2,1)} %bitcast.18, bf16[2,1,80,2240]{3,2,1,0:T(8,128)(2,1)S(1)} %collective-permute-done.1.edge_ref, f32[1,2240]{1,0:T(1,128)S(1)} %broadcast_in_dim.11.gain_ref, ...), custom_call_target="tpu_custom_call" | custom-call | flops 64512000 | bytes 6451200 | tf_op jit(solution)/shard_map/mix/pallas_call | solution.py:273
  (7 shorter events, 0.0 us)
Async XLA Ops:
  0.0 33.4 %copy-start.2 = (f32[2240]{0:T(1024)S(1)}, f32[2240]{0:T(1024)}, u32[]{:S(2)}) copy-start(f32[2240]{0:T(1024)} %param.11) | copy-start | bytes 26884
  0.0 34.8 %copy-start = (f32[9,2240]{1,0:T(8,128)S(1)}, f32[9,2240]{1,0:T(8,128)}, u32[]{:S(2)}) copy-start(f32[9,2240]{1,0:T(8,128)} %vtaps_ref.1) | copy-start | bytes 241924
  0.0 34.8 %copy-start.1 = (f32[9,2240]{1,0:T(8,128)S(1)}, f32[9,2240]{1,0:T(8,128)}, u32[]{:S(2)}) copy-start(f32[9,2240]{1,0:T(8,128)} %gtaps_ref.1) | copy-start | bytes 241924
  3.8 1.7 %collective-permute-start = (bf16[1024,128]{1,0:T(8,128)(2,1)S(1)}, bf16[1024,128]{1,0:T(8,128)(2,1)S(1)}, u32[]{:S(2)}, u32[]{:S(2)}) collective-permute-start(bf16[1024,128]{1,0:T(8,128)(2,1)S(1)} %get-tuple-element.16), channel_id=1, source_target_pairs={{0,1},{1,0},{2,3},{3,2},{4,5},{5,4},{6,7},{7,6},{8,9},{9,8},{10,11... | collective-permute-start | bytes 786440 | tf_op jit(solution)/shard_map/ppermute | solution.py:375
  6.1 28.7 %collective-permute-start.1 = (bf16[2,1,80,2240]{3,2,1,0:T(8,128)(2,1)S(1)}, bf16[2,1,80,2240]{3,2,1,0:T(8,128)(2,1)S(1)}, u32[]{:S(2)}, u32[]{:S(2)}) collective-permute-start(bf16[2,1,80,2240]{3,2,1,0:T(8,128)(2,1)S(1)} %get-tuple-element.18), channel_id=1, source_target_pairs={{0,1},{1,0},{2,3},{3,2},{4,5},{5,4},{6,7},{7,6},{8,9},{9,8},{10,11... | collective-permute-start | bytes 2150408 | tf_op jit(solution)/shard_map/ppermute | solution.py:379
  6.5 6.7 %collective-permute-start.2 = (bf16[512,128]{1,0:T(8,128)(2,1)S(1)}, bf16[512,128]{1,0:T(8,128)(2,1)S(1)}, u32[]{:S(2)}, u32[]{:S(2)}) collective-permute-start(bf16[512,128]{1,0:T(8,128)(2,1)S(1)} %get-tuple-element.20), channel_id=1, source_target_pairs={{0,2},{2,0},{4,6},{6,4},{8,10},{10,8},{12,14},{14,12},{1,3},{3,1},... | collective-permute-start | bytes 393224 | tf_op jit(solution)/shard_map/ppermute | solution.py:381
  13.8 5.3 %collective-permute-start.3 = (bf16[512,128]{1,0:T(8,128)(2,1)S(1)}, bf16[512,128]{1,0:T(8,128)(2,1)S(1)}, u32[]{:S(2)}, u32[]{:S(2)}) collective-permute-start(bf16[512,128]{1,0:T(8,128)(2,1)S(1)} %pair_sum.1.refs_0_), channel_id=1, source_target_pairs={{0,4},{2,6},{4,0},{6,2},{8,12},{10,14},{12,8},{14,10},{1,5},{3,7},... | collective-permute-start | bytes 393224 | tf_op jit(solution)/shard_map/ppermute | solution.py:386
  19.6 8.1 %collective-permute-start.4 = (bf16[512,128]{1,0:T(8,128)(2,1)S(1)}, bf16[512,128]{1,0:T(8,128)(2,1)S(1)}, u32[]{:S(2)}, u32[]{:S(2)}) collective-permute-start(bf16[512,128]{1,0:T(8,128)(2,1)S(1)} %stride_sum.1), channel_id=1, source_target_pairs={{0,8},{2,10},{4,12},{6,14},{8,0},{10,2},{12,4},{14,6},{1,9},{3,11}... | collective-permute-start | bytes 393224 | tf_op jit(solution)/shard_map/ppermute | solution.py:386
  28.4 5.0 %collective-permute-start.5 = (bf16[512,128]{1,0:T(8,128)(2,1)S(1)}, bf16[512,128]{1,0:T(8,128)(2,1)S(1)}, u32[]{:S(2)}, u32[]{:S(2)}) collective-permute-start(bf16[512,128]{1,0:T(8,128)(2,1)S(1)} %get-tuple-element.22), channel_id=1, source_target_pairs={{0,2},{2,0},{4,6},{6,4},{8,10},{10,8},{12,14},{14,12},{1,3},{3,1},... | collective-permute-start | bytes 393224 | tf_op jit(solution)/shard_map/ppermute | solution.py:394
  29.5 4.1 %collective-permute-start.6 = (bf16[512,128]{1,0:T(8,128)(2,1)S(1)}, bf16[512,128]{1,0:T(8,128)(2,1)S(1)}, u32[]{:S(2)}, u32[]{:S(2)}) collective-permute-start(bf16[512,128]{1,0:T(8,128)(2,1)S(1)} %get-tuple-element.21.refs_0_), channel_id=1, source_target_pairs={{0,1},{1,0},{2,3},{3,2},{4,5},{5,4},{6,7},{7,6},{8,9},{9,8},{10,11... | collective-permute-start | bytes 393224 | tf_op jit(solution)/shard_map/ppermute | solution.py:395
  33.4 1.3 %collective-permute-start.7 = (bf16[512,128]{1,0:T(8,128)(2,1)S(1)}, bf16[512,128]{1,0:T(8,128)(2,1)S(1)}, u32[]{:S(2)}, u32[]{:S(2)}) collective-permute-start(bf16[512,128]{1,0:T(8,128)(2,1)S(1)} %collective-permute-done.5.refs_1_), channel_id=1, source_target_pairs={{0,1},{1,0},{2,3},{3,2},{4,5},{5,4},{6,7},{7,6},{8,9},{9,8},{10,11... | collective-permute-start | bytes 393224 | tf_op jit(solution)/shard_map/ppermute | solution.py:395

commit v9 on v8

--- a/solution.py
+++ b/solution.py
@@ -135,65 +135,103 @@
     )(spot, in_hbm(keys), in_hbm(values), *[in_hbm(array) for array in edged])
 
 
+def group_lanes(dim):
+    return [(first, min(GROUP, dim - first)) for first in range(0, dim, GROUP)]
+
+
+def prepare_kernel(dim, queries_ref, residual_ref, edge_ref, features_ref, inputs_ref, same_ref, *refs):
+    held, semaphores = refs
+    tokens = queries_ref.shape[0]
+    full = dim // LANES * LANES
+    parts = [slice(0, full), slice(full, dim)] if full < dim else [slice(0, dim)]
+    copies = [
+        pltpu.make_async_copy(queries_ref, held.at[:tokens], semaphores.at[0]),
+        pltpu.make_async_copy(residual_ref, inputs_ref.at[:tokens], semaphores.at[1]),
+    ]
+    for copy in copies:
+        copy.start()
+    edges, width = edge_ref.shape[1:3]
+    for e in range(edges):
+        here = slice(tokens + e * width, tokens + (e + 1) * width)
+        held[here] = edge_ref[0, e]
+        inputs_ref[here] = edge_ref[1, e]
+    same_ref[...] = jnp.zeros_like(same_ref)
+    lane = lane_iota((HEAD_DIM, LANES))
+    for number, (tiles, first, _) in enumerate(spans(min(GROUP, dim))):
+        for side, j in enumerate(tiles):
+            for h, lo, hi in tile_heads(j, GROUP):
+                start = h * HEAD_DIM - first * LANES
+                block = jnp.where((lane >= lo) & (lane < hi), 1.0, 0.0)
+                same_ref[
+                    number, start : start + HEAD_DIM, side * LANES : (side + 1) * LANES
+                ] = block.astype(jnp.bfloat16)
+    if full < dim:
+        features_ref[:, full:] = jnp.zeros((features_ref.shape[0], LANES), jnp.bfloat16)
+    copies[0].wait()
+    for part in parts:
+        features_ref[:, part] = jnp.maximum(held[:, part], 0)
+    copies[1].wait()
+
+
+def prepare(queries, residual, edge):
+    tokens, dim = queries.shape
+    total = tokens + edge.shape[1] * edge.shape[2]
+    pairs = spans(min(GROUP, dim))
+    depth = max(last - first for _, first, last in pairs) * LANES
+    whole = pl.BlockSpec(memory_space=pltpu.VMEM)
+    return pl.pallas_call(
+        functools.partial(prepare_kernel, dim),
+        out_shape=[
+            pltpu.VMEM((total, cdiv(dim, LANES) * LANES), jnp.bfloat16),
+            pltpu.VMEM((total, dim), jnp.bfloat16),
+            pltpu.VMEM((len(pairs), depth, 2 * LANES), jnp.bfloat16),
+        ],
+        in_specs=[pl.BlockSpec(memory_space=pl.ANY)] * 2 + [whole],
+        out_specs=[whole] * 3,
+        scratch_shapes=[
+            pltpu.VMEM((total, dim), jnp.bfloat16),
+            pltpu.SemaphoreType.DMA((2,)),
+        ],
+        compiler_params=pltpu.CompilerParams(vmem_limit_bytes=24 * 2**20),
+        cost_estimate=pl.CostEstimate(
+            flops=4 * total * dim, bytes_accessed=8 * total * dim, transcendentals=0
+        ),
+        name="prepare",
+    )(in_hbm(queries), in_hbm(residual), edge)
+
+
 def mix_kernel(
     dim, rows, width, edges,
-    place_ref, spots_ref, queries_ref, residual_ref, edge_ref, gain_ref, vtaps_ref, gtaps_ref, *refs,
+    place_ref, spots_ref, features_ref, inputs_ref, same_ref, gain_ref, vtaps_ref, gtaps_ref, *refs,
 ):
-    *pieces, out_ref, states, features, weights, same, numer, squares, windows = refs
-    step = pl.program_id(0)
+    *pieces, out_ref, states, weights, numer, squares, windows, held, semaphores = refs
     tokens = rows * width
-
-    @pl.when(step == 0)
-    def _():
-        weights[...] = jnp.zeros_like(weights)
-        same[...] = jnp.zeros_like(same)
-        lane = lane_iota((HEAD_DIM, LANES))
-        for number, (tiles, first, _) in enumerate(spans(min(GROUP, dim))):
-            for side, j in enumerate(tiles):
-                for h, lo, hi in tile_heads(j, GROUP):
-                    start = h * HEAD_DIM - first * LANES
-                    block = jnp.where((lane >= lo) & (lane < hi), 1.0, 0.0)
-                    same[
-                        number, start : start + HEAD_DIM, side * LANES : (side + 1) * LANES
-                    ] = block.astype(jnp.bfloat16)
-        for k, piece in enumerate(pieces):
-            size = piece.shape[0]
-            states[pl.ds(pl.multiple_of(spots_ref[k] * size, 16), size), :] = piece[...]
-
-    zero = jnp.zeros((), jnp.bfloat16)
+    weights[...] = jnp.zeros_like(weights)
+    for k, piece in enumerate(pieces):
+        size = piece.shape[0]
+        states[pl.ds(pl.multiple_of(spots_ref[k] * size, 16), size), :] = piece[...]
     lane = lane_iota((HEAD_DIM, LANES))
     sublane = lax.broadcasted_iota(jnp.int32, (8, LANES), 0)
 
-    def store_windows(mixed, row, slot):
+    def store_windows(mixed, row, slot, used):
         mixed = mixed.astype(jnp.bfloat16).astype(jnp.float32)
-        windows[slot, 1, row] = mixed
+        windows[slot, 1, row, :, :used] = mixed
         before, after = pltpu.roll(mixed, 1, 0), pltpu.roll(mixed, width - 1, 0)
-        windows[slot, 0, row, :8] = jnp.where(sublane == 0, 0.0, before[:8])
-        windows[slot, 0, row, 8:] = before[8:]
-        windows[slot, 2, row, : width - 8] = after[: width - 8]
-        windows[slot, 2, row, width - 8 :] = jnp.where(sublane == 7, 0.0, after[width - 8 :])
-
-    def body(lanes):
-        count = cdiv(lanes, LANES)
-        end = count * LANES
-        inside = lane_iota((1, end)) < lanes
-        groups = spans(lanes)
-
-        def feature(queries):
-            queries = jnp.maximum(queries, zero)
-            return queries if lanes == end else jnp.where(inside, queries, zero)
-
-        features[:tokens, :end] = feature(queries_ref[:, :end])
-        for e in range(edges):
-            features[tokens + e * width : tokens + (e + 1) * width, :end] = feature(
-                edge_ref[0, e, :, :end]
-            )
+        windows[slot, 0, row, :8, :used] = jnp.where(sublane[:, :used] == 0, 0.0, before[:8])
+        windows[slot, 0, row, 8:, :used] = before[8:]
+        windows[slot, 2, row, : width - 8, :used] = after[: width - 8]
+        windows[slot, 2, row, width - 8 :, :used] = jnp.where(
+            sublane[:, :used] == 7, 0.0, after[width - 8 :]
+        )
+
+    def group(base, lanes):
+        pairs = spans(lanes)
 
         def numerators(number):
-            tiles, first, last = groups[number]
+            tiles, first, last = pairs[number]
             for side, j in enumerate(tiles):
-                row = pl.multiple_of((step * TILES + j) * HEAD_DIM, 16)
-                state = states[pl.ds(row, HEAD_DIM), :].astype(jnp.float32)
+                row = (base // LANES + j) * HEAD_DIM
+                state = states[row : row + HEAD_DIM, :].astype(jnp.float32)
                 for h, lo, hi in tile_heads(j, lanes):
                     start = h * HEAD_DIM - first * LANES
                     block = jnp.where((lane >= lo) & (lane < hi), state, 0.0)
@@ -202,7 +240,7 @@
                     ] = block.astype(jnp.bfloat16)
             depth, wide = (last - first) * LANES, len(tiles) * LANES
             product = jnp.dot(
-                features[:, first * LANES : last * LANES],
+                features_ref[:, base + first * LANES : base + last * LANES],
                 weights[number, :depth, :wide],
                 preferred_element_type=jnp.float32,
             )
@@ -211,96 +249,92 @@
             squares[:, here] = (product * product).astype(jnp.bfloat16)
 
         def head_sums(number):
-            tiles, first, last = groups[number]
+            tiles, first, last = pairs[number]
             depth, wide = (last - first) * LANES, len(tiles) * LANES
             return jnp.dot(
                 squares[:, first * LANES : last * LANES],
-                same[number, :depth, :wide],
+                same_ref[number, :depth, :wide],
                 preferred_element_type=jnp.float32,
             )
 
         def mix_tile(j, sums):
-            here = slice(j * LANES, (j + 1) * LANES)
             slot = j % 2
+            used = min(LANES, lanes - j * LANES)
+            near = slice(j * LANES, j * LANES + used)
+            here = slice(base + j * LANES, base + j * LANES + used)
             gain = gain_ref[:, here] * math.sqrt(HEAD_DIM)
 
-            def mixed(source, residual):
-                normed = numer[source, here] * lax.rsqrt(sums[source] + HEAD_DIM * 1e-06)
-                return residual.astype(jnp.float32) + normed * gain
+            def mixed(source):
+                normed = numer[source, near] * lax.rsqrt(sums[source, :used] + HEAD_DIM * 1e-06)
+                return inputs_ref[source, here].astype(jnp.float32) + normed * gain
 
             outside = [None, None]
             for e in range(edges):
-                source = slice(tokens + e * width, tokens + (e + 1) * width)
-                value = mixed(source, edge_ref[1, e, :, here])
+                value = mixed(slice(tokens + e * width, tokens + (e + 1) * width))
                 for k, row in enumerate((0, rows + 1)):
                     part = jnp.where(place_ref[e] == row, value, 0.0)
                     outside[k] = part if outside[k] is None else outside[k] + part
             for k, row in enumerate((0, rows + 1)):
-                store_windows(outside[k], row, slot)
+                store_windows(outside[k], row, slot, used)
             for row in range(rows):
-                source = slice(row * width, (row + 1) * width)
-                store_windows(mixed(source, residual_ref[source, here]), row + 1, slot)
+                store_windows(mixed(slice(row * width, (row + 1) * width)), row + 1, slot, used)
             for row in range(rows):
                 conv_v = half_g = None
                 for tap in range(9):
-                    window = windows[slot, tap % 3, row + tap // 3]
+                    window = windows[slot, tap % 3, row + tap // 3, :, :used]
                     value = vtaps_ref[tap : tap + 1, here] * window
                     gate = (0.5 * gtaps_ref[tap : tap + 1, here]) * window
                     conv_v = value if tap == 0 else conv_v + value
                     half_g = gate if tap == 0 else half_g + gate
-                result = windows[slot, 1, row + 1] + conv_v * (half_g + half_g * jnp.tanh(half_g))
-                out_ref[row * width : (row + 1) * width, here] = result.astype(jnp.bfloat16)
+                center = windows[slot, 1, row + 1, :, :used]
+                result = center + conv_v * (half_g + half_g * jnp.tanh(half_g))
+                held[row * width : (row + 1) * width, here] = result.astype(jnp.bfloat16)
 
         numerators(0)
-        for number, (tiles, _, _) in enumerate(groups):
-            if number + 1 < len(groups):
+        for number, (tiles, _, _) in enumerate(pairs):
+            if number + 1 < len(pairs):
                 numerators(number + 1)
             sums = head_sums(number)
             for side, j in enumerate(tiles):
                 mix_tile(j, sums[:, side * LANES : (side + 1) * LANES])
 
-    by_group(dim, body)
-
-
-def mix(place, spots, queries, residual, edge, gain, value_taps, gate_taps, pieces, rows, width):
-    tokens, dim = queries.shape
-    edges = edge.shape[1]
-    total = tokens + edges * width
-    pairs = spans(min(GROUP, dim))
-    depth = max(last - first for _, first, last in pairs) * LANES
-    block = pl.BlockSpec((tokens, GROUP), lambda g: (0, g))
-    taps = pl.BlockSpec((value_taps.shape[0], GROUP), lambda g: (0, g))
+    copies = []
+    for base, lanes in group_lanes(dim):
+        group(base, lanes)
+        here = slice(base, base + lanes)
+        copies.append(
+            pltpu.make_async_copy(held.at[:, here], out_ref.at[:, here], semaphores.at[len(copies)])
+        )
+        copies[-1].start()
+    for copy in copies:
+        copy.wait()
+
+
+def mix(place, spots, prepared, gain, value_taps, gate_taps, pieces, rows, width):
+    features, inputs, same = prepared
+    total, dim = inputs.shape
+    tokens = rows * width
+    whole = pl.BlockSpec(memory_space=pltpu.VMEM)
     return pl.pallas_call(
-        functools.partial(mix_kernel, dim, rows, width, edges),
+        functools.partial(mix_kernel, dim, rows, width, (total - tokens) // width),
         out_shape=jax.ShapeDtypeStruct((tokens, dim), jnp.bfloat16),
-        grid=(cdiv(dim, GROUP),),
-        in_specs=[
-            pl.BlockSpec(memory_space=pltpu.SMEM),
-            pl.BlockSpec(memory_space=pltpu.SMEM),
-            block,
-            block,
-            pl.BlockSpec((2, edges, width, GROUP), lambda g: (0, 0, 0, g)),
-            pl.BlockSpec((1, GROUP), lambda g: (0, g)),
-            taps,
-            taps,
-        ]
-        + [pl.BlockSpec(piece.shape, lambda g: (0, 0)) for piece in pieces],
-        out_specs=block,
+        in_specs=[pl.BlockSpec(memory_space=pltpu.SMEM)] * 2 + [whole] * (6 + len(pieces)),
+        out_specs=pl.BlockSpec(memory_space=pl.ANY),
         scratch_shapes=[
             pltpu.VMEM((sum(piece.shape[0] for piece in pieces), LANES), jnp.bfloat16),
-            pltpu.VMEM((total, GROUP), jnp.bfloat16),
-            pltpu.VMEM((len(pairs), depth, 2 * LANES), jnp.bfloat16),
-            pltpu.VMEM((len(pairs), depth, 2 * LANES), jnp.bfloat16),
+            pltpu.VMEM(same.shape, jnp.bfloat16),
             pltpu.VMEM((total, GROUP), jnp.float32),
             pltpu.VMEM((total, GROUP), jnp.bfloat16),
             pltpu.VMEM((2, 3, rows + 2, width, LANES), jnp.float32),
+            pltpu.VMEM((tokens, dim), jnp.bfloat16),
+            pltpu.SemaphoreType.DMA((len(group_lanes(dim)),)),
         ],
         compiler_params=pltpu.CompilerParams(vmem_limit_bytes=36 * 2**20),
         cost_estimate=pl.CostEstimate(
             flops=60 * tokens * dim, bytes_accessed=6 * tokens * dim, transcendentals=2 * tokens * dim
         ),
         name="mix",
-    )(place, spots, in_hbm(queries), in_hbm(residual), edge, gain, value_taps, gate_taps, *pieces)
+    )(place, spots, features, inputs, same, gain, value_taps, gate_taps, *pieces)
 
 
 def edge_rows(queries, residual):
@@ -357,7 +391,7 @@
     theirs_ref[...] = jnp.where(first, both, before + partner).astype(jnp.bfloat16)
 
 
-def running_states(keys, values, queries, residual, rows):
+def running_states(keys, values, queries, residual, rows, beside):
     devices, frames = lax.axis_size("space"), lax.axis_size("frame")
     core, frame = lax.axis_index("space"), lax.axis_index("frame")
     if devices != 2 or frames < 2 or frames & (frames - 1):
@@ -366,7 +400,8 @@
         every = lax.all_gather(state, "frame").astype(jnp.float32)
         reached = (jnp.arange(frames) <= frame)[:, None, None]
         total = jnp.sum(jnp.where(reached, every, 0.0), axis=0).astype(jnp.bfloat16)
-        return [total], jnp.zeros((1,), jnp.int32), edge_rows(queries, residual)
+        edge, place = edge_rows(queries, residual)
+        return [total], jnp.zeros((1,), jnp.int32), place, beside(edge)
     swap = [(0, 1), (1, 0)]
     spot = jnp.stack([lax.rem(frame, 2), frame]).astype(jnp.int32)
     kept, sent, edge = frame_states(
@@ -383,18 +418,27 @@
     earlier = []
     stride = 2
     while stride < frames:
+        if stride * 2 >= frames:
+            total, edge = lax.optimization_barrier((total, edge))
         got = lax.ppermute(total, "frame", [(f, f ^ stride) for f in range(frames)])
         earlier.append(got)
         stride *= 2
         if stride < frames:
             (total,) = small_kernel(sum_body, "stride_sum", [quarter], spot, total, got)
+    last = earlier.pop() if earlier else partner
+    prepared = beside(edge)
+    last, *prepared = lax.optimization_barrier((last, *prepared))
+    if earlier or frames > 2:
+        earlier.append(last)
+    else:
+        partner = last
     mine, theirs = small_kernel(
         pair_sums_body, "pair_sums", [quarter] * 2, spot, own, partner, *earlier
     )
     other = lax.ppermute(theirs, "frame", [(f, f ^ 1) for f in range(frames)])
     pieces = [mine, other, lax.ppermute(mine, "space", swap), lax.ppermute(other, "space", swap)]
     spots = [2 * c + p for c in (core, 1 - core) for p in (spot[0], 1 - spot[0])]
-    return pieces, jnp.stack(spots).astype(jnp.int32), (edge, place)
+    return pieces, jnp.stack(spots).astype(jnp.int32), place, prepared
 
 
 def on_device(queries, keys, values, residual, attn_gain, value_taps, gate_taps):
@@ -402,16 +446,16 @@
     tokens = frames * rows * width
     flat = lambda a: a.reshape(tokens, dim)
     state_rows = cdiv(cdiv(dim, LANES) * HEAD_DIM, 64) * 64
-    pieces, spots, (edge, place) = running_states(
+    pieces, spots, place, prepared = running_states(
         flat(keys),
         flat(values),
         queries.reshape(rows, width, dim),
         residual.reshape(rows, width, dim),
         state_rows,
+        lambda edge: prepare(flat(queries), flat(residual), edge),
     )
     out = mix(
-        place, spots, flat(queries), flat(residual), edge, attn_gain[None], value_taps, gate_taps,
-        pieces, rows, width,
+        place, spots, prepared, attn_gain[None], value_taps, gate_taps, pieces, rows, width
     )
     return out.reshape(frames, rows, width, dim)
 

time: 49.7 us -> 51.2 us (1.030)
  local copies, waits for them, and re-layouts: 0.02 us -> 5.42 us
  waiting for transfers between devices: 19.2 us -> 14.3 us
  Pallas kernels: 21 us -> 21.7 us
    unnamed x6 -> x14, local copies, waits for them, and re-layouts: 0.01 us -> 5.41 us
    ppermute x2, waiting for transfers between devices: 8.85 us -> 4.02 us  [running_states(): got = lax.ppermute(total, 'frame', [(f, f ^ stride) for f in range(frames)])]
    pallas_call x1 -> x2, Pallas kernels: 14.8 us -> 15.6 us  [the longest x1 13.3 us: mix(): pl.pallas_call(functools.partial(mix_kernel, dim, rows, width, (total - t...]
  transfers between devices with their start and end apart: 8 -> 8, of which waited for: 6 -> 6; matrix products, arithmetic and copies ran while one was open for 0% -> 0% of each run, Pallas kernels for 4% -> 7%
where the time goes in v9:
time: 51.2 us; the launch traced here: 51 us
  Pallas kernels  21.7 us (42%)
  waiting for transfers between devices  14.3 us (28%)
  starting transfers between devices  9.2 us (18%)
  local copies, waits for them, and re-layouts  5.42 us (11%)
    pallas_call x1, Pallas kernels, mix(): pl.pallas_call(functools.partial(mix_kernel, dim, rows, width, (total - t...  13.3 us
    unnamed x14, local copies, waits for them, and re-layouts  5.41 us
    ppermute x2, starting transfers between devices, running_states(): got = lax.ppermute(total, 'frame', [(f, f ^ stride) for f in range(frames)])  4.51 us
    ppermute x2, waiting for transfers between devices, running_states(): got = lax.ppermute(total, 'frame', [(f, f ^ stride) for f in range(frames)])  4.02 us
    ppermute x1, waiting for transfers between devices, running_states(): partner = lax.ppermute(sent, 'frame', [(f, f ^ 1) for f in range(frames)])  4.02 us
    ppermute x1, waiting for transfers between devices, running_states(): other = lax.ppermute(theirs, 'frame', [(f, f ^ 1) for f in range(frames)])  3.97 us
    pallas_call x1, Pallas kernels, frame_states(): pl.pallas_call(functools.partial(state_kernel, dim, bool(edged)), out_sha...  3.7 us
    ppermute x1, starting transfers between devices, running_states(): partner = lax.ppermute(sent, 'frame', [(f, f ^ 1) for f in range(frames)])  2.66 us
  transfers between devices with their start and end apart: 8, of which 6 were waited for; matrix products, arithmetic and copies ran while one was open for 0% of the time, Pallas kernels for 7%

profile of v9, /device:TPU:0, one launch (start us, length us, event | category | flops | bytes accessed | tf_op | source)
XLA Modules:
  0.0 51.0 jit_solution(10667325489436756115)
XLA Ops:
  0.0 3.7 %frame_states.1 = (bf16[1024,128]{1,0:T(8,128)(2,1)S(1)}, bf16[1024,128]{1,0:T(8,128)(2,1)S(1)}, bf16[2,1,80,2240]{3,2,1,0:T(8,128)(2,1)S(1)}) custom-call(s32[1]{0:T(128)} %bitcast.7.spot_ref, bf16[480,2240]{1,0:T(8,128)(2,1)} %bitcast.19, bf16[480,2240]{1,0:T(8,128)(2,1)} %bitcast.20, bf16[6,80,2240]{2,1,0:T(8,128)(2,1)} %bitcast.15, ...), custom_call_target="tpu_custom_call" | custom-call | flops 240844800 | bytes 4300800 | tf_op jit(solution)/shard_map/frame_states/pallas_call | solution.py:116
  3.7 0.5 %collective-permute-start = (bf16[1024,128]{1,0:T(8,128)(2,1)S(1)}, bf16[1024,128]{1,0:T(8,128)(2,1)S(1)}, u32[]{:S(2)}, u32[]{:S(2)}) collective-permute-start(bf16[1024,128]{1,0:T(8,128)(2,1)S(1)} %get-tuple-element.24), channel_id=1, source_target_pairs={{0,1},{1,0},{2,3},{3,2},{4,5},{5,4},{6,7},{7,6},{8,9},{9,8},{10,11... | collective-permute-start | bytes 786440 | tf_op jit(solution)/shard_map/ppermute | solution.py:410
  4.3 1.1 %collective-permute-done.got_ref = bf16[1024,128]{1,0:T(8,128)(2,1)S(1)} collective-permute-done((bf16[1024,128]{1,0:T(8,128)(2,1)S(1)}, bf16[1024,128]{1,0:T(8,128)(2,1)S(1)}, u32[]{:S(2)}, u32[]{:S(2)}) %collective-permute-start) | collective-permute-done | bytes 262176 | tf_op jit(solution)/shard_map/ppermute | solution.py:410
  5.4 0.6 %split_sum.1 = (bf16[512,128]{1,0:T(8,128)(2,1)S(1)}, bf16[512,128]{1,0:T(8,128)(2,1)S(1)}) custom-call(s32[2]{0:T(128)S(1)} %pad_add_fusion.1.spot_ref._, bf16[1024,128]{1,0:T(8,128)(2,1)S(1)} %get-tuple-element.23.kept_ref, bf16[1024,128]{1,0:T(8,128)(2,1)S(1)} %collective-permute-done.got_ref), custom_call_target="tpu_custom_call" | custom-call | tf_op jit(solution)/shard_map/split_sum/pallas_call | solution.py:351
  6.0 0.4 collective-permute-start.3
  6.4 2.7 %collective-permute-start.1 = (bf16[512,128]{1,0:T(8,128)(2,1)S(1)}, bf16[512,128]{1,0:T(8,128)(2,1)S(1)}, u32[]{:S(2)}, u32[]{:S(2)}) collective-permute-start(bf16[512,128]{1,0:T(8,128)(2,1)S(1)} %get-tuple-element.28), channel_id=1, source_target_pairs={{0,2},{2,0},{4,6},{6,4},{8,10},{10,8},{12,14},{14,12},{1,3},{3,1},... | collective-permute-start | bytes 393224 | tf_op jit(solution)/shard_map/ppermute | solution.py:416
  9.1 4.0 %collective-permute-done.1.refs_1_.partner_ref = bf16[512,128]{1,0:T(8,128)(2,1)S(1)} collective-permute-done((bf16[512,128]{1,0:T(8,128)(2,1)S(1)}, bf16[512,128]{1,0:T(8,128)(2,1)S(1)}, u32[]{:S(2)}, u32[]{:S(2)}) %collective-permute-start.1) | collective-permute-done | bytes 131104 | tf_op jit(solution)/shard_map/ppermute | solution.py:416
  13.1 0.6 %pair_sum.1.refs_0_ = bf16[512,128]{1,0:T(8,128)(2,1)S(1)} custom-call(s32[2]{0:T(128)S(1)} %pad_add_fusion.1.spot_ref._, bf16[512,128]{1,0:T(8,128)(2,1)S(1)} %get-tuple-element.25.refs_0_.own_ref, bf16[512,128]{1,0:T(8,128)(2,1)S(1)} %collective-permute-done.1.refs_1_.partner_ref), custom_call_target="tpu_custom_call" | custom-call | tf_op jit(solution)/shard_map/pair_sum/pallas_call | solution.py:351
  13.7 1.9 %collective-permute-start.2 = (bf16[512,128]{1,0:T(8,128)(2,1)S(1)}, bf16[512,128]{1,0:T(8,128)(2,1)S(1)}, u32[]{:S(2)}, u32[]{:S(2)}) collective-permute-start(bf16[512,128]{1,0:T(8,128)(2,1)S(1)} %pair_sum.1.refs_0_), channel_id=1, source_target_pairs={{0,4},{2,6},{4,0},{6,2},{8,12},{10,14},{12,8},{14,10},{1,5},{3,7},... | collective-permute-start | bytes 393224 | tf_op jit(solution)/shard_map/ppermute | solution.py:423
  15.6 3.4 %collective-permute-done.2.refs_1_.refs_0_ = bf16[512,128]{1,0:T(8,128)(2,1)S(1)} collective-permute-done((bf16[512,128]{1,0:T(8,128)(2,1)S(1)}, bf16[512,128]{1,0:T(8,128)(2,1)S(1)}, u32[]{:S(2)}, u32[]{:S(2)}) %collective-permute-start.2) | collective-permute-done | bytes 131104 | tf_op jit(solution)/shard_map/ppermute | solution.py:423
  19.0 0.6 %stride_sum.1 = bf16[512,128]{1,0:T(8,128)(2,1)S(1)} custom-call(s32[2]{0:T(128)S(1)} %pad_add_fusion.1.spot_ref._, bf16[512,128]{1,0:T(8,128)(2,1)S(1)} %pair_sum.1.refs_0_, bf16[512,128]{1,0:T(8,128)(2,1)S(1)} %collective-permute-done.2.refs_1_.refs_0_), custom_call_target="tpu_custom_call" | custom-call | tf_op jit(solution)/shard_map/stride_sum/pallas_call | solution.py:351
  19.6 2.6 %collective-permute-start.4 = (bf16[512,128]{1,0:T(8,128)(2,1)S(1)}, bf16[512,128]{1,0:T(8,128)(2,1)S(1)}, u32[]{:S(2)}, u32[]{:S(2)}) collective-permute-start(bf16[512,128]{1,0:T(8,128)(2,1)S(1)} %stride_sum.1), channel_id=1, source_target_pairs={{0,8},{2,10},{4,12},{6,14},{8,0},{10,2},{12,4},{14,6},{1,9},{3,11}... | collective-permute-start | bytes 393224 | tf_op jit(solution)/shard_map/ppermute | solution.py:423
  22.2 2.4 %prepare.1 = (bf16[560,2304]{1,0:T(8,128)(2,1)S(1)}, bf16[560,2240]{1,0:T(8,128)(2,1)S(1)}, bf16[4,512,256]{2,1,0:T(8,128)(2,1)S(1)}) custom-call(bf16[480,2240]{1,0:T(8,128)(2,1)} %bitcast.16, bf16[480,2240]{1,0:T(8,128)(2,1)} %bitcast.18, bf16[2,1,80,2240]{3,2,1,0:T(8,128)(2,1)S(1)} %collective-permute-done.3.edge_ref), custom_call_target="tpu_custom_call" | custom-call | flops 5017600 | bytes 10035200 | tf_op jit(solution)/shard_map/prepare/pallas_call | solution.py:182
  24.6 1.5 %copy-done = bf16[560,2240]{1,0:T(8,128)(2,1)} copy-done((bf16[560,2240]{1,0:T(8,128)(2,1)}, bf16[560,2240]{1,0:T(8,128)(2,1)S(1)}, u32[]{:S(2)}) %copy-start) | copy-done | bytes 2508824
  26.1 1.0 %copy-done.2 = bf16[4,512,256]{2,1,0:T(8,128)(2,1)} copy-done((bf16[4,512,256]{2,1,0:T(8,128)(2,1)}, bf16[4,512,256]{2,1,0:T(8,128)(2,1)S(1)}, u32[]{:S(2)}) %copy-start.2) | copy-done | bytes 1048600
  27.0 0.6 %collective-permute-done.4.refs_1_ = bf16[512,128]{1,0:T(8,128)(2,1)S(1)} collective-permute-done((bf16[512,128]{1,0:T(8,128)(2,1)S(1)}, bf16[512,128]{1,0:T(8,128)(2,1)S(1)}, u32[]{:S(2)}, u32[]{:S(2)}) %collective-permute-start.4) | collective-permute-done | bytes 131104 | tf_op jit(solution)/shard_map/ppermute | solution.py:423
  27.7 0.7 %pair_sums.1 = (bf16[512,128]{1,0:T(8,128)(2,1)S(1)}, bf16[512,128]{1,0:T(8,128)(2,1)S(1)}) custom-call(s32[2]{0:T(128)S(1)} %pad_add_fusion.1.spot_ref._, bf16[512,128]{1,0:T(8,128)(2,1)S(1)} %get-tuple-element.25.refs_0_.own_ref, bf16[512,128]{1,0:T(8,128)(2,1)S(1)} %collective-permute-done.1.refs_1_.partner_ref, ...), custom_call_target="tpu_custom_call" | custom-call | tf_op jit(solution)/shard_map/pair_sums/pallas_call | solution.py:351
  28.3 1.1 %collective-permute-start.5 = (bf16[512,128]{1,0:T(8,128)(2,1)S(1)}, bf16[512,128]{1,0:T(8,128)(2,1)S(1)}, u32[]{:S(2)}, u32[]{:S(2)}) collective-permute-start(bf16[512,128]{1,0:T(8,128)(2,1)S(1)} %get-tuple-element.40), channel_id=1, source_target_pairs={{0,2},{2,0},{4,6},{6,4},{8,10},{10,8},{12,14},{14,12},{1,3},{3,1},... | collective-permute-start | bytes 393224 | tf_op jit(solution)/shard_map/ppermute | solution.py:438
  29.4 4.0 %collective-permute-done.5.refs_1_ = bf16[512,128]{1,0:T(8,128)(2,1)S(1)} collective-permute-done((bf16[512,128]{1,0:T(8,128)(2,1)S(1)}, bf16[512,128]{1,0:T(8,128)(2,1)S(1)}, u32[]{:S(2)}, u32[]{:S(2)}) %collective-permute-start.5) | collective-permute-done | bytes 131104 | tf_op jit(solution)/shard_map/ppermute | solution.py:438
  33.4 0.1 pad_add_fusion.spots_ref
  33.5 1.2 %collective-permute-done.7.refs_3_ = bf16[512,128]{1,0:T(8,128)(2,1)S(1)} collective-permute-done((bf16[512,128]{1,0:T(8,128)(2,1)S(1)}, bf16[512,128]{1,0:T(8,128)(2,1)S(1)}, u32[]{:S(2)}, u32[]{:S(2)}) %collective-permute-start.7) | collective-permute-done | bytes 131104 | tf_op jit(solution)/shard_map/ppermute | solution.py:439
  34.7 1.7 %copy-done.1 = bf16[560,2240]{1,0:T(8,128)(2,1)S(1)} copy-done((bf16[560,2240]{1,0:T(8,128)(2,1)S(1)}, bf16[560,2240]{1,0:T(8,128)(2,1)}, u32[]{:S(2)}) %copy-start.1) | copy-done | bytes 2508824
  36.5 1.2 %copy-done.3 = bf16[4,512,256]{2,1,0:T(8,128)(2,1)S(1)} copy-done((bf16[4,512,256]{2,1,0:T(8,128)(2,1)S(1)}, bf16[4,512,256]{2,1,0:T(8,128)(2,1)}, u32[]{:S(2)}) %copy-start.3) | copy-done | bytes 1048600
  37.7 13.3 %mix.1 = bf16[480,2240]{1,0:T(8,128)(2,1)} custom-call(s32[1]{0:T(128)} %bitcast.place_ref, s32[4]{0:T(128)S(1)} %pad_add_fusion.spots_ref, bf16[560,2304]{1,0:T(8,128)(2,1)S(1)} %get-tuple-element.35.features_ref, bf16[560,2240]{1,0:T(8,128)(2,1)S(1)} %copy-done.1, bf16[4,512,256]{2,1,0:T(8,128)(2,1)S(1)} %copy-done.3, ...), custom_call_target="tpu_custom_call" | custom-call | flops 64512000 | bytes 6451200 | tf_op jit(solution)/shard_map/mix/pallas_call | solution.py:318
  (16 shorter events, 0.1 us)
Async XLA Ops:
  3.7 1.7 %collective-permute-start = (bf16[1024,128]{1,0:T(8,128)(2,1)S(1)}, bf16[1024,128]{1,0:T(8,128)(2,1)S(1)}, u32[]{:S(2)}, u32[]{:S(2)}) collective-permute-start(bf16[1024,128]{1,0:T(8,128)(2,1)S(1)} %get-tuple-element.24), channel_id=1, source_target_pairs={{0,1},{1,0},{2,3},{3,2},{4,5},{5,4},{6,7},{7,6},{8,9},{9,8},{10,11... | collective-permute-start | bytes 786440 | tf_op jit(solution)/shard_map/ppermute | solution.py:410
  6.0 13.5 %collective-permute-start.3 = (bf16[2,1,80,2240]{3,2,1,0:T(8,128)(2,1)S(1)}, bf16[2,1,80,2240]{3,2,1,0:T(8,128)(2,1)S(1)}, u32[]{:S(2)}, u32[]{:S(2)}) collective-permute-start(bf16[2,1,80,2240]{3,2,1,0:T(8,128)(2,1)S(1)} %get-tuple-element.29), channel_id=1, source_target_pairs={{0,1},{1,0},{2,3},{3,2},{4,5},{5,4},{6,7},{7,6},{8,9},{9,8},{10,11... | collective-permute-start | bytes 2150408 | tf_op jit(solution)/shard_map/ppermute | solution.py:414
  6.4 6.7 %collective-permute-start.1 = (bf16[512,128]{1,0:T(8,128)(2,1)S(1)}, bf16[512,128]{1,0:T(8,128)(2,1)S(1)}, u32[]{:S(2)}, u32[]{:S(2)}) collective-permute-start(bf16[512,128]{1,0:T(8,128)(2,1)S(1)} %get-tuple-element.28), channel_id=1, source_target_pairs={{0,2},{2,0},{4,6},{6,4},{8,10},{10,8},{12,14},{14,12},{1,3},{3,1},... | collective-permute-start | bytes 393224 | tf_op jit(solution)/shard_map/ppermute | solution.py:416
  13.7 5.3 %collective-permute-start.2 = (bf16[512,128]{1,0:T(8,128)(2,1)S(1)}, bf16[512,128]{1,0:T(8,128)(2,1)S(1)}, u32[]{:S(2)}, u32[]{:S(2)}) collective-permute-start(bf16[512,128]{1,0:T(8,128)(2,1)S(1)} %pair_sum.1.refs_0_), channel_id=1, source_target_pairs={{0,4},{2,6},{4,0},{6,2},{8,12},{10,14},{12,8},{14,10},{1,5},{3,7},... | collective-permute-start | bytes 393224 | tf_op jit(solution)/shard_map/ppermute | solution.py:423
  19.6 8.1 %collective-permute-start.4 = (bf16[512,128]{1,0:T(8,128)(2,1)S(1)}, bf16[512,128]{1,0:T(8,128)(2,1)S(1)}, u32[]{:S(2)}, u32[]{:S(2)}) collective-permute-start(bf16[512,128]{1,0:T(8,128)(2,1)S(1)} %stride_sum.1), channel_id=1, source_target_pairs={{0,8},{2,10},{4,12},{6,14},{8,0},{10,2},{12,4},{14,6},{1,9},{3,11}... | collective-permute-start | bytes 393224 | tf_op jit(solution)/shard_map/ppermute | solution.py:423
  22.2 11.2 %copy-start.6 = (f32[2240]{0:T(1024)S(1)}, f32[2240]{0:T(1024)}, u32[]{:S(2)}) copy-start(f32[2240]{0:T(1024)} %param.11) | copy-start | bytes 26884
  22.2 12.5 %copy-start.4 = (f32[9,2240]{1,0:T(8,128)S(1)}, f32[9,2240]{1,0:T(8,128)}, u32[]{:S(2)}) copy-start(f32[9,2240]{1,0:T(8,128)} %vtaps_ref.1) | copy-start | bytes 241924
  22.2 12.5 %copy-start.5 = (f32[9,2240]{1,0:T(8,128)S(1)}, f32[9,2240]{1,0:T(8,128)}, u32[]{:S(2)}) copy-start(f32[9,2240]{1,0:T(8,128)} %gtaps_ref.1) | copy-start | bytes 241924
  24.6 1.5 %copy-start = (bf16[560,2240]{1,0:T(8,128)(2,1)}, bf16[560,2240]{1,0:T(8,128)(2,1)S(1)}, u32[]{:S(2)}) copy-start(bf16[560,2240]{1,0:T(8,128)(2,1)S(1)} %get-tuple-element.36.inputs_ref) | copy-start | bytes 7526404
  26.1 1.0 %copy-start.2 = (bf16[4,512,256]{2,1,0:T(8,128)(2,1)}, bf16[4,512,256]{2,1,0:T(8,128)(2,1)S(1)}, u32[]{:S(2)}) copy-start(bf16[4,512,256]{2,1,0:T(8,128)(2,1)S(1)} %get-tuple-element.37.same_ref) | copy-start | bytes 3145732
  28.3 5.0 %collective-permute-start.5 = (bf16[512,128]{1,0:T(8,128)(2,1)S(1)}, bf16[512,128]{1,0:T(8,128)(2,1)S(1)}, u32[]{:S(2)}, u32[]{:S(2)}) collective-permute-start(bf16[512,128]{1,0:T(8,128)(2,1)S(1)} %get-tuple-element.40), channel_id=1, source_target_pairs={{0,2},{2,0},{4,6},{6,4},{8,10},{10,8},{12,14},{14,12},{1,3},{3,1},... | collective-permute-start | bytes 393224 | tf_op jit(solution)/shard_map/ppermute | solution.py:438
  29.4 4.1 %collective-permute-start.6 = (bf16[512,128]{1,0:T(8,128)(2,1)S(1)}, bf16[512,128]{1,0:T(8,128)(2,1)S(1)}, u32[]{:S(2)}, u32[]{:S(2)}) collective-permute-start(bf16[512,128]{1,0:T(8,128)(2,1)S(1)} %get-tuple-element.39.refs_0_), channel_id=1, source_target_pairs={{0,1},{1,0},{2,3},{3,2},{4,5},{5,4},{6,7},{7,6},{8,9},{9,8},{10,11... | collective-permute-start | bytes 393224 | tf_op jit(solution)/shard_map/ppermute | solution.py:439
  33.4 1.3 %collective-permute-start.7 = (bf16[512,128]{1,0:T(8,128)(2,1)S(1)}, bf16[512,128]{1,0:T(8,128)(2,1)S(1)}, u32[]{:S(2)}, u32[]{:S(2)}) collective-permute-start(bf16[512,128]{1,0:T(8,128)(2,1)S(1)} %collective-permute-done.5.refs_1_), channel_id=1, source_target_pairs={{0,1},{1,0},{2,3},{3,2},{4,5},{5,4},{6,7},{7,6},{8,9},{9,8},{10,11... | collective-permute-start | bytes 393224 | tf_op jit(solution)/shard_map/ppermute | solution.py:439
  34.7 1.7 %copy-start.1 = (bf16[560,2240]{1,0:T(8,128)(2,1)S(1)}, bf16[560,2240]{1,0:T(8,128)(2,1)}, u32[]{:S(2)}) copy-start(bf16[560,2240]{1,0:T(8,128)(2,1)} %copy-done) | copy-start | bytes 7526404
  36.5 1.2 %copy-start.3 = (bf16[4,512,256]{2,1,0:T(8,128)(2,1)S(1)}, bf16[4,512,256]{2,1,0:T(8,128)(2,1)}, u32[]{:S(2)}) copy-start(bf16[4,512,256]{2,1,0:T(8,128)(2,1)} %copy-done.2) | copy-start | bytes 3145732

commit v10 on v9

--- a/solution.py
+++ b/solution.py
@@ -51,7 +51,7 @@
         pl.when(pl.program_id(0) >= full)(lambda: body(rest))
 
 
-def state_kernel(dim, with_edge, spot_ref, keys_ref, values_ref, *refs):
+def state_kernel(dim, with_edge, keys_ref, values_ref, *refs):
     step = pl.program_id(0)
     *refs, turned, whole, semaphores = refs
     if with_edge:
@@ -102,14 +102,14 @@
             whole[used:, :] = jnp.zeros((whole.shape[0] - used, LANES), jnp.bfloat16)
         for k, part in enumerate(parts):
             size = part.shape[0]
-            row = pl.multiple_of(lax.rem(spot_ref[0] + k, len(parts)) * size, 16)
-            part[...] = whole[pl.ds(row, size), :]
+            turn = lax.rem(lax.axis_index("space") + k, 2) if len(parts) == 2 else 0
+            part[...] = whole[pl.ds(pl.multiple_of(turn * size, 16), size), :]
         if with_edge:
             for copy in copies:
                 copy.wait()
 
 
-def frame_states(spot, keys, values, rows, parts, edged=()):
+def frame_states(keys, values, rows, parts, edged=()):
     tokens, dim = keys.shape
     part = (rows // parts, LANES)
     block = pl.BlockSpec((tokens, GROUP), lambda g: (0, g))
@@ -118,8 +118,7 @@
         out_shape=[pltpu.VMEM(part, jnp.bfloat16)] * parts
         + [pltpu.VMEM((len(edged), 1, *edged[0].shape[1:]), jnp.bfloat16) for _ in edged[:1]],
         grid=(cdiv(dim, GROUP),),
-        in_specs=[pl.BlockSpec(memory_space=pltpu.SMEM), block, block]
-        + [pl.BlockSpec(memory_space=pl.ANY)] * len(edged),
+        in_specs=[block, block] + [pl.BlockSpec(memory_space=pl.ANY)] * len(edged),
         out_specs=[pl.BlockSpec(part, lambda g: (0, 0))] * parts
         + [pl.BlockSpec(memory_space=pl.ANY) for _ in edged[:1]],
         scratch_shapes=[
@@ -132,15 +131,17 @@
             flops=2 * tokens * dim * HEAD_DIM, bytes_accessed=4 * tokens * dim, transcendentals=0
         ),
         name="frame_states",
-    )(spot, in_hbm(keys), in_hbm(values), *[in_hbm(array) for array in edged])
+    )(in_hbm(keys), in_hbm(values), *[in_hbm(array) for array in edged])
 
 
 def group_lanes(dim):
     return [(first, min(GROUP, dim - first)) for first in range(0, dim, GROUP)]
 
 
-def prepare_kernel(dim, queries_ref, residual_ref, edge_ref, features_ref, inputs_ref, same_ref, *refs):
-    held, semaphores = refs
+def prepare_kernel(
+    dim, queries_ref, residual_ref, edge_ref, gain_ref,
+    features_ref, inputs_ref, scaled_ref, held, semaphores,
+):
     tokens = queries_ref.shape[0]
     full = dim // LANES * LANES
     parts = [slice(0, full), slice(full, dim)] if full < dim else [slice(0, dim)]
@@ -155,16 +156,7 @@
         here = slice(tokens + e * width, tokens + (e + 1) * width)
         held[here] = edge_ref[0, e]
         inputs_ref[here] = edge_ref[1, e]
-    same_ref[...] = jnp.zeros_like(same_ref)
-    lane = lane_iota((HEAD_DIM, LANES))
-    for number, (tiles, first, _) in enumerate(spans(min(GROUP, dim))):
-        for side, j in enumerate(tiles):
-            for h, lo, hi in tile_heads(j, GROUP):
-                start = h * HEAD_DIM - first * LANES
-                block = jnp.where((lane >= lo) & (lane < hi), 1.0, 0.0)
-                same_ref[
-                    number, start : start + HEAD_DIM, side * LANES : (side + 1) * LANES
-                ] = block.astype(jnp.bfloat16)
+    scaled_ref[...] = gain_ref[...] * math.sqrt(HEAD_DIM)
     if full < dim:
         features_ref[:, full:] = jnp.zeros((features_ref.shape[0], LANES), jnp.bfloat16)
     copies[0].wait()
@@ -173,20 +165,18 @@
     copies[1].wait()
 
 
-def prepare(queries, residual, edge):
+def prepare(queries, residual, edge, gain):
     tokens, dim = queries.shape
     total = tokens + edge.shape[1] * edge.shape[2]
-    pairs = spans(min(GROUP, dim))
-    depth = max(last - first for _, first, last in pairs) * LANES
     whole = pl.BlockSpec(memory_space=pltpu.VMEM)
     return pl.pallas_call(
         functools.partial(prepare_kernel, dim),
         out_shape=[
             pltpu.VMEM((total, cdiv(dim, LANES) * LANES), jnp.bfloat16),
             pltpu.VMEM((total, dim), jnp.bfloat16),
-            pltpu.VMEM((len(pairs), depth, 2 * LANES), jnp.bfloat16),
+            pltpu.VMEM((1, dim), jnp.float32),
         ],
-        in_specs=[pl.BlockSpec(memory_space=pl.ANY)] * 2 + [whole],
+        in_specs=[pl.BlockSpec(memory_space=pl.ANY)] * 2 + [whole] * 2,
         out_specs=[whole] * 3,
         scratch_shapes=[
             pltpu.VMEM((total, dim), jnp.bfloat16),
@@ -197,19 +187,21 @@
             flops=4 * total * dim, bytes_accessed=8 * total * dim, transcendentals=0
         ),
         name="prepare",
-    )(in_hbm(queries), in_hbm(residual), edge)
+    )(in_hbm(queries), in_hbm(residual), edge, gain)
 
 
 def mix_kernel(
     dim, rows, width, edges,
-    place_ref, spots_ref, features_ref, inputs_ref, same_ref, gain_ref, vtaps_ref, gtaps_ref, *refs,
+    features_ref, inputs_ref, gain_ref, vtaps_ref, gtaps_ref, *refs,
 ):
-    *pieces, out_ref, states, weights, numer, squares, windows, held, semaphores = refs
+    *pieces, out_ref, states, weights, numer, windows, held, semaphores = refs
+    places = edge_places(lax.axis_size("space"), rows) if edges else []
+    spots = piece_places() if len(pieces) > 1 else [0]
     tokens = rows * width
     weights[...] = jnp.zeros_like(weights)
     for k, piece in enumerate(pieces):
         size = piece.shape[0]
-        states[pl.ds(pl.multiple_of(spots_ref[k] * size, 16), size), :] = piece[...]
+        states[pl.ds(pl.multiple_of(spots[k] * size, 16), size), :] = piece[...]
     lane = lane_iota((HEAD_DIM, LANES))
     sublane = lax.broadcasted_iota(jnp.int32, (8, LANES), 0)
 
@@ -246,33 +238,44 @@
             )
             here = slice(tiles[0] * LANES, tiles[0] * LANES + wide)
             numer[:, here] = product
-            squares[:, here] = (product * product).astype(jnp.bfloat16)
-
-        def head_sums(number):
-            tiles, first, last = pairs[number]
-            depth, wide = (last - first) * LANES, len(tiles) * LANES
-            return jnp.dot(
-                squares[:, first * LANES : last * LANES],
-                same_ref[number, :depth, :wide],
-                preferred_element_type=jnp.float32,
-            )
-
-        def mix_tile(j, sums):
+
+        def tile_sums(j, source):
+            square = numer[source, j * LANES : (j + 1) * LANES]
+            square = square * square
+            heads = tile_heads(j, lanes)
+            if len(heads) == 1:
+                return {heads[0][0]: jnp.sum(square, axis=-1, keepdims=True)}
+            (one, _, bound), (two, _, _) = heads
+            part = jnp.where(lane_iota(square.shape) < bound, square, 0.0)
+            rest = square - part
+            return {
+                one: jnp.sum(part, axis=-1, keepdims=True),
+                two: jnp.sum(rest, axis=-1, keepdims=True),
+            }
+
+        def mix_tile(j):
             slot = j % 2
             used = min(LANES, lanes - j * LANES)
             near = slice(j * LANES, j * LANES + used)
             here = slice(base + j * LANES, base + j * LANES + used)
-            gain = gain_ref[:, here] * math.sqrt(HEAD_DIM)
+            heads = tile_heads(j, lanes)
 
             def mixed(source):
-                normed = numer[source, near] * lax.rsqrt(sums[source, :used] + HEAD_DIM * 1e-06)
-                return inputs_ref[source, here].astype(jnp.float32) + normed * gain
+                sums = [
+                    sum(tiles[head] for tiles in parts[source.start] if head in tiles)
+                    for head, _, _ in heads
+                ]
+                scale = jnp.broadcast_to(sums[0], (width, used))
+                if len(heads) > 1:
+                    scale = jnp.where(lane_iota(scale.shape) < heads[0][2], scale, sums[1])
+                normed = numer[source, near] * lax.rsqrt(scale + HEAD_DIM * 1e-06)
+                return inputs_ref[source, here].astype(jnp.float32) + normed * gain_ref[:, here]
 
             outside = [None, None]
             for e in range(edges):
                 value = mixed(slice(tokens + e * width, tokens + (e + 1) * width))
                 for k, row in enumerate((0, rows + 1)):
-                    part = jnp.where(place_ref[e] == row, value, 0.0)
+                    part = jnp.where(places[e] == row, value, 0.0)
                     outside[k] = part if outside[k] is None else outside[k] + part
             for k, row in enumerate((0, rows + 1)):
                 store_windows(outside[k], row, slot, used)
@@ -290,13 +293,15 @@
                 result = center + conv_v * (half_g + half_g * jnp.tanh(half_g))
                 held[row * width : (row + 1) * width, here] = result.astype(jnp.bfloat16)
 
-        numerators(0)
+        parts = {}
         for number, (tiles, _, _) in enumerate(pairs):
-            if number + 1 < len(pairs):
-                numerators(number + 1)
-            sums = head_sums(number)
-            for side, j in enumerate(tiles):
-                mix_tile(j, sums[:, side * LANES : (side + 1) * LANES])
+            numerators(number)
+            for j in tiles:
+                for row in range(rows + edges):
+                    source = slice(row * width, (row + 1) * width)
+                    parts.setdefault(source.start, []).append(tile_sums(j, source))
+        for j in range(cdiv(lanes, LANES)):
+            mix_tile(j)
 
     copies = []
     for base, lanes in group_lanes(dim):
@@ -310,21 +315,22 @@
         copy.wait()
 
 
-def mix(place, spots, prepared, gain, value_taps, gate_taps, pieces, rows, width):
-    features, inputs, same = prepared
+def mix(prepared, value_taps, gate_taps, pieces, rows, width):
+    features, inputs, gain = prepared
     total, dim = inputs.shape
     tokens = rows * width
+    pairs = spans(min(GROUP, dim))
+    depth = max(last - first for _, first, last in pairs) * LANES
     whole = pl.BlockSpec(memory_space=pltpu.VMEM)
     return pl.pallas_call(
         functools.partial(mix_kernel, dim, rows, width, (total - tokens) // width),
         out_shape=jax.ShapeDtypeStruct((tokens, dim), jnp.bfloat16),
-        in_specs=[pl.BlockSpec(memory_space=pltpu.SMEM)] * 2 + [whole] * (6 + len(pieces)),
+        in_specs=[whole] * (5 + len(pieces)),
         out_specs=pl.BlockSpec(memory_space=pl.ANY),
         scratch_shapes=[
             pltpu.VMEM((sum(piece.shape[0] for piece in pieces), LANES), jnp.bfloat16),
-            pltpu.VMEM(same.shape, jnp.bfloat16),
+            pltpu.VMEM((len(pairs), depth, 2 * LANES), jnp.bfloat16),
             pltpu.VMEM((total, GROUP), jnp.float32),
-            pltpu.VMEM((total, GROUP), jnp.bfloat16),
             pltpu.VMEM((2, 3, rows + 2, width, LANES), jnp.float32),
             pltpu.VMEM((tokens, dim), jnp.bfloat16),
             pltpu.SemaphoreType.DMA((len(group_lanes(dim)),)),
@@ -334,7 +340,7 @@
             flops=60 * tokens * dim, bytes_accessed=6 * tokens * dim, transcendentals=2 * tokens * dim
         ),
         name="mix",
-    )(place, spots, features, inputs, same, gain, value_taps, gate_taps, *pieces)
+    )(features, inputs, gain, value_taps, gate_taps, *pieces)
 
 
 def edge_rows(queries, residual):
@@ -342,21 +348,23 @@
     up = [(i, i + 1) for i in range(devices - 1)]
     down = [(j, i) for i, j in up]
     both = jnp.stack([queries, residual])
+    if devices == 2:
+        first = lax.axis_index("space") == 0
+        return lax.ppermute(jnp.where(first, both[:, rows - 1 :], both[:, :1]), "space", up + down)
     before = lax.ppermute(both[:, rows - 1 :], "space", up)
     after = lax.ppermute(both[:, :1], "space", down)
-    return jnp.concatenate([before, after], axis=1), jnp.array([0, rows + 1], jnp.int32)
-
-
-def small_kernel(body, name, outs, scalars, *arrays):
+    return jnp.concatenate([before, after], axis=1)
+
+
+def small_kernel(body, name, outs, *arrays):
     return pl.pallas_call(
         body,
         out_shape=[pltpu.VMEM(shape, jnp.bfloat16) for shape in outs],
-        in_specs=[pl.BlockSpec(memory_space=pltpu.SMEM)]
-        + [pl.BlockSpec(memory_space=pltpu.VMEM)] * len(arrays),
+        in_specs=[pl.BlockSpec(memory_space=pltpu.VMEM)] * len(arrays),
         out_specs=[pl.BlockSpec(memory_space=pltpu.VMEM)] * len(outs),
         compiler_params=pltpu.CompilerParams(vmem_limit_bytes=4 * 2**20),
         name=name,
-    )(scalars, *arrays)
+    )(*arrays)
 
 
 def add(*values):
@@ -366,79 +374,88 @@
     return total
 
 
-def split_sum_body(spot_ref, kept_ref, got_ref, mine_ref, theirs_ref):
+def parity():
+    return lax.rem(lax.axis_index("frame"), 2)
+
+
+def split_sum_body(kept_ref, got_ref, mine_ref, theirs_ref):
     size = mine_ref.shape[0]
-    for ref, side in ((theirs_ref, 1 - spot_ref[0]), (mine_ref, spot_ref[0])):
+    for ref, side in ((theirs_ref, 1 - parity()), (mine_ref, parity())):
         rows = pl.ds(pl.multiple_of(side * size, 16), size)
         ref[...] = add(kept_ref[rows, :], got_ref[rows, :]).astype(jnp.bfloat16)
 
 
-def sum_body(_, *refs):
+def sum_body(*refs):
     *terms, out_ref = refs
     out_ref[...] = add(*[term[...] for term in terms]).astype(jnp.bfloat16)
 
 
-def pair_sums_body(spot_ref, own_ref, partner_ref, *refs):
+def pair_sums_body(own_ref, partner_ref, *refs):
     *earlier, mine_ref, theirs_ref = refs
     before = jnp.zeros(own_ref.shape, jnp.float32)
     for k, ref in enumerate(earlier):
-        from_before = lax.rem(spot_ref[1] // (2 << k), 2) == 1
+        from_before = lax.rem(lax.axis_index("frame") // (2 << k), 2) == 1
         before = before + jnp.where(from_before, add(ref[...]), 0.0)
     own, partner = add(own_ref[...]), add(partner_ref[...])
-    first = spot_ref[0] == 0
+    first = parity() == 0
     both = before + (own + partner)
     mine_ref[...] = jnp.where(first, before + own, both).astype(jnp.bfloat16)
     theirs_ref[...] = jnp.where(first, both, before + partner).astype(jnp.bfloat16)
 
 
+def paired(devices, frames):
+    return devices == 2 and frames >= 4 and frames & (frames - 1) == 0
+
+
+def piece_places():
+    core = lax.axis_index("space")
+    return [2 * c + p for c in (core, 1 - core) for p in (parity(), 1 - parity())]
+
+
+def edge_places(devices, rows):
+    if devices == 2:
+        return [jnp.where(lax.axis_index("space") == 0, rows + 1, 0)]
+    return [0, rows + 1]
+
+
 def running_states(keys, values, queries, residual, rows, beside):
     devices, frames = lax.axis_size("space"), lax.axis_size("frame")
-    core, frame = lax.axis_index("space"), lax.axis_index("frame")
-    if devices != 2 or frames < 2 or frames & (frames - 1):
-        (state,) = frame_states(jnp.zeros((1,), jnp.int32), keys, values, rows, 1)
+    if not paired(devices, frames):
+        (state,) = frame_states(keys, values, rows, 1)
         state = lax.psum(state.astype(jnp.float32), "space").astype(jnp.bfloat16)
         every = lax.all_gather(state, "frame").astype(jnp.float32)
-        reached = (jnp.arange(frames) <= frame)[:, None, None]
+        reached = (jnp.arange(frames) <= lax.axis_index("frame"))[:, None, None]
         total = jnp.sum(jnp.where(reached, every, 0.0), axis=0).astype(jnp.bfloat16)
-        edge, place = edge_rows(queries, residual)
-        return [total], jnp.zeros((1,), jnp.int32), place, beside(edge)
+        return [total], beside(edge_rows(queries, residual))
     swap = [(0, 1), (1, 0)]
-    spot = jnp.stack([lax.rem(frame, 2), frame]).astype(jnp.int32)
-    kept, sent, edge = frame_states(
-        core.astype(jnp.int32)[None], keys, values, rows, 2, (queries, residual)
+    exchange = lambda array, stride: lax.ppermute(
+        array, "frame", [(f, f ^ stride) for f in range(frames)]
     )
+    kept, sent, edge = frame_states(keys, values, rows, 2, (queries, residual))
     got = lax.ppermute(sent, "space", swap)
     quarter = (rows // 4, LANES)
-    own, sent = small_kernel(split_sum_body, "split_sum", [quarter] * 2, spot, kept, got)
+    own, sent = small_kernel(split_sum_body, "split_sum", [quarter] * 2, kept, got)
     edge, sent = lax.optimization_barrier((edge, sent))
     edge = lax.ppermute(edge, "space", swap)
-    place = jnp.where(core == 0, queries.shape[0] + 1, 0).astype(jnp.int32)[None]
-    partner = lax.ppermute(sent, "frame", [(f, f ^ 1) for f in range(frames)])
-    (total,) = small_kernel(sum_body, "pair_sum", [quarter], spot, own, partner)
+    partner = exchange(sent, 1)
+    (total,) = small_kernel(sum_body, "pair_sum", [quarter], own, partner)
     earlier = []
     stride = 2
     while stride < frames:
-        if stride * 2 >= frames:
+        if stride * 2 == frames:
             total, edge = lax.optimization_barrier((total, edge))
-        got = lax.ppermute(total, "frame", [(f, f ^ stride) for f in range(frames)])
-        earlier.append(got)
+        earlier.append(exchange(total, stride))
         stride *= 2
         if stride < frames:
-            (total,) = small_kernel(sum_body, "stride_sum", [quarter], spot, total, got)
-    last = earlier.pop() if earlier else partner
+            (total,) = small_kernel(sum_body, "stride_sum", [quarter], total, earlier[-1])
     prepared = beside(edge)
-    last, *prepared = lax.optimization_barrier((last, *prepared))
-    if earlier or frames > 2:
-        earlier.append(last)
-    else:
-        partner = last
+    earlier[-1], *prepared = lax.optimization_barrier((earlier[-1], *prepared))
     mine, theirs = small_kernel(
-        pair_sums_body, "pair_sums", [quarter] * 2, spot, own, partner, *earlier
+        pair_sums_body, "pair_sums", [quarter] * 2, own, partner, *earlier
     )
-    other = lax.ppermute(theirs, "frame", [(f, f ^ 1) for f in range(frames)])
+    other = exchange(theirs, 1)
     pieces = [mine, other, lax.ppermute(mine, "space", swap), lax.ppermute(other, "space", swap)]
-    spots = [2 * c + p for c in (core, 1 - core) for p in (spot[0], 1 - spot[0])]
-    return pieces, jnp.stack(spots).astype(jnp.int32), place, prepared
+    return pieces, prepared
 
 
 def on_device(queries, keys, values, residual, attn_gain, value_taps, gate_taps):
@@ -446,17 +463,15 @@
     tokens = frames * rows * width
     flat = lambda a: a.reshape(tokens, dim)
     state_rows = cdiv(cdiv(dim, LANES) * HEAD_DIM, 64) * 64
-    pieces, spots, place, prepared = running_states(
+    pieces, prepared = running_states(
         flat(keys),
         flat(values),
         queries.reshape(rows, width, dim),
         residual.reshape(rows, width, dim),
         state_rows,
-        lambda edge: prepare(flat(queries), flat(residual), edge),
+        lambda edge: prepare(flat(queries), flat(residual), edge, attn_gain[None]),
     )
-    out = mix(
-        place, spots, prepared, attn_gain[None], value_taps, gate_taps, pieces, rows, width
-    )
+    out = mix(prepared, value_taps, gate_taps, pieces, rows, width)
     return out.reshape(frames, rows, width, dim)
 
 

time: 51.2 us -> 45.6 us (0.89)
  local copies, waits for them, and re-layouts: 5.42 us -> 0.02 us
  waiting for transfers between devices: 14.3 us -> 16.9 us
  Pallas kernels: 21.7 us -> 19.2 us
    unnamed x14 -> x6, local copies, waits for them, and re-layouts: 5.41 us -> 0.02 us
    ppermute x4, waiting for transfers between devices: 12 us -> 14.4 us  [running_states(): lax.ppermute(array, 'frame', [(f, f ^ stride) for f in range(frames)])]
    pallas_call x4, Pallas kernels: 2.43 us -> 0.27 us  [small_kernel(): pl.pallas_call(body, out_shape=[pltpu.VMEM(shape, jnp.bfloat16) for shape...]
  transfers between devices with their start and end apart: 8 -> 8, of which waited for: 6 -> 6; matrix products, arithmetic and copies ran while one was open for 0% -> 0% of each run, Pallas kernels for 7% -> 5%
where the time goes in v10:
time: 45.6 us; the launch traced here: 45.4 us
  Pallas kernels  19.2 us (42%)
  waiting for transfers between devices  16.9 us (37%)
  starting transfers between devices  9.2 us (20%)
    ppermute x4, waiting for transfers between devices, running_states(): lax.ppermute(array, 'frame', [(f, f ^ stride) for f in range(frames)])  14.4 us
    pallas_call x1, Pallas kernels, mix(): pl.pallas_call(functools.partial(mix_kernel, dim, rows, width, (total - t...  12.8 us
    ppermute x4, starting transfers between devices, running_states(): lax.ppermute(array, 'frame', [(f, f ^ stride) for f in range(frames)])  8.24 us
    pallas_call x1, Pallas kernels, frame_states(): pl.pallas_call(functools.partial(state_kernel, dim, bool(edged)), out_sha...  3.72 us
    pallas_call x1, Pallas kernels, prepare(): pl.pallas_call(functools.partial(prepare_kernel, dim), out_shape=[pltpu.V...  2.35 us
    ppermute x1, waiting for transfers between devices, running_states(): lax.ppermute(other, 'space', swap)  1.34 us
    ppermute x1, waiting for transfers between devices, running_states(): got = lax.ppermute(sent, 'space', swap)  1.16 us
  transfers between devices with their start and end apart: 8, of which 6 were waited for; matrix products, arithmetic and copies ran while one was open for 0% of the time, Pallas kernels for 5%

profile of v10, /device:TPU:0, one launch (start us, length us, event | category | flops | bytes accessed | tf_op | source)
XLA Modules:
  0.0 45.4 jit_solution(13308688667739385387)
XLA Ops:
  0.0 3.7 %frame_states.1 = (bf16[1024,128]{1,0:T(8,128)(2,1)S(1)}, bf16[1024,128]{1,0:T(8,128)(2,1)S(1)}, bf16[2,1,80,2240]{3,2,1,0:T(8,128)(2,1)S(1)}) custom-call(bf16[480,2240]{1,0:T(8,128)(2,1)} %bitcast.11, bf16[480,2240]{1,0:T(8,128)(2,1)} %bitcast.12, bf16[6,80,2240]{2,1,0:T(8,128)(2,1)} %bitcast.7, bf16[6,80,2240]{2,1,0:T(8,128)(2,1)} %bitcast.9), custom_call_target="tpu_custom_call" | custom-call | flops 240844800 | bytes 4300800 | tf_op jit(solution)/shard_map/frame_states/pallas_call | solution.py:116
  3.7 0.5 %collective-permute-start = (bf16[1024,128]{1,0:T(8,128)(2,1)S(1)}, bf16[1024,128]{1,0:T(8,128)(2,1)S(1)}, u32[]{:S(2)}, u32[]{:S(2)}) collective-permute-start(bf16[1024,128]{1,0:T(8,128)(2,1)S(1)} %get-tuple-element.24), channel_id=1, source_target_pairs={{0,1},{1,0},{2,3},{3,2},{4,5},{5,4},{6,7},{7,6},{8,9},{9,8},{10,11... | collective-permute-start | bytes 786440 | tf_op jit(solution)/shard_map/ppermute | solution.py:435
  4.2 1.2 %collective-permute-done.got_ref = bf16[1024,128]{1,0:T(8,128)(2,1)S(1)} collective-permute-done((bf16[1024,128]{1,0:T(8,128)(2,1)S(1)}, bf16[1024,128]{1,0:T(8,128)(2,1)S(1)}, u32[]{:S(2)}, u32[]{:S(2)}) %collective-permute-start) | collective-permute-done | bytes 262176 | tf_op jit(solution)/shard_map/ppermute | solution.py:435
  5.4 0.1 split_sum.1
  5.5 0.4 collective-permute-start.3
  5.9 2.7 %collective-permute-start.1 = (bf16[512,128]{1,0:T(8,128)(2,1)S(1)}, bf16[512,128]{1,0:T(8,128)(2,1)S(1)}, u32[]{:S(2)}, u32[]{:S(2)}) collective-permute-start(bf16[512,128]{1,0:T(8,128)(2,1)S(1)} %get-tuple-element.28), channel_id=1, source_target_pairs={{0,2},{2,0},{4,6},{6,4},{8,10},{10,8},{12,14},{14,12},{1,3},{3,1},... | collective-permute-start | bytes 393224 | tf_op jit(solution)/shard_map/ppermute | solution.py:431
  8.6 4.0 %collective-permute-done.1.refs_1_.partner_ref = bf16[512,128]{1,0:T(8,128)(2,1)S(1)} collective-permute-done((bf16[512,128]{1,0:T(8,128)(2,1)S(1)}, bf16[512,128]{1,0:T(8,128)(2,1)S(1)}, u32[]{:S(2)}, u32[]{:S(2)}) %collective-permute-start.1) | collective-permute-done | bytes 131104 | tf_op jit(solution)/shard_map/ppermute | solution.py:431
  12.6 1.9 %collective-permute-start.2 = (bf16[512,128]{1,0:T(8,128)(2,1)S(1)}, bf16[512,128]{1,0:T(8,128)(2,1)S(1)}, u32[]{:S(2)}, u32[]{:S(2)}) collective-permute-start(bf16[512,128]{1,0:T(8,128)(2,1)S(1)} %pair_sum.1.refs_0_), channel_id=1, source_target_pairs={{0,4},{2,6},{4,0},{6,2},{8,12},{10,14},{12,8},{14,10},{1,5},{3,7},... | collective-permute-start | bytes 393224 | tf_op jit(solution)/shard_map/ppermute | solution.py:431
  14.5 3.4 %collective-permute-done.2.refs_1_.refs_0_ = bf16[512,128]{1,0:T(8,128)(2,1)S(1)} collective-permute-done((bf16[512,128]{1,0:T(8,128)(2,1)S(1)}, bf16[512,128]{1,0:T(8,128)(2,1)S(1)}, u32[]{:S(2)}, u32[]{:S(2)}) %collective-permute-start.2) | collective-permute-done | bytes 131104 | tf_op jit(solution)/shard_map/ppermute | solution.py:431
  17.9 0.0 collective-permute-done.3.edge_ref
  17.9 2.6 %collective-permute-start.4 = (bf16[512,128]{1,0:T(8,128)(2,1)S(1)}, bf16[512,128]{1,0:T(8,128)(2,1)S(1)}, u32[]{:S(2)}, u32[]{:S(2)}) collective-permute-start(bf16[512,128]{1,0:T(8,128)(2,1)S(1)} %stride_sum.1), channel_id=1, source_target_pairs={{0,8},{2,10},{4,12},{6,14},{8,0},{10,2},{12,4},{14,6},{1,9},{3,11}... | collective-permute-start | bytes 393224 | tf_op jit(solution)/shard_map/ppermute | solution.py:431
  20.6 0.0 copy-done.2
  20.6 0.0 copy-start
  20.6 0.0 copy-start.1
  20.6 2.4 %prepare.1 = (bf16[560,2304]{1,0:T(8,128)(2,1)S(1)}, bf16[560,2240]{1,0:T(8,128)(2,1)S(1)}, f32[1,2240]{1,0:T(1,128)S(1)}) custom-call(bf16[480,2240]{1,0:T(8,128)(2,1)} %bitcast.8, bf16[480,2240]{1,0:T(8,128)(2,1)} %bitcast.10, bf16[2,1,80,2240]{3,2,1,0:T(8,128)(2,1)S(1)} %collective-permute-done.3.edge_ref, f32[1,2240]{1,0:T(1,128)S(1)} %broadcast_in_dim.3.gain_ref), custom_call_target="tpu_custom_call" | custom-call | flops 5017600 | bytes 10035200 | tf_op jit(solution)/shard_map/prepare/pallas_call | solution.py:172
  23.0 3.1 %collective-permute-done.4.refs_1_ = bf16[512,128]{1,0:T(8,128)(2,1)S(1)} collective-permute-done((bf16[512,128]{1,0:T(8,128)(2,1)S(1)}, bf16[512,128]{1,0:T(8,128)(2,1)S(1)}, u32[]{:S(2)}, u32[]{:S(2)}) %collective-permute-start.4) | collective-permute-done | bytes 131104 | tf_op jit(solution)/shard_map/ppermute | solution.py:431
  26.0 0.1 pair_sums.1
  26.2 1.1 %collective-permute-start.5 = (bf16[512,128]{1,0:T(8,128)(2,1)S(1)}, bf16[512,128]{1,0:T(8,128)(2,1)S(1)}, u32[]{:S(2)}, u32[]{:S(2)}) collective-permute-start(bf16[512,128]{1,0:T(8,128)(2,1)S(1)} %get-tuple-element.40), channel_id=1, source_target_pairs={{0,2},{2,0},{4,6},{6,4},{8,10},{10,8},{12,14},{14,12},{1,3},{3,1},... | collective-permute-start | bytes 393224 | tf_op jit(solution)/shard_map/ppermute | solution.py:431
  27.3 0.0 collective-permute-start.6
  27.3 4.0 %collective-permute-done.5.refs_1_ = bf16[512,128]{1,0:T(8,128)(2,1)S(1)} collective-permute-done((bf16[512,128]{1,0:T(8,128)(2,1)S(1)}, bf16[512,128]{1,0:T(8,128)(2,1)S(1)}, u32[]{:S(2)}, u32[]{:S(2)}) %collective-permute-start.5) | collective-permute-done | bytes 131104 | tf_op jit(solution)/shard_map/ppermute | solution.py:431
  31.2 0.0 collective-permute-start.7
  31.2 0.0 collective-permute-done.6.refs_2_
  31.2 1.3 %collective-permute-done.7.refs_3_ = bf16[512,128]{1,0:T(8,128)(2,1)S(1)} collective-permute-done((bf16[512,128]{1,0:T(8,128)(2,1)S(1)}, bf16[512,128]{1,0:T(8,128)(2,1)S(1)}, u32[]{:S(2)}, u32[]{:S(2)}) %collective-permute-start.7) | collective-permute-done | bytes 131104 | tf_op jit(solution)/shard_map/ppermute | solution.py:457
  32.6 12.8 %mix.1 = bf16[480,2240]{1,0:T(8,128)(2,1)} custom-call(bf16[560,2304]{1,0:T(8,128)(2,1)S(1)} %get-tuple-element.35.features_ref, bf16[560,2240]{1,0:T(8,128)(2,1)S(1)} %get-tuple-element.36.inputs_ref, f32[1,2240]{1,0:T(1,128)S(1)} %get-tuple-element.37.gain_ref, f32[9,2240]{1,0:T(8,128)S(1)} %copy-done, f32[9,2240]{1,0:T(8,128)S(1)} %copy-done.1, ...), custom_call_target="tpu_custom_call" | custom-call | flops 64512000 | bytes 6451200 | tf_op jit(solution)/shard_map/mix/pallas_call | solution.py:325
  (6 shorter events, 0.1 us)
Async XLA Ops:
  0.0 20.6 %copy-start.2 = (f32[2240]{0:T(1024)S(1)}, f32[2240]{0:T(1024)}, u32[]{:S(2)}) copy-start(f32[2240]{0:T(1024)} %param.11) | copy-start | bytes 26884
  3.7 1.7 %collective-permute-start = (bf16[1024,128]{1,0:T(8,128)(2,1)S(1)}, bf16[1024,128]{1,0:T(8,128)(2,1)S(1)}, u32[]{:S(2)}, u32[]{:S(2)}) collective-permute-start(bf16[1024,128]{1,0:T(8,128)(2,1)S(1)} %get-tuple-element.24), channel_id=1, source_target_pairs={{0,1},{1,0},{2,3},{3,2},{4,5},{5,4},{6,7},{7,6},{8,9},{9,8},{10,11... | collective-permute-start | bytes 786440 | tf_op jit(solution)/shard_map/ppermute | solution.py:435
  5.5 12.5 %collective-permute-start.3 = (bf16[2,1,80,2240]{3,2,1,0:T(8,128)(2,1)S(1)}, bf16[2,1,80,2240]{3,2,1,0:T(8,128)(2,1)S(1)}, u32[]{:S(2)}, u32[]{:S(2)}) collective-permute-start(bf16[2,1,80,2240]{3,2,1,0:T(8,128)(2,1)S(1)} %get-tuple-element.29), channel_id=1, source_target_pairs={{0,1},{1,0},{2,3},{3,2},{4,5},{5,4},{6,7},{7,6},{8,9},{9,8},{10,11... | collective-permute-start | bytes 2150408 | tf_op jit(solution)/shard_map/ppermute | solution.py:439
  5.9 6.7 %collective-permute-start.1 = (bf16[512,128]{1,0:T(8,128)(2,1)S(1)}, bf16[512,128]{1,0:T(8,128)(2,1)S(1)}, u32[]{:S(2)}, u32[]{:S(2)}) collective-permute-start(bf16[512,128]{1,0:T(8,128)(2,1)S(1)} %get-tuple-element.28), channel_id=1, source_target_pairs={{0,2},{2,0},{4,6},{6,4},{8,10},{10,8},{12,14},{14,12},{1,3},{3,1},... | collective-permute-start | bytes 393224 | tf_op jit(solution)/shard_map/ppermute | solution.py:431
  12.6 5.3 %collective-permute-start.2 = (bf16[512,128]{1,0:T(8,128)(2,1)S(1)}, bf16[512,128]{1,0:T(8,128)(2,1)S(1)}, u32[]{:S(2)}, u32[]{:S(2)}) collective-permute-start(bf16[512,128]{1,0:T(8,128)(2,1)S(1)} %pair_sum.1.refs_0_), channel_id=1, source_target_pairs={{0,4},{2,6},{4,0},{6,2},{8,12},{10,14},{12,8},{14,10},{1,5},{3,7},... | collective-permute-start | bytes 393224 | tf_op jit(solution)/shard_map/ppermute | solution.py:431
  17.9 8.1 %collective-permute-start.4 = (bf16[512,128]{1,0:T(8,128)(2,1)S(1)}, bf16[512,128]{1,0:T(8,128)(2,1)S(1)}, u32[]{:S(2)}, u32[]{:S(2)}) collective-permute-start(bf16[512,128]{1,0:T(8,128)(2,1)S(1)} %stride_sum.1), channel_id=1, source_target_pairs={{0,8},{2,10},{4,12},{6,14},{8,0},{10,2},{12,4},{14,6},{1,9},{3,11}... | collective-permute-start | bytes 393224 | tf_op jit(solution)/shard_map/ppermute | solution.py:431
  20.6 12.0 %copy-start = (f32[9,2240]{1,0:T(8,128)S(1)}, f32[9,2240]{1,0:T(8,128)}, u32[]{:S(2)}) copy-start(f32[9,2240]{1,0:T(8,128)} %vtaps_ref.1) | copy-start | bytes 241924
  20.6 12.0 %copy-start.1 = (f32[9,2240]{1,0:T(8,128)S(1)}, f32[9,2240]{1,0:T(8,128)}, u32[]{:S(2)}) copy-start(f32[9,2240]{1,0:T(8,128)} %gtaps_ref.1) | copy-start | bytes 241924
  26.2 5.0 %collective-permute-start.5 = (bf16[512,128]{1,0:T(8,128)(2,1)S(1)}, bf16[512,128]{1,0:T(8,128)(2,1)S(1)}, u32[]{:S(2)}, u32[]{:S(2)}) collective-permute-start(bf16[512,128]{1,0:T(8,128)(2,1)S(1)} %get-tuple-element.40), channel_id=1, source_target_pairs={{0,2},{2,0},{4,6},{6,4},{8,10},{10,8},{12,14},{14,12},{1,3},{3,1},... | collective-permute-start | bytes 393224 | tf_op jit(solution)/shard_map/ppermute | solution.py:431
  27.3 4.0 %collective-permute-start.6 = (bf16[512,128]{1,0:T(8,128)(2,1)S(1)}, bf16[512,128]{1,0:T(8,128)(2,1)S(1)}, u32[]{:S(2)}, u32[]{:S(2)}) collective-permute-start(bf16[512,128]{1,0:T(8,128)(2,1)S(1)} %get-tuple-element.39.refs_0_), channel_id=1, source_target_pairs={{0,1},{1,0},{2,3},{3,2},{4,5},{5,4},{6,7},{7,6},{8,9},{9,8},{10,11... | collective-permute-start | bytes 393224 | tf_op jit(solution)/shard_map/ppermute | solution.py:457
  31.2 1.3 %collective-permute-start.7 = (bf16[512,128]{1,0:T(8,128)(2,1)S(1)}, bf16[512,128]{1,0:T(8,128)(2,1)S(1)}, u32[]{:S(2)}, u32[]{:S(2)}) collective-permute-start(bf16[512,128]{1,0:T(8,128)(2,1)S(1)} %collective-permute-done.5.refs_1_), channel_id=1, source_target_pairs={{0,1},{1,0},{2,3},{3,2},{4,5},{5,4},{6,7},{7,6},{8,9},{9,8},{10,11... | collective-permute-start | bytes 393224 | tf_op jit(solution)/shard_map/ppermute | solution.py:457

commit v11 on v10

--- a/solution.py
+++ b/solution.py
@@ -40,6 +40,17 @@
         first = tile_heads(tiles[0], lanes)[0][0] * HEAD_DIM // LANES
         last = cdiv((tile_heads(tiles[-1], lanes)[-1][0] + 1) * HEAD_DIM, LANES)
         result.append((tiles, first, last))
+    return result
+
+
+def regions(dim):
+    count = cdiv(dim, GROUP)
+    result, place = [], 0
+    for groups in [range(0, 1), range(1, count)] if count > 1 else [range(0, 1)]:
+        lanes = min(dim, groups.stop * GROUP) - groups.start * GROUP
+        rows = cdiv(cdiv(lanes, LANES) * HEAD_DIM, 64) * 64
+        result.append((groups, place, rows))
+        place += rows
     return result
 
 
@@ -90,27 +101,35 @@
                         side * LANES : (side + 1) * LANES,
                     ]
                     total = jnp.where((lane >= lo) & (lane < hi), part, total)
-                row = pl.multiple_of((step * TILES + j) * HEAD_DIM, 16)
+                row = (step * TILES + j) * HEAD_DIM
+                for groups, place, _ in regions(dim)[1:]:
+                    shift = place - groups.start * TILES * HEAD_DIM
+                    row = jnp.where(step >= groups.start, (step * TILES + j) * HEAD_DIM + shift, row)
+                row = pl.multiple_of(row, 16)
                 whole[pl.ds(row, HEAD_DIM), :] = total.astype(jnp.bfloat16)
 
     by_group(dim, body)
 
     @pl.when(step == pl.num_programs(0) - 1)
     def _():
-        used = cdiv(dim, LANES) * HEAD_DIM
-        if used < whole.shape[0]:
-            whole[used:, :] = jnp.zeros((whole.shape[0] - used, LANES), jnp.bfloat16)
-        for k, part in enumerate(parts):
-            size = part.shape[0]
-            turn = lax.rem(lax.axis_index("space") + k, 2) if len(parts) == 2 else 0
-            part[...] = whole[pl.ds(pl.multiple_of(turn * size, 16), size), :]
+        for groups, place, rows in regions(dim):
+            lanes = min(dim, groups.stop * GROUP) - groups.start * GROUP
+            used = cdiv(lanes, LANES) * HEAD_DIM
+            if used < rows:
+                whole[place + used : place + rows, :] = jnp.zeros((rows - used, LANES), jnp.bfloat16)
+            size = rows // len(parts)
+            for k, part in enumerate(parts):
+                turn = lax.rem(lax.axis_index("space") + k, 2) if len(parts) == 2 else 0
+                source = pl.ds(pl.multiple_of(place + turn * size, 16), size)
+                part[place // len(parts) : place // len(parts) + size, :] = whole[source, :]
         if with_edge:
             for copy in copies:
                 copy.wait()
 
 
-def frame_states(keys, values, rows, parts, edged=()):
+def frame_states(keys, values, parts, edged=()):
     tokens, dim = keys.shape
+    rows = sum(rows for _, _, rows in regions(dim))
     part = (rows // parts, LANES)
     block = pl.BlockSpec((tokens, GROUP), lambda g: (0, g))
     return pl.pallas_call(
@@ -191,10 +210,11 @@
 
 
 def mix_kernel(
-    dim, rows, width, edges,
+    dim, groups, rows, width, edges, count,
     features_ref, inputs_ref, gain_ref, vtaps_ref, gtaps_ref, *refs,
 ):
     *pieces, out_ref, states, weights, numer, windows, held, semaphores = refs
+    pieces = pieces[:count]
     places = edge_places(lax.axis_size("space"), rows) if edges else []
     spots = piece_places() if len(pieces) > 1 else [0]
     tokens = rows * width
@@ -222,7 +242,7 @@
         def numerators(number):
             tiles, first, last = pairs[number]
             for side, j in enumerate(tiles):
-                row = (base // LANES + j) * HEAD_DIM
+                row = ((base - groups.start * GROUP) // LANES + j) * HEAD_DIM
                 state = states[row : row + HEAD_DIM, :].astype(jnp.float32)
                 for h, lo, hi in tile_heads(j, lanes):
                     start = h * HEAD_DIM - first * LANES
@@ -304,7 +324,7 @@
             mix_tile(j)
 
     copies = []
-    for base, lanes in group_lanes(dim):
+    for base, lanes in group_lanes(dim)[groups.start : groups.stop]:
         group(base, lanes)
         here = slice(base, base + lanes)
         copies.append(
@@ -315,32 +335,37 @@
         copy.wait()
 
 
-def mix(prepared, value_taps, gate_taps, pieces, rows, width):
+def mix(groups, out, prepared, value_taps, gate_taps, pieces, rows, width):
     features, inputs, gain = prepared
     total, dim = inputs.shape
     tokens = rows * width
     pairs = spans(min(GROUP, dim))
     depth = max(last - first for _, first, last in pairs) * LANES
     whole = pl.BlockSpec(memory_space=pltpu.VMEM)
+    earlier = [] if out is None else [out]
+    lanes = min(dim, groups.stop * GROUP) - groups.start * GROUP
     return pl.pallas_call(
-        functools.partial(mix_kernel, dim, rows, width, (total - tokens) // width),
+        functools.partial(
+            mix_kernel, dim, groups, rows, width, (total - tokens) // width, len(pieces)
+        ),
         out_shape=jax.ShapeDtypeStruct((tokens, dim), jnp.bfloat16),
-        in_specs=[whole] * (5 + len(pieces)),
+        in_specs=[whole] * (5 + len(pieces)) + [pl.BlockSpec(memory_space=pl.ANY)] * len(earlier),
         out_specs=pl.BlockSpec(memory_space=pl.ANY),
+        input_output_aliases={5 + len(pieces): 0} if earlier else {},
         scratch_shapes=[
             pltpu.VMEM((sum(piece.shape[0] for piece in pieces), LANES), jnp.bfloat16),
             pltpu.VMEM((len(pairs), depth, 2 * LANES), jnp.bfloat16),
             pltpu.VMEM((total, GROUP), jnp.float32),
             pltpu.VMEM((2, 3, rows + 2, width, LANES), jnp.float32),
             pltpu.VMEM((tokens, dim), jnp.bfloat16),
-            pltpu.SemaphoreType.DMA((len(group_lanes(dim)),)),
+            pltpu.SemaphoreType.DMA((len(groups),)),
         ],
         compiler_params=pltpu.CompilerParams(vmem_limit_bytes=36 * 2**20),
         cost_estimate=pl.CostEstimate(
-            flops=60 * tokens * dim, bytes_accessed=6 * tokens * dim, transcendentals=2 * tokens * dim
+            flops=1000 * tokens * lanes, bytes_accessed=6 * tokens * lanes, transcendentals=0
         ),
         name="mix",
-    )(features, inputs, gain, value_taps, gate_taps, *pieces)
+    )(features, inputs, gain, value_taps, gate_taps, *pieces, *earlier)
 
 
 def edge_rows(queries, residual):
@@ -378,11 +403,14 @@
     return lax.rem(lax.axis_index("frame"), 2)
 
 
-def split_sum_body(kept_ref, got_ref, mine_ref, theirs_ref):
-    size = mine_ref.shape[0]
-    for ref, side in ((theirs_ref, 1 - parity()), (mine_ref, parity())):
-        rows = pl.ds(pl.multiple_of(side * size, 16), size)
-        ref[...] = add(kept_ref[rows, :], got_ref[rows, :]).astype(jnp.bfloat16)
+def split_sum_body(dim, kept_ref, got_ref, mine_ref, theirs_ref):
+    for _, place, rows in regions(dim):
+        size = rows // 4
+        for ref, side in ((theirs_ref, 1 - parity()), (mine_ref, parity())):
+            source = pl.ds(pl.multiple_of(place // 2 + side * size, 16), size)
+            ref[place // 4 : place // 4 + size, :] = add(
+                kept_ref[source, :], got_ref[source, :]
+            ).astype(jnp.bfloat16)
 
 
 def sum_body(*refs):
@@ -390,13 +418,20 @@
     out_ref[...] = add(*[term[...] for term in terms]).astype(jnp.bfloat16)
 
 
-def pair_sums_body(own_ref, partner_ref, *refs):
+def region_sum_body(dim, one_ref, other_ref, *out_refs):
+    for (_, place, rows), out_ref in zip(regions(dim), out_refs):
+        here = slice(place // 4, (place + rows) // 4)
+        out_ref[...] = add(one_ref[here, :], other_ref[here, :]).astype(jnp.bfloat16)
+
+
+def pair_sums_body(here, own_ref, partner_ref, *refs):
     *earlier, mine_ref, theirs_ref = refs
-    before = jnp.zeros(own_ref.shape, jnp.float32)
+    before = jnp.zeros(mine_ref.shape, jnp.float32)
     for k, ref in enumerate(earlier):
         from_before = lax.rem(lax.axis_index("frame") // (2 << k), 2) == 1
-        before = before + jnp.where(from_before, add(ref[...]), 0.0)
-    own, partner = add(own_ref[...]), add(partner_ref[...])
+        part = ref[...] if ref.shape == mine_ref.shape else ref[here, :]
+        before = before + jnp.where(from_before, add(part), 0.0)
+    own, partner = add(own_ref[here, :]), add(partner_ref[here, :])
     first = parity() == 0
     both = before + (own + partner)
     mine_ref[...] = jnp.where(first, before + own, both).astype(jnp.bfloat16)
@@ -418,60 +453,78 @@
     return [0, rows + 1]
 
 
-def running_states(keys, values, queries, residual, rows, beside):
+def running_states(keys, values, queries, residual, beside):
     devices, frames = lax.axis_size("space"), lax.axis_size("frame")
+    dim = keys.shape[-1]
     if not paired(devices, frames):
-        (state,) = frame_states(keys, values, rows, 1)
+        (state,) = frame_states(keys, values, 1)
         state = lax.psum(state.astype(jnp.float32), "space").astype(jnp.bfloat16)
         every = lax.all_gather(state, "frame").astype(jnp.float32)
         reached = (jnp.arange(frames) <= lax.axis_index("frame"))[:, None, None]
         total = jnp.sum(jnp.where(reached, every, 0.0), axis=0).astype(jnp.bfloat16)
-        return [total], beside(edge_rows(queries, residual))
+        pieces = [[total[place : place + rows]] for _, place, rows in regions(dim)]
+        return pieces, beside(edge_rows(queries, residual))
     swap = [(0, 1), (1, 0)]
     exchange = lambda array, stride: lax.ppermute(
         array, "frame", [(f, f ^ stride) for f in range(frames)]
     )
-    kept, sent, edge = frame_states(keys, values, rows, 2, (queries, residual))
+    kept, sent, edge = frame_states(keys, values, 2, (queries, residual))
     got = lax.ppermute(sent, "space", swap)
-    quarter = (rows // 4, LANES)
-    own, sent = small_kernel(split_sum_body, "split_sum", [quarter] * 2, kept, got)
-    edge, sent = lax.optimization_barrier((edge, sent))
+    quarter = (got.shape[0] // 2, LANES)
+    own, sent = small_kernel(
+        functools.partial(split_sum_body, dim), "split_sum", [quarter] * 2, kept, got
+    )
+    partner = exchange(sent, 1)
+    partner, edge = lax.optimization_barrier((partner, edge))
     edge = lax.ppermute(edge, "space", swap)
-    partner = exchange(sent, 1)
-    (total,) = small_kernel(sum_body, "pair_sum", [quarter], own, partner)
+    total, other = own, partner
     earlier = []
     stride = 2
-    while stride < frames:
-        if stride * 2 == frames:
-            total, edge = lax.optimization_barrier((total, edge))
-        earlier.append(exchange(total, stride))
+    while stride * 2 < frames:
+        (total,) = small_kernel(sum_body, "sum", [quarter], total, other)
+        other = exchange(total, stride)
+        earlier.append(other)
         stride *= 2
-        if stride < frames:
-            (total,) = small_kernel(sum_body, "stride_sum", [quarter], total, earlier[-1])
+    shapes = [(rows // 4, LANES) for _, _, rows in regions(dim)]
+    totals = small_kernel(
+        functools.partial(region_sum_body, dim), "region_sum", shapes, total, other
+    )
+    *totals, edge = lax.optimization_barrier((*totals, edge))
+    last = [exchange(total, stride) for total in totals]
     prepared = beside(edge)
-    earlier[-1], *prepared = lax.optimization_barrier((earlier[-1], *prepared))
-    mine, theirs = small_kernel(
-        pair_sums_body, "pair_sums", [quarter] * 2, own, partner, *earlier
-    )
-    other = exchange(theirs, 1)
-    pieces = [mine, other, lax.ppermute(mine, "space", swap), lax.ppermute(other, "space", swap)]
-    return pieces, prepared
+    last[0], *prepared = lax.optimization_barrier((last[0], *prepared))
+    across = [(2 * f + c, 2 * (f ^ 1) + 1 - c) for f in range(frames) for c in range(2)]
+    results = []
+    for k, (_, place, rows) in enumerate(regions(dim)):
+        here = slice(place // 4, (place + rows) // 4)
+        mine, theirs = small_kernel(
+            functools.partial(pair_sums_body, here), "pair_sums", [shapes[k]] * 2,
+            own, partner, *earlier, last[k],
+        )
+        theirs_here = exchange(theirs, 1)
+        mine_there = lax.ppermute(mine, "space", swap)
+        if k == 0:
+            theirs_there = lax.ppermute(theirs_here, "space", swap)
+        else:
+            theirs_there = lax.ppermute(theirs, ("frame", "space"), across)
+        results.append([mine, theirs_here, mine_there, theirs_there])
+    return results, prepared
 
 
 def on_device(queries, keys, values, residual, attn_gain, value_taps, gate_taps):
     frames, rows, width, dim = queries.shape
     tokens = frames * rows * width
     flat = lambda a: a.reshape(tokens, dim)
-    state_rows = cdiv(cdiv(dim, LANES) * HEAD_DIM, 64) * 64
-    pieces, prepared = running_states(
+    results, prepared = running_states(
         flat(keys),
         flat(values),
         queries.reshape(rows, width, dim),
         residual.reshape(rows, width, dim),
-        state_rows,
         lambda edge: prepare(flat(queries), flat(residual), edge, attn_gain[None]),
     )
-    out = mix(prepared, value_taps, gate_taps, pieces, rows, width)
+    out = None
+    for (groups, _, _), pieces in zip(regions(dim), results):
+        out = mix(groups, out, prepared, value_taps, gate_taps, pieces, rows, width)
     return out.reshape(frames, rows, width, dim)
 
 

time: 45.6 us -> 45.5 us (level); the launches traced: 45.4 us -> 44.6 us
  waiting for transfers between devices: 16.9 us -> 12.2 us
  starting transfers between devices: 9.2 us -> 12.2 us
  Pallas kernels: 19.2 us -> 20.1 us
    ppermute x4 -> x6, waiting for transfers between devices: 14.4 us -> 11 us  [running_states(): lax.ppermute(array, 'frame', [(f, f ^ stride) for f in range(frames)])]
    ppermute x2 -> x4, starting transfers between devices: 0.01 us -> 1.78 us  [the longest x1 1.2 us: running_states(): theirs_there = lax.ppermute(theirs, ('frame', 'space'), across)]
    ppermute x4 -> x6, starting transfers between devices: 8.24 us -> 9.9 us  [running_states(): lax.ppermute(array, 'frame', [(f, f ^ stride) for f in range(frames)])]
    ppermute x2 -> x4, waiting for transfers between devices: 1.34 us -> 0.01 us  [the longest x2 0.01 us: running_states(): mine_there = lax.ppermute(mine, 'space', swap)]
    pallas_call x1 -> x2, Pallas kernels: 12.8 us -> 13.8 us  [mix(): pl.pallas_call(functools.partial(mix_kernel, dim, groups, rows, width, (t...]
  transfers between devices with their start and end apart: 8 -> 12, of which waited for: 6 -> 5; matrix products, arithmetic and copies ran while one was open for 0% -> 0% of each run, Pallas kernels for 5% -> 18%
where the time goes in v11:
time: 45.5 us; the launch traced here: 44.6 us
  Pallas kernels  20.1 us (44%)
  starting transfers between devices  12.2 us (27%)
  waiting for transfers between devices  12.2 us (27%)
    pallas_call x2, Pallas kernels, mix(): pl.pallas_call(functools.partial(mix_kernel, dim, groups, rows, width, (t...  13.8 us
    ppermute x6, waiting for transfers between devices, running_states(): lax.ppermute(array, 'frame', [(f, f ^ stride) for f in range(frames)])  11 us
    ppermute x6, starting transfers between devices, running_states(): lax.ppermute(array, 'frame', [(f, f ^ stride) for f in range(frames)])  9.9 us
    pallas_call x1, Pallas kernels, frame_states(): pl.pallas_call(functools.partial(state_kernel, dim, bool(edged)), out_sha...  3.72 us
    pallas_call x1, Pallas kernels, prepare(): pl.pallas_call(functools.partial(prepare_kernel, dim), out_shape=[pltpu.V...  2.35 us
    ppermute x1, starting transfers between devices, running_states(): theirs_there = lax.ppermute(theirs, ('frame', 'space'), across)  1.2 us
    ppermute x1, waiting for transfers between devices, running_states(): got = lax.ppermute(sent, 'space', swap)  1.17 us
  transfers between devices with their start and end apart: 12, of which 5 were waited for; matrix products, arithmetic and copies ran while one was open for 0% of the time, Pallas kernels for 18%

profile of v11, /device:TPU:0, one launch (start us, length us, event | category | flops | bytes accessed | tf_op | source)
XLA Modules:
  0.0 44.6 jit_solution(2950327225380995453)
XLA Ops:
  0.0 3.7 %frame_states.1 = (bf16[1056,128]{1,0:T(8,128)(2,1)S(1)}, bf16[1056,128]{1,0:T(8,128)(2,1)S(1)}, bf16[2,1,80,2240]{3,2,1,0:T(8,128)(2,1)S(1)}) custom-call(bf16[480,2240]{1,0:T(8,128)(2,1)} %bitcast.11, bf16[480,2240]{1,0:T(8,128)(2,1)} %bitcast.12, bf16[6,80,2240]{2,1,0:T(8,128)(2,1)} %bitcast.7, bf16[6,80,2240]{2,1,0:T(8,128)(2,1)} %bitcast.9), custom_call_target="tpu_custom_call" | custom-call | flops 240844800 | bytes 4300800 | tf_op jit(solution)/shard_map/frame_states/pallas_call | solution.py:135
  3.7 0.5 %collective-permute-start = (bf16[1056,128]{1,0:T(8,128)(2,1)S(1)}, bf16[1056,128]{1,0:T(8,128)(2,1)S(1)}, u32[]{:S(2)}, u32[]{:S(2)}) collective-permute-start(bf16[1056,128]{1,0:T(8,128)(2,1)S(1)} %get-tuple-element.29), channel_id=1, source_target_pairs={{0,1},{1,0},{2,3},{3,2},{4,5},{5,4},{6,7},{7,6},{8,9},{9,8},{10,11... | collective-permute-start | bytes 811016 | tf_op jit(solution)/shard_map/ppermute | solution.py:472
  4.3 1.2 %collective-permute-done.got_ref = bf16[1056,128]{1,0:T(8,128)(2,1)S(1)} collective-permute-done((bf16[1056,128]{1,0:T(8,128)(2,1)S(1)}, bf16[1056,128]{1,0:T(8,128)(2,1)S(1)}, u32[]{:S(2)}, u32[]{:S(2)}) %collective-permute-start) | collective-permute-done | bytes 270368 | tf_op jit(solution)/shard_map/ppermute | solution.py:472
  5.4 0.1 split_sum.1
  5.5 3.0 %collective-permute-start.1 = (bf16[528,128]{1,0:T(8,128)(2,1)S(1)}, bf16[528,128]{1,0:T(8,128)(2,1)S(1)}, u32[]{:S(2)}, u32[]{:S(2)}) collective-permute-start(bf16[528,128]{1,0:T(8,128)(2,1)S(1)} %get-tuple-element.31), channel_id=1, source_target_pairs={{0,2},{2,0},{4,6},{6,4},{8,10},{10,8},{12,14},{14,12},{1,3},{3,1},... | collective-permute-start | bytes 405512 | tf_op jit(solution)/shard_map/ppermute | solution.py:468
  8.4 3.9 %collective-permute-done.1.refs_1_.partner_ref = bf16[528,128]{1,0:T(8,128)(2,1)S(1)} collective-permute-done((bf16[528,128]{1,0:T(8,128)(2,1)S(1)}, bf16[528,128]{1,0:T(8,128)(2,1)S(1)}, u32[]{:S(2)}, u32[]{:S(2)}) %collective-permute-start.1) | collective-permute-done | bytes 135200 | tf_op jit(solution)/shard_map/ppermute | solution.py:468
  12.3 0.0 collective-permute-start.3
  12.4 1.9 %collective-permute-start.2 = (bf16[528,128]{1,0:T(8,128)(2,1)S(1)}, bf16[528,128]{1,0:T(8,128)(2,1)S(1)}, u32[]{:S(2)}, u32[]{:S(2)}) collective-permute-start(bf16[528,128]{1,0:T(8,128)(2,1)S(1)} %sum.1.one_ref), channel_id=1, source_target_pairs={{0,4},{2,6},{4,0},{6,2},{8,12},{10,14},{12,8},{14,10},{1,5},{3,7},... | collective-permute-start | bytes 405512 | tf_op jit(solution)/shard_map/ppermute | solution.py:468
  14.2 4.3 %collective-permute-done.2.other_ref.refs_0_ = bf16[528,128]{1,0:T(8,128)(2,1)S(1)} collective-permute-done((bf16[528,128]{1,0:T(8,128)(2,1)S(1)}, bf16[528,128]{1,0:T(8,128)(2,1)S(1)}, u32[]{:S(2)}, u32[]{:S(2)}) %collective-permute-start.2) | collective-permute-done | bytes 135200 | tf_op jit(solution)/shard_map/ppermute | solution.py:468
  18.5 2.8 %collective-permute-start.4 = (bf16[208,128]{1,0:T(8,128)(2,1)S(1)}, bf16[208,128]{1,0:T(8,128)(2,1)S(1)}, u32[]{:S(2)}, u32[]{:S(2)}) collective-permute-start(bf16[208,128]{1,0:T(8,128)(2,1)S(1)} %get-tuple-element.37), channel_id=1, source_target_pairs={{0,8},{2,10},{4,12},{6,14},{8,0},{10,2},{12,4},{14,6},{1,9},{3,11}... | collective-permute-start | bytes 159752 | tf_op jit(solution)/shard_map/ppermute | solution.py:468
  21.4 0.2 collective-permute-start.5
  21.5 0.0 copy-start
  21.6 0.0 copy-start.1
  21.6 2.4 %prepare.1 = (bf16[560,2304]{1,0:T(8,128)(2,1)S(1)}, bf16[560,2240]{1,0:T(8,128)(2,1)S(1)}, f32[1,2240]{1,0:T(1,128)S(1)}) custom-call(bf16[480,2240]{1,0:T(8,128)(2,1)} %bitcast.8, bf16[480,2240]{1,0:T(8,128)(2,1)} %bitcast.10, bf16[2,1,80,2240]{3,2,1,0:T(8,128)(2,1)S(1)} %collective-permute-done.3.edge_ref, f32[1,2240]{1,0:T(1,128)S(1)} %broadcast_in_dim.3.gain_ref), custom_call_target="tpu_custom_call" | custom-call | flops 5017600 | bytes 10035200 | tf_op jit(solution)/shard_map/prepare/pallas_call | solution.py:191
  23.9 0.2 collective-permute-done.4.refs_1_
  24.1 0.1 pair_sums.3
  24.2 1.6 %collective-permute-start.9 = (bf16[208,128]{1,0:T(8,128)(2,1)S(1)}, bf16[208,128]{1,0:T(8,128)(2,1)S(1)}, u32[]{:S(2)}, u32[]{:S(2)}) collective-permute-start(bf16[208,128]{1,0:T(8,128)(2,1)S(1)} %get-tuple-element.50), channel_id=1, source_target_pairs={{0,2},{2,0},{4,6},{6,4},{8,10},{10,8},{12,14},{14,12},{1,3},{3,1},... | collective-permute-start | bytes 159752 | tf_op jit(solution)/shard_map/ppermute | solution.py:468
  25.8 2.6 %collective-permute-done.9.refs_1_ = bf16[208,128]{1,0:T(8,128)(2,1)S(1)} collective-permute-done((bf16[208,128]{1,0:T(8,128)(2,1)S(1)}, bf16[208,128]{1,0:T(8,128)(2,1)S(1)}, u32[]{:S(2)}, u32[]{:S(2)}) %collective-permute-start.9) | collective-permute-done | bytes 53280 | tf_op jit(solution)/shard_map/ppermute | solution.py:468
  28.4 0.1 pair_sums.2
  28.5 0.6 %collective-permute-start.7 = (bf16[320,128]{1,0:T(8,128)(2,1)S(1)}, bf16[320,128]{1,0:T(8,128)(2,1)S(1)}, u32[]{:S(2)}, u32[]{:S(2)}) collective-permute-start(bf16[320,128]{1,0:T(8,128)(2,1)S(1)} %get-tuple-element.46.refs_0_), channel_id=1, source_target_pairs={{0,1},{1,0},{2,3},{3,2},{4,5},{5,4},{6,7},{7,6},{8,9},{9,8},{10,11... | collective-permute-start | bytes 245768 | tf_op jit(solution)/shard_map/ppermute | solution.py:505
  29.1 1.2 %collective-permute-start.8 = (bf16[320,128]{1,0:T(8,128)(2,1)S(1)}, bf16[320,128]{1,0:T(8,128)(2,1)S(1)}, u32[]{:S(2)}, u32[]{:S(2)}) collective-permute-start(bf16[320,128]{1,0:T(8,128)(2,1)S(1)} %get-tuple-element.47), channel_id=1, source_target_pairs={{0,3},{1,2},{2,1},{3,0},{4,7},{5,6},{6,5},{7,4},{8,11},{9,10},{10,... | collective-permute-start | bytes 245768 | tf_op jit(solution)/shard_map/ppermute | solution.py:509
  30.3 0.5 %collective-permute-start.6 = (bf16[320,128]{1,0:T(8,128)(2,1)S(1)}, bf16[320,128]{1,0:T(8,128)(2,1)S(1)}, u32[]{:S(2)}, u32[]{:S(2)}) collective-permute-start(bf16[320,128]{1,0:T(8,128)(2,1)S(1)} %get-tuple-element.47), channel_id=1, source_target_pairs={{0,2},{2,0},{4,6},{6,4},{8,10},{10,8},{12,14},{14,12},{1,3},{3,1},... | collective-permute-start | bytes 245768 | tf_op jit(solution)/shard_map/ppermute | solution.py:468
  30.8 5.6 %mix.2.refs_4_ = bf16[480,2240]{1,0:T(8,128)(2,1)} custom-call(bf16[560,2304]{1,0:T(8,128)(2,1)S(1)} %get-tuple-element.42.features_ref, bf16[560,2240]{1,0:T(8,128)(2,1)S(1)} %get-tuple-element.43.inputs_ref, f32[1,2240]{1,0:T(1,128)S(1)} %get-tuple-element.44.gain_ref, f32[9,2240]{1,0:T(8,128)S(1)} %copy-done, f32[9,2240]{1,0:T(8,128)S(1)} %copy-done.1, ...), custom_call_target="tpu_custom_call" | custom-call | flops 430080000 | bytes 2580480 | tf_op jit(solution)/shard_map/mix/pallas_call | solution.py:347
  36.5 8.2 %mix.3 = bf16[480,2240]{1,0:T(8,128)(2,1)} custom-call(bf16[560,2304]{1,0:T(8,128)(2,1)S(1)} %get-tuple-element.42.features_ref, bf16[560,2240]{1,0:T(8,128)(2,1)S(1)} %get-tuple-element.43.inputs_ref, f32[1,2240]{1,0:T(1,128)S(1)} %get-tuple-element.44.gain_ref, f32[9,2240]{1,0:T(8,128)S(1)} %copy-done, ...), custom_call_target="tpu_custom_call", output_to_operand_aliasing={{}: (9, {})} | custom-call | flops 645120000 | bytes 3870720 | tf_op jit(solution)/shard_map/mix/pallas_call | solution.py:347
  (16 shorter events, 0.1 us)
Async XLA Ops:
  0.0 21.5 %copy-start.2 = (f32[2240]{0:T(1024)S(1)}, f32[2240]{0:T(1024)}, u32[]{:S(2)}) copy-start(f32[2240]{0:T(1024)} %param.11) | copy-start | bytes 26884
  3.7 1.7 %collective-permute-start = (bf16[1056,128]{1,0:T(8,128)(2,1)S(1)}, bf16[1056,128]{1,0:T(8,128)(2,1)S(1)}, u32[]{:S(2)}, u32[]{:S(2)}) collective-permute-start(bf16[1056,128]{1,0:T(8,128)(2,1)S(1)} %get-tuple-element.29), channel_id=1, source_target_pairs={{0,1},{1,0},{2,3},{3,2},{4,5},{5,4},{6,7},{7,6},{8,9},{9,8},{10,11... | collective-permute-start | bytes 811016 | tf_op jit(solution)/shard_map/ppermute | solution.py:472
  5.5 6.8 %collective-permute-start.1 = (bf16[528,128]{1,0:T(8,128)(2,1)S(1)}, bf16[528,128]{1,0:T(8,128)(2,1)S(1)}, u32[]{:S(2)}, u32[]{:S(2)}) collective-permute-start(bf16[528,128]{1,0:T(8,128)(2,1)S(1)} %get-tuple-element.31), channel_id=1, source_target_pairs={{0,2},{2,0},{4,6},{6,4},{8,10},{10,8},{12,14},{14,12},{1,3},{3,1},... | collective-permute-start | bytes 405512 | tf_op jit(solution)/shard_map/ppermute | solution.py:468
  12.3 6.2 %collective-permute-start.3 = (bf16[2,1,80,2240]{3,2,1,0:T(8,128)(2,1)S(1)}, bf16[2,1,80,2240]{3,2,1,0:T(8,128)(2,1)S(1)}, u32[]{:S(2)}, u32[]{:S(2)}) collective-permute-start(bf16[2,1,80,2240]{3,2,1,0:T(8,128)(2,1)S(1)} %get-tuple-element.36), channel_id=1, source_target_pairs={{0,1},{1,0},{2,3},{3,2},{4,5},{5,4},{6,7},{7,6},{8,9},{9,8},{10,11... | collective-permute-start | bytes 2150408 | tf_op jit(solution)/shard_map/ppermute | solution.py:479
  12.4 6.1 %collective-permute-start.2 = (bf16[528,128]{1,0:T(8,128)(2,1)S(1)}, bf16[528,128]{1,0:T(8,128)(2,1)S(1)}, u32[]{:S(2)}, u32[]{:S(2)}) collective-permute-start(bf16[528,128]{1,0:T(8,128)(2,1)S(1)} %sum.1.one_ref), channel_id=1, source_target_pairs={{0,4},{2,6},{4,0},{6,2},{8,12},{10,14},{12,8},{14,10},{1,5},{3,7},... | collective-permute-start | bytes 405512 | tf_op jit(solution)/shard_map/ppermute | solution.py:468
  18.5 5.6 %collective-permute-start.4 = (bf16[208,128]{1,0:T(8,128)(2,1)S(1)}, bf16[208,128]{1,0:T(8,128)(2,1)S(1)}, u32[]{:S(2)}, u32[]{:S(2)}) collective-permute-start(bf16[208,128]{1,0:T(8,128)(2,1)S(1)} %get-tuple-element.37), channel_id=1, source_target_pairs={{0,8},{2,10},{4,12},{6,14},{8,0},{10,2},{12,4},{14,6},{1,9},{3,11}... | collective-permute-start | bytes 159752 | tf_op jit(solution)/shard_map/ppermute | solution.py:468
  21.4 7.1 %collective-permute-start.5 = (bf16[320,128]{1,0:T(8,128)(2,1)S(1)}, bf16[320,128]{1,0:T(8,128)(2,1)S(1)}, u32[]{:S(2)}, u32[]{:S(2)}) collective-permute-start(bf16[320,128]{1,0:T(8,128)(2,1)S(1)} %get-tuple-element.45), channel_id=1, source_target_pairs={{0,8},{2,10},{4,12},{6,14},{8,0},{10,2},{12,4},{14,6},{1,9},{3,11}... | collective-permute-start | bytes 245768 | tf_op jit(solution)/shard_map/ppermute | solution.py:468
  21.5 9.3 %copy-start = (f32[9,2240]{1,0:T(8,128)S(1)}, f32[9,2240]{1,0:T(8,128)}, u32[]{:S(2)}) copy-start(f32[9,2240]{1,0:T(8,128)} %vtaps_ref.3) | copy-start | bytes 241924
  21.6 9.3 %copy-start.1 = (f32[9,2240]{1,0:T(8,128)S(1)}, f32[9,2240]{1,0:T(8,128)}, u32[]{:S(2)}) copy-start(f32[9,2240]{1,0:T(8,128)} %gtaps_ref.3) | copy-start | bytes 241924
  24.2 4.2 %collective-permute-start.9 = (bf16[208,128]{1,0:T(8,128)(2,1)S(1)}, bf16[208,128]{1,0:T(8,128)(2,1)S(1)}, u32[]{:S(2)}, u32[]{:S(2)}) collective-permute-start(bf16[208,128]{1,0:T(8,128)(2,1)S(1)} %get-tuple-element.50), channel_id=1, source_target_pairs={{0,2},{2,0},{4,6},{6,4},{8,10},{10,8},{12,14},{14,12},{1,3},{3,1},... | collective-permute-start | bytes 159752 | tf_op jit(solution)/shard_map/ppermute | solution.py:468
  25.8 5.0 %collective-permute-start.10 = (bf16[208,128]{1,0:T(8,128)(2,1)S(1)}, bf16[208,128]{1,0:T(8,128)(2,1)S(1)}, u32[]{:S(2)}, u32[]{:S(2)}) collective-permute-start(bf16[208,128]{1,0:T(8,128)(2,1)S(1)} %get-tuple-element.49.refs_0_), channel_id=1, source_target_pairs={{0,1},{1,0},{2,3},{3,2},{4,5},{5,4},{6,7},{7,6},{8,9},{9,8},{10,11... | collective-permute-start | bytes 159752 | tf_op jit(solution)/shard_map/ppermute | solution.py:505
  28.4 2.4 %collective-permute-start.11 = (bf16[208,128]{1,0:T(8,128)(2,1)S(1)}, bf16[208,128]{1,0:T(8,128)(2,1)S(1)}, u32[]{:S(2)}, u32[]{:S(2)}) collective-permute-start(bf16[208,128]{1,0:T(8,128)(2,1)S(1)} %collective-permute-done.9.refs_1_), channel_id=1, source_target_pairs={{0,1},{1,0},{2,3},{3,2},{4,5},{5,4},{6,7},{7,6},{8,9},{9,8},{10,11... | collective-permute-start | bytes 159752 | tf_op jit(solution)/shard_map/ppermute | solution.py:507
  28.5 7.9 %collective-permute-start.7 = (bf16[320,128]{1,0:T(8,128)(2,1)S(1)}, bf16[320,128]{1,0:T(8,128)(2,1)S(1)}, u32[]{:S(2)}, u32[]{:S(2)}) collective-permute-start(bf16[320,128]{1,0:T(8,128)(2,1)S(1)} %get-tuple-element.46.refs_0_), channel_id=1, source_target_pairs={{0,1},{1,0},{2,3},{3,2},{4,5},{5,4},{6,7},{7,6},{8,9},{9,8},{10,11... | collective-permute-start | bytes 245768 | tf_op jit(solution)/shard_map/ppermute | solution.py:505
  29.1 7.3 %collective-permute-start.8 = (bf16[320,128]{1,0:T(8,128)(2,1)S(1)}, bf16[320,128]{1,0:T(8,128)(2,1)S(1)}, u32[]{:S(2)}, u32[]{:S(2)}) collective-permute-start(bf16[320,128]{1,0:T(8,128)(2,1)S(1)} %get-tuple-element.47), channel_id=1, source_target_pairs={{0,3},{1,2},{2,1},{3,0},{4,7},{5,6},{6,5},{7,4},{8,11},{9,10},{10,... | collective-permute-start | bytes 245768 | tf_op jit(solution)/shard_map/ppermute | solution.py:509
  30.3 6.1 %collective-permute-start.6 = (bf16[320,128]{1,0:T(8,128)(2,1)S(1)}, bf16[320,128]{1,0:T(8,128)(2,1)S(1)}, u32[]{:S(2)}, u32[]{:S(2)}) collective-permute-start(bf16[320,128]{1,0:T(8,128)(2,1)S(1)} %get-tuple-element.47), channel_id=1, source_target_pairs={{0,2},{2,0},{4,6},{6,4},{8,10},{10,8},{12,14},{14,12},{1,3},{3,1},... | collective-permute-start | bytes 245768 | tf_op jit(solution)/shard_map/ppermute | solution.py:468

commit v12 on v10

--- a/solution.py
+++ b/solution.py
@@ -51,7 +51,7 @@
         pl.when(pl.program_id(0) >= full)(lambda: body(rest))
 
 
-def state_kernel(dim, with_edge, keys_ref, values_ref, *refs):
+def state_kernel(dim, with_edge, keys_refs, values_refs, refs):
     step = pl.program_id(0)
     *refs, turned, whole, semaphores = refs
     if with_edge:
@@ -72,15 +72,19 @@
         parts = refs
 
     def body(lanes):
-        turned[...] = jnp.maximum(keys_ref[...], 0).T
+        for k, keys_ref in enumerate(keys_refs):
+            turned[k] = jnp.maximum(keys_ref[...], 0).T
         lane = lane_iota((HEAD_DIM, LANES))
         for tiles, _, _ in spans(lanes):
             begin = tile_heads(tiles[0], lanes)[0][0]
             end = tile_heads(tiles[-1], lanes)[-1][0] + 1
-            product = jnp.dot(
-                turned[begin * HEAD_DIM : end * HEAD_DIM, :],
-                values_ref[:, tiles[0] * LANES : (tiles[-1] + 1) * LANES],
-                preferred_element_type=jnp.float32,
+            product = sum(
+                jnp.dot(
+                    turned[k, begin * HEAD_DIM : end * HEAD_DIM, :],
+                    values_ref[:, tiles[0] * LANES : (tiles[-1] + 1) * LANES],
+                    preferred_element_type=jnp.float32,
+                )
+                for k, values_ref in enumerate(values_refs)
             )
             for side, j in enumerate(tiles):
                 total = jnp.zeros((HEAD_DIM, LANES), jnp.float32)
@@ -112,17 +116,25 @@
 def frame_states(keys, values, rows, parts, edged=()):
     tokens, dim = keys.shape
     part = (rows // parts, LANES)
-    block = pl.BlockSpec((tokens, GROUP), lambda g: (0, g))
+    slabs = 2 if tokens % 32 == 0 else 1
+    blocks = [
+        pl.BlockSpec((tokens // slabs, GROUP), functools.partial(lambda k, g: (k, g), k))
+        for k in range(slabs)
+    ]
+
+    def body(*refs):
+        state_kernel(dim, bool(edged), refs[:slabs], refs[slabs : 2 * slabs], refs[2 * slabs :])
+
     return pl.pallas_call(
-        functools.partial(state_kernel, dim, bool(edged)),
+        body,
         out_shape=[pltpu.VMEM(part, jnp.bfloat16)] * parts
         + [pltpu.VMEM((len(edged), 1, *edged[0].shape[1:]), jnp.bfloat16) for _ in edged[:1]],
         grid=(cdiv(dim, GROUP),),
-        in_specs=[block, block] + [pl.BlockSpec(memory_space=pl.ANY)] * len(edged),
+        in_specs=blocks + blocks + [pl.BlockSpec(memory_space=pl.ANY)] * len(edged),
         out_specs=[pl.BlockSpec(part, lambda g: (0, 0))] * parts
         + [pl.BlockSpec(memory_space=pl.ANY) for _ in edged[:1]],
         scratch_shapes=[
-            pltpu.VMEM((GROUP, tokens), jnp.bfloat16),
+            pltpu.VMEM((slabs, GROUP, tokens // slabs), jnp.bfloat16),
             pltpu.VMEM((rows, LANES), jnp.bfloat16),
             pltpu.SemaphoreType.DMA((2,)),
         ],
@@ -131,7 +143,7 @@
             flops=2 * tokens * dim * HEAD_DIM, bytes_accessed=4 * tokens * dim, transcendentals=0
         ),
         name="frame_states",
-    )(in_hbm(keys), in_hbm(values), *[in_hbm(array) for array in edged])
+    )(*[in_hbm(keys)] * slabs, *[in_hbm(values)] * slabs, *[in_hbm(array) for array in edged])
 
 
 def group_lanes(dim):
@@ -194,7 +206,7 @@
     dim, rows, width, edges,
     features_ref, inputs_ref, gain_ref, vtaps_ref, gtaps_ref, *refs,
 ):
-    *pieces, out_ref, states, weights, numer, windows, held, semaphores = refs
+    *pieces, out_ref, states, weights, numer, rounded, windows, results, held, semaphores = refs
     places = edge_places(lax.axis_size("space"), rows) if edges else []
     spots = piece_places() if len(pieces) > 1 else [0]
     tokens = rows * width
@@ -205,16 +217,18 @@
     lane = lane_iota((HEAD_DIM, LANES))
     sublane = lax.broadcasted_iota(jnp.int32, (8, LANES), 0)
 
+    half = width // 2
+    even, odd = pl.ds(0, half, stride=2), pl.ds(1, half, stride=2)
+
     def store_windows(mixed, row, slot, used):
-        mixed = mixed.astype(jnp.bfloat16).astype(jnp.float32)
-        windows[slot, 1, row, :, :used] = mixed
-        before, after = pltpu.roll(mixed, 1, 0), pltpu.roll(mixed, width - 1, 0)
-        windows[slot, 0, row, :8, :used] = jnp.where(sublane[:, :used] == 0, 0.0, before[:8])
-        windows[slot, 0, row, 8:, :used] = before[8:]
-        windows[slot, 2, row, : width - 8, :used] = after[: width - 8]
-        windows[slot, 2, row, width - 8 :, :used] = jnp.where(
-            sublane[:, :used] == 7, 0.0, after[width - 8 :]
-        )
+        rounded[slot, row, :, :used] = mixed.astype(jnp.bfloat16).astype(jnp.float32)
+        left, right = rounded[slot, row, even, :used], rounded[slot, row, odd, :used]
+        sub = sublane[:, :used]
+        before, after = pltpu.roll(right, 1, 0), pltpu.roll(left, half - 1, 0)
+        before = jnp.concatenate([jnp.where(sub == 0, 0.0, before[:8]), before[8:]], axis=0)
+        after = jnp.concatenate([after[: half - 8], jnp.where(sub == 7, 0.0, after[half - 8 :])], axis=0)
+        for k, window in enumerate((before - right, left + right, right - left, left - after)):
+            windows[slot, k, row, :, :used] = window
 
     def group(base, lanes):
         pairs = spans(lanes)
@@ -281,17 +295,38 @@
                 store_windows(outside[k], row, slot, used)
             for row in range(rows):
                 store_windows(mixed(slice(row * width, (row + 1) * width)), row + 1, slot, used)
+            taps = []
+            for ref, factor in ((vtaps_ref, 1.0), (gtaps_ref, 0.5)):
+                for tap_row in range(3):
+                    one, two, three = [
+                        ref[3 * tap_row + i : 3 * tap_row + i + 1, here] * factor for i in range(3)
+                    ]
+                    outer = 0.5 * (one + three)
+                    taps.append((one, outer + 0.5 * two, outer - 0.5 * two, three))
             for row in range(rows):
-                conv_v = half_g = None
-                for tap in range(9):
-                    window = windows[slot, tap % 3, row + tap // 3, :, :used]
-                    value = vtaps_ref[tap : tap + 1, here] * window
-                    gate = (0.5 * gtaps_ref[tap : tap + 1, here]) * window
-                    conv_v = value if tap == 0 else conv_v + value
-                    half_g = gate if tap == 0 else half_g + gate
-                center = windows[slot, 1, row + 1, :, :used]
-                result = center + conv_v * (half_g + half_g * jnp.tanh(half_g))
-                held[row * width : (row + 1) * width, here] = result.astype(jnp.bfloat16)
+                columns = []
+                for f in range(2):
+                    products = []
+                    for k in range(4):
+                        total = None
+                        for tap_row in range(3):
+                            term = taps[3 * f + tap_row][k] * windows[slot, k, row + tap_row, :, :used]
+                            total = term if total is None else total + term
+                        products.append(total)
+                    columns.append(
+                        (
+                            products[0] + products[1] + products[2],
+                            products[1] - products[2] - products[3],
+                        )
+                    )
+                for side, (conv_v, half_g) in zip((even, odd), zip(*columns)):
+                    center = rounded[slot, row + 1, side, :used]
+                    results[slot, row, side, :used] = center + conv_v * (
+                        half_g + half_g * jnp.tanh(half_g)
+                    )
+                held[row * width : (row + 1) * width, here] = results[slot, row, :, :used].astype(
+                    jnp.bfloat16
+                )
 
         parts = {}
         for number, (tiles, _, _) in enumerate(pairs):
@@ -331,7 +366,9 @@
             pltpu.VMEM((sum(piece.shape[0] for piece in pieces), LANES), jnp.bfloat16),
             pltpu.VMEM((len(pairs), depth, 2 * LANES), jnp.bfloat16),
             pltpu.VMEM((total, GROUP), jnp.float32),
-            pltpu.VMEM((2, 3, rows + 2, width, LANES), jnp.float32),
+            pltpu.VMEM((2, rows + 2, width, LANES), jnp.float32),
+            pltpu.VMEM((2, 4, rows + 2, width // 2, LANES), jnp.float32),
+            pltpu.VMEM((2, rows, width, LANES), jnp.float32),
             pltpu.VMEM((tokens, dim), jnp.bfloat16),
             pltpu.SemaphoreType.DMA((len(group_lanes(dim)),)),
         ],

time: 45.6 us -> 44.1 us (0.967)
  Pallas kernels: 19.2 us -> 17.8 us
    pallas_call x1, Pallas kernels: 12.8 us -> 11.4 us  [mix(): pl.pallas_call(functools.partial(mix_kernel, dim, rows, width, (total - t...]
where the time goes in v12:
time: 44.1 us; the launch traced here: 44 us
  Pallas kernels  17.8 us (40%)
  waiting for transfers between devices  16.9 us (38%)
  starting transfers between devices  9.21 us (21%)
    ppermute x4, waiting for transfers between devices, running_states(): lax.ppermute(array, 'frame', [(f, f ^ stride) for f in range(frames)])  14.4 us
    pallas_call x1, Pallas kernels, mix(): pl.pallas_call(functools.partial(mix_kernel, dim, rows, width, (total - t...  11.4 us
    ppermute x4, starting transfers between devices, running_states(): lax.ppermute(array, 'frame', [(f, f ^ stride) for f in range(frames)])  8.24 us
    pallas_call x1, Pallas kernels, frame_states(): pl.pallas_call(body, out_shape=[pltpu.VMEM(part, jnp.bfloat16)] * parts +...  3.73 us
    pallas_call x1, Pallas kernels, prepare(): pl.pallas_call(functools.partial(prepare_kernel, dim), out_shape=[pltpu.V...  2.35 us
    ppermute x1, waiting for transfers between devices, running_states(): lax.ppermute(other, 'space', swap)  1.34 us
    ppermute x1, waiting for transfers between devices, running_states(): got = lax.ppermute(sent, 'space', swap)  1.16 us
  transfers between devices with their start and end apart: 8, of which 6 were waited for; matrix products, arithmetic and copies ran while one was open for 0% of the time, Pallas kernels for 5%

profile of v12, /device:TPU:0, one launch (start us, length us, event | category | flops | bytes accessed | tf_op | source)
XLA Modules:
  0.0 44.0 jit_solution(18329293822368852422)
XLA Ops:
  0.0 3.7 %frame_states.1 = (bf16[1024,128]{1,0:T(8,128)(2,1)S(1)}, bf16[1024,128]{1,0:T(8,128)(2,1)S(1)}, bf16[2,1,80,2240]{3,2,1,0:T(8,128)(2,1)S(1)}) custom-call(bf16[480,2240]{1,0:T(8,128)(2,1)} %bitcast.7, bf16[480,2240]{1,0:T(8,128)(2,1)} %bitcast.8, bf16[480,2240]{1,0:T(8,128)(2,1)} %bitcast.9, bf16[480,2240]{1,0:T(8,128)(2,1)} %bitcast.10, ...), custom_call_target="tpu_custom_call" | custom-call | flops 240844800 | bytes 4300800 | tf_op jit(solution)/shard_map/frame_states/pallas_call | solution.py:128
  3.7 0.5 %collective-permute-start = (bf16[1024,128]{1,0:T(8,128)(2,1)S(1)}, bf16[1024,128]{1,0:T(8,128)(2,1)S(1)}, u32[]{:S(2)}, u32[]{:S(2)}) collective-permute-start(bf16[1024,128]{1,0:T(8,128)(2,1)S(1)} %get-tuple-element.24), channel_id=1, source_target_pairs={{0,1},{1,0},{2,3},{3,2},{4,5},{5,4},{6,7},{7,6},{8,9},{9,8},{10,11... | collective-permute-start | bytes 786440 | tf_op jit(solution)/shard_map/ppermute | solution.py:472
  4.3 1.2 %collective-permute-done.got_ref = bf16[1024,128]{1,0:T(8,128)(2,1)S(1)} collective-permute-done((bf16[1024,128]{1,0:T(8,128)(2,1)S(1)}, bf16[1024,128]{1,0:T(8,128)(2,1)S(1)}, u32[]{:S(2)}, u32[]{:S(2)}) %collective-permute-start) | collective-permute-done | bytes 262176 | tf_op jit(solution)/shard_map/ppermute | solution.py:472
  5.4 0.1 split_sum.1
  5.5 0.4 collective-permute-start.3
  5.9 2.7 %collective-permute-start.1 = (bf16[512,128]{1,0:T(8,128)(2,1)S(1)}, bf16[512,128]{1,0:T(8,128)(2,1)S(1)}, u32[]{:S(2)}, u32[]{:S(2)}) collective-permute-start(bf16[512,128]{1,0:T(8,128)(2,1)S(1)} %get-tuple-element.28), channel_id=1, source_target_pairs={{0,2},{2,0},{4,6},{6,4},{8,10},{10,8},{12,14},{14,12},{1,3},{3,1},... | collective-permute-start | bytes 393224 | tf_op jit(solution)/shard_map/ppermute | solution.py:468
  8.6 4.0 %collective-permute-done.1.refs_1_.partner_ref = bf16[512,128]{1,0:T(8,128)(2,1)S(1)} collective-permute-done((bf16[512,128]{1,0:T(8,128)(2,1)S(1)}, bf16[512,128]{1,0:T(8,128)(2,1)S(1)}, u32[]{:S(2)}, u32[]{:S(2)}) %collective-permute-start.1) | collective-permute-done | bytes 131104 | tf_op jit(solution)/shard_map/ppermute | solution.py:468
  12.7 1.9 %collective-permute-start.2 = (bf16[512,128]{1,0:T(8,128)(2,1)S(1)}, bf16[512,128]{1,0:T(8,128)(2,1)S(1)}, u32[]{:S(2)}, u32[]{:S(2)}) collective-permute-start(bf16[512,128]{1,0:T(8,128)(2,1)S(1)} %pair_sum.1.refs_0_), channel_id=1, source_target_pairs={{0,4},{2,6},{4,0},{6,2},{8,12},{10,14},{12,8},{14,10},{1,5},{3,7},... | collective-permute-start | bytes 393224 | tf_op jit(solution)/shard_map/ppermute | solution.py:468
  14.5 3.4 %collective-permute-done.2.refs_1_.refs_0_ = bf16[512,128]{1,0:T(8,128)(2,1)S(1)} collective-permute-done((bf16[512,128]{1,0:T(8,128)(2,1)S(1)}, bf16[512,128]{1,0:T(8,128)(2,1)S(1)}, u32[]{:S(2)}, u32[]{:S(2)}) %collective-permute-start.2) | collective-permute-done | bytes 131104 | tf_op jit(solution)/shard_map/ppermute | solution.py:468
  18.0 0.0 collective-permute-done.3.edge_ref
  18.0 2.6 %collective-permute-start.4 = (bf16[512,128]{1,0:T(8,128)(2,1)S(1)}, bf16[512,128]{1,0:T(8,128)(2,1)S(1)}, u32[]{:S(2)}, u32[]{:S(2)}) collective-permute-start(bf16[512,128]{1,0:T(8,128)(2,1)S(1)} %stride_sum.1), channel_id=1, source_target_pairs={{0,8},{2,10},{4,12},{6,14},{8,0},{10,2},{12,4},{14,6},{1,9},{3,11}... | collective-permute-start | bytes 393224 | tf_op jit(solution)/shard_map/ppermute | solution.py:468
  20.6 0.0 copy-start
  20.6 0.0 copy-start.1
  20.7 2.4 %prepare.1 = (bf16[560,2304]{1,0:T(8,128)(2,1)S(1)}, bf16[560,2240]{1,0:T(8,128)(2,1)S(1)}, f32[1,2240]{1,0:T(1,128)S(1)}) custom-call(bf16[480,2240]{1,0:T(8,128)(2,1)} %bitcast.12, bf16[480,2240]{1,0:T(8,128)(2,1)} %bitcast.14, bf16[2,1,80,2240]{3,2,1,0:T(8,128)(2,1)S(1)} %collective-permute-done.3.edge_ref, f32[1,2240]{1,0:T(1,128)S(1)} %broadcast_in_dim.3.gain_ref), custom_call_target="tpu_custom_call" | custom-call | flops 5017600 | bytes 10035200 | tf_op jit(solution)/shard_map/prepare/pallas_call | solution.py:184
  23.0 3.0 %collective-permute-done.4.refs_1_ = bf16[512,128]{1,0:T(8,128)(2,1)S(1)} collective-permute-done((bf16[512,128]{1,0:T(8,128)(2,1)S(1)}, bf16[512,128]{1,0:T(8,128)(2,1)S(1)}, u32[]{:S(2)}, u32[]{:S(2)}) %collective-permute-start.4) | collective-permute-done | bytes 131104 | tf_op jit(solution)/shard_map/ppermute | solution.py:468
  26.1 0.1 pair_sums.1
  26.2 1.1 %collective-permute-start.5 = (bf16[512,128]{1,0:T(8,128)(2,1)S(1)}, bf16[512,128]{1,0:T(8,128)(2,1)S(1)}, u32[]{:S(2)}, u32[]{:S(2)}) collective-permute-start(bf16[512,128]{1,0:T(8,128)(2,1)S(1)} %get-tuple-element.40), channel_id=1, source_target_pairs={{0,2},{2,0},{4,6},{6,4},{8,10},{10,8},{12,14},{14,12},{1,3},{3,1},... | collective-permute-start | bytes 393224 | tf_op jit(solution)/shard_map/ppermute | solution.py:468
  27.3 0.0 collective-permute-start.6
  27.3 4.0 %collective-permute-done.5.refs_1_ = bf16[512,128]{1,0:T(8,128)(2,1)S(1)} collective-permute-done((bf16[512,128]{1,0:T(8,128)(2,1)S(1)}, bf16[512,128]{1,0:T(8,128)(2,1)S(1)}, u32[]{:S(2)}, u32[]{:S(2)}) %collective-permute-start.5) | collective-permute-done | bytes 131104 | tf_op jit(solution)/shard_map/ppermute | solution.py:468
  31.2 0.0 collective-permute-start.7
  31.2 0.0 collective-permute-done.6.refs_2_
  31.3 1.3 %collective-permute-done.7.refs_3_ = bf16[512,128]{1,0:T(8,128)(2,1)S(1)} collective-permute-done((bf16[512,128]{1,0:T(8,128)(2,1)S(1)}, bf16[512,128]{1,0:T(8,128)(2,1)S(1)}, u32[]{:S(2)}, u32[]{:S(2)}) %collective-permute-start.7) | collective-permute-done | bytes 131104 | tf_op jit(solution)/shard_map/ppermute | solution.py:494
  32.6 0.0 copy-done.1
  32.6 11.4 %mix.1 = bf16[480,2240]{1,0:T(8,128)(2,1)} custom-call(bf16[560,2304]{1,0:T(8,128)(2,1)S(1)} %get-tuple-element.35.features_ref, bf16[560,2240]{1,0:T(8,128)(2,1)S(1)} %get-tuple-element.36.inputs_ref, f32[1,2240]{1,0:T(1,128)S(1)} %get-tuple-element.37.gain_ref, f32[9,2240]{1,0:T(8,128)S(1)} %copy-done, f32[9,2240]{1,0:T(8,128)S(1)} %copy-done.1, ...), custom_call_target="tpu_custom_call" | custom-call | flops 64512000 | bytes 6451200 | tf_op jit(solution)/shard_map/mix/pallas_call | solution.py:360
  (6 shorter events, 0.1 us)
Async XLA Ops:
  0.0 20.6 %copy-start.2 = (f32[2240]{0:T(1024)S(1)}, f32[2240]{0:T(1024)}, u32[]{:S(2)}) copy-start(f32[2240]{0:T(1024)} %param.11) | copy-start | bytes 26884
  3.7 1.7 %collective-permute-start = (bf16[1024,128]{1,0:T(8,128)(2,1)S(1)}, bf16[1024,128]{1,0:T(8,128)(2,1)S(1)}, u32[]{:S(2)}, u32[]{:S(2)}) collective-permute-start(bf16[1024,128]{1,0:T(8,128)(2,1)S(1)} %get-tuple-element.24), channel_id=1, source_target_pairs={{0,1},{1,0},{2,3},{3,2},{4,5},{5,4},{6,7},{7,6},{8,9},{9,8},{10,11... | collective-permute-start | bytes 786440 | tf_op jit(solution)/shard_map/ppermute | solution.py:472
  5.5 12.5 %collective-permute-start.3 = (bf16[2,1,80,2240]{3,2,1,0:T(8,128)(2,1)S(1)}, bf16[2,1,80,2240]{3,2,1,0:T(8,128)(2,1)S(1)}, u32[]{:S(2)}, u32[]{:S(2)}) collective-permute-start(bf16[2,1,80,2240]{3,2,1,0:T(8,128)(2,1)S(1)} %get-tuple-element.29), channel_id=1, source_target_pairs={{0,1},{1,0},{2,3},{3,2},{4,5},{5,4},{6,7},{7,6},{8,9},{9,8},{10,11... | collective-permute-start | bytes 2150408 | tf_op jit(solution)/shard_map/ppermute | solution.py:476
  5.9 6.7 %collective-permute-start.1 = (bf16[512,128]{1,0:T(8,128)(2,1)S(1)}, bf16[512,128]{1,0:T(8,128)(2,1)S(1)}, u32[]{:S(2)}, u32[]{:S(2)}) collective-permute-start(bf16[512,128]{1,0:T(8,128)(2,1)S(1)} %get-tuple-element.28), channel_id=1, source_target_pairs={{0,2},{2,0},{4,6},{6,4},{8,10},{10,8},{12,14},{14,12},{1,3},{3,1},... | collective-permute-start | bytes 393224 | tf_op jit(solution)/shard_map/ppermute | solution.py:468
  12.7 5.3 %collective-permute-start.2 = (bf16[512,128]{1,0:T(8,128)(2,1)S(1)}, bf16[512,128]{1,0:T(8,128)(2,1)S(1)}, u32[]{:S(2)}, u32[]{:S(2)}) collective-permute-start(bf16[512,128]{1,0:T(8,128)(2,1)S(1)} %pair_sum.1.refs_0_), channel_id=1, source_target_pairs={{0,4},{2,6},{4,0},{6,2},{8,12},{10,14},{12,8},{14,10},{1,5},{3,7},... | collective-permute-start | bytes 393224 | tf_op jit(solution)/shard_map/ppermute | solution.py:468
  18.0 8.1 %collective-permute-start.4 = (bf16[512,128]{1,0:T(8,128)(2,1)S(1)}, bf16[512,128]{1,0:T(8,128)(2,1)S(1)}, u32[]{:S(2)}, u32[]{:S(2)}) collective-permute-start(bf16[512,128]{1,0:T(8,128)(2,1)S(1)} %stride_sum.1), channel_id=1, source_target_pairs={{0,8},{2,10},{4,12},{6,14},{8,0},{10,2},{12,4},{14,6},{1,9},{3,11}... | collective-permute-start | bytes 393224 | tf_op jit(solution)/shard_map/ppermute | solution.py:468
  20.6 12.0 %copy-start = (f32[9,2240]{1,0:T(8,128)S(1)}, f32[9,2240]{1,0:T(8,128)}, u32[]{:S(2)}) copy-start(f32[9,2240]{1,0:T(8,128)} %vtaps_ref.1) | copy-start | bytes 241924
  20.6 12.0 %copy-start.1 = (f32[9,2240]{1,0:T(8,128)S(1)}, f32[9,2240]{1,0:T(8,128)}, u32[]{:S(2)}) copy-start(f32[9,2240]{1,0:T(8,128)} %gtaps_ref.1) | copy-start | bytes 241924
  26.2 5.0 %collective-permute-start.5 = (bf16[512,128]{1,0:T(8,128)(2,1)S(1)}, bf16[512,128]{1,0:T(8,128)(2,1)S(1)}, u32[]{:S(2)}, u32[]{:S(2)}) collective-permute-start(bf16[512,128]{1,0:T(8,128)(2,1)S(1)} %get-tuple-element.40), channel_id=1, source_target_pairs={{0,2},{2,0},{4,6},{6,4},{8,10},{10,8},{12,14},{14,12},{1,3},{3,1},... | collective-permute-start | bytes 393224 | tf_op jit(solution)/shard_map/ppermute | solution.py:468
  27.3 4.0 %collective-permute-start.6 = (bf16[512,128]{1,0:T(8,128)(2,1)S(1)}, bf16[512,128]{1,0:T(8,128)(2,1)S(1)}, u32[]{:S(2)}, u32[]{:S(2)}) collective-permute-start(bf16[512,128]{1,0:T(8,128)(2,1)S(1)} %get-tuple-element.39.refs_0_), channel_id=1, source_target_pairs={{0,1},{1,0},{2,3},{3,2},{4,5},{5,4},{6,7},{7,6},{8,9},{9,8},{10,11... | collective-permute-start | bytes 393224 | tf_op jit(solution)/shard_map/ppermute | solution.py:494
  31.2 1.3 %collective-permute-start.7 = (bf16[512,128]{1,0:T(8,128)(2,1)S(1)}, bf16[512,128]{1,0:T(8,128)(2,1)S(1)}, u32[]{:S(2)}, u32[]{:S(2)}) collective-permute-start(bf16[512,128]{1,0:T(8,128)(2,1)S(1)} %collective-permute-done.5.refs_1_), channel_id=1, source_target_pairs={{0,1},{1,0},{2,3},{3,2},{4,5},{5,4},{6,7},{7,6},{8,9},{9,8},{10,11... | collective-permute-start | bytes 393224 | tf_op jit(solution)/shard_map/ppermute | solution.py:494

commit v13 on v12

--- a/solution.py
+++ b/solution.py
@@ -12,6 +12,7 @@
 LANES = 128
 GROUP = math.lcm(HEAD_DIM, LANES)
 TILES = GROUP // LANES
+HEADS = GROUP // HEAD_DIM
 
 
 def cdiv(a, b):
@@ -152,29 +153,44 @@
 
 def prepare_kernel(
     dim, queries_ref, residual_ref, edge_ref, gain_ref,
-    features_ref, inputs_ref, scaled_ref, held, semaphores,
+    features_ref, inputs_ref, heads_ref, spread_ref, held, semaphores,
 ):
     tokens = queries_ref.shape[0]
     full = dim // LANES * LANES
     parts = [slice(0, full), slice(full, dim)] if full < dim else [slice(0, dim)]
     copies = [
-        pltpu.make_async_copy(queries_ref, held.at[:tokens], semaphores.at[0]),
-        pltpu.make_async_copy(residual_ref, inputs_ref.at[:tokens], semaphores.at[1]),
+        pltpu.make_async_copy(source, held.at[k, :tokens], semaphores.at[k])
+        for k, source in enumerate((queries_ref, residual_ref))
     ]
     for copy in copies:
         copy.start()
     edges, width = edge_ref.shape[1:3]
     for e in range(edges):
         here = slice(tokens + e * width, tokens + (e + 1) * width)
-        held[here] = edge_ref[0, e]
-        inputs_ref[here] = edge_ref[1, e]
-    scaled_ref[...] = gain_ref[...] * math.sqrt(HEAD_DIM)
+        held[0, here] = edge_ref[0, e]
+        held[1, here] = edge_ref[1, e]
+    head = lax.rem(lane_iota((GROUP, LANES)), HEADS)
+    lane = lax.broadcasted_iota(jnp.int32, (GROUP, LANES), 0) - head * HEAD_DIM
+    inside = (lane >= 0) & (lane < HEAD_DIM) & (lane_iota((GROUP, LANES)) < 3 * HEADS)
+    heads_ref[...] = jnp.where(inside, 1.0, 0.0).astype(jnp.bfloat16)
+    spread_ref[...] = jnp.zeros_like(spread_ref)
+    used = cdiv(3 * HEADS, 16) * 16
+    for group, (base, lanes) in enumerate(group_lanes(dim)):
+        row = lax.broadcasted_iota(jnp.int32, (used, lanes), 0)
+        lane = lane_iota((used, lanes)) - lax.rem(row, HEADS) * HEAD_DIM
+        inside = (lane >= 0) & (lane < HEAD_DIM) & (row < 3 * HEADS)
+        scaled = gain_ref[:, base : base + lanes] * math.sqrt(HEAD_DIM)
+        coarse = scaled.astype(jnp.bfloat16).astype(jnp.float32)
+        value = jnp.where((row >= HEADS) & (row < 2 * HEADS), scaled - coarse, coarse)
+        spread_ref[group, :used, :lanes] = jnp.where(inside, value, 0.0).astype(jnp.bfloat16)
     if full < dim:
         features_ref[:, full:] = jnp.zeros((features_ref.shape[0], LANES), jnp.bfloat16)
     copies[0].wait()
     for part in parts:
-        features_ref[:, part] = jnp.maximum(held[:, part], 0)
+        features_ref[:, part] = jnp.maximum(held[0, :, part], 0)
     copies[1].wait()
+    for part in parts:
+        inputs_ref[:, part] = held[1, :, part].astype(jnp.float32)
 
 
 def prepare(queries, residual, edge, gain):
@@ -185,13 +201,14 @@
         functools.partial(prepare_kernel, dim),
         out_shape=[
             pltpu.VMEM((total, cdiv(dim, LANES) * LANES), jnp.bfloat16),
-            pltpu.VMEM((total, dim), jnp.bfloat16),
-            pltpu.VMEM((1, dim), jnp.float32),
+            pltpu.VMEM((total, dim), jnp.float32),
+            pltpu.VMEM((GROUP, LANES), jnp.bfloat16),
+            pltpu.VMEM((len(group_lanes(dim)), LANES, GROUP), jnp.bfloat16),
         ],
         in_specs=[pl.BlockSpec(memory_space=pl.ANY)] * 2 + [whole] * 2,
-        out_specs=[whole] * 3,
+        out_specs=[whole] * 4,
         scratch_shapes=[
-            pltpu.VMEM((total, dim), jnp.bfloat16),
+            pltpu.VMEM((2, total, dim), jnp.bfloat16),
             pltpu.SemaphoreType.DMA((2,)),
         ],
         compiler_params=pltpu.CompilerParams(vmem_limit_bytes=24 * 2**20),
@@ -204,13 +221,15 @@
 
 def mix_kernel(
     dim, rows, width, edges,
-    features_ref, inputs_ref, gain_ref, vtaps_ref, gtaps_ref, *refs,
+    features_ref, inputs_ref, heads_ref, spread_ref, vtaps_ref, gtaps_ref, *refs,
 ):
-    *pieces, out_ref, states, weights, numer, rounded, windows, results, held, semaphores = refs
+    *pieces, out_ref, states, weights, numer, squares, mixed, windows, results, held, semaphores = refs
     places = edge_places(lax.axis_size("space"), rows) if edges else []
     spots = piece_places() if len(pieces) > 1 else [0]
     tokens = rows * width
     weights[...] = jnp.zeros_like(weights)
+    for row in (0, rows + 1):
+        windows[:, :, row] = jnp.zeros((2, 4, width // 2, LANES), jnp.float32)
     for k, piece in enumerate(pieces):
         size = piece.shape[0]
         states[pl.ds(pl.multiple_of(spots[k] * size, 16), size), :] = piece[...]
@@ -220,15 +239,15 @@
     half = width // 2
     even, odd = pl.ds(0, half, stride=2), pl.ds(1, half, stride=2)
 
-    def store_windows(mixed, row, slot, used):
-        rounded[slot, row, :, :used] = mixed.astype(jnp.bfloat16).astype(jnp.float32)
-        left, right = rounded[slot, row, even, :used], rounded[slot, row, odd, :used]
+    def store_windows(value, slot, used, row, place):
+        mixed[slot, row, :, :used] = value
+        left, right = mixed[slot, row, even, :used], mixed[slot, row, odd, :used]
         sub = sublane[:, :used]
         before, after = pltpu.roll(right, 1, 0), pltpu.roll(left, half - 1, 0)
         before = jnp.concatenate([jnp.where(sub == 0, 0.0, before[:8]), before[8:]], axis=0)
         after = jnp.concatenate([after[: half - 8], jnp.where(sub == 7, 0.0, after[half - 8 :])], axis=0)
         for k, window in enumerate((before - right, left + right, right - left, left - after)):
-            windows[slot, k, row, :, :used] = window
+            windows[slot, k, place, :, :used] = window
 
     def group(base, lanes):
         pairs = spans(lanes)
@@ -252,49 +271,21 @@
             )
             here = slice(tiles[0] * LANES, tiles[0] * LANES + wide)
             numer[:, here] = product
-
-        def tile_sums(j, source):
-            square = numer[source, j * LANES : (j + 1) * LANES]
-            square = square * square
-            heads = tile_heads(j, lanes)
-            if len(heads) == 1:
-                return {heads[0][0]: jnp.sum(square, axis=-1, keepdims=True)}
-            (one, _, bound), (two, _, _) = heads
-            part = jnp.where(lane_iota(square.shape) < bound, square, 0.0)
-            rest = square - part
-            return {
-                one: jnp.sum(part, axis=-1, keepdims=True),
-                two: jnp.sum(rest, axis=-1, keepdims=True),
-            }
-
-        def mix_tile(j):
+            squares[:, here] = (product * product).astype(jnp.bfloat16)
+
+        def mix_tile(j, scale):
             slot = j % 2
             used = min(LANES, lanes - j * LANES)
             near = slice(j * LANES, j * LANES + used)
             here = slice(base + j * LANES, base + j * LANES + used)
-            heads = tile_heads(j, lanes)
-
-            def mixed(source):
-                sums = [
-                    sum(tiles[head] for tiles in parts[source.start] if head in tiles)
-                    for head, _, _ in heads
-                ]
-                scale = jnp.broadcast_to(sums[0], (width, used))
-                if len(heads) > 1:
-                    scale = jnp.where(lane_iota(scale.shape) < heads[0][2], scale, sums[1])
-                normed = numer[source, near] * lax.rsqrt(scale + HEAD_DIM * 1e-06)
-                return inputs_ref[source, here].astype(jnp.float32) + normed * gain_ref[:, here]
-
-            outside = [None, None]
-            for e in range(edges):
-                value = mixed(slice(tokens + e * width, tokens + (e + 1) * width))
-                for k, row in enumerate((0, rows + 1)):
-                    part = jnp.where(places[e] == row, value, 0.0)
-                    outside[k] = part if outside[k] is None else outside[k] + part
-            for k, row in enumerate((0, rows + 1)):
-                store_windows(outside[k], row, slot, used)
-            for row in range(rows):
-                store_windows(mixed(slice(row * width, (row + 1) * width)), row + 1, slot, used)
+            for row in range(rows + edges):
+                source = slice(row * width, (row + 1) * width)
+                value = inputs_ref[source, here] + numer[source, near] * scale[source, :used]
+                if row < rows:
+                    store_windows(value, slot, used, row + 1, row + 1)
+                else:
+                    edge = row - rows
+                    store_windows(value, slot, used, edge * (rows + 1), places[edge])
             taps = []
             for ref, factor in ((vtaps_ref, 1.0), (gtaps_ref, 0.5)):
                 for tap_row in range(3):
@@ -320,7 +311,7 @@
                         )
                     )
                 for side, (conv_v, half_g) in zip((even, odd), zip(*columns)):
-                    center = rounded[slot, row + 1, side, :used]
+                    center = mixed[slot, row + 1, side, :used]
                     results[slot, row, side, :used] = center + conv_v * (
                         half_g + half_g * jnp.tanh(half_g)
                     )
@@ -328,15 +319,25 @@
                     jnp.bfloat16
                 )
 
-        parts = {}
-        for number, (tiles, _, _) in enumerate(pairs):
+        for number in range(len(pairs)):
             numerators(number)
-            for j in tiles:
-                for row in range(rows + edges):
-                    source = slice(row * width, (row + 1) * width)
-                    parts.setdefault(source.start, []).append(tile_sums(j, source))
-        for j in range(cdiv(lanes, LANES)):
-            mix_tile(j)
+        depth = cdiv(lanes, LANES) * LANES
+        sums = jnp.dot(
+            squares[:, :depth], heads_ref[:depth, :], preferred_element_type=jnp.float32
+        )
+        scale = lax.rsqrt(sums + HEAD_DIM * 1e-06)
+        coarse = scale.astype(jnp.bfloat16).astype(jnp.float32)
+        terms = jnp.where(lane_iota(scale.shape) < 2 * HEADS, coarse, scale - coarse)
+        terms = terms.astype(jnp.bfloat16)
+        for tiles, _, _ in pairs:
+            here = slice(tiles[0] * LANES, (tiles[-1] + 1) * LANES)
+            spread = jnp.dot(
+                terms,
+                spread_ref[base // GROUP, :, here],
+                preferred_element_type=jnp.float32,
+            )
+            for side, j in enumerate(tiles):
+                mix_tile(j, spread[:, side * LANES : (side + 1) * LANES])
 
     copies = []
     for base, lanes in group_lanes(dim):
@@ -351,7 +352,7 @@
 
 
 def mix(prepared, value_taps, gate_taps, pieces, rows, width):
-    features, inputs, gain = prepared
+    features, inputs, heads, spread = prepared
     total, dim = inputs.shape
     tokens = rows * width
     pairs = spans(min(GROUP, dim))
@@ -360,24 +361,25 @@
     return pl.pallas_call(
         functools.partial(mix_kernel, dim, rows, width, (total - tokens) // width),
         out_shape=jax.ShapeDtypeStruct((tokens, dim), jnp.bfloat16),
-        in_specs=[whole] * (5 + len(pieces)),
+        in_specs=[whole] * (6 + len(pieces)),
         out_specs=pl.BlockSpec(memory_space=pl.ANY),
         scratch_shapes=[
             pltpu.VMEM((sum(piece.shape[0] for piece in pieces), LANES), jnp.bfloat16),
             pltpu.VMEM((len(pairs), depth, 2 * LANES), jnp.bfloat16),
             pltpu.VMEM((total, GROUP), jnp.float32),
+            pltpu.VMEM((total, GROUP), jnp.bfloat16),
             pltpu.VMEM((2, rows + 2, width, LANES), jnp.float32),
             pltpu.VMEM((2, 4, rows + 2, width // 2, LANES), jnp.float32),
             pltpu.VMEM((2, rows, width, LANES), jnp.float32),
             pltpu.VMEM((tokens, dim), jnp.bfloat16),
             pltpu.SemaphoreType.DMA((len(group_lanes(dim)),)),
         ],
-        compiler_params=pltpu.CompilerParams(vmem_limit_bytes=36 * 2**20),
+        compiler_params=pltpu.CompilerParams(vmem_limit_bytes=28 * 2**20),
         cost_estimate=pl.CostEstimate(
             flops=60 * tokens * dim, bytes_accessed=6 * tokens * dim, transcendentals=2 * tokens * dim
         ),
         name="mix",
-    )(features, inputs, gain, value_taps, gate_taps, *pieces)
+    )(features, inputs, heads, spread, value_taps, gate_taps, *pieces)
 
 
 def edge_rows(queries, residual):

time: 44.1 us -> 44.3 us (level)
  transfers between devices with their start and end apart: 8 -> 8, of which waited for: 6 -> 6; matrix products, arithmetic and copies ran while one was open for 0% -> 0% of each run, Pallas kernels for 5% -> 6%
where the time goes in v13:
time: 44.3 us; the launch traced here: 44.1 us
  Pallas kernels  18.2 us (41%)
  waiting for transfers between devices  16.6 us (37%)
  starting transfers between devices  9.21 us (21%)
    ppermute x4, waiting for transfers between devices, running_states(): lax.ppermute(array, 'frame', [(f, f ^ stride) for f in range(frames)])  14.1 us
    pallas_call x1, Pallas kernels, mix(): pl.pallas_call(functools.partial(mix_kernel, dim, rows, width, (total - t...  11.5 us
    ppermute x4, starting transfers between devices, running_states(): lax.ppermute(array, 'frame', [(f, f ^ stride) for f in range(frames)])  8.24 us
    pallas_call x1, Pallas kernels, frame_states(): pl.pallas_call(body, out_shape=[pltpu.VMEM(part, jnp.bfloat16)] * parts +...  3.73 us
    pallas_call x1, Pallas kernels, prepare(): pl.pallas_call(functools.partial(prepare_kernel, dim), out_shape=[pltpu.V...  2.69 us
    ppermute x1, waiting for transfers between devices, running_states(): lax.ppermute(other, 'space', swap)  1.34 us
    ppermute x1, waiting for transfers between devices, running_states(): got = lax.ppermute(sent, 'space', swap)  1.16 us
  transfers between devices with their start and end apart: 8, of which 6 were waited for; matrix products, arithmetic and copies ran while one was open for 0% of the time, Pallas kernels for 6%

profile of v13, /device:TPU:0, one launch (start us, length us, event | category | flops | bytes accessed | tf_op | source)
XLA Modules:
  0.0 44.1 jit_solution(9777586412435111057)
XLA Ops:
  0.0 3.7 %frame_states.1 = (bf16[1024,128]{1,0:T(8,128)(2,1)S(1)}, bf16[1024,128]{1,0:T(8,128)(2,1)S(1)}, bf16[2,1,80,2240]{3,2,1,0:T(8,128)(2,1)S(1)}) custom-call(bf16[480,2240]{1,0:T(8,128)(2,1)} %bitcast.7, bf16[480,2240]{1,0:T(8,128)(2,1)} %bitcast.8, bf16[480,2240]{1,0:T(8,128)(2,1)} %bitcast.9, bf16[480,2240]{1,0:T(8,128)(2,1)} %bitcast.10, ...), custom_call_target="tpu_custom_call" | custom-call | flops 240844800 | bytes 4300800 | tf_op jit(solution)/shard_map/frame_states/pallas_call | solution.py:129
  3.7 0.5 %collective-permute-start = (bf16[1024,128]{1,0:T(8,128)(2,1)S(1)}, bf16[1024,128]{1,0:T(8,128)(2,1)S(1)}, u32[]{:S(2)}, u32[]{:S(2)}) collective-permute-start(bf16[1024,128]{1,0:T(8,128)(2,1)S(1)} %get-tuple-element.26), channel_id=1, source_target_pairs={{0,1},{1,0},{2,3},{3,2},{4,5},{5,4},{6,7},{7,6},{8,9},{9,8},{10,11... | collective-permute-start | bytes 786440 | tf_op jit(solution)/shard_map/ppermute | solution.py:474
  4.3 1.2 %collective-permute-done.got_ref = bf16[1024,128]{1,0:T(8,128)(2,1)S(1)} collective-permute-done((bf16[1024,128]{1,0:T(8,128)(2,1)S(1)}, bf16[1024,128]{1,0:T(8,128)(2,1)S(1)}, u32[]{:S(2)}, u32[]{:S(2)}) %collective-permute-start) | collective-permute-done | bytes 262176 | tf_op jit(solution)/shard_map/ppermute | solution.py:474
  5.4 0.1 split_sum.1
  5.5 0.4 collective-permute-start.3
  5.9 2.7 %collective-permute-start.1 = (bf16[512,128]{1,0:T(8,128)(2,1)S(1)}, bf16[512,128]{1,0:T(8,128)(2,1)S(1)}, u32[]{:S(2)}, u32[]{:S(2)}) collective-permute-start(bf16[512,128]{1,0:T(8,128)(2,1)S(1)} %get-tuple-element.30), channel_id=1, source_target_pairs={{0,2},{2,0},{4,6},{6,4},{8,10},{10,8},{12,14},{14,12},{1,3},{3,1},... | collective-permute-start | bytes 393224 | tf_op jit(solution)/shard_map/ppermute | solution.py:470
  8.6 4.0 %collective-permute-done.1.refs_1_.partner_ref = bf16[512,128]{1,0:T(8,128)(2,1)S(1)} collective-permute-done((bf16[512,128]{1,0:T(8,128)(2,1)S(1)}, bf16[512,128]{1,0:T(8,128)(2,1)S(1)}, u32[]{:S(2)}, u32[]{:S(2)}) %collective-permute-start.1) | collective-permute-done | bytes 131104 | tf_op jit(solution)/shard_map/ppermute | solution.py:470
  12.7 1.9 %collective-permute-start.2 = (bf16[512,128]{1,0:T(8,128)(2,1)S(1)}, bf16[512,128]{1,0:T(8,128)(2,1)S(1)}, u32[]{:S(2)}, u32[]{:S(2)}) collective-permute-start(bf16[512,128]{1,0:T(8,128)(2,1)S(1)} %pair_sum.1.refs_0_), channel_id=1, source_target_pairs={{0,4},{2,6},{4,0},{6,2},{8,12},{10,14},{12,8},{14,10},{1,5},{3,7},... | collective-permute-start | bytes 393224 | tf_op jit(solution)/shard_map/ppermute | solution.py:470
  14.5 3.4 %collective-permute-done.2.refs_1_.refs_0_ = bf16[512,128]{1,0:T(8,128)(2,1)S(1)} collective-permute-done((bf16[512,128]{1,0:T(8,128)(2,1)S(1)}, bf16[512,128]{1,0:T(8,128)(2,1)S(1)}, u32[]{:S(2)}, u32[]{:S(2)}) %collective-permute-start.2) | collective-permute-done | bytes 131104 | tf_op jit(solution)/shard_map/ppermute | solution.py:470
  18.0 0.0 collective-permute-done.3.edge_ref
  18.0 2.6 %collective-permute-start.4 = (bf16[512,128]{1,0:T(8,128)(2,1)S(1)}, bf16[512,128]{1,0:T(8,128)(2,1)S(1)}, u32[]{:S(2)}, u32[]{:S(2)}) collective-permute-start(bf16[512,128]{1,0:T(8,128)(2,1)S(1)} %stride_sum.1), channel_id=1, source_target_pairs={{0,8},{2,10},{4,12},{6,14},{8,0},{10,2},{12,4},{14,6},{1,9},{3,11}... | collective-permute-start | bytes 393224 | tf_op jit(solution)/shard_map/ppermute | solution.py:470
  20.6 0.0 copy-start
  20.6 0.0 copy-start.1
  20.7 2.7 %prepare.1 = (bf16[560,2304]{1,0:T(8,128)(2,1)S(1)}, f32[560,2240]{1,0:T(8,128)S(1)}, bf16[896,128]{1,0:T(8,128)(2,1)S(1)}, bf16[3,128,896]{2,1,0:T(8,128)(2,1)S(1)}) custom-call(bf16[480,2240]{1,0:T(8,128)(2,1)} %bitcast.12, bf16[480,2240]{1,0:T(8,128)(2,1)} %bitcast.14, bf16[2,1,80,2240]{3,2,1,0:T(8,128)(2,1)S(1)} %collective-permute-done.3.edge_ref, ...), custom_call_target="tpu_custom_call" | custom-call | flops 5017600 | bytes 10035200 | tf_op jit(solution)/shard_map/prepare/pallas_call | solution.py:200
  23.3 2.7 %collective-permute-done.4.refs_1_ = bf16[512,128]{1,0:T(8,128)(2,1)S(1)} collective-permute-done((bf16[512,128]{1,0:T(8,128)(2,1)S(1)}, bf16[512,128]{1,0:T(8,128)(2,1)S(1)}, u32[]{:S(2)}, u32[]{:S(2)}) %collective-permute-start.4) | collective-permute-done | bytes 131104 | tf_op jit(solution)/shard_map/ppermute | solution.py:470
  26.1 0.1 pair_sums.1
  26.2 1.1 %collective-permute-start.5 = (bf16[512,128]{1,0:T(8,128)(2,1)S(1)}, bf16[512,128]{1,0:T(8,128)(2,1)S(1)}, u32[]{:S(2)}, u32[]{:S(2)}) collective-permute-start(bf16[512,128]{1,0:T(8,128)(2,1)S(1)} %get-tuple-element.44), channel_id=1, source_target_pairs={{0,2},{2,0},{4,6},{6,4},{8,10},{10,8},{12,14},{14,12},{1,3},{3,1},... | collective-permute-start | bytes 393224 | tf_op jit(solution)/shard_map/ppermute | solution.py:470
  27.3 0.0 collective-permute-start.6
  27.3 4.0 %collective-permute-done.5.refs_1_ = bf16[512,128]{1,0:T(8,128)(2,1)S(1)} collective-permute-done((bf16[512,128]{1,0:T(8,128)(2,1)S(1)}, bf16[512,128]{1,0:T(8,128)(2,1)S(1)}, u32[]{:S(2)}, u32[]{:S(2)}) %collective-permute-start.5) | collective-permute-done | bytes 131104 | tf_op jit(solution)/shard_map/ppermute | solution.py:470
  31.2 0.0 collective-permute-start.7
  31.2 0.0 collective-permute-done.6.refs_2_
  31.3 1.3 %collective-permute-done.7.refs_3_ = bf16[512,128]{1,0:T(8,128)(2,1)S(1)} collective-permute-done((bf16[512,128]{1,0:T(8,128)(2,1)S(1)}, bf16[512,128]{1,0:T(8,128)(2,1)S(1)}, u32[]{:S(2)}, u32[]{:S(2)}) %collective-permute-start.7) | collective-permute-done | bytes 131104 | tf_op jit(solution)/shard_map/ppermute | solution.py:496
  32.6 0.0 copy-done
  32.6 11.5 %mix.1 = bf16[480,2240]{1,0:T(8,128)(2,1)} custom-call(bf16[560,2304]{1,0:T(8,128)(2,1)S(1)} %get-tuple-element.38.features_ref, f32[560,2240]{1,0:T(8,128)S(1)} %get-tuple-element.39.inputs_ref, bf16[896,128]{1,0:T(8,128)(2,1)S(1)} %get-tuple-element.40.heads_ref, bf16[3,128,896]{2,1,0:T(8,128)(2,1)S(1)} %get-tuple-element.41.spread_ref, ...), custom_call_target="tpu_custom_call" | custom-call | flops 64512000 | bytes 6451200 | tf_op jit(solution)/shard_map/mix/pallas_call | solution.py:361
  (6 shorter events, 0.1 us)
Async XLA Ops:
  0.0 20.6 %copy-start.2 = (f32[2240]{0:T(1024)S(1)}, f32[2240]{0:T(1024)}, u32[]{:S(2)}) copy-start(f32[2240]{0:T(1024)} %param.11) | copy-start | bytes 26884
  3.7 1.7 %collective-permute-start = (bf16[1024,128]{1,0:T(8,128)(2,1)S(1)}, bf16[1024,128]{1,0:T(8,128)(2,1)S(1)}, u32[]{:S(2)}, u32[]{:S(2)}) collective-permute-start(bf16[1024,128]{1,0:T(8,128)(2,1)S(1)} %get-tuple-element.26), channel_id=1, source_target_pairs={{0,1},{1,0},{2,3},{3,2},{4,5},{5,4},{6,7},{7,6},{8,9},{9,8},{10,11... | collective-permute-start | bytes 786440 | tf_op jit(solution)/shard_map/ppermute | solution.py:474
  5.5 12.5 %collective-permute-start.3 = (bf16[2,1,80,2240]{3,2,1,0:T(8,128)(2,1)S(1)}, bf16[2,1,80,2240]{3,2,1,0:T(8,128)(2,1)S(1)}, u32[]{:S(2)}, u32[]{:S(2)}) collective-permute-start(bf16[2,1,80,2240]{3,2,1,0:T(8,128)(2,1)S(1)} %get-tuple-element.31), channel_id=1, source_target_pairs={{0,1},{1,0},{2,3},{3,2},{4,5},{5,4},{6,7},{7,6},{8,9},{9,8},{10,11... | collective-permute-start | bytes 2150408 | tf_op jit(solution)/shard_map/ppermute | solution.py:478
  5.9 6.7 %collective-permute-start.1 = (bf16[512,128]{1,0:T(8,128)(2,1)S(1)}, bf16[512,128]{1,0:T(8,128)(2,1)S(1)}, u32[]{:S(2)}, u32[]{:S(2)}) collective-permute-start(bf16[512,128]{1,0:T(8,128)(2,1)S(1)} %get-tuple-element.30), channel_id=1, source_target_pairs={{0,2},{2,0},{4,6},{6,4},{8,10},{10,8},{12,14},{14,12},{1,3},{3,1},... | collective-permute-start | bytes 393224 | tf_op jit(solution)/shard_map/ppermute | solution.py:470
  12.7 5.3 %collective-permute-start.2 = (bf16[512,128]{1,0:T(8,128)(2,1)S(1)}, bf16[512,128]{1,0:T(8,128)(2,1)S(1)}, u32[]{:S(2)}, u32[]{:S(2)}) collective-permute-start(bf16[512,128]{1,0:T(8,128)(2,1)S(1)} %pair_sum.1.refs_0_), channel_id=1, source_target_pairs={{0,4},{2,6},{4,0},{6,2},{8,12},{10,14},{12,8},{14,10},{1,5},{3,7},... | collective-permute-start | bytes 393224 | tf_op jit(solution)/shard_map/ppermute | solution.py:470
  18.0 8.1 %collective-permute-start.4 = (bf16[512,128]{1,0:T(8,128)(2,1)S(1)}, bf16[512,128]{1,0:T(8,128)(2,1)S(1)}, u32[]{:S(2)}, u32[]{:S(2)}) collective-permute-start(bf16[512,128]{1,0:T(8,128)(2,1)S(1)} %stride_sum.1), channel_id=1, source_target_pairs={{0,8},{2,10},{4,12},{6,14},{8,0},{10,2},{12,4},{14,6},{1,9},{3,11}... | collective-permute-start | bytes 393224 | tf_op jit(solution)/shard_map/ppermute | solution.py:470
  20.6 12.0 %copy-start = (f32[9,2240]{1,0:T(8,128)S(1)}, f32[9,2240]{1,0:T(8,128)}, u32[]{:S(2)}) copy-start(f32[9,2240]{1,0:T(8,128)} %vtaps_ref.1) | copy-start | bytes 241924
  20.6 12.0 %copy-start.1 = (f32[9,2240]{1,0:T(8,128)S(1)}, f32[9,2240]{1,0:T(8,128)}, u32[]{:S(2)}) copy-start(f32[9,2240]{1,0:T(8,128)} %gtaps_ref.1) | copy-start | bytes 241924
  26.2 5.0 %collective-permute-start.5 = (bf16[512,128]{1,0:T(8,128)(2,1)S(1)}, bf16[512,128]{1,0:T(8,128)(2,1)S(1)}, u32[]{:S(2)}, u32[]{:S(2)}) collective-permute-start(bf16[512,128]{1,0:T(8,128)(2,1)S(1)} %get-tuple-element.44), channel_id=1, source_target_pairs={{0,2},{2,0},{4,6},{6,4},{8,10},{10,8},{12,14},{14,12},{1,3},{3,1},... | collective-permute-start | bytes 393224 | tf_op jit(solution)/shard_map/ppermute | solution.py:470
  27.3 4.0 %collective-permute-start.6 = (bf16[512,128]{1,0:T(8,128)(2,1)S(1)}, bf16[512,128]{1,0:T(8,128)(2,1)S(1)}, u32[]{:S(2)}, u32[]{:S(2)}) collective-permute-start(bf16[512,128]{1,0:T(8,128)(2,1)S(1)} %get-tuple-element.43.refs_0_), channel_id=1, source_target_pairs={{0,1},{1,0},{2,3},{3,2},{4,5},{5,4},{6,7},{7,6},{8,9},{9,8},{10,11... | collective-permute-start | bytes 393224 | tf_op jit(solution)/shard_map/ppermute | solution.py:496
  31.2 1.3 %collective-permute-start.7 = (bf16[512,128]{1,0:T(8,128)(2,1)S(1)}, bf16[512,128]{1,0:T(8,128)(2,1)S(1)}, u32[]{:S(2)}, u32[]{:S(2)}) collective-permute-start(bf16[512,128]{1,0:T(8,128)(2,1)S(1)} %collective-permute-done.5.refs_1_), channel_id=1, source_target_pairs={{0,1},{1,0},{2,3},{3,2},{4,5},{5,4},{6,7},{7,6},{8,9},{9,8},{10,11... | collective-permute-start | bytes 393224 | tf_op jit(solution)/shard_map/ppermute | solution.py:496

commit v14 on v13

--- a/solution.py
+++ b/solution.py
@@ -223,11 +223,11 @@
     dim, rows, width, edges,
     features_ref, inputs_ref, heads_ref, spread_ref, vtaps_ref, gtaps_ref, *refs,
 ):
-    *pieces, out_ref, states, weights, numer, squares, mixed, windows, results, held, semaphores = refs
+    *pieces, out_ref, states, weights, numer, squares, spreads, mixed, windows, results, held = refs[:-1]
+    semaphores = refs[-1]
     places = edge_places(lax.axis_size("space"), rows) if edges else []
     spots = piece_places() if len(pieces) > 1 else [0]
     tokens = rows * width
-    weights[...] = jnp.zeros_like(weights)
     for row in (0, rows + 1):
         windows[:, :, row] = jnp.zeros((2, 4, width // 2, LANES), jnp.float32)
     for k, piece in enumerate(pieces):
@@ -249,38 +249,62 @@
         for k, window in enumerate((before - right, left + right, right - left, left - after)):
             windows[slot, k, place, :, :used] = window
 
-    def group(base, lanes):
+    def group(base, lanes, turn):
         pairs = spans(lanes)
 
         def numerators(number):
             tiles, first, last = pairs[number]
+            depth, wide = (last - first) * LANES, len(tiles) * LANES
             for side, j in enumerate(tiles):
                 row = (base // LANES + j) * HEAD_DIM
                 state = states[row : row + HEAD_DIM, :].astype(jnp.float32)
-                for h, lo, hi in tile_heads(j, lanes):
-                    start = h * HEAD_DIM - first * LANES
-                    block = jnp.where((lane >= lo) & (lane < hi), state, 0.0)
-                    weights[
-                        number, start : start + HEAD_DIM, side * LANES : (side + 1) * LANES
-                    ] = block.astype(jnp.bfloat16)
-            depth, wide = (last - first) * LANES, len(tiles) * LANES
+                heads = tile_heads(j, lanes)
+                start = heads[0][0] * HEAD_DIM - first * LANES
+                blocks = [jnp.where((lane >= lo) & (lane < hi), state, 0.0) for _, lo, hi in heads]
+                rest = depth - start - len(heads) * HEAD_DIM
+                if start:
+                    blocks.insert(0, jnp.zeros((start, LANES), jnp.float32))
+                if rest:
+                    blocks.append(jnp.zeros((rest, LANES), jnp.float32))
+                weights[turn, number, :depth, side * LANES : (side + 1) * LANES] = jnp.concatenate(
+                    blocks, axis=0
+                ).astype(jnp.bfloat16)
             product = jnp.dot(
                 features_ref[:, base + first * LANES : base + last * LANES],
-                weights[number, :depth, :wide],
+                weights[turn, number, :depth, :wide],
                 preferred_element_type=jnp.float32,
             )
             here = slice(tiles[0] * LANES, tiles[0] * LANES + wide)
-            numer[:, here] = product
-            squares[:, here] = (product * product).astype(jnp.bfloat16)
-
-        def mix_tile(j, scale):
+            numer[turn, :, here] = product
+            squares[turn, :, here] = (product * product).astype(jnp.bfloat16)
+
+        terms = []
+
+        def scales():
+            depth = cdiv(lanes, LANES) * LANES
+            sums = jnp.dot(
+                squares[turn, :, :depth], heads_ref[:depth, :], preferred_element_type=jnp.float32
+            )
+            scale = lax.rsqrt(sums + HEAD_DIM * 1e-06)
+            coarse = scale.astype(jnp.bfloat16).astype(jnp.float32)
+            fine = jnp.where(lane_iota(scale.shape) < 2 * HEADS, coarse, scale - coarse)
+            terms.append(fine.astype(jnp.bfloat16))
+
+        def spread(number):
+            tiles, _, _ = pairs[number]
+            here = slice(tiles[0] * LANES, (tiles[-1] + 1) * LANES)
+            spreads[turn, :, here] = jnp.dot(
+                terms[0], spread_ref[base // GROUP, :, here], preferred_element_type=jnp.float32
+            )
+
+        def mix_tile(j):
             slot = j % 2
             used = min(LANES, lanes - j * LANES)
             near = slice(j * LANES, j * LANES + used)
             here = slice(base + j * LANES, base + j * LANES + used)
             for row in range(rows + edges):
                 source = slice(row * width, (row + 1) * width)
-                value = inputs_ref[source, here] + numer[source, near] * scale[source, :used]
+                value = inputs_ref[source, here] + numer[turn, source, near] * spreads[turn, source, near]
                 if row < rows:
                     store_windows(value, slot, used, row + 1, row + 1)
                 else:
@@ -319,32 +343,26 @@
                     jnp.bfloat16
                 )
 
-        for number in range(len(pairs)):
-            numerators(number)
-        depth = cdiv(lanes, LANES) * LANES
-        sums = jnp.dot(
-            squares[:, :depth], heads_ref[:depth, :], preferred_element_type=jnp.float32
-        )
-        scale = lax.rsqrt(sums + HEAD_DIM * 1e-06)
-        coarse = scale.astype(jnp.bfloat16).astype(jnp.float32)
-        terms = jnp.where(lane_iota(scale.shape) < 2 * HEADS, coarse, scale - coarse)
-        terms = terms.astype(jnp.bfloat16)
-        for tiles, _, _ in pairs:
-            here = slice(tiles[0] * LANES, (tiles[-1] + 1) * LANES)
-            spread = jnp.dot(
-                terms,
-                spread_ref[base // GROUP, :, here],
-                preferred_element_type=jnp.float32,
-            )
-            for side, j in enumerate(tiles):
-                mix_tile(j, spread[:, side * LANES : (side + 1) * LANES])
-
+        numbers = range(len(pairs))
+        ahead = [functools.partial(numerators, n) for n in numbers]
+        ahead += [scales] + [functools.partial(spread, n) for n in numbers]
+        return ahead, [functools.partial(mix_tile, j) for j in range(cdiv(lanes, LANES))]
+
+    order = sorted(group_lanes(dim), key=lambda item: item[1])
+    steps = [group(base, lanes, k % 2) for k, (base, lanes) in enumerate(order)]
+    for step in steps[0][0]:
+        step()
     copies = []
-    for base, lanes in group_lanes(dim):
-        group(base, lanes)
+    for k, (base, lanes) in enumerate(order):
+        tiles = steps[k][1]
+        ahead = steps[k + 1][0] if k + 1 < len(steps) else []
+        for n, tile in enumerate(tiles):
+            for step in ahead[len(ahead) * n // len(tiles) : len(ahead) * (n + 1) // len(tiles)]:
+                step()
+            tile()
         here = slice(base, base + lanes)
         copies.append(
-            pltpu.make_async_copy(held.at[:, here], out_ref.at[:, here], semaphores.at[len(copies)])
+            pltpu.make_async_copy(held.at[:, here], out_ref.at[:, here], semaphores.at[k])
         )
         copies[-1].start()
     for copy in copies:
@@ -365,16 +383,17 @@
         out_specs=pl.BlockSpec(memory_space=pl.ANY),
         scratch_shapes=[
             pltpu.VMEM((sum(piece.shape[0] for piece in pieces), LANES), jnp.bfloat16),
-            pltpu.VMEM((len(pairs), depth, 2 * LANES), jnp.bfloat16),
-            pltpu.VMEM((total, GROUP), jnp.float32),
-            pltpu.VMEM((total, GROUP), jnp.bfloat16),
+            pltpu.VMEM((2, len(pairs), depth, 2 * LANES), jnp.bfloat16),
+            pltpu.VMEM((2, total, GROUP), jnp.float32),
+            pltpu.VMEM((2, total, GROUP), jnp.bfloat16),
+            pltpu.VMEM((2, total, GROUP), jnp.float32),
             pltpu.VMEM((2, rows + 2, width, LANES), jnp.float32),
             pltpu.VMEM((2, 4, rows + 2, width // 2, LANES), jnp.float32),
             pltpu.VMEM((2, rows, width, LANES), jnp.float32),
             pltpu.VMEM((tokens, dim), jnp.bfloat16),
             pltpu.SemaphoreType.DMA((len(group_lanes(dim)),)),
         ],
-        compiler_params=pltpu.CompilerParams(vmem_limit_bytes=28 * 2**20),
+        compiler_params=pltpu.CompilerParams(vmem_limit_bytes=36 * 2**20),
         cost_estimate=pl.CostEstimate(
             flops=60 * tokens * dim, bytes_accessed=6 * tokens * dim, transcendentals=2 * tokens * dim
         ),

time: 44.3 us -> 44.4 us (level)
  no operation moved by 1% of the time
where the time goes in v14:
time: 44.4 us; the launch traced here: 44.3 us
  Pallas kernels  18.3 us (41%)
  waiting for transfers between devices  16.6 us (37%)
  starting transfers between devices  9.21 us (21%)
    ppermute x4, waiting for transfers between devices, running_states(): lax.ppermute(array, 'frame', [(f, f ^ stride) for f in range(frames)])  14.1 us
    pallas_call x1, Pallas kernels, mix(): pl.pallas_call(functools.partial(mix_kernel, dim, rows, width, (total - t...  11.7 us
    ppermute x4, starting transfers between devices, running_states(): lax.ppermute(array, 'frame', [(f, f ^ stride) for f in range(frames)])  8.24 us
    pallas_call x1, Pallas kernels, frame_states(): pl.pallas_call(body, out_shape=[pltpu.VMEM(part, jnp.bfloat16)] * parts +...  3.73 us
    pallas_call x1, Pallas kernels, prepare(): pl.pallas_call(functools.partial(prepare_kernel, dim), out_shape=[pltpu.V...  2.69 us
    ppermute x1, waiting for transfers between devices, running_states(): lax.ppermute(other, 'space', swap)  1.34 us
    ppermute x1, waiting for transfers between devices, running_states(): got = lax.ppermute(sent, 'space', swap)  1.16 us
  transfers between devices with their start and end apart: 8, of which 6 were waited for; matrix products, arithmetic and copies ran while one was open for 0% of the time, Pallas kernels for 6%

profile of v14, /device:TPU:0, one launch (start us, length us, event | category | flops | bytes accessed | tf_op | source)
XLA Modules:
  0.0 44.3 jit_solution(10758316536084759074)
XLA Ops:
  0.0 3.7 %frame_states.1 = (bf16[1024,128]{1,0:T(8,128)(2,1)S(1)}, bf16[1024,128]{1,0:T(8,128)(2,1)S(1)}, bf16[2,1,80,2240]{3,2,1,0:T(8,128)(2,1)S(1)}) custom-call(bf16[480,2240]{1,0:T(8,128)(2,1)} %bitcast.7, bf16[480,2240]{1,0:T(8,128)(2,1)} %bitcast.8, bf16[480,2240]{1,0:T(8,128)(2,1)} %bitcast.9, bf16[480,2240]{1,0:T(8,128)(2,1)} %bitcast.10, ...), custom_call_target="tpu_custom_call" | custom-call | flops 240844800 | bytes 4300800 | tf_op jit(solution)/shard_map/frame_states/pallas_call | solution.py:129
  3.7 0.5 %collective-permute-start = (bf16[1024,128]{1,0:T(8,128)(2,1)S(1)}, bf16[1024,128]{1,0:T(8,128)(2,1)S(1)}, u32[]{:S(2)}, u32[]{:S(2)}) collective-permute-start(bf16[1024,128]{1,0:T(8,128)(2,1)S(1)} %get-tuple-element.26), channel_id=1, source_target_pairs={{0,1},{1,0},{2,3},{3,2},{4,5},{5,4},{6,7},{7,6},{8,9},{9,8},{10,11... | collective-permute-start | bytes 786440 | tf_op jit(solution)/shard_map/ppermute | solution.py:493
  4.3 1.2 %collective-permute-done.got_ref = bf16[1024,128]{1,0:T(8,128)(2,1)S(1)} collective-permute-done((bf16[1024,128]{1,0:T(8,128)(2,1)S(1)}, bf16[1024,128]{1,0:T(8,128)(2,1)S(1)}, u32[]{:S(2)}, u32[]{:S(2)}) %collective-permute-start) | collective-permute-done | bytes 262176 | tf_op jit(solution)/shard_map/ppermute | solution.py:493
  5.4 0.1 split_sum.1
  5.5 0.4 collective-permute-start.3
  5.9 2.7 %collective-permute-start.1 = (bf16[512,128]{1,0:T(8,128)(2,1)S(1)}, bf16[512,128]{1,0:T(8,128)(2,1)S(1)}, u32[]{:S(2)}, u32[]{:S(2)}) collective-permute-start(bf16[512,128]{1,0:T(8,128)(2,1)S(1)} %get-tuple-element.30), channel_id=1, source_target_pairs={{0,2},{2,0},{4,6},{6,4},{8,10},{10,8},{12,14},{14,12},{1,3},{3,1},... | collective-permute-start | bytes 393224 | tf_op jit(solution)/shard_map/ppermute | solution.py:489
  8.6 4.0 %collective-permute-done.1.refs_1_.partner_ref = bf16[512,128]{1,0:T(8,128)(2,1)S(1)} collective-permute-done((bf16[512,128]{1,0:T(8,128)(2,1)S(1)}, bf16[512,128]{1,0:T(8,128)(2,1)S(1)}, u32[]{:S(2)}, u32[]{:S(2)}) %collective-permute-start.1) | collective-permute-done | bytes 131104 | tf_op jit(solution)/shard_map/ppermute | solution.py:489
  12.7 1.9 %collective-permute-start.2 = (bf16[512,128]{1,0:T(8,128)(2,1)S(1)}, bf16[512,128]{1,0:T(8,128)(2,1)S(1)}, u32[]{:S(2)}, u32[]{:S(2)}) collective-permute-start(bf16[512,128]{1,0:T(8,128)(2,1)S(1)} %pair_sum.1.refs_0_), channel_id=1, source_target_pairs={{0,4},{2,6},{4,0},{6,2},{8,12},{10,14},{12,8},{14,10},{1,5},{3,7},... | collective-permute-start | bytes 393224 | tf_op jit(solution)/shard_map/ppermute | solution.py:489
  14.5 3.4 %collective-permute-done.2.refs_1_.refs_0_ = bf16[512,128]{1,0:T(8,128)(2,1)S(1)} collective-permute-done((bf16[512,128]{1,0:T(8,128)(2,1)S(1)}, bf16[512,128]{1,0:T(8,128)(2,1)S(1)}, u32[]{:S(2)}, u32[]{:S(2)}) %collective-permute-start.2) | collective-permute-done | bytes 131104 | tf_op jit(solution)/shard_map/ppermute | solution.py:489
  18.0 0.0 collective-permute-done.3.edge_ref
  18.0 2.6 %collective-permute-start.4 = (bf16[512,128]{1,0:T(8,128)(2,1)S(1)}, bf16[512,128]{1,0:T(8,128)(2,1)S(1)}, u32[]{:S(2)}, u32[]{:S(2)}) collective-permute-start(bf16[512,128]{1,0:T(8,128)(2,1)S(1)} %stride_sum.1), channel_id=1, source_target_pairs={{0,8},{2,10},{4,12},{6,14},{8,0},{10,2},{12,4},{14,6},{1,9},{3,11}... | collective-permute-start | bytes 393224 | tf_op jit(solution)/shard_map/ppermute | solution.py:489
  20.6 0.0 copy-done.2
  20.6 0.0 copy-start
  20.6 0.0 copy-start.1
  20.7 2.7 %prepare.1 = (bf16[560,2304]{1,0:T(8,128)(2,1)S(1)}, f32[560,2240]{1,0:T(8,128)S(1)}, bf16[896,128]{1,0:T(8,128)(2,1)S(1)}, bf16[3,128,896]{2,1,0:T(8,128)(2,1)S(1)}) custom-call(bf16[480,2240]{1,0:T(8,128)(2,1)} %bitcast.12, bf16[480,2240]{1,0:T(8,128)(2,1)} %bitcast.14, bf16[2,1,80,2240]{3,2,1,0:T(8,128)(2,1)S(1)} %collective-permute-done.3.edge_ref, ...), custom_call_target="tpu_custom_call" | custom-call | flops 5017600 | bytes 10035200 | tf_op jit(solution)/shard_map/prepare/pallas_call | solution.py:200
  23.3 2.7 %collective-permute-done.4.refs_1_ = bf16[512,128]{1,0:T(8,128)(2,1)S(1)} collective-permute-done((bf16[512,128]{1,0:T(8,128)(2,1)S(1)}, bf16[512,128]{1,0:T(8,128)(2,1)S(1)}, u32[]{:S(2)}, u32[]{:S(2)}) %collective-permute-start.4) | collective-permute-done | bytes 131104 | tf_op jit(solution)/shard_map/ppermute | solution.py:489
  26.1 0.1 pair_sums.1
  26.2 1.1 %collective-permute-start.5 = (bf16[512,128]{1,0:T(8,128)(2,1)S(1)}, bf16[512,128]{1,0:T(8,128)(2,1)S(1)}, u32[]{:S(2)}, u32[]{:S(2)}) collective-permute-start(bf16[512,128]{1,0:T(8,128)(2,1)S(1)} %get-tuple-element.44), channel_id=1, source_target_pairs={{0,2},{2,0},{4,6},{6,4},{8,10},{10,8},{12,14},{14,12},{1,3},{3,1},... | collective-permute-start | bytes 393224 | tf_op jit(solution)/shard_map/ppermute | solution.py:489
  27.3 0.0 collective-permute-start.6
  27.3 4.0 %collective-permute-done.5.refs_1_ = bf16[512,128]{1,0:T(8,128)(2,1)S(1)} collective-permute-done((bf16[512,128]{1,0:T(8,128)(2,1)S(1)}, bf16[512,128]{1,0:T(8,128)(2,1)S(1)}, u32[]{:S(2)}, u32[]{:S(2)}) %collective-permute-start.5) | collective-permute-done | bytes 131104 | tf_op jit(solution)/shard_map/ppermute | solution.py:489
  31.2 0.0 collective-permute-start.7
  31.3 0.0 collective-permute-done.6.refs_2_
  31.3 1.3 %collective-permute-done.7.refs_3_ = bf16[512,128]{1,0:T(8,128)(2,1)S(1)} collective-permute-done((bf16[512,128]{1,0:T(8,128)(2,1)S(1)}, bf16[512,128]{1,0:T(8,128)(2,1)S(1)}, u32[]{:S(2)}, u32[]{:S(2)}) %collective-permute-start.7) | collective-permute-done | bytes 131104 | tf_op jit(solution)/shard_map/ppermute | solution.py:515
  32.6 11.7 %mix.1 = bf16[480,2240]{1,0:T(8,128)(2,1)} custom-call(bf16[560,2304]{1,0:T(8,128)(2,1)S(1)} %get-tuple-element.38.features_ref, f32[560,2240]{1,0:T(8,128)S(1)} %get-tuple-element.39.inputs_ref, bf16[896,128]{1,0:T(8,128)(2,1)S(1)} %get-tuple-element.40.heads_ref, bf16[3,128,896]{2,1,0:T(8,128)(2,1)S(1)} %get-tuple-element.41.spread_ref, ...), custom_call_target="tpu_custom_call" | custom-call | flops 64512000 | bytes 6451200 | tf_op jit(solution)/shard_map/mix/pallas_call | solution.py:379
  (6 shorter events, 0.1 us)
Async XLA Ops:
  0.0 20.6 %copy-start.2 = (f32[2240]{0:T(1024)S(1)}, f32[2240]{0:T(1024)}, u32[]{:S(2)}) copy-start(f32[2240]{0:T(1024)} %param.11) | copy-start | bytes 26884
  3.7 1.7 %collective-permute-start = (bf16[1024,128]{1,0:T(8,128)(2,1)S(1)}, bf16[1024,128]{1,0:T(8,128)(2,1)S(1)}, u32[]{:S(2)}, u32[]{:S(2)}) collective-permute-start(bf16[1024,128]{1,0:T(8,128)(2,1)S(1)} %get-tuple-element.26), channel_id=1, source_target_pairs={{0,1},{1,0},{2,3},{3,2},{4,5},{5,4},{6,7},{7,6},{8,9},{9,8},{10,11... | collective-permute-start | bytes 786440 | tf_op jit(solution)/shard_map/ppermute | solution.py:493
  5.5 12.5 %collective-permute-start.3 = (bf16[2,1,80,2240]{3,2,1,0:T(8,128)(2,1)S(1)}, bf16[2,1,80,2240]{3,2,1,0:T(8,128)(2,1)S(1)}, u32[]{:S(2)}, u32[]{:S(2)}) collective-permute-start(bf16[2,1,80,2240]{3,2,1,0:T(8,128)(2,1)S(1)} %get-tuple-element.31), channel_id=1, source_target_pairs={{0,1},{1,0},{2,3},{3,2},{4,5},{5,4},{6,7},{7,6},{8,9},{9,8},{10,11... | collective-permute-start | bytes 2150408 | tf_op jit(solution)/shard_map/ppermute | solution.py:497
  5.9 6.7 %collective-permute-start.1 = (bf16[512,128]{1,0:T(8,128)(2,1)S(1)}, bf16[512,128]{1,0:T(8,128)(2,1)S(1)}, u32[]{:S(2)}, u32[]{:S(2)}) collective-permute-start(bf16[512,128]{1,0:T(8,128)(2,1)S(1)} %get-tuple-element.30), channel_id=1, source_target_pairs={{0,2},{2,0},{4,6},{6,4},{8,10},{10,8},{12,14},{14,12},{1,3},{3,1},... | collective-permute-start | bytes 393224 | tf_op jit(solution)/shard_map/ppermute | solution.py:489
  12.7 5.3 %collective-permute-start.2 = (bf16[512,128]{1,0:T(8,128)(2,1)S(1)}, bf16[512,128]{1,0:T(8,128)(2,1)S(1)}, u32[]{:S(2)}, u32[]{:S(2)}) collective-permute-start(bf16[512,128]{1,0:T(8,128)(2,1)S(1)} %pair_sum.1.refs_0_), channel_id=1, source_target_pairs={{0,4},{2,6},{4,0},{6,2},{8,12},{10,14},{12,8},{14,10},{1,5},{3,7},... | collective-permute-start | bytes 393224 | tf_op jit(solution)/shard_map/ppermute | solution.py:489
  18.0 8.1 %collective-permute-start.4 = (bf16[512,128]{1,0:T(8,128)(2,1)S(1)}, bf16[512,128]{1,0:T(8,128)(2,1)S(1)}, u32[]{:S(2)}, u32[]{:S(2)}) collective-permute-start(bf16[512,128]{1,0:T(8,128)(2,1)S(1)} %stride_sum.1), channel_id=1, source_target_pairs={{0,8},{2,10},{4,12},{6,14},{8,0},{10,2},{12,4},{14,6},{1,9},{3,11}... | collective-permute-start | bytes 393224 | tf_op jit(solution)/shard_map/ppermute | solution.py:489
  20.6 12.0 %copy-start = (f32[9,2240]{1,0:T(8,128)S(1)}, f32[9,2240]{1,0:T(8,128)}, u32[]{:S(2)}) copy-start(f32[9,2240]{1,0:T(8,128)} %vtaps_ref.1) | copy-start | bytes 241924
  20.6 12.0 %copy-start.1 = (f32[9,2240]{1,0:T(8,128)S(1)}, f32[9,2240]{1,0:T(8,128)}, u32[]{:S(2)}) copy-start(f32[9,2240]{1,0:T(8,128)} %gtaps_ref.1) | copy-start | bytes 241924
  26.2 5.0 %collective-permute-start.5 = (bf16[512,128]{1,0:T(8,128)(2,1)S(1)}, bf16[512,128]{1,0:T(8,128)(2,1)S(1)}, u32[]{:S(2)}, u32[]{:S(2)}) collective-permute-start(bf16[512,128]{1,0:T(8,128)(2,1)S(1)} %get-tuple-element.44), channel_id=1, source_target_pairs={{0,2},{2,0},{4,6},{6,4},{8,10},{10,8},{12,14},{14,12},{1,3},{3,1},... | collective-permute-start | bytes 393224 | tf_op jit(solution)/shard_map/ppermute | solution.py:489
  27.3 4.0 %collective-permute-start.6 = (bf16[512,128]{1,0:T(8,128)(2,1)S(1)}, bf16[512,128]{1,0:T(8,128)(2,1)S(1)}, u32[]{:S(2)}, u32[]{:S(2)}) collective-permute-start(bf16[512,128]{1,0:T(8,128)(2,1)S(1)} %get-tuple-element.43.refs_0_), channel_id=1, source_target_pairs={{0,1},{1,0},{2,3},{3,2},{4,5},{5,4},{6,7},{7,6},{8,9},{9,8},{10,11... | collective-permute-start | bytes 393224 | tf_op jit(solution)/shard_map/ppermute | solution.py:515
  31.2 1.3 %collective-permute-start.7 = (bf16[512,128]{1,0:T(8,128)(2,1)S(1)}, bf16[512,128]{1,0:T(8,128)(2,1)S(1)}, u32[]{:S(2)}, u32[]{:S(2)}) collective-permute-start(bf16[512,128]{1,0:T(8,128)(2,1)S(1)} %collective-permute-done.5.refs_1_), channel_id=1, source_target_pairs={{0,1},{1,0},{2,3},{3,2},{4,5},{5,4},{6,7},{7,6},{8,9},{9,8},{10,11... | collective-permute-start | bytes 393224 | tf_op jit(solution)/shard_map/ppermute | solution.py:515

commit v15 on v14

--- a/solution.py
+++ b/solution.py
@@ -228,8 +228,6 @@
     places = edge_places(lax.axis_size("space"), rows) if edges else []
     spots = piece_places() if len(pieces) > 1 else [0]
     tokens = rows * width
-    for row in (0, rows + 1):
-        windows[:, :, row] = jnp.zeros((2, 4, width // 2, LANES), jnp.float32)
     for k, piece in enumerate(pieces):
         size = piece.shape[0]
         states[pl.ds(pl.multiple_of(spots[k] * size, 16), size), :] = piece[...]
@@ -239,7 +237,7 @@
     half = width // 2
     even, odd = pl.ds(0, half, stride=2), pl.ds(1, half, stride=2)
 
-    def store_windows(value, slot, used, row, place):
+    def store_windows(value, slot, used, row):
         mixed[slot, row, :, :used] = value
         left, right = mixed[slot, row, even, :used], mixed[slot, row, odd, :used]
         sub = sublane[:, :used]
@@ -247,7 +245,7 @@
         before = jnp.concatenate([jnp.where(sub == 0, 0.0, before[:8]), before[8:]], axis=0)
         after = jnp.concatenate([after[: half - 8], jnp.where(sub == 7, 0.0, after[half - 8 :])], axis=0)
         for k, window in enumerate((before - right, left + right, right - left, left - after)):
-            windows[slot, k, place, :, :used] = window
+            windows[slot, k, row, :, :used] = window
 
     def group(base, lanes, turn):
         pairs = spans(lanes)
@@ -302,14 +300,18 @@
             used = min(LANES, lanes - j * LANES)
             near = slice(j * LANES, j * LANES + used)
             here = slice(base + j * LANES, base + j * LANES + used)
+            outside = [None, None]
             for row in range(rows + edges):
                 source = slice(row * width, (row + 1) * width)
                 value = inputs_ref[source, here] + numer[turn, source, near] * spreads[turn, source, near]
                 if row < rows:
-                    store_windows(value, slot, used, row + 1, row + 1)
-                else:
-                    edge = row - rows
-                    store_windows(value, slot, used, edge * (rows + 1), places[edge])
+                    store_windows(value, slot, used, row + 1)
+                    continue
+                for k, place in enumerate((0, rows + 1)):
+                    part = jnp.where(places[row - rows] == place, value, 0.0)
+                    outside[k] = part if outside[k] is None else outside[k] + part
+            for k, place in enumerate((0, rows + 1)):
+                store_windows(outside[k], slot, used, place)
             taps = []
             for ref, factor in ((vtaps_ref, 1.0), (gtaps_ref, 0.5)):
                 for tap_row in range(3):

time: 44.4 us -> 44.6 us (level)
  no operation moved by 1% of the time
where the time goes in v15:
time: 44.6 us; the launch traced here: 44.5 us
  Pallas kernels  18.6 us (42%)
  waiting for transfers between devices  16.6 us (37%)
  starting transfers between devices  9.21 us (21%)
    ppermute x4, waiting for transfers between devices, running_states(): lax.ppermute(array, 'frame', [(f, f ^ stride) for f in range(frames)])  14.1 us
    pallas_call x1, Pallas kernels, mix(): pl.pallas_call(functools.partial(mix_kernel, dim, rows, width, (total - t...  11.9 us
    ppermute x4, starting transfers between devices, running_states(): lax.ppermute(array, 'frame', [(f, f ^ stride) for f in range(frames)])  8.24 us
    pallas_call x1, Pallas kernels, frame_states(): pl.pallas_call(body, out_shape=[pltpu.VMEM(part, jnp.bfloat16)] * parts +...  3.73 us
    pallas_call x1, Pallas kernels, prepare(): pl.pallas_call(functools.partial(prepare_kernel, dim), out_shape=[pltpu.V...  2.69 us
    ppermute x1, waiting for transfers between devices, running_states(): lax.ppermute(other, 'space', swap)  1.34 us
    ppermute x1, waiting for transfers between devices, running_states(): got = lax.ppermute(sent, 'space', swap)  1.16 us
  transfers between devices with their start and end apart: 8, of which 6 were waited for; matrix products, arithmetic and copies ran while one was open for 0% of the time, Pallas kernels for 6%

profile of v15, /device:TPU:0, one launch (start us, length us, event | category | flops | bytes accessed | tf_op | source)
XLA Modules:
  0.0 44.5 jit_solution(17145423237798905225)
XLA Ops:
  0.0 3.7 %frame_states.1 = (bf16[1024,128]{1,0:T(8,128)(2,1)S(1)}, bf16[1024,128]{1,0:T(8,128)(2,1)S(1)}, bf16[2,1,80,2240]{3,2,1,0:T(8,128)(2,1)S(1)}) custom-call(bf16[480,2240]{1,0:T(8,128)(2,1)} %bitcast.7, bf16[480,2240]{1,0:T(8,128)(2,1)} %bitcast.8, bf16[480,2240]{1,0:T(8,128)(2,1)} %bitcast.9, bf16[480,2240]{1,0:T(8,128)(2,1)} %bitcast.10, ...), custom_call_target="tpu_custom_call" | custom-call | flops 240844800 | bytes 4300800 | tf_op jit(solution)/shard_map/frame_states/pallas_call | solution.py:129
  3.7 0.5 %collective-permute-start = (bf16[1024,128]{1,0:T(8,128)(2,1)S(1)}, bf16[1024,128]{1,0:T(8,128)(2,1)S(1)}, u32[]{:S(2)}, u32[]{:S(2)}) collective-permute-start(bf16[1024,128]{1,0:T(8,128)(2,1)S(1)} %get-tuple-element.26), channel_id=1, source_target_pairs={{0,1},{1,0},{2,3},{3,2},{4,5},{5,4},{6,7},{7,6},{8,9},{9,8},{10,11... | collective-permute-start | bytes 786440 | tf_op jit(solution)/shard_map/ppermute | solution.py:495
  4.3 1.2 %collective-permute-done.got_ref = bf16[1024,128]{1,0:T(8,128)(2,1)S(1)} collective-permute-done((bf16[1024,128]{1,0:T(8,128)(2,1)S(1)}, bf16[1024,128]{1,0:T(8,128)(2,1)S(1)}, u32[]{:S(2)}, u32[]{:S(2)}) %collective-permute-start) | collective-permute-done | bytes 262176 | tf_op jit(solution)/shard_map/ppermute | solution.py:495
  5.4 0.1 split_sum.1
  5.5 0.4 collective-permute-start.3
  5.9 2.7 %collective-permute-start.1 = (bf16[512,128]{1,0:T(8,128)(2,1)S(1)}, bf16[512,128]{1,0:T(8,128)(2,1)S(1)}, u32[]{:S(2)}, u32[]{:S(2)}) collective-permute-start(bf16[512,128]{1,0:T(8,128)(2,1)S(1)} %get-tuple-element.30), channel_id=1, source_target_pairs={{0,2},{2,0},{4,6},{6,4},{8,10},{10,8},{12,14},{14,12},{1,3},{3,1},... | collective-permute-start | bytes 393224 | tf_op jit(solution)/shard_map/ppermute | solution.py:491
  8.6 4.0 %collective-permute-done.1.refs_1_.partner_ref = bf16[512,128]{1,0:T(8,128)(2,1)S(1)} collective-permute-done((bf16[512,128]{1,0:T(8,128)(2,1)S(1)}, bf16[512,128]{1,0:T(8,128)(2,1)S(1)}, u32[]{:S(2)}, u32[]{:S(2)}) %collective-permute-start.1) | collective-permute-done | bytes 131104 | tf_op jit(solution)/shard_map/ppermute | solution.py:491
  12.7 1.9 %collective-permute-start.2 = (bf16[512,128]{1,0:T(8,128)(2,1)S(1)}, bf16[512,128]{1,0:T(8,128)(2,1)S(1)}, u32[]{:S(2)}, u32[]{:S(2)}) collective-permute-start(bf16[512,128]{1,0:T(8,128)(2,1)S(1)} %pair_sum.1.refs_0_), channel_id=1, source_target_pairs={{0,4},{2,6},{4,0},{6,2},{8,12},{10,14},{12,8},{14,10},{1,5},{3,7},... | collective-permute-start | bytes 393224 | tf_op jit(solution)/shard_map/ppermute | solution.py:491
  14.5 3.4 %collective-permute-done.2.refs_1_.refs_0_ = bf16[512,128]{1,0:T(8,128)(2,1)S(1)} collective-permute-done((bf16[512,128]{1,0:T(8,128)(2,1)S(1)}, bf16[512,128]{1,0:T(8,128)(2,1)S(1)}, u32[]{:S(2)}, u32[]{:S(2)}) %collective-permute-start.2) | collective-permute-done | bytes 131104 | tf_op jit(solution)/shard_map/ppermute | solution.py:491
  18.0 0.0 collective-permute-done.3.edge_ref
  18.0 2.6 %collective-permute-start.4 = (bf16[512,128]{1,0:T(8,128)(2,1)S(1)}, bf16[512,128]{1,0:T(8,128)(2,1)S(1)}, u32[]{:S(2)}, u32[]{:S(2)}) collective-permute-start(bf16[512,128]{1,0:T(8,128)(2,1)S(1)} %stride_sum.1), channel_id=1, source_target_pairs={{0,8},{2,10},{4,12},{6,14},{8,0},{10,2},{12,4},{14,6},{1,9},{3,11}... | collective-permute-start | bytes 393224 | tf_op jit(solution)/shard_map/ppermute | solution.py:491
  20.6 0.0 copy-done.2
  20.6 0.0 copy-start
  20.6 0.0 copy-start.1
  20.7 2.7 %prepare.1 = (bf16[560,2304]{1,0:T(8,128)(2,1)S(1)}, f32[560,2240]{1,0:T(8,128)S(1)}, bf16[896,128]{1,0:T(8,128)(2,1)S(1)}, bf16[3,128,896]{2,1,0:T(8,128)(2,1)S(1)}) custom-call(bf16[480,2240]{1,0:T(8,128)(2,1)} %bitcast.12, bf16[480,2240]{1,0:T(8,128)(2,1)} %bitcast.14, bf16[2,1,80,2240]{3,2,1,0:T(8,128)(2,1)S(1)} %collective-permute-done.3.edge_ref, ...), custom_call_target="tpu_custom_call" | custom-call | flops 5017600 | bytes 10035200 | tf_op jit(solution)/shard_map/prepare/pallas_call | solution.py:200
  23.3 2.7 %collective-permute-done.4.refs_1_ = bf16[512,128]{1,0:T(8,128)(2,1)S(1)} collective-permute-done((bf16[512,128]{1,0:T(8,128)(2,1)S(1)}, bf16[512,128]{1,0:T(8,128)(2,1)S(1)}, u32[]{:S(2)}, u32[]{:S(2)}) %collective-permute-start.4) | collective-permute-done | bytes 131104 | tf_op jit(solution)/shard_map/ppermute | solution.py:491
  26.1 0.1 pair_sums.1
  26.2 1.1 %collective-permute-start.5 = (bf16[512,128]{1,0:T(8,128)(2,1)S(1)}, bf16[512,128]{1,0:T(8,128)(2,1)S(1)}, u32[]{:S(2)}, u32[]{:S(2)}) collective-permute-start(bf16[512,128]{1,0:T(8,128)(2,1)S(1)} %get-tuple-element.44), channel_id=1, source_target_pairs={{0,2},{2,0},{4,6},{6,4},{8,10},{10,8},{12,14},{14,12},{1,3},{3,1},... | collective-permute-start | bytes 393224 | tf_op jit(solution)/shard_map/ppermute | solution.py:491
  27.3 0.0 collective-permute-start.6
  27.3 4.0 %collective-permute-done.5.refs_1_ = bf16[512,128]{1,0:T(8,128)(2,1)S(1)} collective-permute-done((bf16[512,128]{1,0:T(8,128)(2,1)S(1)}, bf16[512,128]{1,0:T(8,128)(2,1)S(1)}, u32[]{:S(2)}, u32[]{:S(2)}) %collective-permute-start.5) | collective-permute-done | bytes 131104 | tf_op jit(solution)/shard_map/ppermute | solution.py:491
  31.2 0.0 collective-permute-start.7
  31.3 0.0 collective-permute-done.6.refs_2_
  31.3 1.3 %collective-permute-done.7.refs_3_ = bf16[512,128]{1,0:T(8,128)(2,1)S(1)} collective-permute-done((bf16[512,128]{1,0:T(8,128)(2,1)S(1)}, bf16[512,128]{1,0:T(8,128)(2,1)S(1)}, u32[]{:S(2)}, u32[]{:S(2)}) %collective-permute-start.7) | collective-permute-done | bytes 131104 | tf_op jit(solution)/shard_map/ppermute | solution.py:517
  32.6 11.9 %mix.1 = bf16[480,2240]{1,0:T(8,128)(2,1)} custom-call(bf16[560,2304]{1,0:T(8,128)(2,1)S(1)} %get-tuple-element.38.features_ref, f32[560,2240]{1,0:T(8,128)S(1)} %get-tuple-element.39.inputs_ref, bf16[896,128]{1,0:T(8,128)(2,1)S(1)} %get-tuple-element.40.heads_ref, bf16[3,128,896]{2,1,0:T(8,128)(2,1)S(1)} %get-tuple-element.41.spread_ref, ...), custom_call_target="tpu_custom_call" | custom-call | flops 64512000 | bytes 6451200 | tf_op jit(solution)/shard_map/mix/pallas_call | solution.py:381
  (6 shorter events, 0.1 us)
Async XLA Ops:
  0.0 20.6 %copy-start.2 = (f32[2240]{0:T(1024)S(1)}, f32[2240]{0:T(1024)}, u32[]{:S(2)}) copy-start(f32[2240]{0:T(1024)} %param.11) | copy-start | bytes 26884
  3.7 1.7 %collective-permute-start = (bf16[1024,128]{1,0:T(8,128)(2,1)S(1)}, bf16[1024,128]{1,0:T(8,128)(2,1)S(1)}, u32[]{:S(2)}, u32[]{:S(2)}) collective-permute-start(bf16[1024,128]{1,0:T(8,128)(2,1)S(1)} %get-tuple-element.26), channel_id=1, source_target_pairs={{0,1},{1,0},{2,3},{3,2},{4,5},{5,4},{6,7},{7,6},{8,9},{9,8},{10,11... | collective-permute-start | bytes 786440 | tf_op jit(solution)/shard_map/ppermute | solution.py:495
  5.5 12.5 %collective-permute-start.3 = (bf16[2,1,80,2240]{3,2,1,0:T(8,128)(2,1)S(1)}, bf16[2,1,80,2240]{3,2,1,0:T(8,128)(2,1)S(1)}, u32[]{:S(2)}, u32[]{:S(2)}) collective-permute-start(bf16[2,1,80,2240]{3,2,1,0:T(8,128)(2,1)S(1)} %get-tuple-element.31), channel_id=1, source_target_pairs={{0,1},{1,0},{2,3},{3,2},{4,5},{5,4},{6,7},{7,6},{8,9},{9,8},{10,11... | collective-permute-start | bytes 2150408 | tf_op jit(solution)/shard_map/ppermute | solution.py:499
  5.9 6.7 %collective-permute-start.1 = (bf16[512,128]{1,0:T(8,128)(2,1)S(1)}, bf16[512,128]{1,0:T(8,128)(2,1)S(1)}, u32[]{:S(2)}, u32[]{:S(2)}) collective-permute-start(bf16[512,128]{1,0:T(8,128)(2,1)S(1)} %get-tuple-element.30), channel_id=1, source_target_pairs={{0,2},{2,0},{4,6},{6,4},{8,10},{10,8},{12,14},{14,12},{1,3},{3,1},... | collective-permute-start | bytes 393224 | tf_op jit(solution)/shard_map/ppermute | solution.py:491
  12.7 5.3 %collective-permute-start.2 = (bf16[512,128]{1,0:T(8,128)(2,1)S(1)}, bf16[512,128]{1,0:T(8,128)(2,1)S(1)}, u32[]{:S(2)}, u32[]{:S(2)}) collective-permute-start(bf16[512,128]{1,0:T(8,128)(2,1)S(1)} %pair_sum.1.refs_0_), channel_id=1, source_target_pairs={{0,4},{2,6},{4,0},{6,2},{8,12},{10,14},{12,8},{14,10},{1,5},{3,7},... | collective-permute-start | bytes 393224 | tf_op jit(solution)/shard_map/ppermute | solution.py:491
  18.0 8.1 %collective-permute-start.4 = (bf16[512,128]{1,0:T(8,128)(2,1)S(1)}, bf16[512,128]{1,0:T(8,128)(2,1)S(1)}, u32[]{:S(2)}, u32[]{:S(2)}) collective-permute-start(bf16[512,128]{1,0:T(8,128)(2,1)S(1)} %stride_sum.1), channel_id=1, source_target_pairs={{0,8},{2,10},{4,12},{6,14},{8,0},{10,2},{12,4},{14,6},{1,9},{3,11}... | collective-permute-start | bytes 393224 | tf_op jit(solution)/shard_map/ppermute | solution.py:491
  20.6 12.0 %copy-start = (f32[9,2240]{1,0:T(8,128)S(1)}, f32[9,2240]{1,0:T(8,128)}, u32[]{:S(2)}) copy-start(f32[9,2240]{1,0:T(8,128)} %vtaps_ref.1) | copy-start | bytes 241924
  20.6 12.0 %copy-start.1 = (f32[9,2240]{1,0:T(8,128)S(1)}, f32[9,2240]{1,0:T(8,128)}, u32[]{:S(2)}) copy-start(f32[9,2240]{1,0:T(8,128)} %gtaps_ref.1) | copy-start | bytes 241924
  26.2 5.0 %collective-permute-start.5 = (bf16[512,128]{1,0:T(8,128)(2,1)S(1)}, bf16[512,128]{1,0:T(8,128)(2,1)S(1)}, u32[]{:S(2)}, u32[]{:S(2)}) collective-permute-start(bf16[512,128]{1,0:T(8,128)(2,1)S(1)} %get-tuple-element.44), channel_id=1, source_target_pairs={{0,2},{2,0},{4,6},{6,4},{8,10},{10,8},{12,14},{14,12},{1,3},{3,1},... | collective-permute-start | bytes 393224 | tf_op jit(solution)/shard_map/ppermute | solution.py:491
  27.3 4.0 %collective-permute-start.6 = (bf16[512,128]{1,0:T(8,128)(2,1)S(1)}, bf16[512,128]{1,0:T(8,128)(2,1)S(1)}, u32[]{:S(2)}, u32[]{:S(2)}) collective-permute-start(bf16[512,128]{1,0:T(8,128)(2,1)S(1)} %get-tuple-element.43.refs_0_), channel_id=1, source_target_pairs={{0,1},{1,0},{2,3},{3,2},{4,5},{5,4},{6,7},{7,6},{8,9},{9,8},{10,11... | collective-permute-start | bytes 393224 | tf_op jit(solution)/shard_map/ppermute | solution.py:517
  31.2 1.3 %collective-permute-start.7 = (bf16[512,128]{1,0:T(8,128)(2,1)S(1)}, bf16[512,128]{1,0:T(8,128)(2,1)S(1)}, u32[]{:S(2)}, u32[]{:S(2)}) collective-permute-start(bf16[512,128]{1,0:T(8,128)(2,1)S(1)} %collective-permute-done.5.refs_1_), channel_id=1, source_target_pairs={{0,1},{1,0},{2,3},{3,2},{4,5},{5,4},{6,7},{7,6},{8,9},{9,8},{10,11... | collective-permute-start | bytes 393224 | tf_op jit(solution)/shard_map/ppermute | solution.py:517

commit v16 on v12

--- a/solution.py
+++ b/solution.py
@@ -152,29 +152,46 @@
 
 def prepare_kernel(
     dim, queries_ref, residual_ref, edge_ref, gain_ref,
-    features_ref, inputs_ref, scaled_ref, held, semaphores,
+    features_ref, inputs_ref, scaled_ref, held, wide, semaphores,
 ):
     tokens = queries_ref.shape[0]
-    full = dim // LANES * LANES
-    parts = [slice(0, full), slice(full, dim)] if full < dim else [slice(0, dim)]
     copies = [
-        pltpu.make_async_copy(queries_ref, held.at[:tokens], semaphores.at[0]),
-        pltpu.make_async_copy(residual_ref, inputs_ref.at[:tokens], semaphores.at[1]),
+        pltpu.make_async_copy(source, held.at[k, :tokens], semaphores.at[k])
+        for k, source in enumerate((queries_ref, residual_ref))
     ]
     for copy in copies:
         copy.start()
     edges, width = edge_ref.shape[1:3]
     for e in range(edges):
         here = slice(tokens + e * width, tokens + (e + 1) * width)
-        held[here] = edge_ref[0, e]
-        inputs_ref[here] = edge_ref[1, e]
+        held[0, here] = edge_ref[0, e]
+        held[1, here] = edge_ref[1, e]
     scaled_ref[...] = gain_ref[...] * math.sqrt(HEAD_DIM)
-    if full < dim:
-        features_ref[:, full:] = jnp.zeros((features_ref.shape[0], LANES), jnp.bfloat16)
-    copies[0].wait()
-    for part in parts:
-        features_ref[:, part] = jnp.maximum(held[:, part], 0)
-    copies[1].wait()
+    half = width // 2
+    for k, copy in enumerate(copies):
+        copy.wait()
+        for j in range(cdiv(dim, LANES)):
+            here = slice(j * LANES, min((j + 1) * LANES, dim))
+            used = here.stop - here.start
+            slot = j % 2
+            if k == 0 and used < LANES:
+                features_ref[:, here.stop :] = jnp.zeros(
+                    (features_ref.shape[0], LANES - used), jnp.bfloat16
+                )
+            wide[slot, :, :used] = held[k, :, here].astype(jnp.float32)
+            for row in range(wide.shape[1] // width):
+                value = jnp.concatenate(
+                    [
+                        wide[slot, pl.ds(row * width + side, half, stride=2), :used]
+                        for side in range(2)
+                    ],
+                    axis=0,
+                )
+                source = slice(row * width, (row + 1) * width)
+                if k == 0:
+                    features_ref[source, here] = jnp.maximum(value, 0.0).astype(jnp.bfloat16)
+                else:
+                    inputs_ref[source, here] = value
 
 
 def prepare(queries, residual, edge, gain):
@@ -185,13 +202,14 @@
         functools.partial(prepare_kernel, dim),
         out_shape=[
             pltpu.VMEM((total, cdiv(dim, LANES) * LANES), jnp.bfloat16),
-            pltpu.VMEM((total, dim), jnp.bfloat16),
+            pltpu.VMEM((total, dim), jnp.float32),
             pltpu.VMEM((1, dim), jnp.float32),
         ],
         in_specs=[pl.BlockSpec(memory_space=pl.ANY)] * 2 + [whole] * 2,
         out_specs=[whole] * 3,
         scratch_shapes=[
-            pltpu.VMEM((total, dim), jnp.bfloat16),
+            pltpu.VMEM((2, total, dim), jnp.bfloat16),
+            pltpu.VMEM((2, total, LANES), jnp.float32),
             pltpu.SemaphoreType.DMA((2,)),
         ],
         compiler_params=pltpu.CompilerParams(vmem_limit_bytes=24 * 2**20),
@@ -206,11 +224,13 @@
     dim, rows, width, edges,
     features_ref, inputs_ref, gain_ref, vtaps_ref, gtaps_ref, *refs,
 ):
-    *pieces, out_ref, states, weights, numer, rounded, windows, results, held, semaphores = refs
+    *pieces, out_ref, states, weights, numer, mixed_rows, windows, results, held, semaphores = refs
     places = edge_places(lax.axis_size("space"), rows) if edges else []
     spots = piece_places() if len(pieces) > 1 else [0]
     tokens = rows * width
     weights[...] = jnp.zeros_like(weights)
+    for row in (0, rows + 1):
+        windows[:, :, row] = jnp.zeros((2, 4, width // 2, LANES), jnp.float32)
     for k, piece in enumerate(pieces):
         size = piece.shape[0]
         states[pl.ds(pl.multiple_of(spots[k] * size, 16), size), :] = piece[...]
@@ -220,15 +240,16 @@
     half = width // 2
     even, odd = pl.ds(0, half, stride=2), pl.ds(1, half, stride=2)
 
-    def store_windows(mixed, row, slot, used):
-        rounded[slot, row, :, :used] = mixed.astype(jnp.bfloat16).astype(jnp.float32)
-        left, right = rounded[slot, row, even, :used], rounded[slot, row, odd, :used]
+    def store_windows(value, slot, used, row, place):
+        left, right = value[:half], value[half:]
+        if 0 < row <= rows:
+            mixed_rows[slot, row, :, :used] = value
         sub = sublane[:, :used]
         before, after = pltpu.roll(right, 1, 0), pltpu.roll(left, half - 1, 0)
         before = jnp.concatenate([jnp.where(sub == 0, 0.0, before[:8]), before[8:]], axis=0)
         after = jnp.concatenate([after[: half - 8], jnp.where(sub == 7, 0.0, after[half - 8 :])], axis=0)
         for k, window in enumerate((before - right, left + right, right - left, left - after)):
-            windows[slot, k, row, :, :used] = window
+            windows[slot, k, place, :, :used] = window
 
     def group(base, lanes):
         pairs = spans(lanes)
@@ -283,18 +304,14 @@
                 if len(heads) > 1:
                     scale = jnp.where(lane_iota(scale.shape) < heads[0][2], scale, sums[1])
                 normed = numer[source, near] * lax.rsqrt(scale + HEAD_DIM * 1e-06)
-                return inputs_ref[source, here].astype(jnp.float32) + normed * gain_ref[:, here]
-
-            outside = [None, None]
+                return inputs_ref[source, here] + normed * gain_ref[:, here]
+
+            for row in range(rows):
+                value = mixed(slice(row * width, (row + 1) * width))
+                store_windows(value, slot, used, row + 1, row + 1)
             for e in range(edges):
                 value = mixed(slice(tokens + e * width, tokens + (e + 1) * width))
-                for k, row in enumerate((0, rows + 1)):
-                    part = jnp.where(places[e] == row, value, 0.0)
-                    outside[k] = part if outside[k] is None else outside[k] + part
-            for k, row in enumerate((0, rows + 1)):
-                store_windows(outside[k], row, slot, used)
-            for row in range(rows):
-                store_windows(mixed(slice(row * width, (row + 1) * width)), row + 1, slot, used)
+                store_windows(value, slot, used, 0, places[e])
             taps = []
             for ref, factor in ((vtaps_ref, 1.0), (gtaps_ref, 0.5)):
                 for tap_row in range(3):
@@ -319,8 +336,8 @@
                             products[1] - products[2] - products[3],
                         )
                     )
-                for side, (conv_v, half_g) in zip((even, odd), zip(*columns)):
-                    center = rounded[slot, row + 1, side, :used]
+                for k, (side, (conv_v, half_g)) in enumerate(zip((even, odd), zip(*columns))):
+                    center = mixed_rows[slot, row + 1, k * half : (k + 1) * half, :used]
                     results[slot, row, side, :used] = center + conv_v * (
                         half_g + half_g * jnp.tanh(half_g)
                     )

time: 44.1 us -> 43.5 us (0.986)
  waiting for transfers between devices: 16.9 us -> 15.9 us
    ppermute x4, waiting for transfers between devices: 14.4 us -> 13.4 us  [running_states(): lax.ppermute(array, 'frame', [(f, f ^ stride) for f in range(frames)])]
    pallas_call x1, Pallas kernels: 2.35 us -> 3.38 us  [prepare(): pl.pallas_call(functools.partial(prepare_kernel, dim), out_shape=[pltpu.V...]
    pallas_call x1, Pallas kernels: 11.4 us -> 10.7 us  [mix(): pl.pallas_call(functools.partial(mix_kernel, dim, rows, width, (total - t...]
  transfers between devices with their start and end apart: 8 -> 8, of which waited for: 6 -> 6; matrix products, arithmetic and copies ran while one was open for 0% -> 0% of each run, Pallas kernels for 5% -> 8%
where the time goes in v16:
time: 43.5 us; the launch traced here: 43.3 us
  Pallas kernels  18.1 us (42%)
  waiting for transfers between devices  15.9 us (37%)
  starting transfers between devices  9.21 us (21%)
    ppermute x4, waiting for transfers between devices, running_states(): lax.ppermute(array, 'frame', [(f, f ^ stride) for f in range(frames)])  13.4 us
    pallas_call x1, Pallas kernels, mix(): pl.pallas_call(functools.partial(mix_kernel, dim, rows, width, (total - t...  10.7 us
    ppermute x4, starting transfers between devices, running_states(): lax.ppermute(array, 'frame', [(f, f ^ stride) for f in range(frames)])  8.24 us
    pallas_call x1, Pallas kernels, frame_states(): pl.pallas_call(body, out_shape=[pltpu.VMEM(part, jnp.bfloat16)] * parts +...  3.73 us
    pallas_call x1, Pallas kernels, prepare(): pl.pallas_call(functools.partial(prepare_kernel, dim), out_shape=[pltpu.V...  3.38 us
    ppermute x1, waiting for transfers between devices, running_states(): lax.ppermute(other, 'space', swap)  1.34 us
    ppermute x1, waiting for transfers between devices, running_states(): got = lax.ppermute(sent, 'space', swap)  1.16 us
  transfers between devices with their start and end apart: 8, of which 6 were waited for; matrix products, arithmetic and copies ran while one was open for 0% of the time, Pallas kernels for 8%

profile of v16, /device:TPU:0, one launch (start us, length us, event | category | flops | bytes accessed | tf_op | source)
XLA Modules:
  0.0 43.3 jit_solution(5600484661395494109)
XLA Ops:
  0.0 3.7 %frame_states.1 = (bf16[1024,128]{1,0:T(8,128)(2,1)S(1)}, bf16[1024,128]{1,0:T(8,128)(2,1)S(1)}, bf16[2,1,80,2240]{3,2,1,0:T(8,128)(2,1)S(1)}) custom-call(bf16[480,2240]{1,0:T(8,128)(2,1)} %bitcast.7, bf16[480,2240]{1,0:T(8,128)(2,1)} %bitcast.8, bf16[480,2240]{1,0:T(8,128)(2,1)} %bitcast.9, bf16[480,2240]{1,0:T(8,128)(2,1)} %bitcast.10, ...), custom_call_target="tpu_custom_call" | custom-call | flops 240844800 | bytes 4300800 | tf_op jit(solution)/shard_map/frame_states/pallas_call | solution.py:128
  3.7 0.5 %collective-permute-start = (bf16[1024,128]{1,0:T(8,128)(2,1)S(1)}, bf16[1024,128]{1,0:T(8,128)(2,1)S(1)}, u32[]{:S(2)}, u32[]{:S(2)}) collective-permute-start(bf16[1024,128]{1,0:T(8,128)(2,1)S(1)} %get-tuple-element.24), channel_id=1, source_target_pairs={{0,1},{1,0},{2,3},{3,2},{4,5},{5,4},{6,7},{7,6},{8,9},{9,8},{10,11... | collective-permute-start | bytes 786440 | tf_op jit(solution)/shard_map/ppermute | solution.py:489
  4.3 1.2 %collective-permute-done.got_ref = bf16[1024,128]{1,0:T(8,128)(2,1)S(1)} collective-permute-done((bf16[1024,128]{1,0:T(8,128)(2,1)S(1)}, bf16[1024,128]{1,0:T(8,128)(2,1)S(1)}, u32[]{:S(2)}, u32[]{:S(2)}) %collective-permute-start) | collective-permute-done | bytes 262176 | tf_op jit(solution)/shard_map/ppermute | solution.py:489
  5.4 0.1 split_sum.1
  5.5 0.4 %collective-permute-start.3 = (bf16[2,1,80,2240]{3,2,1,0:T(8,128)(2,1)S(1)}, bf16[2,1,80,2240]{3,2,1,0:T(8,128)(2,1)S(1)}, u32[]{:S(2)}, u32[]{:S(2)}) collective-permute-start(bf16[2,1,80,2240]{3,2,1,0:T(8,128)(2,1)S(1)} %get-tuple-element.29), channel_id=1, source_target_pairs={{0,1},{1,0},{2,3},{3,2},{4,5},{5,4},{6,7},{7,6},{8,9},{9,8},{10,11... | collective-permute-start | bytes 2150408 | tf_op jit(solution)/shard_map/ppermute | solution.py:493
  5.9 2.7 %collective-permute-start.1 = (bf16[512,128]{1,0:T(8,128)(2,1)S(1)}, bf16[512,128]{1,0:T(8,128)(2,1)S(1)}, u32[]{:S(2)}, u32[]{:S(2)}) collective-permute-start(bf16[512,128]{1,0:T(8,128)(2,1)S(1)} %get-tuple-element.28), channel_id=1, source_target_pairs={{0,2},{2,0},{4,6},{6,4},{8,10},{10,8},{12,14},{14,12},{1,3},{3,1},... | collective-permute-start | bytes 393224 | tf_op jit(solution)/shard_map/ppermute | solution.py:485
  8.6 4.0 %collective-permute-done.1.refs_1_.partner_ref = bf16[512,128]{1,0:T(8,128)(2,1)S(1)} collective-permute-done((bf16[512,128]{1,0:T(8,128)(2,1)S(1)}, bf16[512,128]{1,0:T(8,128)(2,1)S(1)}, u32[]{:S(2)}, u32[]{:S(2)}) %collective-permute-start.1) | collective-permute-done | bytes 131104 | tf_op jit(solution)/shard_map/ppermute | solution.py:485
  12.7 1.9 %collective-permute-start.2 = (bf16[512,128]{1,0:T(8,128)(2,1)S(1)}, bf16[512,128]{1,0:T(8,128)(2,1)S(1)}, u32[]{:S(2)}, u32[]{:S(2)}) collective-permute-start(bf16[512,128]{1,0:T(8,128)(2,1)S(1)} %pair_sum.1.refs_0_), channel_id=1, source_target_pairs={{0,4},{2,6},{4,0},{6,2},{8,12},{10,14},{12,8},{14,10},{1,5},{3,7},... | collective-permute-start | bytes 393224 | tf_op jit(solution)/shard_map/ppermute | solution.py:485
  14.5 3.4 %collective-permute-done.2.refs_1_.refs_0_ = bf16[512,128]{1,0:T(8,128)(2,1)S(1)} collective-permute-done((bf16[512,128]{1,0:T(8,128)(2,1)S(1)}, bf16[512,128]{1,0:T(8,128)(2,1)S(1)}, u32[]{:S(2)}, u32[]{:S(2)}) %collective-permute-start.2) | collective-permute-done | bytes 131104 | tf_op jit(solution)/shard_map/ppermute | solution.py:485
  18.0 0.0 collective-permute-done.3.edge_ref
  18.0 2.6 %collective-permute-start.4 = (bf16[512,128]{1,0:T(8,128)(2,1)S(1)}, bf16[512,128]{1,0:T(8,128)(2,1)S(1)}, u32[]{:S(2)}, u32[]{:S(2)}) collective-permute-start(bf16[512,128]{1,0:T(8,128)(2,1)S(1)} %stride_sum.1), channel_id=1, source_target_pairs={{0,8},{2,10},{4,12},{6,14},{8,0},{10,2},{12,4},{14,6},{1,9},{3,11}... | collective-permute-start | bytes 393224 | tf_op jit(solution)/shard_map/ppermute | solution.py:485
  20.6 0.0 copy-start
  20.6 0.0 copy-start.1
  20.7 3.4 %prepare.1 = (bf16[560,2304]{1,0:T(8,128)(2,1)S(1)}, f32[560,2240]{1,0:T(8,128)S(1)}, f32[1,2240]{1,0:T(1,128)S(1)}) custom-call(bf16[480,2240]{1,0:T(8,128)(2,1)} %bitcast.12, bf16[480,2240]{1,0:T(8,128)(2,1)} %bitcast.14, bf16[2,1,80,2240]{3,2,1,0:T(8,128)(2,1)S(1)} %collective-permute-done.3.edge_ref, f32[1,2240]{1,0:T(1,128)S(1)} %broadcast_in_dim.3.gain_ref), custom_call_target="tpu_custom_call" | custom-call | flops 5017600 | bytes 10035200 | tf_op jit(solution)/shard_map/prepare/pallas_call | solution.py:201
  24.0 2.0 %collective-permute-done.4.refs_1_ = bf16[512,128]{1,0:T(8,128)(2,1)S(1)} collective-permute-done((bf16[512,128]{1,0:T(8,128)(2,1)S(1)}, bf16[512,128]{1,0:T(8,128)(2,1)S(1)}, u32[]{:S(2)}, u32[]{:S(2)}) %collective-permute-start.4) | collective-permute-done | bytes 131104 | tf_op jit(solution)/shard_map/ppermute | solution.py:485
  26.1 0.1 pair_sums.1
  26.2 1.1 %collective-permute-start.5 = (bf16[512,128]{1,0:T(8,128)(2,1)S(1)}, bf16[512,128]{1,0:T(8,128)(2,1)S(1)}, u32[]{:S(2)}, u32[]{:S(2)}) collective-permute-start(bf16[512,128]{1,0:T(8,128)(2,1)S(1)} %get-tuple-element.40), channel_id=1, source_target_pairs={{0,2},{2,0},{4,6},{6,4},{8,10},{10,8},{12,14},{14,12},{1,3},{3,1},... | collective-permute-start | bytes 393224 | tf_op jit(solution)/shard_map/ppermute | solution.py:485
  27.3 0.0 collective-permute-start.6
  27.3 4.0 %collective-permute-done.5.refs_1_ = bf16[512,128]{1,0:T(8,128)(2,1)S(1)} collective-permute-done((bf16[512,128]{1,0:T(8,128)(2,1)S(1)}, bf16[512,128]{1,0:T(8,128)(2,1)S(1)}, u32[]{:S(2)}, u32[]{:S(2)}) %collective-permute-start.5) | collective-permute-done | bytes 131104 | tf_op jit(solution)/shard_map/ppermute | solution.py:485
  31.2 0.0 collective-permute-start.7
  31.2 0.0 collective-permute-done.6.refs_2_
  31.3 1.3 %collective-permute-done.7.refs_3_ = bf16[512,128]{1,0:T(8,128)(2,1)S(1)} collective-permute-done((bf16[512,128]{1,0:T(8,128)(2,1)S(1)}, bf16[512,128]{1,0:T(8,128)(2,1)S(1)}, u32[]{:S(2)}, u32[]{:S(2)}) %collective-permute-start.7) | collective-permute-done | bytes 131104 | tf_op jit(solution)/shard_map/ppermute | solution.py:511
  32.6 0.0 copy-done
  32.6 10.7 %mix.1 = bf16[480,2240]{1,0:T(8,128)(2,1)} custom-call(bf16[560,2304]{1,0:T(8,128)(2,1)S(1)} %get-tuple-element.35.features_ref, f32[560,2240]{1,0:T(8,128)S(1)} %get-tuple-element.36.inputs_ref, f32[1,2240]{1,0:T(1,128)S(1)} %get-tuple-element.37.gain_ref, f32[9,2240]{1,0:T(8,128)S(1)} %copy-done, f32[9,2240]{1,0:T(8,128)S(1)} %copy-done.1, ...), custom_call_target="tpu_custom_call" | custom-call | flops 64512000 | bytes 6451200 | tf_op jit(solution)/shard_map/mix/pallas_call | solution.py:377
  (6 shorter events, 0.1 us)
Async XLA Ops:
  0.0 20.6 %copy-start.2 = (f32[2240]{0:T(1024)S(1)}, f32[2240]{0:T(1024)}, u32[]{:S(2)}) copy-start(f32[2240]{0:T(1024)} %param.11) | copy-start | bytes 26884
  3.7 1.7 %collective-permute-start = (bf16[1024,128]{1,0:T(8,128)(2,1)S(1)}, bf16[1024,128]{1,0:T(8,128)(2,1)S(1)}, u32[]{:S(2)}, u32[]{:S(2)}) collective-permute-start(bf16[1024,128]{1,0:T(8,128)(2,1)S(1)} %get-tuple-element.24), channel_id=1, source_target_pairs={{0,1},{1,0},{2,3},{3,2},{4,5},{5,4},{6,7},{7,6},{8,9},{9,8},{10,11... | collective-permute-start | bytes 786440 | tf_op jit(solution)/shard_map/ppermute | solution.py:489
  5.5 12.5 %collective-permute-start.3 = (bf16[2,1,80,2240]{3,2,1,0:T(8,128)(2,1)S(1)}, bf16[2,1,80,2240]{3,2,1,0:T(8,128)(2,1)S(1)}, u32[]{:S(2)}, u32[]{:S(2)}) collective-permute-start(bf16[2,1,80,2240]{3,2,1,0:T(8,128)(2,1)S(1)} %get-tuple-element.29), channel_id=1, source_target_pairs={{0,1},{1,0},{2,3},{3,2},{4,5},{5,4},{6,7},{7,6},{8,9},{9,8},{10,11... | collective-permute-start | bytes 2150408 | tf_op jit(solution)/shard_map/ppermute | solution.py:493
  5.9 6.7 %collective-permute-start.1 = (bf16[512,128]{1,0:T(8,128)(2,1)S(1)}, bf16[512,128]{1,0:T(8,128)(2,1)S(1)}, u32[]{:S(2)}, u32[]{:S(2)}) collective-permute-start(bf16[512,128]{1,0:T(8,128)(2,1)S(1)} %get-tuple-element.28), channel_id=1, source_target_pairs={{0,2},{2,0},{4,6},{6,4},{8,10},{10,8},{12,14},{14,12},{1,3},{3,1},... | collective-permute-start | bytes 393224 | tf_op jit(solution)/shard_map/ppermute | solution.py:485
  12.7 5.3 %collective-permute-start.2 = (bf16[512,128]{1,0:T(8,128)(2,1)S(1)}, bf16[512,128]{1,0:T(8,128)(2,1)S(1)}, u32[]{:S(2)}, u32[]{:S(2)}) collective-permute-start(bf16[512,128]{1,0:T(8,128)(2,1)S(1)} %pair_sum.1.refs_0_), channel_id=1, source_target_pairs={{0,4},{2,6},{4,0},{6,2},{8,12},{10,14},{12,8},{14,10},{1,5},{3,7},... | collective-permute-start | bytes 393224 | tf_op jit(solution)/shard_map/ppermute | solution.py:485
  18.0 8.1 %collective-permute-start.4 = (bf16[512,128]{1,0:T(8,128)(2,1)S(1)}, bf16[512,128]{1,0:T(8,128)(2,1)S(1)}, u32[]{:S(2)}, u32[]{:S(2)}) collective-permute-start(bf16[512,128]{1,0:T(8,128)(2,1)S(1)} %stride_sum.1), channel_id=1, source_target_pairs={{0,8},{2,10},{4,12},{6,14},{8,0},{10,2},{12,4},{14,6},{1,9},{3,11}... | collective-permute-start | bytes 393224 | tf_op jit(solution)/shard_map/ppermute | solution.py:485
  20.6 12.0 %copy-start = (f32[9,2240]{1,0:T(8,128)S(1)}, f32[9,2240]{1,0:T(8,128)}, u32[]{:S(2)}) copy-start(f32[9,2240]{1,0:T(8,128)} %vtaps_ref.1) | copy-start | bytes 241924
  20.6 12.0 %copy-start.1 = (f32[9,2240]{1,0:T(8,128)S(1)}, f32[9,2240]{1,0:T(8,128)}, u32[]{:S(2)}) copy-start(f32[9,2240]{1,0:T(8,128)} %gtaps_ref.1) | copy-start | bytes 241924
  26.2 5.0 %collective-permute-start.5 = (bf16[512,128]{1,0:T(8,128)(2,1)S(1)}, bf16[512,128]{1,0:T(8,128)(2,1)S(1)}, u32[]{:S(2)}, u32[]{:S(2)}) collective-permute-start(bf16[512,128]{1,0:T(8,128)(2,1)S(1)} %get-tuple-element.40), channel_id=1, source_target_pairs={{0,2},{2,0},{4,6},{6,4},{8,10},{10,8},{12,14},{14,12},{1,3},{3,1},... | collective-permute-start | bytes 393224 | tf_op jit(solution)/shard_map/ppermute | solution.py:485
  27.3 4.0 %collective-permute-start.6 = (bf16[512,128]{1,0:T(8,128)(2,1)S(1)}, bf16[512,128]{1,0:T(8,128)(2,1)S(1)}, u32[]{:S(2)}, u32[]{:S(2)}) collective-permute-start(bf16[512,128]{1,0:T(8,128)(2,1)S(1)} %get-tuple-element.39.refs_0_), channel_id=1, source_target_pairs={{0,1},{1,0},{2,3},{3,2},{4,5},{5,4},{6,7},{7,6},{8,9},{9,8},{10,11... | collective-permute-start | bytes 393224 | tf_op jit(solution)/shard_map/ppermute | solution.py:511
  31.2 1.3 %collective-permute-start.7 = (bf16[512,128]{1,0:T(8,128)(2,1)S(1)}, bf16[512,128]{1,0:T(8,128)(2,1)S(1)}, u32[]{:S(2)}, u32[]{:S(2)}) collective-permute-start(bf16[512,128]{1,0:T(8,128)(2,1)S(1)} %collective-permute-done.5.refs_1_), channel_id=1, source_target_pairs={{0,1},{1,0},{2,3},{3,2},{4,5},{5,4},{6,7},{7,6},{8,9},{9,8},{10,11... | collective-permute-start | bytes 393224 | tf_op jit(solution)/shard_map/ppermute | solution.py:511

commit v17 on v16

--- a/solution.py
+++ b/solution.py
@@ -151,8 +151,8 @@
 
 
 def prepare_kernel(
-    dim, queries_ref, residual_ref, edge_ref, gain_ref,
-    features_ref, inputs_ref, scaled_ref, held, wide, semaphores,
+    dim, queries_ref, residual_ref, edge_ref, gain_ref, vtaps_ref, gtaps_ref,
+    features_ref, inputs_ref, scaled_ref, taps_ref, held, wide, semaphores,
 ):
     tokens = queries_ref.shape[0]
     copies = [
@@ -168,6 +168,17 @@
         held[1, here] = edge_ref[1, e]
     scaled_ref[...] = gain_ref[...] * math.sqrt(HEAD_DIM)
     half = width // 2
+    for j in range(cdiv(dim, LANES)):
+        here = slice(j * LANES, min((j + 1) * LANES, dim))
+        used = here.stop - here.start
+        number = 0
+        for ref, factor in ((vtaps_ref, 1.0), (gtaps_ref, 0.5)):
+            for tap in (0, 3, 6):
+                one, two, three = [ref[tap + i : tap + i + 1, here] * factor for i in range(3)]
+                outer = 0.5 * (one + three)
+                for row in (one, outer + 0.5 * two, outer - 0.5 * two, three):
+                    taps_ref[j, number, :, :used] = jnp.broadcast_to(row, (8, used))
+                    number += 1
     for k, copy in enumerate(copies):
         copy.wait()
         for j in range(cdiv(dim, LANES)):
@@ -194,7 +205,7 @@
                     inputs_ref[source, here] = value
 
 
-def prepare(queries, residual, edge, gain):
+def prepare(queries, residual, edge, gain, value_taps, gate_taps):
     tokens, dim = queries.shape
     total = tokens + edge.shape[1] * edge.shape[2]
     whole = pl.BlockSpec(memory_space=pltpu.VMEM)
@@ -204,9 +215,10 @@
             pltpu.VMEM((total, cdiv(dim, LANES) * LANES), jnp.bfloat16),
             pltpu.VMEM((total, dim), jnp.float32),
             pltpu.VMEM((1, dim), jnp.float32),
+            pltpu.VMEM((cdiv(dim, LANES), 24, 8, LANES), jnp.float32),
         ],
-        in_specs=[pl.BlockSpec(memory_space=pl.ANY)] * 2 + [whole] * 2,
-        out_specs=[whole] * 3,
+        in_specs=[pl.BlockSpec(memory_space=pl.ANY)] * 2 + [whole] * 4,
+        out_specs=[whole] * 4,
         scratch_shapes=[
             pltpu.VMEM((2, total, dim), jnp.bfloat16),
             pltpu.VMEM((2, total, LANES), jnp.float32),
@@ -217,12 +229,12 @@
             flops=4 * total * dim, bytes_accessed=8 * total * dim, transcendentals=0
         ),
         name="prepare",
-    )(in_hbm(queries), in_hbm(residual), edge, gain)
+    )(in_hbm(queries), in_hbm(residual), edge, gain, value_taps, gate_taps)
 
 
 def mix_kernel(
     dim, rows, width, edges,
-    features_ref, inputs_ref, gain_ref, vtaps_ref, gtaps_ref, *refs,
+    features_ref, inputs_ref, gain_ref, taps_ref, *refs,
 ):
     *pieces, out_ref, states, weights, numer, mixed_rows, windows, results, held, semaphores = refs
     places = edge_places(lax.axis_size("space"), rows) if edges else []
@@ -230,7 +242,7 @@
     tokens = rows * width
     weights[...] = jnp.zeros_like(weights)
     for row in (0, rows + 1):
-        windows[:, :, row] = jnp.zeros((2, 4, width // 2, LANES), jnp.float32)
+        windows[:, :, row] = jnp.zeros((2, 4, width // 16, 8, LANES), jnp.float32)
     for k, piece in enumerate(pieces):
         size = piece.shape[0]
         states[pl.ds(pl.multiple_of(spots[k] * size, 16), size), :] = piece[...]
@@ -249,7 +261,7 @@
         before = jnp.concatenate([jnp.where(sub == 0, 0.0, before[:8]), before[8:]], axis=0)
         after = jnp.concatenate([after[: half - 8], jnp.where(sub == 7, 0.0, after[half - 8 :])], axis=0)
         for k, window in enumerate((before - right, left + right, right - left, left - after)):
-            windows[slot, k, place, :, :used] = window
+            windows[slot, k, place, :, :, :used] = window.reshape(half // 8, 8, used)
 
     def group(base, lanes):
         pairs = spans(lanes)
@@ -277,16 +289,14 @@
         def tile_sums(j, source):
             square = numer[source, j * LANES : (j + 1) * LANES]
             square = square * square
-            heads = tile_heads(j, lanes)
-            if len(heads) == 1:
-                return {heads[0][0]: jnp.sum(square, axis=-1, keepdims=True)}
-            (one, _, bound), (two, _, _) = heads
-            part = jnp.where(lane_iota(square.shape) < bound, square, 0.0)
-            rest = square - part
-            return {
-                one: jnp.sum(part, axis=-1, keepdims=True),
-                two: jnp.sum(rest, axis=-1, keepdims=True),
-            }
+            position = lane_iota(square.shape)
+            sums = {}
+            for head, lo, hi in tile_heads(j, lanes):
+                ends = (head + 1) * HEAD_DIM <= (j + 1) * LANES
+                fill = HEAD_DIM * 1e-06 / (LANES - (hi - lo)) if ends else 0.0
+                mine = position < hi if lo == 0 else position >= lo
+                sums[head] = jnp.sum(jnp.where(mine, square, fill), axis=-1, keepdims=True)
+            return sums
 
         def mix_tile(j):
             slot = j % 2
@@ -303,7 +313,7 @@
                 scale = jnp.broadcast_to(sums[0], (width, used))
                 if len(heads) > 1:
                     scale = jnp.where(lane_iota(scale.shape) < heads[0][2], scale, sums[1])
-                normed = numer[source, near] * lax.rsqrt(scale + HEAD_DIM * 1e-06)
+                normed = numer[source, near] * lax.rsqrt(scale)
                 return inputs_ref[source, here] + normed * gain_ref[:, here]
 
             for row in range(rows):
@@ -312,14 +322,6 @@
             for e in range(edges):
                 value = mixed(slice(tokens + e * width, tokens + (e + 1) * width))
                 store_windows(value, slot, used, 0, places[e])
-            taps = []
-            for ref, factor in ((vtaps_ref, 1.0), (gtaps_ref, 0.5)):
-                for tap_row in range(3):
-                    one, two, three = [
-                        ref[3 * tap_row + i : 3 * tap_row + i + 1, here] * factor for i in range(3)
-                    ]
-                    outer = 0.5 * (one + three)
-                    taps.append((one, outer + 0.5 * two, outer - 0.5 * two, three))
             for row in range(rows):
                 columns = []
                 for f in range(2):
@@ -327,7 +329,8 @@
                     for k in range(4):
                         total = None
                         for tap_row in range(3):
-                            term = taps[3 * f + tap_row][k] * windows[slot, k, row + tap_row, :, :used]
+                            tap = taps_ref[base // LANES + j, 12 * f + 4 * tap_row + k, :, :used]
+                            term = tap * windows[slot, k, row + tap_row, :, :, :used]
                             total = term if total is None else total + term
                         products.append(total)
                     columns.append(
@@ -338,9 +341,8 @@
                     )
                 for k, (side, (conv_v, half_g)) in enumerate(zip((even, odd), zip(*columns))):
                     center = mixed_rows[slot, row + 1, k * half : (k + 1) * half, :used]
-                    results[slot, row, side, :used] = center + conv_v * (
-                        half_g + half_g * jnp.tanh(half_g)
-                    )
+                    gated = conv_v * (half_g + half_g * jnp.tanh(half_g))
+                    results[slot, row, side, :used] = center + gated.reshape(half, used)
                 held[row * width : (row + 1) * width, here] = results[slot, row, :, :used].astype(
                     jnp.bfloat16
                 )
@@ -367,8 +369,8 @@
         copy.wait()
 
 
-def mix(prepared, value_taps, gate_taps, pieces, rows, width):
-    features, inputs, gain = prepared
+def mix(prepared, pieces, rows, width):
+    features, inputs, gain, taps = prepared
     total, dim = inputs.shape
     tokens = rows * width
     pairs = spans(min(GROUP, dim))
@@ -377,14 +379,14 @@
     return pl.pallas_call(
         functools.partial(mix_kernel, dim, rows, width, (total - tokens) // width),
         out_shape=jax.ShapeDtypeStruct((tokens, dim), jnp.bfloat16),
-        in_specs=[whole] * (5 + len(pieces)),
+        in_specs=[whole] * (4 + len(pieces)),
         out_specs=pl.BlockSpec(memory_space=pl.ANY),
         scratch_shapes=[
             pltpu.VMEM((sum(piece.shape[0] for piece in pieces), LANES), jnp.bfloat16),
             pltpu.VMEM((len(pairs), depth, 2 * LANES), jnp.bfloat16),
             pltpu.VMEM((total, GROUP), jnp.float32),
             pltpu.VMEM((2, rows + 2, width, LANES), jnp.float32),
-            pltpu.VMEM((2, 4, rows + 2, width // 2, LANES), jnp.float32),
+            pltpu.VMEM((2, 4, rows + 2, width // 16, 8, LANES), jnp.float32),
             pltpu.VMEM((2, rows, width, LANES), jnp.float32),
             pltpu.VMEM((tokens, dim), jnp.bfloat16),
             pltpu.SemaphoreType.DMA((len(group_lanes(dim)),)),
@@ -394,7 +396,7 @@
             flops=60 * tokens * dim, bytes_accessed=6 * tokens * dim, transcendentals=2 * tokens * dim
         ),
         name="mix",
-    )(features, inputs, gain, value_taps, gate_taps, *pieces)
+    )(features, inputs, gain, taps, *pieces)
 
 
 def edge_rows(queries, residual):
@@ -523,9 +525,11 @@
         queries.reshape(rows, width, dim),
         residual.reshape(rows, width, dim),
         state_rows,
-        lambda edge: prepare(flat(queries), flat(residual), edge, attn_gain[None]),
+        lambda edge: prepare(
+            flat(queries), flat(residual), edge, attn_gain[None], value_taps, gate_taps
+        ),
     )
-    out = mix(prepared, value_taps, gate_taps, pieces, rows, width)
+    out = mix(prepared, pieces, rows, width)
     return out.reshape(frames, rows, width, dim)
 
 

time: 43.5 us -> 43.5 us (level)
  no operation moved by 1% of the time
where the time goes in v17:
time: 43.5 us; the launch traced here: 43.3 us
  Pallas kernels  18.1 us (42%)
  waiting for transfers between devices  16 us (37%)
  starting transfers between devices  9.22 us (21%)
    ppermute x4, waiting for transfers between devices, running_states(): lax.ppermute(array, 'frame', [(f, f ^ stride) for f in range(frames)])  13.5 us
    pallas_call x1, Pallas kernels, mix(): pl.pallas_call(functools.partial(mix_kernel, dim, rows, width, (total - t...  10.7 us
    ppermute x4, starting transfers between devices, running_states(): lax.ppermute(array, 'frame', [(f, f ^ stride) for f in range(frames)])  8.24 us
    pallas_call x1, Pallas kernels, frame_states(): pl.pallas_call(body, out_shape=[pltpu.VMEM(part, jnp.bfloat16)] * parts +...  3.74 us
    pallas_call x1, Pallas kernels, prepare(): pl.pallas_call(functools.partial(prepare_kernel, dim), out_shape=[pltpu.V...  3.33 us
    ppermute x1, waiting for transfers between devices, running_states(): lax.ppermute(other, 'space', swap)  1.34 us
    ppermute x1, waiting for transfers between devices, running_states(): got = lax.ppermute(sent, 'space', swap)  1.16 us
  transfers between devices with their start and end apart: 8, of which 6 were waited for; matrix products, arithmetic and copies ran while one was open for 0% of the time, Pallas kernels for 8%

profile of v17, /device:TPU:0, one launch (start us, length us, event | category | flops | bytes accessed | tf_op | source)
XLA Modules:
  0.0 43.3 jit_solution(6106359473521381755)
XLA Ops:
  0.0 3.7 %frame_states.1 = (bf16[1024,128]{1,0:T(8,128)(2,1)S(1)}, bf16[1024,128]{1,0:T(8,128)(2,1)S(1)}, bf16[2,1,80,2240]{3,2,1,0:T(8,128)(2,1)S(1)}) custom-call(bf16[480,2240]{1,0:T(8,128)(2,1)} %bitcast.7, bf16[480,2240]{1,0:T(8,128)(2,1)} %bitcast.8, bf16[480,2240]{1,0:T(8,128)(2,1)} %bitcast.9, bf16[480,2240]{1,0:T(8,128)(2,1)} %bitcast.10, ...), custom_call_target="tpu_custom_call" | custom-call | flops 240844800 | bytes 4300800 | tf_op jit(solution)/shard_map/frame_states/pallas_call | solution.py:128
  3.8 0.5 %collective-permute-start = (bf16[1024,128]{1,0:T(8,128)(2,1)S(1)}, bf16[1024,128]{1,0:T(8,128)(2,1)S(1)}, u32[]{:S(2)}, u32[]{:S(2)}) collective-permute-start(bf16[1024,128]{1,0:T(8,128)(2,1)S(1)} %get-tuple-element.26), channel_id=1, source_target_pairs={{0,1},{1,0},{2,3},{3,2},{4,5},{5,4},{6,7},{7,6},{8,9},{9,8},{10,11... | collective-permute-start | bytes 786440 | tf_op jit(solution)/shard_map/ppermute | solution.py:491
  4.3 1.2 %collective-permute-done.got_ref = bf16[1024,128]{1,0:T(8,128)(2,1)S(1)} collective-permute-done((bf16[1024,128]{1,0:T(8,128)(2,1)S(1)}, bf16[1024,128]{1,0:T(8,128)(2,1)S(1)}, u32[]{:S(2)}, u32[]{:S(2)}) %collective-permute-start) | collective-permute-done | bytes 262176 | tf_op jit(solution)/shard_map/ppermute | solution.py:491
  5.5 0.1 split_sum.1
  5.5 0.4 %collective-permute-start.3 = (bf16[2,1,80,2240]{3,2,1,0:T(8,128)(2,1)S(1)}, bf16[2,1,80,2240]{3,2,1,0:T(8,128)(2,1)S(1)}, u32[]{:S(2)}, u32[]{:S(2)}) collective-permute-start(bf16[2,1,80,2240]{3,2,1,0:T(8,128)(2,1)S(1)} %get-tuple-element.31), channel_id=1, source_target_pairs={{0,1},{1,0},{2,3},{3,2},{4,5},{5,4},{6,7},{7,6},{8,9},{9,8},{10,11... | collective-permute-start | bytes 2150408 | tf_op jit(solution)/shard_map/ppermute | solution.py:495
  6.0 2.7 %collective-permute-start.1 = (bf16[512,128]{1,0:T(8,128)(2,1)S(1)}, bf16[512,128]{1,0:T(8,128)(2,1)S(1)}, u32[]{:S(2)}, u32[]{:S(2)}) collective-permute-start(bf16[512,128]{1,0:T(8,128)(2,1)S(1)} %get-tuple-element.30), channel_id=1, source_target_pairs={{0,2},{2,0},{4,6},{6,4},{8,10},{10,8},{12,14},{14,12},{1,3},{3,1},... | collective-permute-start | bytes 393224 | tf_op jit(solution)/shard_map/ppermute | solution.py:487
  8.6 4.0 %collective-permute-done.1.refs_1_.partner_ref = bf16[512,128]{1,0:T(8,128)(2,1)S(1)} collective-permute-done((bf16[512,128]{1,0:T(8,128)(2,1)S(1)}, bf16[512,128]{1,0:T(8,128)(2,1)S(1)}, u32[]{:S(2)}, u32[]{:S(2)}) %collective-permute-start.1) | collective-permute-done | bytes 131104 | tf_op jit(solution)/shard_map/ppermute | solution.py:487
  12.7 1.9 %collective-permute-start.2 = (bf16[512,128]{1,0:T(8,128)(2,1)S(1)}, bf16[512,128]{1,0:T(8,128)(2,1)S(1)}, u32[]{:S(2)}, u32[]{:S(2)}) collective-permute-start(bf16[512,128]{1,0:T(8,128)(2,1)S(1)} %pair_sum.1.refs_0_), channel_id=1, source_target_pairs={{0,4},{2,6},{4,0},{6,2},{8,12},{10,14},{12,8},{14,10},{1,5},{3,7},... | collective-permute-start | bytes 393224 | tf_op jit(solution)/shard_map/ppermute | solution.py:487
  14.5 3.4 %collective-permute-done.2.refs_1_.refs_0_ = bf16[512,128]{1,0:T(8,128)(2,1)S(1)} collective-permute-done((bf16[512,128]{1,0:T(8,128)(2,1)S(1)}, bf16[512,128]{1,0:T(8,128)(2,1)S(1)}, u32[]{:S(2)}, u32[]{:S(2)}) %collective-permute-start.2) | collective-permute-done | bytes 131104 | tf_op jit(solution)/shard_map/ppermute | solution.py:487
  18.0 0.0 collective-permute-done.3.edge_ref
  18.0 2.6 %collective-permute-start.4 = (bf16[512,128]{1,0:T(8,128)(2,1)S(1)}, bf16[512,128]{1,0:T(8,128)(2,1)S(1)}, u32[]{:S(2)}, u32[]{:S(2)}) collective-permute-start(bf16[512,128]{1,0:T(8,128)(2,1)S(1)} %stride_sum.1), channel_id=1, source_target_pairs={{0,8},{2,10},{4,12},{6,14},{8,0},{10,2},{12,4},{14,6},{1,9},{3,11}... | collective-permute-start | bytes 393224 | tf_op jit(solution)/shard_map/ppermute | solution.py:487
  20.6 0.0 copy-done.2
  20.6 0.0 copy-done
  20.7 0.0 copy-done.1
  20.7 3.3 %prepare.1 = (bf16[560,2304]{1,0:T(8,128)(2,1)S(1)}, f32[560,2240]{1,0:T(8,128)S(1)}, f32[1,2240]{1,0:T(1,128)S(1)}, f32[18,24,8,128]{3,2,1,0:T(8,128)S(1)}) custom-call(bf16[480,2240]{1,0:T(8,128)(2,1)} %bitcast.12, bf16[480,2240]{1,0:T(8,128)(2,1)} %bitcast.14, bf16[2,1,80,2240]{3,2,1,0:T(8,128)(2,1)S(1)} %collective-permute-done.3.edge_ref, ...), custom_call_target="tpu_custom_call" | custom-call | flops 5017600 | bytes 10035200 | tf_op jit(solution)/shard_map/prepare/pallas_call | solution.py:212
  24.0 2.1 %collective-permute-done.4.refs_1_ = bf16[512,128]{1,0:T(8,128)(2,1)S(1)} collective-permute-done((bf16[512,128]{1,0:T(8,128)(2,1)S(1)}, bf16[512,128]{1,0:T(8,128)(2,1)S(1)}, u32[]{:S(2)}, u32[]{:S(2)}) %collective-permute-start.4) | collective-permute-done | bytes 131104 | tf_op jit(solution)/shard_map/ppermute | solution.py:487
  26.1 0.1 pair_sums.1
  26.2 1.1 %collective-permute-start.5 = (bf16[512,128]{1,0:T(8,128)(2,1)S(1)}, bf16[512,128]{1,0:T(8,128)(2,1)S(1)}, u32[]{:S(2)}, u32[]{:S(2)}) collective-permute-start(bf16[512,128]{1,0:T(8,128)(2,1)S(1)} %get-tuple-element.44), channel_id=1, source_target_pairs={{0,2},{2,0},{4,6},{6,4},{8,10},{10,8},{12,14},{14,12},{1,3},{3,1},... | collective-permute-start | bytes 393224 | tf_op jit(solution)/shard_map/ppermute | solution.py:487
  27.3 0.0 collective-permute-start.6
  27.3 4.0 %collective-permute-done.5.refs_1_ = bf16[512,128]{1,0:T(8,128)(2,1)S(1)} collective-permute-done((bf16[512,128]{1,0:T(8,128)(2,1)S(1)}, bf16[512,128]{1,0:T(8,128)(2,1)S(1)}, u32[]{:S(2)}, u32[]{:S(2)}) %collective-permute-start.5) | collective-permute-done | bytes 131104 | tf_op jit(solution)/shard_map/ppermute | solution.py:487
  31.3 0.0 collective-permute-start.7
  31.3 0.0 collective-permute-done.6.refs_2_
  31.3 1.3 %collective-permute-done.7.refs_3_ = bf16[512,128]{1,0:T(8,128)(2,1)S(1)} collective-permute-done((bf16[512,128]{1,0:T(8,128)(2,1)S(1)}, bf16[512,128]{1,0:T(8,128)(2,1)S(1)}, u32[]{:S(2)}, u32[]{:S(2)}) %collective-permute-start.7) | collective-permute-done | bytes 131104 | tf_op jit(solution)/shard_map/ppermute | solution.py:513
  32.6 10.7 %mix.1 = bf16[480,2240]{1,0:T(8,128)(2,1)} custom-call(bf16[560,2304]{1,0:T(8,128)(2,1)S(1)} %get-tuple-element.38.features_ref, f32[560,2240]{1,0:T(8,128)S(1)} %get-tuple-element.39.inputs_ref, f32[1,2240]{1,0:T(1,128)S(1)} %get-tuple-element.40.gain_ref, f32[18,24,8,128]{3,2,1,0:T(8,128)S(1)} %get-tuple-element.41.taps_ref, ...), custom_call_target="tpu_custom_call" | custom-call | flops 64512000 | bytes 6451200 | tf_op jit(solution)/shard_map/mix/pallas_call | solution.py:379
  (6 shorter events, 0.1 us)
Async XLA Ops:
  0.0 20.6 %copy-start.2 = (f32[2240]{0:T(1024)S(1)}, f32[2240]{0:T(1024)}, u32[]{:S(2)}) copy-start(f32[2240]{0:T(1024)} %param.11) | copy-start | bytes 26884
  0.0 20.6 %copy-start = (f32[9,2240]{1,0:T(8,128)S(1)}, f32[9,2240]{1,0:T(8,128)}, u32[]{:S(2)}) copy-start(f32[9,2240]{1,0:T(8,128)} %vtaps_ref.1) | copy-start | bytes 241924
  0.0 20.7 %copy-start.1 = (f32[9,2240]{1,0:T(8,128)S(1)}, f32[9,2240]{1,0:T(8,128)}, u32[]{:S(2)}) copy-start(f32[9,2240]{1,0:T(8,128)} %gtaps_ref.1) | copy-start | bytes 241924
  3.8 1.7 %collective-permute-start = (bf16[1024,128]{1,0:T(8,128)(2,1)S(1)}, bf16[1024,128]{1,0:T(8,128)(2,1)S(1)}, u32[]{:S(2)}, u32[]{:S(2)}) collective-permute-start(bf16[1024,128]{1,0:T(8,128)(2,1)S(1)} %get-tuple-element.26), channel_id=1, source_target_pairs={{0,1},{1,0},{2,3},{3,2},{4,5},{5,4},{6,7},{7,6},{8,9},{9,8},{10,11... | collective-permute-start | bytes 786440 | tf_op jit(solution)/shard_map/ppermute | solution.py:491
  5.5 12.5 %collective-permute-start.3 = (bf16[2,1,80,2240]{3,2,1,0:T(8,128)(2,1)S(1)}, bf16[2,1,80,2240]{3,2,1,0:T(8,128)(2,1)S(1)}, u32[]{:S(2)}, u32[]{:S(2)}) collective-permute-start(bf16[2,1,80,2240]{3,2,1,0:T(8,128)(2,1)S(1)} %get-tuple-element.31), channel_id=1, source_target_pairs={{0,1},{1,0},{2,3},{3,2},{4,5},{5,4},{6,7},{7,6},{8,9},{9,8},{10,11... | collective-permute-start | bytes 2150408 | tf_op jit(solution)/shard_map/ppermute | solution.py:495
  6.0 6.7 %collective-permute-start.1 = (bf16[512,128]{1,0:T(8,128)(2,1)S(1)}, bf16[512,128]{1,0:T(8,128)(2,1)S(1)}, u32[]{:S(2)}, u32[]{:S(2)}) collective-permute-start(bf16[512,128]{1,0:T(8,128)(2,1)S(1)} %get-tuple-element.30), channel_id=1, source_target_pairs={{0,2},{2,0},{4,6},{6,4},{8,10},{10,8},{12,14},{14,12},{1,3},{3,1},... | collective-permute-start | bytes 393224 | tf_op jit(solution)/shard_map/ppermute | solution.py:487
  12.7 5.3 %collective-permute-start.2 = (bf16[512,128]{1,0:T(8,128)(2,1)S(1)}, bf16[512,128]{1,0:T(8,128)(2,1)S(1)}, u32[]{:S(2)}, u32[]{:S(2)}) collective-permute-start(bf16[512,128]{1,0:T(8,128)(2,1)S(1)} %pair_sum.1.refs_0_), channel_id=1, source_target_pairs={{0,4},{2,6},{4,0},{6,2},{8,12},{10,14},{12,8},{14,10},{1,5},{3,7},... | collective-permute-start | bytes 393224 | tf_op jit(solution)/shard_map/ppermute | solution.py:487
  18.0 8.1 %collective-permute-start.4 = (bf16[512,128]{1,0:T(8,128)(2,1)S(1)}, bf16[512,128]{1,0:T(8,128)(2,1)S(1)}, u32[]{:S(2)}, u32[]{:S(2)}) collective-permute-start(bf16[512,128]{1,0:T(8,128)(2,1)S(1)} %stride_sum.1), channel_id=1, source_target_pairs={{0,8},{2,10},{4,12},{6,14},{8,0},{10,2},{12,4},{14,6},{1,9},{3,11}... | collective-permute-start | bytes 393224 | tf_op jit(solution)/shard_map/ppermute | solution.py:487
  26.2 5.0 %collective-permute-start.5 = (bf16[512,128]{1,0:T(8,128)(2,1)S(1)}, bf16[512,128]{1,0:T(8,128)(2,1)S(1)}, u32[]{:S(2)}, u32[]{:S(2)}) collective-permute-start(bf16[512,128]{1,0:T(8,128)(2,1)S(1)} %get-tuple-element.44), channel_id=1, source_target_pairs={{0,2},{2,0},{4,6},{6,4},{8,10},{10,8},{12,14},{14,12},{1,3},{3,1},... | collective-permute-start | bytes 393224 | tf_op jit(solution)/shard_map/ppermute | solution.py:487
  27.3 4.0 %collective-permute-start.6 = (bf16[512,128]{1,0:T(8,128)(2,1)S(1)}, bf16[512,128]{1,0:T(8,128)(2,1)S(1)}, u32[]{:S(2)}, u32[]{:S(2)}) collective-permute-start(bf16[512,128]{1,0:T(8,128)(2,1)S(1)} %get-tuple-element.43.refs_0_), channel_id=1, source_target_pairs={{0,1},{1,0},{2,3},{3,2},{4,5},{5,4},{6,7},{7,6},{8,9},{9,8},{10,11... | collective-permute-start | bytes 393224 | tf_op jit(solution)/shard_map/ppermute | solution.py:513
  31.3 1.3 %collective-permute-start.7 = (bf16[512,128]{1,0:T(8,128)(2,1)S(1)}, bf16[512,128]{1,0:T(8,128)(2,1)S(1)}, u32[]{:S(2)}, u32[]{:S(2)}) collective-permute-start(bf16[512,128]{1,0:T(8,128)(2,1)S(1)} %collective-permute-done.5.refs_1_), channel_id=1, source_target_pairs={{0,1},{1,0},{2,3},{3,2},{4,5},{5,4},{6,7},{7,6},{8,9},{9,8},{10,11... | collective-permute-start | bytes 393224 | tf_op jit(solution)/shard_map/ppermute | solution.py:513

commit v18 on v17

--- a/solution.py
+++ b/solution.py
@@ -285,10 +285,15 @@
             )
             here = slice(tiles[0] * LANES, tiles[0] * LANES + wide)
             numer[:, here] = product
-
-        def tile_sums(j, source):
-            square = numer[source, j * LANES : (j + 1) * LANES]
-            square = square * square
+            for side, j in enumerate(tiles):
+                for row in range(rows + edges):
+                    source = slice(row * width, (row + 1) * width)
+                    square = product[source, side * LANES : (side + 1) * LANES]
+                    parts.setdefault(source.start, []).append(tile_sums(j, square * square))
+
+        parts = {}
+
+        def tile_sums(j, square):
             position = lane_iota(square.shape)
             sums = {}
             for head, lo, hi in tile_heads(j, lanes):
@@ -323,23 +328,26 @@
                 value = mixed(slice(tokens + e * width, tokens + (e + 1) * width))
                 store_windows(value, slot, used, 0, places[e])
             for row in range(rows):
-                columns = []
-                for f in range(2):
-                    products = []
-                    for k in range(4):
-                        total = None
-                        for tap_row in range(3):
+                lefts, rights = [], []
+                for k in range(4):
+                    products = [None, None]
+                    for tap_row in range(3):
+                        window = windows[slot, k, row + tap_row, :, :, :used]
+                        for f in range(2):
                             tap = taps_ref[base // LANES + j, 12 * f + 4 * tap_row + k, :, :used]
-                            term = tap * windows[slot, k, row + tap_row, :, :, :used]
-                            total = term if total is None else total + term
-                        products.append(total)
-                    columns.append(
-                        (
-                            products[0] + products[1] + products[2],
-                            products[1] - products[2] - products[3],
-                        )
-                    )
-                for k, (side, (conv_v, half_g)) in enumerate(zip((even, odd), zip(*columns))):
+                            term = tap * window
+                            products[f] = term if tap_row == 0 else products[f] + term
+                    if k == 0:
+                        lefts = products
+                    elif k == 1:
+                        lefts = [one + two for one, two in zip(lefts, products)]
+                        rights = products
+                    elif k == 2:
+                        lefts = [one + two for one, two in zip(lefts, products)]
+                        rights = [one - two for one, two in zip(rights, products)]
+                    else:
+                        rights = [one - two for one, two in zip(rights, products)]
+                for k, (side, (conv_v, half_g)) in enumerate(zip((even, odd), (lefts, rights))):
                     center = mixed_rows[slot, row + 1, k * half : (k + 1) * half, :used]
                     gated = conv_v * (half_g + half_g * jnp.tanh(half_g))
                     results[slot, row, side, :used] = center + gated.reshape(half, used)
@@ -347,13 +355,8 @@
                     jnp.bfloat16
                 )
 
-        parts = {}
-        for number, (tiles, _, _) in enumerate(pairs):
+        for number in range(len(pairs)):
             numerators(number)
-            for j in tiles:
-                for row in range(rows + edges):
-                    source = slice(row * width, (row + 1) * width)
-                    parts.setdefault(source.start, []).append(tile_sums(j, source))
         for j in range(cdiv(lanes, LANES)):
             mix_tile(j)
 

time: 43.5 us -> 43.4 us (level)
  no operation moved by 1% of the time
where the time goes in v18:
time: 43.4 us; the launch traced here: 43.3 us
  Pallas kernels  18 us (41%)
  waiting for transfers between devices  16 us (37%)
  starting transfers between devices  9.22 us (21%)
    ppermute x4, waiting for transfers between devices, running_states(): lax.ppermute(array, 'frame', [(f, f ^ stride) for f in range(frames)])  13.5 us
    pallas_call x1, Pallas kernels, mix(): pl.pallas_call(functools.partial(mix_kernel, dim, rows, width, (total - t...  10.7 us
    ppermute x4, starting transfers between devices, running_states(): lax.ppermute(array, 'frame', [(f, f ^ stride) for f in range(frames)])  8.24 us
    pallas_call x1, Pallas kernels, frame_states(): pl.pallas_call(body, out_shape=[pltpu.VMEM(part, jnp.bfloat16)] * parts +...  3.74 us
    pallas_call x1, Pallas kernels, prepare(): pl.pallas_call(functools.partial(prepare_kernel, dim), out_shape=[pltpu.V...  3.33 us
    ppermute x1, waiting for transfers between devices, running_states(): lax.ppermute(other, 'space', swap)  1.34 us
    ppermute x1, waiting for transfers between devices, running_states(): got = lax.ppermute(sent, 'space', swap)  1.16 us
  transfers between devices with their start and end apart: 8, of which 6 were waited for; matrix products, arithmetic and copies ran while one was open for 0% of the time, Pallas kernels for 8%

profile of v18, /device:TPU:0, one launch (start us, length us, event | category | flops | bytes accessed | tf_op | source)
XLA Modules:
  0.0 43.3 jit_solution(159804939166852617)
XLA Ops:
  0.0 3.7 %frame_states.1 = (bf16[1024,128]{1,0:T(8,128)(2,1)S(1)}, bf16[1024,128]{1,0:T(8,128)(2,1)S(1)}, bf16[2,1,80,2240]{3,2,1,0:T(8,128)(2,1)S(1)}) custom-call(bf16[480,2240]{1,0:T(8,128)(2,1)} %bitcast.7, bf16[480,2240]{1,0:T(8,128)(2,1)} %bitcast.8, bf16[480,2240]{1,0:T(8,128)(2,1)} %bitcast.9, bf16[480,2240]{1,0:T(8,128)(2,1)} %bitcast.10, ...), custom_call_target="tpu_custom_call" | custom-call | flops 240844800 | bytes 4300800 | tf_op jit(solution)/shard_map/frame_states/pallas_call | solution.py:128
  3.8 0.5 %collective-permute-start = (bf16[1024,128]{1,0:T(8,128)(2,1)S(1)}, bf16[1024,128]{1,0:T(8,128)(2,1)S(1)}, u32[]{:S(2)}, u32[]{:S(2)}) collective-permute-start(bf16[1024,128]{1,0:T(8,128)(2,1)S(1)} %get-tuple-element.26), channel_id=1, source_target_pairs={{0,1},{1,0},{2,3},{3,2},{4,5},{5,4},{6,7},{7,6},{8,9},{9,8},{10,11... | collective-permute-start | bytes 786440 | tf_op jit(solution)/shard_map/ppermute | solution.py:494
  4.3 1.2 %collective-permute-done.got_ref = bf16[1024,128]{1,0:T(8,128)(2,1)S(1)} collective-permute-done((bf16[1024,128]{1,0:T(8,128)(2,1)S(1)}, bf16[1024,128]{1,0:T(8,128)(2,1)S(1)}, u32[]{:S(2)}, u32[]{:S(2)}) %collective-permute-start) | collective-permute-done | bytes 262176 | tf_op jit(solution)/shard_map/ppermute | solution.py:494
  5.5 0.1 split_sum.1
  5.5 0.4 %collective-permute-start.3 = (bf16[2,1,80,2240]{3,2,1,0:T(8,128)(2,1)S(1)}, bf16[2,1,80,2240]{3,2,1,0:T(8,128)(2,1)S(1)}, u32[]{:S(2)}, u32[]{:S(2)}) collective-permute-start(bf16[2,1,80,2240]{3,2,1,0:T(8,128)(2,1)S(1)} %get-tuple-element.31), channel_id=1, source_target_pairs={{0,1},{1,0},{2,3},{3,2},{4,5},{5,4},{6,7},{7,6},{8,9},{9,8},{10,11... | collective-permute-start | bytes 2150408 | tf_op jit(solution)/shard_map/ppermute | solution.py:498
  6.0 2.7 %collective-permute-start.1 = (bf16[512,128]{1,0:T(8,128)(2,1)S(1)}, bf16[512,128]{1,0:T(8,128)(2,1)S(1)}, u32[]{:S(2)}, u32[]{:S(2)}) collective-permute-start(bf16[512,128]{1,0:T(8,128)(2,1)S(1)} %get-tuple-element.30), channel_id=1, source_target_pairs={{0,2},{2,0},{4,6},{6,4},{8,10},{10,8},{12,14},{14,12},{1,3},{3,1},... | collective-permute-start | bytes 393224 | tf_op jit(solution)/shard_map/ppermute | solution.py:490
  8.6 4.0 %collective-permute-done.1.refs_1_.partner_ref = bf16[512,128]{1,0:T(8,128)(2,1)S(1)} collective-permute-done((bf16[512,128]{1,0:T(8,128)(2,1)S(1)}, bf16[512,128]{1,0:T(8,128)(2,1)S(1)}, u32[]{:S(2)}, u32[]{:S(2)}) %collective-permute-start.1) | collective-permute-done | bytes 131104 | tf_op jit(solution)/shard_map/ppermute | solution.py:490
  12.7 1.9 %collective-permute-start.2 = (bf16[512,128]{1,0:T(8,128)(2,1)S(1)}, bf16[512,128]{1,0:T(8,128)(2,1)S(1)}, u32[]{:S(2)}, u32[]{:S(2)}) collective-permute-start(bf16[512,128]{1,0:T(8,128)(2,1)S(1)} %pair_sum.1.refs_0_), channel_id=1, source_target_pairs={{0,4},{2,6},{4,0},{6,2},{8,12},{10,14},{12,8},{14,10},{1,5},{3,7},... | collective-permute-start | bytes 393224 | tf_op jit(solution)/shard_map/ppermute | solution.py:490
  14.5 3.4 %collective-permute-done.2.refs_1_.refs_0_ = bf16[512,128]{1,0:T(8,128)(2,1)S(1)} collective-permute-done((bf16[512,128]{1,0:T(8,128)(2,1)S(1)}, bf16[512,128]{1,0:T(8,128)(2,1)S(1)}, u32[]{:S(2)}, u32[]{:S(2)}) %collective-permute-start.2) | collective-permute-done | bytes 131104 | tf_op jit(solution)/shard_map/ppermute | solution.py:490
  18.0 0.0 collective-permute-done.3.edge_ref
  18.0 2.6 %collective-permute-start.4 = (bf16[512,128]{1,0:T(8,128)(2,1)S(1)}, bf16[512,128]{1,0:T(8,128)(2,1)S(1)}, u32[]{:S(2)}, u32[]{:S(2)}) collective-permute-start(bf16[512,128]{1,0:T(8,128)(2,1)S(1)} %stride_sum.1), channel_id=1, source_target_pairs={{0,8},{2,10},{4,12},{6,14},{8,0},{10,2},{12,4},{14,6},{1,9},{3,11}... | collective-permute-start | bytes 393224 | tf_op jit(solution)/shard_map/ppermute | solution.py:490
  20.6 0.0 copy-done.2
  20.6 0.0 copy-done
  20.7 0.0 copy-done.1
  20.7 3.3 %prepare.1 = (bf16[560,2304]{1,0:T(8,128)(2,1)S(1)}, f32[560,2240]{1,0:T(8,128)S(1)}, f32[1,2240]{1,0:T(1,128)S(1)}, f32[18,24,8,128]{3,2,1,0:T(8,128)S(1)}) custom-call(bf16[480,2240]{1,0:T(8,128)(2,1)} %bitcast.12, bf16[480,2240]{1,0:T(8,128)(2,1)} %bitcast.14, bf16[2,1,80,2240]{3,2,1,0:T(8,128)(2,1)S(1)} %collective-permute-done.3.edge_ref, ...), custom_call_target="tpu_custom_call" | custom-call | flops 5017600 | bytes 10035200 | tf_op jit(solution)/shard_map/prepare/pallas_call | solution.py:212
  24.0 2.1 %collective-permute-done.4.refs_1_ = bf16[512,128]{1,0:T(8,128)(2,1)S(1)} collective-permute-done((bf16[512,128]{1,0:T(8,128)(2,1)S(1)}, bf16[512,128]{1,0:T(8,128)(2,1)S(1)}, u32[]{:S(2)}, u32[]{:S(2)}) %collective-permute-start.4) | collective-permute-done | bytes 131104 | tf_op jit(solution)/shard_map/ppermute | solution.py:490
  26.1 0.1 pair_sums.1
  26.2 1.1 %collective-permute-start.5 = (bf16[512,128]{1,0:T(8,128)(2,1)S(1)}, bf16[512,128]{1,0:T(8,128)(2,1)S(1)}, u32[]{:S(2)}, u32[]{:S(2)}) collective-permute-start(bf16[512,128]{1,0:T(8,128)(2,1)S(1)} %get-tuple-element.44), channel_id=1, source_target_pairs={{0,2},{2,0},{4,6},{6,4},{8,10},{10,8},{12,14},{14,12},{1,3},{3,1},... | collective-permute-start | bytes 393224 | tf_op jit(solution)/shard_map/ppermute | solution.py:490
  27.3 0.0 collective-permute-start.6
  27.3 4.0 %collective-permute-done.5.refs_1_ = bf16[512,128]{1,0:T(8,128)(2,1)S(1)} collective-permute-done((bf16[512,128]{1,0:T(8,128)(2,1)S(1)}, bf16[512,128]{1,0:T(8,128)(2,1)S(1)}, u32[]{:S(2)}, u32[]{:S(2)}) %collective-permute-start.5) | collective-permute-done | bytes 131104 | tf_op jit(solution)/shard_map/ppermute | solution.py:490
  31.3 0.0 collective-permute-start.7
  31.3 0.0 collective-permute-done.6.refs_2_
  31.3 1.3 %collective-permute-done.7.refs_3_ = bf16[512,128]{1,0:T(8,128)(2,1)S(1)} collective-permute-done((bf16[512,128]{1,0:T(8,128)(2,1)S(1)}, bf16[512,128]{1,0:T(8,128)(2,1)S(1)}, u32[]{:S(2)}, u32[]{:S(2)}) %collective-permute-start.7) | collective-permute-done | bytes 131104 | tf_op jit(solution)/shard_map/ppermute | solution.py:516
  32.6 10.7 %mix.1 = bf16[480,2240]{1,0:T(8,128)(2,1)} custom-call(bf16[560,2304]{1,0:T(8,128)(2,1)S(1)} %get-tuple-element.38.features_ref, f32[560,2240]{1,0:T(8,128)S(1)} %get-tuple-element.39.inputs_ref, f32[1,2240]{1,0:T(1,128)S(1)} %get-tuple-element.40.gain_ref, f32[18,24,8,128]{3,2,1,0:T(8,128)S(1)} %get-tuple-element.41.taps_ref, ...), custom_call_target="tpu_custom_call" | custom-call | flops 64512000 | bytes 6451200 | tf_op jit(solution)/shard_map/mix/pallas_call | solution.py:382
  (6 shorter events, 0.1 us)
Async XLA Ops:
  0.0 20.6 %copy-start.2 = (f32[2240]{0:T(1024)S(1)}, f32[2240]{0:T(1024)}, u32[]{:S(2)}) copy-start(f32[2240]{0:T(1024)} %param.11) | copy-start | bytes 26884
  0.0 20.6 %copy-start = (f32[9,2240]{1,0:T(8,128)S(1)}, f32[9,2240]{1,0:T(8,128)}, u32[]{:S(2)}) copy-start(f32[9,2240]{1,0:T(8,128)} %vtaps_ref.1) | copy-start | bytes 241924
  0.0 20.7 %copy-start.1 = (f32[9,2240]{1,0:T(8,128)S(1)}, f32[9,2240]{1,0:T(8,128)}, u32[]{:S(2)}) copy-start(f32[9,2240]{1,0:T(8,128)} %gtaps_ref.1) | copy-start | bytes 241924
  3.8 1.7 %collective-permute-start = (bf16[1024,128]{1,0:T(8,128)(2,1)S(1)}, bf16[1024,128]{1,0:T(8,128)(2,1)S(1)}, u32[]{:S(2)}, u32[]{:S(2)}) collective-permute-start(bf16[1024,128]{1,0:T(8,128)(2,1)S(1)} %get-tuple-element.26), channel_id=1, source_target_pairs={{0,1},{1,0},{2,3},{3,2},{4,5},{5,4},{6,7},{7,6},{8,9},{9,8},{10,11... | collective-permute-start | bytes 786440 | tf_op jit(solution)/shard_map/ppermute | solution.py:494
  5.5 12.5 %collective-permute-start.3 = (bf16[2,1,80,2240]{3,2,1,0:T(8,128)(2,1)S(1)}, bf16[2,1,80,2240]{3,2,1,0:T(8,128)(2,1)S(1)}, u32[]{:S(2)}, u32[]{:S(2)}) collective-permute-start(bf16[2,1,80,2240]{3,2,1,0:T(8,128)(2,1)S(1)} %get-tuple-element.31), channel_id=1, source_target_pairs={{0,1},{1,0},{2,3},{3,2},{4,5},{5,4},{6,7},{7,6},{8,9},{9,8},{10,11... | collective-permute-start | bytes 2150408 | tf_op jit(solution)/shard_map/ppermute | solution.py:498
  6.0 6.7 %collective-permute-start.1 = (bf16[512,128]{1,0:T(8,128)(2,1)S(1)}, bf16[512,128]{1,0:T(8,128)(2,1)S(1)}, u32[]{:S(2)}, u32[]{:S(2)}) collective-permute-start(bf16[512,128]{1,0:T(8,128)(2,1)S(1)} %get-tuple-element.30), channel_id=1, source_target_pairs={{0,2},{2,0},{4,6},{6,4},{8,10},{10,8},{12,14},{14,12},{1,3},{3,1},... | collective-permute-start | bytes 393224 | tf_op jit(solution)/shard_map/ppermute | solution.py:490
  12.7 5.3 %collective-permute-start.2 = (bf16[512,128]{1,0:T(8,128)(2,1)S(1)}, bf16[512,128]{1,0:T(8,128)(2,1)S(1)}, u32[]{:S(2)}, u32[]{:S(2)}) collective-permute-start(bf16[512,128]{1,0:T(8,128)(2,1)S(1)} %pair_sum.1.refs_0_), channel_id=1, source_target_pairs={{0,4},{2,6},{4,0},{6,2},{8,12},{10,14},{12,8},{14,10},{1,5},{3,7},... | collective-permute-start | bytes 393224 | tf_op jit(solution)/shard_map/ppermute | solution.py:490
  18.0 8.1 %collective-permute-start.4 = (bf16[512,128]{1,0:T(8,128)(2,1)S(1)}, bf16[512,128]{1,0:T(8,128)(2,1)S(1)}, u32[]{:S(2)}, u32[]{:S(2)}) collective-permute-start(bf16[512,128]{1,0:T(8,128)(2,1)S(1)} %stride_sum.1), channel_id=1, source_target_pairs={{0,8},{2,10},{4,12},{6,14},{8,0},{10,2},{12,4},{14,6},{1,9},{3,11}... | collective-permute-start | bytes 393224 | tf_op jit(solution)/shard_map/ppermute | solution.py:490
  26.2 5.0 %collective-permute-start.5 = (bf16[512,128]{1,0:T(8,128)(2,1)S(1)}, bf16[512,128]{1,0:T(8,128)(2,1)S(1)}, u32[]{:S(2)}, u32[]{:S(2)}) collective-permute-start(bf16[512,128]{1,0:T(8,128)(2,1)S(1)} %get-tuple-element.44), channel_id=1, source_target_pairs={{0,2},{2,0},{4,6},{6,4},{8,10},{10,8},{12,14},{14,12},{1,3},{3,1},... | collective-permute-start | bytes 393224 | tf_op jit(solution)/shard_map/ppermute | solution.py:490
  27.3 4.0 %collective-permute-start.6 = (bf16[512,128]{1,0:T(8,128)(2,1)S(1)}, bf16[512,128]{1,0:T(8,128)(2,1)S(1)}, u32[]{:S(2)}, u32[]{:S(2)}) collective-permute-start(bf16[512,128]{1,0:T(8,128)(2,1)S(1)} %get-tuple-element.43.refs_0_), channel_id=1, source_target_pairs={{0,1},{1,0},{2,3},{3,2},{4,5},{5,4},{6,7},{7,6},{8,9},{9,8},{10,11... | collective-permute-start | bytes 393224 | tf_op jit(solution)/shard_map/ppermute | solution.py:516
  31.3 1.3 %collective-permute-start.7 = (bf16[512,128]{1,0:T(8,128)(2,1)S(1)}, bf16[512,128]{1,0:T(8,128)(2,1)S(1)}, u32[]{:S(2)}, u32[]{:S(2)}) collective-permute-start(bf16[512,128]{1,0:T(8,128)(2,1)S(1)} %collective-permute-done.5.refs_1_), channel_id=1, source_target_pairs={{0,1},{1,0},{2,3},{3,2},{4,5},{5,4},{6,7},{7,6},{8,9},{9,8},{10,11... | collective-permute-start | bytes 393224 | tf_op jit(solution)/shard_map/ppermute | solution.py:516

commit v19 on v18

--- a/solution.py
+++ b/solution.py
@@ -43,107 +43,95 @@
     return result
 
 
-def by_group(dim, body):
-    full, rest = divmod(dim, GROUP)
-    if full:
-        pl.when(pl.program_id(0) < full)(lambda: body(GROUP))
-    if rest:
-        pl.when(pl.program_id(0) >= full)(lambda: body(rest))
-
-
-def state_kernel(dim, with_edge, keys_refs, values_refs, refs):
-    step = pl.program_id(0)
-    *refs, turned, whole, semaphores = refs
-    if with_edge:
-        *sources, edge_ref = refs[:2] + refs[-1:]
-        parts = refs[2:-1]
-        row = (sources[0].shape[0] - 1) * (1 - lax.axis_index("space"))
-        copies = [
-            pltpu.make_async_copy(source.at[row], edge_ref.at[k, 0], semaphores.at[k])
-            for k, source in enumerate(sources)
+def state_kernel(dim, parts, keys_ref, values_ref, *refs):
+    *refs, keys, values, turned, whole, semaphores = refs
+    sources, part_refs, edge_refs = refs[: -parts - 1], refs[-parts - 1 : -1], refs[-1:]
+    if not sources:
+        part_refs, edge_refs = refs, ()
+    order = sorted(group_lanes(dim), key=lambda item: item[1])
+    copies = []
+    for k, (base, lanes) in enumerate(order):
+        here = slice(base, base + lanes)
+        copies += [
+            pltpu.make_async_copy(ref.at[:, here], held.at[:, here], semaphores.at[2 * k + i])
+            for i, (ref, held) in enumerate(((keys_ref, keys), (values_ref, values)))
         ]
-
-        @pl.when(step == 0)
-        def _():
-            for copy in copies:
-                copy.start()
-
-    else:
-        parts = refs
-
-    def body(lanes):
-        for k, keys_ref in enumerate(keys_refs):
-            turned[k] = jnp.maximum(keys_ref[...], 0).T
-        lane = lane_iota((HEAD_DIM, LANES))
+    for k, source in enumerate(sources):
+        row = (source.shape[0] - 1) * (1 - lax.axis_index("space"))
+        copies.append(
+            pltpu.make_async_copy(
+                source.at[row], edge_refs[0].at[k, 0], semaphores.at[2 * len(order) + k]
+            )
+        )
+    for copy in copies:
+        copy.start()
+    used = cdiv(dim, LANES) * HEAD_DIM
+    if used < whole.shape[0]:
+        whole[used:, :] = jnp.zeros((whole.shape[0] - used, LANES), jnp.bfloat16)
+    lane = lane_iota((HEAD_DIM, LANES))
+    for k, (base, lanes) in enumerate(order):
+        for copy in copies[2 * k : 2 * k + 2]:
+            copy.wait()
+        turn = turned.at[k % 2]
+        turn[:lanes, :] = jnp.maximum(keys[:, base : base + lanes], 0).T
         for tiles, _, _ in spans(lanes):
             begin = tile_heads(tiles[0], lanes)[0][0]
             end = tile_heads(tiles[-1], lanes)[-1][0] + 1
-            product = sum(
-                jnp.dot(
-                    turned[k, begin * HEAD_DIM : end * HEAD_DIM, :],
-                    values_ref[:, tiles[0] * LANES : (tiles[-1] + 1) * LANES],
-                    preferred_element_type=jnp.float32,
-                )
-                for k, values_ref in enumerate(values_refs)
+            first, last = tiles[0] * LANES, min((tiles[-1] + 1) * LANES, lanes)
+            product = jnp.dot(
+                turn[begin * HEAD_DIM : end * HEAD_DIM, :],
+                values[:, base + first : base + last],
+                preferred_element_type=jnp.float32,
             )
-            for side, j in enumerate(tiles):
-                total = jnp.zeros((HEAD_DIM, LANES), jnp.float32)
-                for h, lo, hi in tile_heads(j, lanes):
-                    part = product[
+            for j in tiles:
+                wide = min(LANES, lanes - j * LANES)
+                blocks = [
+                    product[
                         (h - begin) * HEAD_DIM : (h - begin + 1) * HEAD_DIM,
-                        side * LANES : (side + 1) * LANES,
+                        j * LANES - first : j * LANES - first + wide,
                     ]
-                    total = jnp.where((lane >= lo) & (lane < hi), part, total)
-                row = pl.multiple_of((step * TILES + j) * HEAD_DIM, 16)
-                whole[pl.ds(row, HEAD_DIM), :] = total.astype(jnp.bfloat16)
-
-    by_group(dim, body)
-
-    @pl.when(step == pl.num_programs(0) - 1)
-    def _():
-        used = cdiv(dim, LANES) * HEAD_DIM
-        if used < whole.shape[0]:
-            whole[used:, :] = jnp.zeros((whole.shape[0] - used, LANES), jnp.bfloat16)
-        for k, part in enumerate(parts):
-            size = part.shape[0]
-            turn = lax.rem(lax.axis_index("space") + k, 2) if len(parts) == 2 else 0
-            part[...] = whole[pl.ds(pl.multiple_of(turn * size, 16), size), :]
-        if with_edge:
-            for copy in copies:
-                copy.wait()
+                    for h, _, _ in tile_heads(j, lanes)
+                ]
+                total = blocks[0]
+                if len(blocks) > 1:
+                    total = jnp.where(lane < tile_heads(j, lanes)[0][2], blocks[0], blocks[1])
+                if wide < LANES:
+                    total = jnp.concatenate(
+                        [total, jnp.zeros((HEAD_DIM, LANES - wide), jnp.float32)], axis=1
+                    )
+                row = (base // LANES + j) * HEAD_DIM
+                whole[row : row + HEAD_DIM, :] = total.astype(jnp.bfloat16)
+    for k, part in enumerate(part_refs):
+        size = part.shape[0]
+        place = lax.rem(lax.axis_index("space") + k, 2) if parts == 2 else 0
+        part[...] = whole[pl.ds(pl.multiple_of(place * size, 16), size), :]
+    for copy in copies[2 * len(order) :]:
+        copy.wait()
 
 
 def frame_states(keys, values, rows, parts, edged=()):
     tokens, dim = keys.shape
     part = (rows // parts, LANES)
-    slabs = 2 if tokens % 32 == 0 else 1
-    blocks = [
-        pl.BlockSpec((tokens // slabs, GROUP), functools.partial(lambda k, g: (k, g), k))
-        for k in range(slabs)
-    ]
-
-    def body(*refs):
-        state_kernel(dim, bool(edged), refs[:slabs], refs[slabs : 2 * slabs], refs[2 * slabs :])
-
+    outside = pl.BlockSpec(memory_space=pl.ANY)
     return pl.pallas_call(
-        body,
+        functools.partial(state_kernel, dim, parts),
         out_shape=[pltpu.VMEM(part, jnp.bfloat16)] * parts
         + [pltpu.VMEM((len(edged), 1, *edged[0].shape[1:]), jnp.bfloat16) for _ in edged[:1]],
-        grid=(cdiv(dim, GROUP),),
-        in_specs=blocks + blocks + [pl.BlockSpec(memory_space=pl.ANY)] * len(edged),
-        out_specs=[pl.BlockSpec(part, lambda g: (0, 0))] * parts
-        + [pl.BlockSpec(memory_space=pl.ANY) for _ in edged[:1]],
+        in_specs=[outside] * (2 + len(edged)),
+        out_specs=[pl.BlockSpec(memory_space=pltpu.VMEM)] * parts + [outside for _ in edged[:1]],
         scratch_shapes=[
-            pltpu.VMEM((slabs, GROUP, tokens // slabs), jnp.bfloat16),
+            pltpu.VMEM((tokens, dim), jnp.bfloat16),
+            pltpu.VMEM((tokens, dim), jnp.bfloat16),
+            pltpu.VMEM((2, GROUP, tokens), jnp.bfloat16),
             pltpu.VMEM((rows, LANES), jnp.bfloat16),
-            pltpu.SemaphoreType.DMA((2,)),
+            pltpu.SemaphoreType.DMA((2 * len(group_lanes(dim)) + len(edged),)),
         ],
-        compiler_params=pltpu.CompilerParams(vmem_limit_bytes=60 * 2**20),
+        compiler_params=pltpu.CompilerParams(vmem_limit_bytes=32 * 2**20),
         cost_estimate=pl.CostEstimate(
             flops=2 * tokens * dim * HEAD_DIM, bytes_accessed=4 * tokens * dim, transcendentals=0
         ),
         name="frame_states",
-    )(*[in_hbm(keys)] * slabs, *[in_hbm(values)] * slabs, *[in_hbm(array) for array in edged])
+    )(in_hbm(keys), in_hbm(values), *[in_hbm(array) for array in edged])
 
 
 def group_lanes(dim):

time: 43.4 us -> 42.7 us (0.984)
  Pallas kernels: 18 us -> 17.3 us
    pallas_call x1, Pallas kernels: 3.74 us -> 3.01 us  [frame_states(): pl.pallas_call(functools.partial(state_kernel, dim, parts), out_shape=[pl...]
where the time goes in v19:
time: 42.7 us; the launch traced here: 42.5 us
  Pallas kernels  17.3 us (41%)
  waiting for transfers between devices  16 us (37%)
  starting transfers between devices  9.21 us (22%)
    ppermute x4, waiting for transfers between devices, running_states(): lax.ppermute(array, 'frame', [(f, f ^ stride) for f in range(frames)])  13.5 us
    pallas_call x1, Pallas kernels, mix(): pl.pallas_call(functools.partial(mix_kernel, dim, rows, width, (total - t...  10.7 us
    ppermute x4, starting transfers between devices, running_states(): lax.ppermute(array, 'frame', [(f, f ^ stride) for f in range(frames)])  8.24 us
    pallas_call x1, Pallas kernels, prepare(): pl.pallas_call(functools.partial(prepare_kernel, dim), out_shape=[pltpu.V...  3.33 us
    pallas_call x1, Pallas kernels, frame_states(): pl.pallas_call(functools.partial(state_kernel, dim, parts), out_shape=[pl...  3.01 us
    ppermute x1, waiting for transfers between devices, running_states(): lax.ppermute(other, 'space', swap)  1.34 us
    ppermute x1, waiting for transfers between devices, running_states(): got = lax.ppermute(sent, 'space', swap)  1.16 us
  transfers between devices with their start and end apart: 8, of which 6 were waited for; matrix products, arithmetic and copies ran while one was open for 0% of the time, Pallas kernels for 8%

profile of v19, /device:TPU:0, one launch (start us, length us, event | category | flops | bytes accessed | tf_op | source)
XLA Modules:
  0.0 42.5 jit_solution(14265784563231689654)
XLA Ops:
  0.0 3.0 %frame_states.1 = (bf16[1024,128]{1,0:T(8,128)(2,1)S(1)}, bf16[1024,128]{1,0:T(8,128)(2,1)S(1)}, bf16[2,1,80,2240]{3,2,1,0:T(8,128)(2,1)S(1)}) custom-call(bf16[480,2240]{1,0:T(8,128)(2,1)} %bitcast.11, bf16[480,2240]{1,0:T(8,128)(2,1)} %bitcast.12, bf16[6,80,2240]{2,1,0:T(8,128)(2,1)} %bitcast.7, bf16[6,80,2240]{2,1,0:T(8,128)(2,1)} %bitcast.9), custom_call_target="tpu_custom_call" | custom-call | flops 240844800 | bytes 4300800 | tf_op jit(solution)/shard_map/frame_states/pallas_call | solution.py:116
  3.0 0.5 %collective-permute-start = (bf16[1024,128]{1,0:T(8,128)(2,1)S(1)}, bf16[1024,128]{1,0:T(8,128)(2,1)S(1)}, u32[]{:S(2)}, u32[]{:S(2)}) collective-permute-start(bf16[1024,128]{1,0:T(8,128)(2,1)S(1)} %get-tuple-element.26), channel_id=1, source_target_pairs={{0,1},{1,0},{2,3},{3,2},{4,5},{5,4},{6,7},{7,6},{8,9},{9,8},{10,11... | collective-permute-start | bytes 786440 | tf_op jit(solution)/shard_map/ppermute | solution.py:482
  3.6 1.2 %collective-permute-done.got_ref = bf16[1024,128]{1,0:T(8,128)(2,1)S(1)} collective-permute-done((bf16[1024,128]{1,0:T(8,128)(2,1)S(1)}, bf16[1024,128]{1,0:T(8,128)(2,1)S(1)}, u32[]{:S(2)}, u32[]{:S(2)}) %collective-permute-start) | collective-permute-done | bytes 262176 | tf_op jit(solution)/shard_map/ppermute | solution.py:482
  4.7 0.1 split_sum.1
  4.8 0.4 %collective-permute-start.3 = (bf16[2,1,80,2240]{3,2,1,0:T(8,128)(2,1)S(1)}, bf16[2,1,80,2240]{3,2,1,0:T(8,128)(2,1)S(1)}, u32[]{:S(2)}, u32[]{:S(2)}) collective-permute-start(bf16[2,1,80,2240]{3,2,1,0:T(8,128)(2,1)S(1)} %get-tuple-element.31), channel_id=1, source_target_pairs={{0,1},{1,0},{2,3},{3,2},{4,5},{5,4},{6,7},{7,6},{8,9},{9,8},{10,11... | collective-permute-start | bytes 2150408 | tf_op jit(solution)/shard_map/ppermute | solution.py:486
  5.2 2.7 %collective-permute-start.1 = (bf16[512,128]{1,0:T(8,128)(2,1)S(1)}, bf16[512,128]{1,0:T(8,128)(2,1)S(1)}, u32[]{:S(2)}, u32[]{:S(2)}) collective-permute-start(bf16[512,128]{1,0:T(8,128)(2,1)S(1)} %get-tuple-element.30), channel_id=1, source_target_pairs={{0,2},{2,0},{4,6},{6,4},{8,10},{10,8},{12,14},{14,12},{1,3},{3,1},... | collective-permute-start | bytes 393224 | tf_op jit(solution)/shard_map/ppermute | solution.py:478
  7.9 4.0 %collective-permute-done.1.refs_1_.partner_ref = bf16[512,128]{1,0:T(8,128)(2,1)S(1)} collective-permute-done((bf16[512,128]{1,0:T(8,128)(2,1)S(1)}, bf16[512,128]{1,0:T(8,128)(2,1)S(1)}, u32[]{:S(2)}, u32[]{:S(2)}) %collective-permute-start.1) | collective-permute-done | bytes 131104 | tf_op jit(solution)/shard_map/ppermute | solution.py:478
  11.9 1.9 %collective-permute-start.2 = (bf16[512,128]{1,0:T(8,128)(2,1)S(1)}, bf16[512,128]{1,0:T(8,128)(2,1)S(1)}, u32[]{:S(2)}, u32[]{:S(2)}) collective-permute-start(bf16[512,128]{1,0:T(8,128)(2,1)S(1)} %pair_sum.1.refs_0_), channel_id=1, source_target_pairs={{0,4},{2,6},{4,0},{6,2},{8,12},{10,14},{12,8},{14,10},{1,5},{3,7},... | collective-permute-start | bytes 393224 | tf_op jit(solution)/shard_map/ppermute | solution.py:478
  13.8 3.4 %collective-permute-done.2.refs_1_.refs_0_ = bf16[512,128]{1,0:T(8,128)(2,1)S(1)} collective-permute-done((bf16[512,128]{1,0:T(8,128)(2,1)S(1)}, bf16[512,128]{1,0:T(8,128)(2,1)S(1)}, u32[]{:S(2)}, u32[]{:S(2)}) %collective-permute-start.2) | collective-permute-done | bytes 131104 | tf_op jit(solution)/shard_map/ppermute | solution.py:478
  17.2 0.0 collective-permute-done.3.edge_ref
  17.2 2.6 %collective-permute-start.4 = (bf16[512,128]{1,0:T(8,128)(2,1)S(1)}, bf16[512,128]{1,0:T(8,128)(2,1)S(1)}, u32[]{:S(2)}, u32[]{:S(2)}) collective-permute-start(bf16[512,128]{1,0:T(8,128)(2,1)S(1)} %stride_sum.1), channel_id=1, source_target_pairs={{0,8},{2,10},{4,12},{6,14},{8,0},{10,2},{12,4},{14,6},{1,9},{3,11}... | collective-permute-start | bytes 393224 | tf_op jit(solution)/shard_map/ppermute | solution.py:478
  19.9 0.0 copy-done.2
  19.9 0.0 copy-done
  19.9 0.0 copy-done.1
  19.9 3.3 %prepare.1 = (bf16[560,2304]{1,0:T(8,128)(2,1)S(1)}, f32[560,2240]{1,0:T(8,128)S(1)}, f32[1,2240]{1,0:T(1,128)S(1)}, f32[18,24,8,128]{3,2,1,0:T(8,128)S(1)}) custom-call(bf16[480,2240]{1,0:T(8,128)(2,1)} %bitcast.8, bf16[480,2240]{1,0:T(8,128)(2,1)} %bitcast.10, bf16[2,1,80,2240]{3,2,1,0:T(8,128)(2,1)S(1)} %collective-permute-done.3.edge_ref, ...), custom_call_target="tpu_custom_call" | custom-call | flops 5017600 | bytes 10035200 | tf_op jit(solution)/shard_map/prepare/pallas_call | solution.py:200
  23.3 2.1 %collective-permute-done.4.refs_1_ = bf16[512,128]{1,0:T(8,128)(2,1)S(1)} collective-permute-done((bf16[512,128]{1,0:T(8,128)(2,1)S(1)}, bf16[512,128]{1,0:T(8,128)(2,1)S(1)}, u32[]{:S(2)}, u32[]{:S(2)}) %collective-permute-start.4) | collective-permute-done | bytes 131104 | tf_op jit(solution)/shard_map/ppermute | solution.py:478
  25.3 0.1 pair_sums.1
  25.5 1.1 %collective-permute-start.5 = (bf16[512,128]{1,0:T(8,128)(2,1)S(1)}, bf16[512,128]{1,0:T(8,128)(2,1)S(1)}, u32[]{:S(2)}, u32[]{:S(2)}) collective-permute-start(bf16[512,128]{1,0:T(8,128)(2,1)S(1)} %get-tuple-element.44), channel_id=1, source_target_pairs={{0,2},{2,0},{4,6},{6,4},{8,10},{10,8},{12,14},{14,12},{1,3},{3,1},... | collective-permute-start | bytes 393224 | tf_op jit(solution)/shard_map/ppermute | solution.py:478
  26.6 0.0 collective-permute-start.6
  26.6 4.0 %collective-permute-done.5.refs_1_ = bf16[512,128]{1,0:T(8,128)(2,1)S(1)} collective-permute-done((bf16[512,128]{1,0:T(8,128)(2,1)S(1)}, bf16[512,128]{1,0:T(8,128)(2,1)S(1)}, u32[]{:S(2)}, u32[]{:S(2)}) %collective-permute-start.5) | collective-permute-done | bytes 131104 | tf_op jit(solution)/shard_map/ppermute | solution.py:478
  30.5 0.0 collective-permute-start.7
  30.5 0.0 collective-permute-done.6.refs_2_
  30.5 1.3 %collective-permute-done.7.refs_3_ = bf16[512,128]{1,0:T(8,128)(2,1)S(1)} collective-permute-done((bf16[512,128]{1,0:T(8,128)(2,1)S(1)}, bf16[512,128]{1,0:T(8,128)(2,1)S(1)}, u32[]{:S(2)}, u32[]{:S(2)}) %collective-permute-start.7) | collective-permute-done | bytes 131104 | tf_op jit(solution)/shard_map/ppermute | solution.py:504
  31.9 10.7 %mix.1 = bf16[480,2240]{1,0:T(8,128)(2,1)} custom-call(bf16[560,2304]{1,0:T(8,128)(2,1)S(1)} %get-tuple-element.38.features_ref, f32[560,2240]{1,0:T(8,128)S(1)} %get-tuple-element.39.inputs_ref, f32[1,2240]{1,0:T(1,128)S(1)} %get-tuple-element.40.gain_ref, f32[18,24,8,128]{3,2,1,0:T(8,128)S(1)} %get-tuple-element.41.taps_ref, ...), custom_call_target="tpu_custom_call" | custom-call | flops 64512000 | bytes 6451200 | tf_op jit(solution)/shard_map/mix/pallas_call | solution.py:370
  (6 shorter events, 0.1 us)
Async XLA Ops:
  0.0 19.9 %copy-start.2 = (f32[2240]{0:T(1024)S(1)}, f32[2240]{0:T(1024)}, u32[]{:S(2)}) copy-start(f32[2240]{0:T(1024)} %param.11) | copy-start | bytes 26884
  0.0 19.9 %copy-start = (f32[9,2240]{1,0:T(8,128)S(1)}, f32[9,2240]{1,0:T(8,128)}, u32[]{:S(2)}) copy-start(f32[9,2240]{1,0:T(8,128)} %vtaps_ref.1) | copy-start | bytes 241924
  0.0 19.9 %copy-start.1 = (f32[9,2240]{1,0:T(8,128)S(1)}, f32[9,2240]{1,0:T(8,128)}, u32[]{:S(2)}) copy-start(f32[9,2240]{1,0:T(8,128)} %gtaps_ref.1) | copy-start | bytes 241924
  3.0 1.7 %collective-permute-start = (bf16[1024,128]{1,0:T(8,128)(2,1)S(1)}, bf16[1024,128]{1,0:T(8,128)(2,1)S(1)}, u32[]{:S(2)}, u32[]{:S(2)}) collective-permute-start(bf16[1024,128]{1,0:T(8,128)(2,1)S(1)} %get-tuple-element.26), channel_id=1, source_target_pairs={{0,1},{1,0},{2,3},{3,2},{4,5},{5,4},{6,7},{7,6},{8,9},{9,8},{10,11... | collective-permute-start | bytes 786440 | tf_op jit(solution)/shard_map/ppermute | solution.py:482
  4.8 12.5 %collective-permute-start.3 = (bf16[2,1,80,2240]{3,2,1,0:T(8,128)(2,1)S(1)}, bf16[2,1,80,2240]{3,2,1,0:T(8,128)(2,1)S(1)}, u32[]{:S(2)}, u32[]{:S(2)}) collective-permute-start(bf16[2,1,80,2240]{3,2,1,0:T(8,128)(2,1)S(1)} %get-tuple-element.31), channel_id=1, source_target_pairs={{0,1},{1,0},{2,3},{3,2},{4,5},{5,4},{6,7},{7,6},{8,9},{9,8},{10,11... | collective-permute-start | bytes 2150408 | tf_op jit(solution)/shard_map/ppermute | solution.py:486
  5.2 6.7 %collective-permute-start.1 = (bf16[512,128]{1,0:T(8,128)(2,1)S(1)}, bf16[512,128]{1,0:T(8,128)(2,1)S(1)}, u32[]{:S(2)}, u32[]{:S(2)}) collective-permute-start(bf16[512,128]{1,0:T(8,128)(2,1)S(1)} %get-tuple-element.30), channel_id=1, source_target_pairs={{0,2},{2,0},{4,6},{6,4},{8,10},{10,8},{12,14},{14,12},{1,3},{3,1},... | collective-permute-start | bytes 393224 | tf_op jit(solution)/shard_map/ppermute | solution.py:478
  11.9 5.3 %collective-permute-start.2 = (bf16[512,128]{1,0:T(8,128)(2,1)S(1)}, bf16[512,128]{1,0:T(8,128)(2,1)S(1)}, u32[]{:S(2)}, u32[]{:S(2)}) collective-permute-start(bf16[512,128]{1,0:T(8,128)(2,1)S(1)} %pair_sum.1.refs_0_), channel_id=1, source_target_pairs={{0,4},{2,6},{4,0},{6,2},{8,12},{10,14},{12,8},{14,10},{1,5},{3,7},... | collective-permute-start | bytes 393224 | tf_op jit(solution)/shard_map/ppermute | solution.py:478
  17.2 8.1 %collective-permute-start.4 = (bf16[512,128]{1,0:T(8,128)(2,1)S(1)}, bf16[512,128]{1,0:T(8,128)(2,1)S(1)}, u32[]{:S(2)}, u32[]{:S(2)}) collective-permute-start(bf16[512,128]{1,0:T(8,128)(2,1)S(1)} %stride_sum.1), channel_id=1, source_target_pairs={{0,8},{2,10},{4,12},{6,14},{8,0},{10,2},{12,4},{14,6},{1,9},{3,11}... | collective-permute-start | bytes 393224 | tf_op jit(solution)/shard_map/ppermute | solution.py:478
  25.5 5.0 %collective-permute-start.5 = (bf16[512,128]{1,0:T(8,128)(2,1)S(1)}, bf16[512,128]{1,0:T(8,128)(2,1)S(1)}, u32[]{:S(2)}, u32[]{:S(2)}) collective-permute-start(bf16[512,128]{1,0:T(8,128)(2,1)S(1)} %get-tuple-element.44), channel_id=1, source_target_pairs={{0,2},{2,0},{4,6},{6,4},{8,10},{10,8},{12,14},{14,12},{1,3},{3,1},... | collective-permute-start | bytes 393224 | tf_op jit(solution)/shard_map/ppermute | solution.py:478
  26.6 4.0 %collective-permute-start.6 = (bf16[512,128]{1,0:T(8,128)(2,1)S(1)}, bf16[512,128]{1,0:T(8,128)(2,1)S(1)}, u32[]{:S(2)}, u32[]{:S(2)}) collective-permute-start(bf16[512,128]{1,0:T(8,128)(2,1)S(1)} %get-tuple-element.43.refs_0_), channel_id=1, source_target_pairs={{0,1},{1,0},{2,3},{3,2},{4,5},{5,4},{6,7},{7,6},{8,9},{9,8},{10,11... | collective-permute-start | bytes 393224 | tf_op jit(solution)/shard_map/ppermute | solution.py:504
  30.5 1.3 %collective-permute-start.7 = (bf16[512,128]{1,0:T(8,128)(2,1)S(1)}, bf16[512,128]{1,0:T(8,128)(2,1)S(1)}, u32[]{:S(2)}, u32[]{:S(2)}) collective-permute-start(bf16[512,128]{1,0:T(8,128)(2,1)S(1)} %collective-permute-done.5.refs_1_), channel_id=1, source_target_pairs={{0,1},{1,0},{2,3},{3,2},{4,5},{5,4},{6,7},{7,6},{8,9},{9,8},{10,11... | collective-permute-start | bytes 393224 | tf_op jit(solution)/shard_map/ppermute | solution.py:504

commit v20 on v19

--- a/solution.py
+++ b/solution.py
@@ -177,8 +177,9 @@
                 features_ref[:, here.stop :] = jnp.zeros(
                     (features_ref.shape[0], LANES - used), jnp.bfloat16
                 )
-            wide[slot, :, :used] = held[k, :, here].astype(jnp.float32)
-            for row in range(wide.shape[1] // width):
+            total = held.shape[1]
+            wide[slot, :total, :used] = held[k, :, here].astype(jnp.float32)
+            for row in range(total // width):
                 value = jnp.concatenate(
                     [
                         wide[slot, pl.ds(row * width + side, half, stride=2), :used]
@@ -209,7 +210,7 @@
         out_specs=[whole] * 4,
         scratch_shapes=[
             pltpu.VMEM((2, total, dim), jnp.bfloat16),
-            pltpu.VMEM((2, total, LANES), jnp.float32),
+            pltpu.VMEM((2, total + 8, LANES), jnp.float32),
             pltpu.SemaphoreType.DMA((2,)),
         ],
         compiler_params=pltpu.CompilerParams(vmem_limit_bytes=24 * 2**20),
@@ -339,7 +340,7 @@
                     center = mixed_rows[slot, row + 1, k * half : (k + 1) * half, :used]
                     gated = conv_v * (half_g + half_g * jnp.tanh(half_g))
                     results[slot, row, side, :used] = center + gated.reshape(half, used)
-                held[row * width : (row + 1) * width, here] = results[slot, row, :, :used].astype(
+                held[row * width : (row + 1) * width, here] = results[slot, row, :width, :used].astype(
                     jnp.bfloat16
                 )
 
@@ -378,7 +379,7 @@
             pltpu.VMEM((total, GROUP), jnp.float32),
             pltpu.VMEM((2, rows + 2, width, LANES), jnp.float32),
             pltpu.VMEM((2, 4, rows + 2, width // 16, 8, LANES), jnp.float32),
-            pltpu.VMEM((2, rows, width, LANES), jnp.float32),
+            pltpu.VMEM((2, rows, width + 8, LANES), jnp.float32),
             pltpu.VMEM((tokens, dim), jnp.bfloat16),
             pltpu.SemaphoreType.DMA((len(group_lanes(dim)),)),
         ],

time: 42.7 us -> 42.7 us (level)
  no operation moved by 1% of the time
where the time goes in v20:
time: 42.7 us; the launch traced here: 42.5 us
  Pallas kernels  17.3 us (41%)
  waiting for transfers between devices  16 us (37%)
  starting transfers between devices  9.21 us (22%)
    ppermute x4, waiting for transfers between devices, running_states(): lax.ppermute(array, 'frame', [(f, f ^ stride) for f in range(frames)])  13.5 us
    pallas_call x1, Pallas kernels, mix(): pl.pallas_call(functools.partial(mix_kernel, dim, rows, width, (total - t...  10.6 us
    ppermute x4, starting transfers between devices, running_states(): lax.ppermute(array, 'frame', [(f, f ^ stride) for f in range(frames)])  8.24 us
    pallas_call x1, Pallas kernels, prepare(): pl.pallas_call(functools.partial(prepare_kernel, dim), out_shape=[pltpu.V...  3.33 us
    pallas_call x1, Pallas kernels, frame_states(): pl.pallas_call(functools.partial(state_kernel, dim, parts), out_shape=[pl...  3.01 us
    ppermute x1, waiting for transfers between devices, running_states(): lax.ppermute(other, 'space', swap)  1.34 us
    ppermute x1, waiting for transfers between devices, running_states(): got = lax.ppermute(sent, 'space', swap)  1.16 us
  transfers between devices with their start and end apart: 8, of which 6 were waited for; matrix products, arithmetic and copies ran while one was open for 0% of the time, Pallas kernels for 8%

profile of v20, /device:TPU:0, one launch (start us, length us, event | category | flops | bytes accessed | tf_op | source)
XLA Modules:
  0.0 42.5 jit_solution(12197136547846391427)
XLA Ops:
  0.0 3.0 %frame_states.1 = (bf16[1024,128]{1,0:T(8,128)(2,1)S(1)}, bf16[1024,128]{1,0:T(8,128)(2,1)S(1)}, bf16[2,1,80,2240]{3,2,1,0:T(8,128)(2,1)S(1)}) custom-call(bf16[480,2240]{1,0:T(8,128)(2,1)} %bitcast.11, bf16[480,2240]{1,0:T(8,128)(2,1)} %bitcast.12, bf16[6,80,2240]{2,1,0:T(8,128)(2,1)} %bitcast.7, bf16[6,80,2240]{2,1,0:T(8,128)(2,1)} %bitcast.9), custom_call_target="tpu_custom_call" | custom-call | flops 240844800 | bytes 4300800 | tf_op jit(solution)/shard_map/frame_states/pallas_call | solution.py:116
  3.0 0.5 %collective-permute-start = (bf16[1024,128]{1,0:T(8,128)(2,1)S(1)}, bf16[1024,128]{1,0:T(8,128)(2,1)S(1)}, u32[]{:S(2)}, u32[]{:S(2)}) collective-permute-start(bf16[1024,128]{1,0:T(8,128)(2,1)S(1)} %get-tuple-element.26), channel_id=1, source_target_pairs={{0,1},{1,0},{2,3},{3,2},{4,5},{5,4},{6,7},{7,6},{8,9},{9,8},{10,11... | collective-permute-start | bytes 786440 | tf_op jit(solution)/shard_map/ppermute | solution.py:483
  3.6 1.2 %collective-permute-done.got_ref = bf16[1024,128]{1,0:T(8,128)(2,1)S(1)} collective-permute-done((bf16[1024,128]{1,0:T(8,128)(2,1)S(1)}, bf16[1024,128]{1,0:T(8,128)(2,1)S(1)}, u32[]{:S(2)}, u32[]{:S(2)}) %collective-permute-start) | collective-permute-done | bytes 262176 | tf_op jit(solution)/shard_map/ppermute | solution.py:483
  4.7 0.1 split_sum.1
  4.8 0.4 %collective-permute-start.3 = (bf16[2,1,80,2240]{3,2,1,0:T(8,128)(2,1)S(1)}, bf16[2,1,80,2240]{3,2,1,0:T(8,128)(2,1)S(1)}, u32[]{:S(2)}, u32[]{:S(2)}) collective-permute-start(bf16[2,1,80,2240]{3,2,1,0:T(8,128)(2,1)S(1)} %get-tuple-element.31), channel_id=1, source_target_pairs={{0,1},{1,0},{2,3},{3,2},{4,5},{5,4},{6,7},{7,6},{8,9},{9,8},{10,11... | collective-permute-start | bytes 2150408 | tf_op jit(solution)/shard_map/ppermute | solution.py:487
  5.2 2.7 %collective-permute-start.1 = (bf16[512,128]{1,0:T(8,128)(2,1)S(1)}, bf16[512,128]{1,0:T(8,128)(2,1)S(1)}, u32[]{:S(2)}, u32[]{:S(2)}) collective-permute-start(bf16[512,128]{1,0:T(8,128)(2,1)S(1)} %get-tuple-element.30), channel_id=1, source_target_pairs={{0,2},{2,0},{4,6},{6,4},{8,10},{10,8},{12,14},{14,12},{1,3},{3,1},... | collective-permute-start | bytes 393224 | tf_op jit(solution)/shard_map/ppermute | solution.py:479
  7.9 4.0 %collective-permute-done.1.refs_1_.partner_ref = bf16[512,128]{1,0:T(8,128)(2,1)S(1)} collective-permute-done((bf16[512,128]{1,0:T(8,128)(2,1)S(1)}, bf16[512,128]{1,0:T(8,128)(2,1)S(1)}, u32[]{:S(2)}, u32[]{:S(2)}) %collective-permute-start.1) | collective-permute-done | bytes 131104 | tf_op jit(solution)/shard_map/ppermute | solution.py:479
  11.9 1.9 %collective-permute-start.2 = (bf16[512,128]{1,0:T(8,128)(2,1)S(1)}, bf16[512,128]{1,0:T(8,128)(2,1)S(1)}, u32[]{:S(2)}, u32[]{:S(2)}) collective-permute-start(bf16[512,128]{1,0:T(8,128)(2,1)S(1)} %pair_sum.1.refs_0_), channel_id=1, source_target_pairs={{0,4},{2,6},{4,0},{6,2},{8,12},{10,14},{12,8},{14,10},{1,5},{3,7},... | collective-permute-start | bytes 393224 | tf_op jit(solution)/shard_map/ppermute | solution.py:479
  13.8 3.4 %collective-permute-done.2.refs_1_.refs_0_ = bf16[512,128]{1,0:T(8,128)(2,1)S(1)} collective-permute-done((bf16[512,128]{1,0:T(8,128)(2,1)S(1)}, bf16[512,128]{1,0:T(8,128)(2,1)S(1)}, u32[]{:S(2)}, u32[]{:S(2)}) %collective-permute-start.2) | collective-permute-done | bytes 131104 | tf_op jit(solution)/shard_map/ppermute | solution.py:479
  17.2 0.0 collective-permute-done.3.edge_ref
  17.2 2.6 %collective-permute-start.4 = (bf16[512,128]{1,0:T(8,128)(2,1)S(1)}, bf16[512,128]{1,0:T(8,128)(2,1)S(1)}, u32[]{:S(2)}, u32[]{:S(2)}) collective-permute-start(bf16[512,128]{1,0:T(8,128)(2,1)S(1)} %stride_sum.1), channel_id=1, source_target_pairs={{0,8},{2,10},{4,12},{6,14},{8,0},{10,2},{12,4},{14,6},{1,9},{3,11}... | collective-permute-start | bytes 393224 | tf_op jit(solution)/shard_map/ppermute | solution.py:479
  19.9 0.0 copy-done.2
  19.9 0.0 copy-done
  19.9 0.0 copy-done.1
  19.9 3.3 %prepare.1 = (bf16[560,2304]{1,0:T(8,128)(2,1)S(1)}, f32[560,2240]{1,0:T(8,128)S(1)}, f32[1,2240]{1,0:T(1,128)S(1)}, f32[18,24,8,128]{3,2,1,0:T(8,128)S(1)}) custom-call(bf16[480,2240]{1,0:T(8,128)(2,1)} %bitcast.8, bf16[480,2240]{1,0:T(8,128)(2,1)} %bitcast.10, bf16[2,1,80,2240]{3,2,1,0:T(8,128)(2,1)S(1)} %collective-permute-done.3.edge_ref, ...), custom_call_target="tpu_custom_call" | custom-call | flops 5017600 | bytes 10035200 | tf_op jit(solution)/shard_map/prepare/pallas_call | solution.py:201
  23.3 2.1 %collective-permute-done.4.refs_1_ = bf16[512,128]{1,0:T(8,128)(2,1)S(1)} collective-permute-done((bf16[512,128]{1,0:T(8,128)(2,1)S(1)}, bf16[512,128]{1,0:T(8,128)(2,1)S(1)}, u32[]{:S(2)}, u32[]{:S(2)}) %collective-permute-start.4) | collective-permute-done | bytes 131104 | tf_op jit(solution)/shard_map/ppermute | solution.py:479
  25.3 0.1 pair_sums.1
  25.5 1.1 %collective-permute-start.5 = (bf16[512,128]{1,0:T(8,128)(2,1)S(1)}, bf16[512,128]{1,0:T(8,128)(2,1)S(1)}, u32[]{:S(2)}, u32[]{:S(2)}) collective-permute-start(bf16[512,128]{1,0:T(8,128)(2,1)S(1)} %get-tuple-element.44), channel_id=1, source_target_pairs={{0,2},{2,0},{4,6},{6,4},{8,10},{10,8},{12,14},{14,12},{1,3},{3,1},... | collective-permute-start | bytes 393224 | tf_op jit(solution)/shard_map/ppermute | solution.py:479
  26.6 0.0 collective-permute-start.6
  26.6 4.0 %collective-permute-done.5.refs_1_ = bf16[512,128]{1,0:T(8,128)(2,1)S(1)} collective-permute-done((bf16[512,128]{1,0:T(8,128)(2,1)S(1)}, bf16[512,128]{1,0:T(8,128)(2,1)S(1)}, u32[]{:S(2)}, u32[]{:S(2)}) %collective-permute-start.5) | collective-permute-done | bytes 131104 | tf_op jit(solution)/shard_map/ppermute | solution.py:479
  30.5 0.0 collective-permute-start.7
  30.5 0.0 collective-permute-done.6.refs_2_
  30.5 1.3 %collective-permute-done.7.refs_3_ = bf16[512,128]{1,0:T(8,128)(2,1)S(1)} collective-permute-done((bf16[512,128]{1,0:T(8,128)(2,1)S(1)}, bf16[512,128]{1,0:T(8,128)(2,1)S(1)}, u32[]{:S(2)}, u32[]{:S(2)}) %collective-permute-start.7) | collective-permute-done | bytes 131104 | tf_op jit(solution)/shard_map/ppermute | solution.py:505
  31.9 10.6 %mix.1 = bf16[480,2240]{1,0:T(8,128)(2,1)} custom-call(bf16[560,2304]{1,0:T(8,128)(2,1)S(1)} %get-tuple-element.38.features_ref, f32[560,2240]{1,0:T(8,128)S(1)} %get-tuple-element.39.inputs_ref, f32[1,2240]{1,0:T(1,128)S(1)} %get-tuple-element.40.gain_ref, f32[18,24,8,128]{3,2,1,0:T(8,128)S(1)} %get-tuple-element.41.taps_ref, ...), custom_call_target="tpu_custom_call" | custom-call | flops 64512000 | bytes 6451200 | tf_op jit(solution)/shard_map/mix/pallas_call | solution.py:371
  (6 shorter events, 0.1 us)
Async XLA Ops:
  0.0 19.9 %copy-start.2 = (f32[2240]{0:T(1024)S(1)}, f32[2240]{0:T(1024)}, u32[]{:S(2)}) copy-start(f32[2240]{0:T(1024)} %param.11) | copy-start | bytes 26884
  0.0 19.9 %copy-start = (f32[9,2240]{1,0:T(8,128)S(1)}, f32[9,2240]{1,0:T(8,128)}, u32[]{:S(2)}) copy-start(f32[9,2240]{1,0:T(8,128)} %vtaps_ref.1) | copy-start | bytes 241924
  0.0 19.9 %copy-start.1 = (f32[9,2240]{1,0:T(8,128)S(1)}, f32[9,2240]{1,0:T(8,128)}, u32[]{:S(2)}) copy-start(f32[9,2240]{1,0:T(8,128)} %gtaps_ref.1) | copy-start | bytes 241924
  3.0 1.7 %collective-permute-start = (bf16[1024,128]{1,0:T(8,128)(2,1)S(1)}, bf16[1024,128]{1,0:T(8,128)(2,1)S(1)}, u32[]{:S(2)}, u32[]{:S(2)}) collective-permute-start(bf16[1024,128]{1,0:T(8,128)(2,1)S(1)} %get-tuple-element.26), channel_id=1, source_target_pairs={{0,1},{1,0},{2,3},{3,2},{4,5},{5,4},{6,7},{7,6},{8,9},{9,8},{10,11... | collective-permute-start | bytes 786440 | tf_op jit(solution)/shard_map/ppermute | solution.py:483
  4.8 12.5 %collective-permute-start.3 = (bf16[2,1,80,2240]{3,2,1,0:T(8,128)(2,1)S(1)}, bf16[2,1,80,2240]{3,2,1,0:T(8,128)(2,1)S(1)}, u32[]{:S(2)}, u32[]{:S(2)}) collective-permute-start(bf16[2,1,80,2240]{3,2,1,0:T(8,128)(2,1)S(1)} %get-tuple-element.31), channel_id=1, source_target_pairs={{0,1},{1,0},{2,3},{3,2},{4,5},{5,4},{6,7},{7,6},{8,9},{9,8},{10,11... | collective-permute-start | bytes 2150408 | tf_op jit(solution)/shard_map/ppermute | solution.py:487
  5.2 6.7 %collective-permute-start.1 = (bf16[512,128]{1,0:T(8,128)(2,1)S(1)}, bf16[512,128]{1,0:T(8,128)(2,1)S(1)}, u32[]{:S(2)}, u32[]{:S(2)}) collective-permute-start(bf16[512,128]{1,0:T(8,128)(2,1)S(1)} %get-tuple-element.30), channel_id=1, source_target_pairs={{0,2},{2,0},{4,6},{6,4},{8,10},{10,8},{12,14},{14,12},{1,3},{3,1},... | collective-permute-start | bytes 393224 | tf_op jit(solution)/shard_map/ppermute | solution.py:479
  11.9 5.3 %collective-permute-start.2 = (bf16[512,128]{1,0:T(8,128)(2,1)S(1)}, bf16[512,128]{1,0:T(8,128)(2,1)S(1)}, u32[]{:S(2)}, u32[]{:S(2)}) collective-permute-start(bf16[512,128]{1,0:T(8,128)(2,1)S(1)} %pair_sum.1.refs_0_), channel_id=1, source_target_pairs={{0,4},{2,6},{4,0},{6,2},{8,12},{10,14},{12,8},{14,10},{1,5},{3,7},... | collective-permute-start | bytes 393224 | tf_op jit(solution)/shard_map/ppermute | solution.py:479
  17.2 8.1 %collective-permute-start.4 = (bf16[512,128]{1,0:T(8,128)(2,1)S(1)}, bf16[512,128]{1,0:T(8,128)(2,1)S(1)}, u32[]{:S(2)}, u32[]{:S(2)}) collective-permute-start(bf16[512,128]{1,0:T(8,128)(2,1)S(1)} %stride_sum.1), channel_id=1, source_target_pairs={{0,8},{2,10},{4,12},{6,14},{8,0},{10,2},{12,4},{14,6},{1,9},{3,11}... | collective-permute-start | bytes 393224 | tf_op jit(solution)/shard_map/ppermute | solution.py:479
  25.5 5.0 %collective-permute-start.5 = (bf16[512,128]{1,0:T(8,128)(2,1)S(1)}, bf16[512,128]{1,0:T(8,128)(2,1)S(1)}, u32[]{:S(2)}, u32[]{:S(2)}) collective-permute-start(bf16[512,128]{1,0:T(8,128)(2,1)S(1)} %get-tuple-element.44), channel_id=1, source_target_pairs={{0,2},{2,0},{4,6},{6,4},{8,10},{10,8},{12,14},{14,12},{1,3},{3,1},... | collective-permute-start | bytes 393224 | tf_op jit(solution)/shard_map/ppermute | solution.py:479
  26.6 4.0 %collective-permute-start.6 = (bf16[512,128]{1,0:T(8,128)(2,1)S(1)}, bf16[512,128]{1,0:T(8,128)(2,1)S(1)}, u32[]{:S(2)}, u32[]{:S(2)}) collective-permute-start(bf16[512,128]{1,0:T(8,128)(2,1)S(1)} %get-tuple-element.43.refs_0_), channel_id=1, source_target_pairs={{0,1},{1,0},{2,3},{3,2},{4,5},{5,4},{6,7},{7,6},{8,9},{9,8},{10,11... | collective-permute-start | bytes 393224 | tf_op jit(solution)/shard_map/ppermute | solution.py:505
  30.5 1.3 %collective-permute-start.7 = (bf16[512,128]{1,0:T(8,128)(2,1)S(1)}, bf16[512,128]{1,0:T(8,128)(2,1)S(1)}, u32[]{:S(2)}, u32[]{:S(2)}) collective-permute-start(bf16[512,128]{1,0:T(8,128)(2,1)S(1)} %collective-permute-done.5.refs_1_), channel_id=1, source_target_pairs={{0,1},{1,0},{2,3},{3,2},{4,5},{5,4},{6,7},{7,6},{8,9},{9,8},{10,11... | collective-permute-start | bytes 393224 | tf_op jit(solution)/shard_map/ppermute | solution.py:505

commit v21 on v20

--- a/solution.py
+++ b/solution.py
@@ -344,10 +344,12 @@
                     jnp.bfloat16
                 )
 
-        for number in range(len(pairs)):
-            numerators(number)
-        for j in range(cdiv(lanes, LANES)):
-            mix_tile(j)
+        numerators(0)
+        for number, (tiles, _, _) in enumerate(pairs):
+            if number + 1 < len(pairs):
+                numerators(number + 1)
+            for j in tiles:
+                mix_tile(j)
 
     copies = []
     for base, lanes in group_lanes(dim):

time: 42.7 us -> 42.7 us (level)
  no operation moved by 1% of the time
where the time goes in v21:
time: 42.7 us; the launch traced here: 42.5 us
  Pallas kernels  17.3 us (41%)
  waiting for transfers between devices  16 us (37%)
  starting transfers between devices  9.21 us (22%)
    ppermute x4, waiting for transfers between devices, running_states(): lax.ppermute(array, 'frame', [(f, f ^ stride) for f in range(frames)])  13.5 us
    pallas_call x1, Pallas kernels, mix(): pl.pallas_call(functools.partial(mix_kernel, dim, rows, width, (total - t...  10.6 us
    ppermute x4, starting transfers between devices, running_states(): lax.ppermute(array, 'frame', [(f, f ^ stride) for f in range(frames)])  8.24 us
    pallas_call x1, Pallas kernels, prepare(): pl.pallas_call(functools.partial(prepare_kernel, dim), out_shape=[pltpu.V...  3.33 us
    pallas_call x1, Pallas kernels, frame_states(): pl.pallas_call(functools.partial(state_kernel, dim, parts), out_shape=[pl...  3.01 us
    ppermute x1, waiting for transfers between devices, running_states(): lax.ppermute(other, 'space', swap)  1.34 us
    ppermute x1, waiting for transfers between devices, running_states(): got = lax.ppermute(sent, 'space', swap)  1.16 us
  transfers between devices with their start and end apart: 8, of which 6 were waited for; matrix products, arithmetic and copies ran while one was open for 0% of the time, Pallas kernels for 8%

profile of v21, /device:TPU:0, one launch (start us, length us, event | category | flops | bytes accessed | tf_op | source)
XLA Modules:
  0.0 42.5 jit_solution(12197136547846391427)
XLA Ops:
  0.0 3.0 %frame_states.1 = (bf16[1024,128]{1,0:T(8,128)(2,1)S(1)}, bf16[1024,128]{1,0:T(8,128)(2,1)S(1)}, bf16[2,1,80,2240]{3,2,1,0:T(8,128)(2,1)S(1)}) custom-call(bf16[480,2240]{1,0:T(8,128)(2,1)} %bitcast.11, bf16[480,2240]{1,0:T(8,128)(2,1)} %bitcast.12, bf16[6,80,2240]{2,1,0:T(8,128)(2,1)} %bitcast.7, bf16[6,80,2240]{2,1,0:T(8,128)(2,1)} %bitcast.9), custom_call_target="tpu_custom_call" | custom-call | flops 240844800 | bytes 4300800 | tf_op jit(solution)/shard_map/frame_states/pallas_call | solution.py:116
  3.0 0.5 %collective-permute-start = (bf16[1024,128]{1,0:T(8,128)(2,1)S(1)}, bf16[1024,128]{1,0:T(8,128)(2,1)S(1)}, u32[]{:S(2)}, u32[]{:S(2)}) collective-permute-start(bf16[1024,128]{1,0:T(8,128)(2,1)S(1)} %get-tuple-element.26), channel_id=1, source_target_pairs={{0,1},{1,0},{2,3},{3,2},{4,5},{5,4},{6,7},{7,6},{8,9},{9,8},{10,11... | collective-permute-start | bytes 786440 | tf_op jit(solution)/shard_map/ppermute | solution.py:485
  3.6 1.2 %collective-permute-done.got_ref = bf16[1024,128]{1,0:T(8,128)(2,1)S(1)} collective-permute-done((bf16[1024,128]{1,0:T(8,128)(2,1)S(1)}, bf16[1024,128]{1,0:T(8,128)(2,1)S(1)}, u32[]{:S(2)}, u32[]{:S(2)}) %collective-permute-start) | collective-permute-done | bytes 262176 | tf_op jit(solution)/shard_map/ppermute | solution.py:485
  4.7 0.1 split_sum.1
  4.8 0.4 %collective-permute-start.3 = (bf16[2,1,80,2240]{3,2,1,0:T(8,128)(2,1)S(1)}, bf16[2,1,80,2240]{3,2,1,0:T(8,128)(2,1)S(1)}, u32[]{:S(2)}, u32[]{:S(2)}) collective-permute-start(bf16[2,1,80,2240]{3,2,1,0:T(8,128)(2,1)S(1)} %get-tuple-element.31), channel_id=1, source_target_pairs={{0,1},{1,0},{2,3},{3,2},{4,5},{5,4},{6,7},{7,6},{8,9},{9,8},{10,11... | collective-permute-start | bytes 2150408 | tf_op jit(solution)/shard_map/ppermute | solution.py:489
  5.2 2.7 %collective-permute-start.1 = (bf16[512,128]{1,0:T(8,128)(2,1)S(1)}, bf16[512,128]{1,0:T(8,128)(2,1)S(1)}, u32[]{:S(2)}, u32[]{:S(2)}) collective-permute-start(bf16[512,128]{1,0:T(8,128)(2,1)S(1)} %get-tuple-element.30), channel_id=1, source_target_pairs={{0,2},{2,0},{4,6},{6,4},{8,10},{10,8},{12,14},{14,12},{1,3},{3,1},... | collective-permute-start | bytes 393224 | tf_op jit(solution)/shard_map/ppermute | solution.py:481
  7.9 4.0 %collective-permute-done.1.refs_1_.partner_ref = bf16[512,128]{1,0:T(8,128)(2,1)S(1)} collective-permute-done((bf16[512,128]{1,0:T(8,128)(2,1)S(1)}, bf16[512,128]{1,0:T(8,128)(2,1)S(1)}, u32[]{:S(2)}, u32[]{:S(2)}) %collective-permute-start.1) | collective-permute-done | bytes 131104 | tf_op jit(solution)/shard_map/ppermute | solution.py:481
  11.9 1.9 %collective-permute-start.2 = (bf16[512,128]{1,0:T(8,128)(2,1)S(1)}, bf16[512,128]{1,0:T(8,128)(2,1)S(1)}, u32[]{:S(2)}, u32[]{:S(2)}) collective-permute-start(bf16[512,128]{1,0:T(8,128)(2,1)S(1)} %pair_sum.1.refs_0_), channel_id=1, source_target_pairs={{0,4},{2,6},{4,0},{6,2},{8,12},{10,14},{12,8},{14,10},{1,5},{3,7},... | collective-permute-start | bytes 393224 | tf_op jit(solution)/shard_map/ppermute | solution.py:481
  13.8 3.4 %collective-permute-done.2.refs_1_.refs_0_ = bf16[512,128]{1,0:T(8,128)(2,1)S(1)} collective-permute-done((bf16[512,128]{1,0:T(8,128)(2,1)S(1)}, bf16[512,128]{1,0:T(8,128)(2,1)S(1)}, u32[]{:S(2)}, u32[]{:S(2)}) %collective-permute-start.2) | collective-permute-done | bytes 131104 | tf_op jit(solution)/shard_map/ppermute | solution.py:481
  17.2 0.0 collective-permute-done.3.edge_ref
  17.2 2.6 %collective-permute-start.4 = (bf16[512,128]{1,0:T(8,128)(2,1)S(1)}, bf16[512,128]{1,0:T(8,128)(2,1)S(1)}, u32[]{:S(2)}, u32[]{:S(2)}) collective-permute-start(bf16[512,128]{1,0:T(8,128)(2,1)S(1)} %stride_sum.1), channel_id=1, source_target_pairs={{0,8},{2,10},{4,12},{6,14},{8,0},{10,2},{12,4},{14,6},{1,9},{3,11}... | collective-permute-start | bytes 393224 | tf_op jit(solution)/shard_map/ppermute | solution.py:481
  19.9 0.0 copy-done.2
  19.9 0.0 copy-done
  19.9 0.0 copy-done.1
  19.9 3.3 %prepare.1 = (bf16[560,2304]{1,0:T(8,128)(2,1)S(1)}, f32[560,2240]{1,0:T(8,128)S(1)}, f32[1,2240]{1,0:T(1,128)S(1)}, f32[18,24,8,128]{3,2,1,0:T(8,128)S(1)}) custom-call(bf16[480,2240]{1,0:T(8,128)(2,1)} %bitcast.8, bf16[480,2240]{1,0:T(8,128)(2,1)} %bitcast.10, bf16[2,1,80,2240]{3,2,1,0:T(8,128)(2,1)S(1)} %collective-permute-done.3.edge_ref, ...), custom_call_target="tpu_custom_call" | custom-call | flops 5017600 | bytes 10035200 | tf_op jit(solution)/shard_map/prepare/pallas_call | solution.py:201
  23.3 2.1 %collective-permute-done.4.refs_1_ = bf16[512,128]{1,0:T(8,128)(2,1)S(1)} collective-permute-done((bf16[512,128]{1,0:T(8,128)(2,1)S(1)}, bf16[512,128]{1,0:T(8,128)(2,1)S(1)}, u32[]{:S(2)}, u32[]{:S(2)}) %collective-permute-start.4) | collective-permute-done | bytes 131104 | tf_op jit(solution)/shard_map/ppermute | solution.py:481
  25.3 0.1 pair_sums.1
  25.5 1.1 %collective-permute-start.5 = (bf16[512,128]{1,0:T(8,128)(2,1)S(1)}, bf16[512,128]{1,0:T(8,128)(2,1)S(1)}, u32[]{:S(2)}, u32[]{:S(2)}) collective-permute-start(bf16[512,128]{1,0:T(8,128)(2,1)S(1)} %get-tuple-element.44), channel_id=1, source_target_pairs={{0,2},{2,0},{4,6},{6,4},{8,10},{10,8},{12,14},{14,12},{1,3},{3,1},... | collective-permute-start | bytes 393224 | tf_op jit(solution)/shard_map/ppermute | solution.py:481
  26.6 0.0 collective-permute-start.6
  26.6 4.0 %collective-permute-done.5.refs_1_ = bf16[512,128]{1,0:T(8,128)(2,1)S(1)} collective-permute-done((bf16[512,128]{1,0:T(8,128)(2,1)S(1)}, bf16[512,128]{1,0:T(8,128)(2,1)S(1)}, u32[]{:S(2)}, u32[]{:S(2)}) %collective-permute-start.5) | collective-permute-done | bytes 131104 | tf_op jit(solution)/shard_map/ppermute | solution.py:481
  30.5 0.0 collective-permute-start.7
  30.5 0.0 collective-permute-done.6.refs_2_
  30.5 1.3 %collective-permute-done.7.refs_3_ = bf16[512,128]{1,0:T(8,128)(2,1)S(1)} collective-permute-done((bf16[512,128]{1,0:T(8,128)(2,1)S(1)}, bf16[512,128]{1,0:T(8,128)(2,1)S(1)}, u32[]{:S(2)}, u32[]{:S(2)}) %collective-permute-start.7) | collective-permute-done | bytes 131104 | tf_op jit(solution)/shard_map/ppermute | solution.py:507
  31.9 10.6 %mix.1 = bf16[480,2240]{1,0:T(8,128)(2,1)} custom-call(bf16[560,2304]{1,0:T(8,128)(2,1)S(1)} %get-tuple-element.38.features_ref, f32[560,2240]{1,0:T(8,128)S(1)} %get-tuple-element.39.inputs_ref, f32[1,2240]{1,0:T(1,128)S(1)} %get-tuple-element.40.gain_ref, f32[18,24,8,128]{3,2,1,0:T(8,128)S(1)} %get-tuple-element.41.taps_ref, ...), custom_call_target="tpu_custom_call" | custom-call | flops 64512000 | bytes 6451200 | tf_op jit(solution)/shard_map/mix/pallas_call | solution.py:373
  (6 shorter events, 0.1 us)
Async XLA Ops:
  0.0 19.9 %copy-start.2 = (f32[2240]{0:T(1024)S(1)}, f32[2240]{0:T(1024)}, u32[]{:S(2)}) copy-start(f32[2240]{0:T(1024)} %param.11) | copy-start | bytes 26884
  0.0 19.9 %copy-start = (f32[9,2240]{1,0:T(8,128)S(1)}, f32[9,2240]{1,0:T(8,128)}, u32[]{:S(2)}) copy-start(f32[9,2240]{1,0:T(8,128)} %vtaps_ref.1) | copy-start | bytes 241924
  0.0 19.9 %copy-start.1 = (f32[9,2240]{1,0:T(8,128)S(1)}, f32[9,2240]{1,0:T(8,128)}, u32[]{:S(2)}) copy-start(f32[9,2240]{1,0:T(8,128)} %gtaps_ref.1) | copy-start | bytes 241924
  3.0 1.7 %collective-permute-start = (bf16[1024,128]{1,0:T(8,128)(2,1)S(1)}, bf16[1024,128]{1,0:T(8,128)(2,1)S(1)}, u32[]{:S(2)}, u32[]{:S(2)}) collective-permute-start(bf16[1024,128]{1,0:T(8,128)(2,1)S(1)} %get-tuple-element.26), channel_id=1, source_target_pairs={{0,1},{1,0},{2,3},{3,2},{4,5},{5,4},{6,7},{7,6},{8,9},{9,8},{10,11... | collective-permute-start | bytes 786440 | tf_op jit(solution)/shard_map/ppermute | solution.py:485
  4.8 12.5 %collective-permute-start.3 = (bf16[2,1,80,2240]{3,2,1,0:T(8,128)(2,1)S(1)}, bf16[2,1,80,2240]{3,2,1,0:T(8,128)(2,1)S(1)}, u32[]{:S(2)}, u32[]{:S(2)}) collective-permute-start(bf16[2,1,80,2240]{3,2,1,0:T(8,128)(2,1)S(1)} %get-tuple-element.31), channel_id=1, source_target_pairs={{0,1},{1,0},{2,3},{3,2},{4,5},{5,4},{6,7},{7,6},{8,9},{9,8},{10,11... | collective-permute-start | bytes 2150408 | tf_op jit(solution)/shard_map/ppermute | solution.py:489
  5.2 6.7 %collective-permute-start.1 = (bf16[512,128]{1,0:T(8,128)(2,1)S(1)}, bf16[512,128]{1,0:T(8,128)(2,1)S(1)}, u32[]{:S(2)}, u32[]{:S(2)}) collective-permute-start(bf16[512,128]{1,0:T(8,128)(2,1)S(1)} %get-tuple-element.30), channel_id=1, source_target_pairs={{0,2},{2,0},{4,6},{6,4},{8,10},{10,8},{12,14},{14,12},{1,3},{3,1},... | collective-permute-start | bytes 393224 | tf_op jit(solution)/shard_map/ppermute | solution.py:481
  11.9 5.3 %collective-permute-start.2 = (bf16[512,128]{1,0:T(8,128)(2,1)S(1)}, bf16[512,128]{1,0:T(8,128)(2,1)S(1)}, u32[]{:S(2)}, u32[]{:S(2)}) collective-permute-start(bf16[512,128]{1,0:T(8,128)(2,1)S(1)} %pair_sum.1.refs_0_), channel_id=1, source_target_pairs={{0,4},{2,6},{4,0},{6,2},{8,12},{10,14},{12,8},{14,10},{1,5},{3,7},... | collective-permute-start | bytes 393224 | tf_op jit(solution)/shard_map/ppermute | solution.py:481
  17.2 8.1 %collective-permute-start.4 = (bf16[512,128]{1,0:T(8,128)(2,1)S(1)}, bf16[512,128]{1,0:T(8,128)(2,1)S(1)}, u32[]{:S(2)}, u32[]{:S(2)}) collective-permute-start(bf16[512,128]{1,0:T(8,128)(2,1)S(1)} %stride_sum.1), channel_id=1, source_target_pairs={{0,8},{2,10},{4,12},{6,14},{8,0},{10,2},{12,4},{14,6},{1,9},{3,11}... | collective-permute-start | bytes 393224 | tf_op jit(solution)/shard_map/ppermute | solution.py:481
  25.5 5.0 %collective-permute-start.5 = (bf16[512,128]{1,0:T(8,128)(2,1)S(1)}, bf16[512,128]{1,0:T(8,128)(2,1)S(1)}, u32[]{:S(2)}, u32[]{:S(2)}) collective-permute-start(bf16[512,128]{1,0:T(8,128)(2,1)S(1)} %get-tuple-element.44), channel_id=1, source_target_pairs={{0,2},{2,0},{4,6},{6,4},{8,10},{10,8},{12,14},{14,12},{1,3},{3,1},... | collective-permute-start | bytes 393224 | tf_op jit(solution)/shard_map/ppermute | solution.py:481
  26.6 4.0 %collective-permute-start.6 = (bf16[512,128]{1,0:T(8,128)(2,1)S(1)}, bf16[512,128]{1,0:T(8,128)(2,1)S(1)}, u32[]{:S(2)}, u32[]{:S(2)}) collective-permute-start(bf16[512,128]{1,0:T(8,128)(2,1)S(1)} %get-tuple-element.43.refs_0_), channel_id=1, source_target_pairs={{0,1},{1,0},{2,3},{3,2},{4,5},{5,4},{6,7},{7,6},{8,9},{9,8},{10,11... | collective-permute-start | bytes 393224 | tf_op jit(solution)/shard_map/ppermute | solution.py:507
  30.5 1.3 %collective-permute-start.7 = (bf16[512,128]{1,0:T(8,128)(2,1)S(1)}, bf16[512,128]{1,0:T(8,128)(2,1)S(1)}, u32[]{:S(2)}, u32[]{:S(2)}) collective-permute-start(bf16[512,128]{1,0:T(8,128)(2,1)S(1)} %collective-permute-done.5.refs_1_), channel_id=1, source_target_pairs={{0,1},{1,0},{2,3},{3,2},{4,5},{5,4},{6,7},{7,6},{8,9},{9,8},{10,11... | collective-permute-start | bytes 393224 | tf_op jit(solution)/shard_map/ppermute | solution.py:507

commit v22 on v21

--- a/solution.py
+++ b/solution.py
@@ -70,10 +70,10 @@
         whole[used:, :] = jnp.zeros((whole.shape[0] - used, LANES), jnp.bfloat16)
     lane = lane_iota((HEAD_DIM, LANES))
     for k, (base, lanes) in enumerate(order):
-        for copy in copies[2 * k : 2 * k + 2]:
-            copy.wait()
         turn = turned.at[k % 2]
+        copies[2 * k].wait()
         turn[:lanes, :] = jnp.maximum(keys[:, base : base + lanes], 0).T
+        copies[2 * k + 1].wait()
         for tiles, _, _ in spans(lanes):
             begin = tile_heads(tiles[0], lanes)[0][0]
             end = tile_heads(tiles[-1], lanes)[-1][0] + 1

time: 42.7 us -> 43 us (level)
  no operation moved by 1% of the time
where the time goes in v22:
time: 43 us; the launch traced here: 42.9 us
  Pallas kernels  17.6 us (41%)
  waiting for transfers between devices  16 us (37%)
  starting transfers between devices  9.2 us (21%)
    ppermute x4, waiting for transfers between devices, running_states(): lax.ppermute(array, 'frame', [(f, f ^ stride) for f in range(frames)])  13.5 us
    pallas_call x1, Pallas kernels, mix(): pl.pallas_call(functools.partial(mix_kernel, dim, rows, width, (total - t...  10.6 us
    ppermute x4, starting transfers between devices, running_states(): lax.ppermute(array, 'frame', [(f, f ^ stride) for f in range(frames)])  8.24 us
    pallas_call x1, Pallas kernels, frame_states(): pl.pallas_call(functools.partial(state_kernel, dim, parts), out_shape=[pl...  3.35 us
    pallas_call x1, Pallas kernels, prepare(): pl.pallas_call(functools.partial(prepare_kernel, dim), out_shape=[pltpu.V...  3.33 us
    ppermute x1, waiting for transfers between devices, running_states(): lax.ppermute(other, 'space', swap)  1.34 us
    ppermute x1, waiting for transfers between devices, running_states(): got = lax.ppermute(sent, 'space', swap)  1.16 us
  transfers between devices with their start and end apart: 8, of which 6 were waited for; matrix products, arithmetic and copies ran while one was open for 0% of the time, Pallas kernels for 8%

profile of v22, /device:TPU:0, one launch (start us, length us, event | category | flops | bytes accessed | tf_op | source)
XLA Modules:
  0.0 42.9 jit_solution(12988956213066058409)
XLA Ops:
  0.0 3.3 %frame_states.1 = (bf16[1024,128]{1,0:T(8,128)(2,1)S(1)}, bf16[1024,128]{1,0:T(8,128)(2,1)S(1)}, bf16[2,1,80,2240]{3,2,1,0:T(8,128)(2,1)S(1)}) custom-call(bf16[480,2240]{1,0:T(8,128)(2,1)} %bitcast.11, bf16[480,2240]{1,0:T(8,128)(2,1)} %bitcast.12, bf16[6,80,2240]{2,1,0:T(8,128)(2,1)} %bitcast.7, bf16[6,80,2240]{2,1,0:T(8,128)(2,1)} %bitcast.9), custom_call_target="tpu_custom_call" | custom-call | flops 240844800 | bytes 4300800 | tf_op jit(solution)/shard_map/frame_states/pallas_call | solution.py:116
  3.4 0.5 %collective-permute-start = (bf16[1024,128]{1,0:T(8,128)(2,1)S(1)}, bf16[1024,128]{1,0:T(8,128)(2,1)S(1)}, u32[]{:S(2)}, u32[]{:S(2)}) collective-permute-start(bf16[1024,128]{1,0:T(8,128)(2,1)S(1)} %get-tuple-element.26), channel_id=1, source_target_pairs={{0,1},{1,0},{2,3},{3,2},{4,5},{5,4},{6,7},{7,6},{8,9},{9,8},{10,11... | collective-permute-start | bytes 786440 | tf_op jit(solution)/shard_map/ppermute | solution.py:485
  3.9 1.2 %collective-permute-done.got_ref = bf16[1024,128]{1,0:T(8,128)(2,1)S(1)} collective-permute-done((bf16[1024,128]{1,0:T(8,128)(2,1)S(1)}, bf16[1024,128]{1,0:T(8,128)(2,1)S(1)}, u32[]{:S(2)}, u32[]{:S(2)}) %collective-permute-start) | collective-permute-done | bytes 262176 | tf_op jit(solution)/shard_map/ppermute | solution.py:485
  5.0 0.1 split_sum.1
  5.1 0.4 %collective-permute-start.3 = (bf16[2,1,80,2240]{3,2,1,0:T(8,128)(2,1)S(1)}, bf16[2,1,80,2240]{3,2,1,0:T(8,128)(2,1)S(1)}, u32[]{:S(2)}, u32[]{:S(2)}) collective-permute-start(bf16[2,1,80,2240]{3,2,1,0:T(8,128)(2,1)S(1)} %get-tuple-element.31), channel_id=1, source_target_pairs={{0,1},{1,0},{2,3},{3,2},{4,5},{5,4},{6,7},{7,6},{8,9},{9,8},{10,11... | collective-permute-start | bytes 2150408 | tf_op jit(solution)/shard_map/ppermute | solution.py:489
  5.6 2.7 %collective-permute-start.1 = (bf16[512,128]{1,0:T(8,128)(2,1)S(1)}, bf16[512,128]{1,0:T(8,128)(2,1)S(1)}, u32[]{:S(2)}, u32[]{:S(2)}) collective-permute-start(bf16[512,128]{1,0:T(8,128)(2,1)S(1)} %get-tuple-element.30), channel_id=1, source_target_pairs={{0,2},{2,0},{4,6},{6,4},{8,10},{10,8},{12,14},{14,12},{1,3},{3,1},... | collective-permute-start | bytes 393224 | tf_op jit(solution)/shard_map/ppermute | solution.py:481
  8.2 4.0 %collective-permute-done.1.refs_1_.partner_ref = bf16[512,128]{1,0:T(8,128)(2,1)S(1)} collective-permute-done((bf16[512,128]{1,0:T(8,128)(2,1)S(1)}, bf16[512,128]{1,0:T(8,128)(2,1)S(1)}, u32[]{:S(2)}, u32[]{:S(2)}) %collective-permute-start.1) | collective-permute-done | bytes 131104 | tf_op jit(solution)/shard_map/ppermute | solution.py:481
  12.3 1.9 %collective-permute-start.2 = (bf16[512,128]{1,0:T(8,128)(2,1)S(1)}, bf16[512,128]{1,0:T(8,128)(2,1)S(1)}, u32[]{:S(2)}, u32[]{:S(2)}) collective-permute-start(bf16[512,128]{1,0:T(8,128)(2,1)S(1)} %pair_sum.1.refs_0_), channel_id=1, source_target_pairs={{0,4},{2,6},{4,0},{6,2},{8,12},{10,14},{12,8},{14,10},{1,5},{3,7},... | collective-permute-start | bytes 393224 | tf_op jit(solution)/shard_map/ppermute | solution.py:481
  14.1 3.4 %collective-permute-done.2.refs_1_.refs_0_ = bf16[512,128]{1,0:T(8,128)(2,1)S(1)} collective-permute-done((bf16[512,128]{1,0:T(8,128)(2,1)S(1)}, bf16[512,128]{1,0:T(8,128)(2,1)S(1)}, u32[]{:S(2)}, u32[]{:S(2)}) %collective-permute-start.2) | collective-permute-done | bytes 131104 | tf_op jit(solution)/shard_map/ppermute | solution.py:481
  17.6 0.0 collective-permute-done.3.edge_ref
  17.6 2.6 %collective-permute-start.4 = (bf16[512,128]{1,0:T(8,128)(2,1)S(1)}, bf16[512,128]{1,0:T(8,128)(2,1)S(1)}, u32[]{:S(2)}, u32[]{:S(2)}) collective-permute-start(bf16[512,128]{1,0:T(8,128)(2,1)S(1)} %stride_sum.1), channel_id=1, source_target_pairs={{0,8},{2,10},{4,12},{6,14},{8,0},{10,2},{12,4},{14,6},{1,9},{3,11}... | collective-permute-start | bytes 393224 | tf_op jit(solution)/shard_map/ppermute | solution.py:481
  20.2 0.0 copy-done.2
  20.2 0.0 copy-done
  20.3 0.0 copy-done.1
  20.3 3.3 %prepare.1 = (bf16[560,2304]{1,0:T(8,128)(2,1)S(1)}, f32[560,2240]{1,0:T(8,128)S(1)}, f32[1,2240]{1,0:T(1,128)S(1)}, f32[18,24,8,128]{3,2,1,0:T(8,128)S(1)}) custom-call(bf16[480,2240]{1,0:T(8,128)(2,1)} %bitcast.8, bf16[480,2240]{1,0:T(8,128)(2,1)} %bitcast.10, bf16[2,1,80,2240]{3,2,1,0:T(8,128)(2,1)S(1)} %collective-permute-done.3.edge_ref, ...), custom_call_target="tpu_custom_call" | custom-call | flops 5017600 | bytes 10035200 | tf_op jit(solution)/shard_map/prepare/pallas_call | solution.py:201
  23.6 2.1 %collective-permute-done.4.refs_1_ = bf16[512,128]{1,0:T(8,128)(2,1)S(1)} collective-permute-done((bf16[512,128]{1,0:T(8,128)(2,1)S(1)}, bf16[512,128]{1,0:T(8,128)(2,1)S(1)}, u32[]{:S(2)}, u32[]{:S(2)}) %collective-permute-start.4) | collective-permute-done | bytes 131104 | tf_op jit(solution)/shard_map/ppermute | solution.py:481
  25.7 0.1 pair_sums.1
  25.8 1.1 %collective-permute-start.5 = (bf16[512,128]{1,0:T(8,128)(2,1)S(1)}, bf16[512,128]{1,0:T(8,128)(2,1)S(1)}, u32[]{:S(2)}, u32[]{:S(2)}) collective-permute-start(bf16[512,128]{1,0:T(8,128)(2,1)S(1)} %get-tuple-element.44), channel_id=1, source_target_pairs={{0,2},{2,0},{4,6},{6,4},{8,10},{10,8},{12,14},{14,12},{1,3},{3,1},... | collective-permute-start | bytes 393224 | tf_op jit(solution)/shard_map/ppermute | solution.py:481
  26.9 0.0 collective-permute-start.6
  26.9 4.0 %collective-permute-done.5.refs_1_ = bf16[512,128]{1,0:T(8,128)(2,1)S(1)} collective-permute-done((bf16[512,128]{1,0:T(8,128)(2,1)S(1)}, bf16[512,128]{1,0:T(8,128)(2,1)S(1)}, u32[]{:S(2)}, u32[]{:S(2)}) %collective-permute-start.5) | collective-permute-done | bytes 131104 | tf_op jit(solution)/shard_map/ppermute | solution.py:481
  30.9 0.0 collective-permute-start.7
  30.9 0.0 collective-permute-done.6.refs_2_
  30.9 1.3 %collective-permute-done.7.refs_3_ = bf16[512,128]{1,0:T(8,128)(2,1)S(1)} collective-permute-done((bf16[512,128]{1,0:T(8,128)(2,1)S(1)}, bf16[512,128]{1,0:T(8,128)(2,1)S(1)}, u32[]{:S(2)}, u32[]{:S(2)}) %collective-permute-start.7) | collective-permute-done | bytes 131104 | tf_op jit(solution)/shard_map/ppermute | solution.py:507
  32.2 10.6 %mix.1 = bf16[480,2240]{1,0:T(8,128)(2,1)} custom-call(bf16[560,2304]{1,0:T(8,128)(2,1)S(1)} %get-tuple-element.38.features_ref, f32[560,2240]{1,0:T(8,128)S(1)} %get-tuple-element.39.inputs_ref, f32[1,2240]{1,0:T(1,128)S(1)} %get-tuple-element.40.gain_ref, f32[18,24,8,128]{3,2,1,0:T(8,128)S(1)} %get-tuple-element.41.taps_ref, ...), custom_call_target="tpu_custom_call" | custom-call | flops 64512000 | bytes 6451200 | tf_op jit(solution)/shard_map/mix/pallas_call | solution.py:373
  (6 shorter events, 0.1 us)
Async XLA Ops:
  0.0 20.2 %copy-start.2 = (f32[2240]{0:T(1024)S(1)}, f32[2240]{0:T(1024)}, u32[]{:S(2)}) copy-start(f32[2240]{0:T(1024)} %param.11) | copy-start | bytes 26884
  0.0 20.2 %copy-start = (f32[9,2240]{1,0:T(8,128)S(1)}, f32[9,2240]{1,0:T(8,128)}, u32[]{:S(2)}) copy-start(f32[9,2240]{1,0:T(8,128)} %vtaps_ref.1) | copy-start | bytes 241924
  0.0 20.2 %copy-start.1 = (f32[9,2240]{1,0:T(8,128)S(1)}, f32[9,2240]{1,0:T(8,128)}, u32[]{:S(2)}) copy-start(f32[9,2240]{1,0:T(8,128)} %gtaps_ref.1) | copy-start | bytes 241924
  3.4 1.7 %collective-permute-start = (bf16[1024,128]{1,0:T(8,128)(2,1)S(1)}, bf16[1024,128]{1,0:T(8,128)(2,1)S(1)}, u32[]{:S(2)}, u32[]{:S(2)}) collective-permute-start(bf16[1024,128]{1,0:T(8,128)(2,1)S(1)} %get-tuple-element.26), channel_id=1, source_target_pairs={{0,1},{1,0},{2,3},{3,2},{4,5},{5,4},{6,7},{7,6},{8,9},{9,8},{10,11... | collective-permute-start | bytes 786440 | tf_op jit(solution)/shard_map/ppermute | solution.py:485
  5.1 12.5 %collective-permute-start.3 = (bf16[2,1,80,2240]{3,2,1,0:T(8,128)(2,1)S(1)}, bf16[2,1,80,2240]{3,2,1,0:T(8,128)(2,1)S(1)}, u32[]{:S(2)}, u32[]{:S(2)}) collective-permute-start(bf16[2,1,80,2240]{3,2,1,0:T(8,128)(2,1)S(1)} %get-tuple-element.31), channel_id=1, source_target_pairs={{0,1},{1,0},{2,3},{3,2},{4,5},{5,4},{6,7},{7,6},{8,9},{9,8},{10,11... | collective-permute-start | bytes 2150408 | tf_op jit(solution)/shard_map/ppermute | solution.py:489
  5.6 6.7 %collective-permute-start.1 = (bf16[512,128]{1,0:T(8,128)(2,1)S(1)}, bf16[512,128]{1,0:T(8,128)(2,1)S(1)}, u32[]{:S(2)}, u32[]{:S(2)}) collective-permute-start(bf16[512,128]{1,0:T(8,128)(2,1)S(1)} %get-tuple-element.30), channel_id=1, source_target_pairs={{0,2},{2,0},{4,6},{6,4},{8,10},{10,8},{12,14},{14,12},{1,3},{3,1},... | collective-permute-start | bytes 393224 | tf_op jit(solution)/shard_map/ppermute | solution.py:481
  12.3 5.3 %collective-permute-start.2 = (bf16[512,128]{1,0:T(8,128)(2,1)S(1)}, bf16[512,128]{1,0:T(8,128)(2,1)S(1)}, u32[]{:S(2)}, u32[]{:S(2)}) collective-permute-start(bf16[512,128]{1,0:T(8,128)(2,1)S(1)} %pair_sum.1.refs_0_), channel_id=1, source_target_pairs={{0,4},{2,6},{4,0},{6,2},{8,12},{10,14},{12,8},{14,10},{1,5},{3,7},... | collective-permute-start | bytes 393224 | tf_op jit(solution)/shard_map/ppermute | solution.py:481
  17.6 8.1 %collective-permute-start.4 = (bf16[512,128]{1,0:T(8,128)(2,1)S(1)}, bf16[512,128]{1,0:T(8,128)(2,1)S(1)}, u32[]{:S(2)}, u32[]{:S(2)}) collective-permute-start(bf16[512,128]{1,0:T(8,128)(2,1)S(1)} %stride_sum.1), channel_id=1, source_target_pairs={{0,8},{2,10},{4,12},{6,14},{8,0},{10,2},{12,4},{14,6},{1,9},{3,11}... | collective-permute-start | bytes 393224 | tf_op jit(solution)/shard_map/ppermute | solution.py:481
  25.8 5.0 %collective-permute-start.5 = (bf16[512,128]{1,0:T(8,128)(2,1)S(1)}, bf16[512,128]{1,0:T(8,128)(2,1)S(1)}, u32[]{:S(2)}, u32[]{:S(2)}) collective-permute-start(bf16[512,128]{1,0:T(8,128)(2,1)S(1)} %get-tuple-element.44), channel_id=1, source_target_pairs={{0,2},{2,0},{4,6},{6,4},{8,10},{10,8},{12,14},{14,12},{1,3},{3,1},... | collective-permute-start | bytes 393224 | tf_op jit(solution)/shard_map/ppermute | solution.py:481
  26.9 4.0 %collective-permute-start.6 = (bf16[512,128]{1,0:T(8,128)(2,1)S(1)}, bf16[512,128]{1,0:T(8,128)(2,1)S(1)}, u32[]{:S(2)}, u32[]{:S(2)}) collective-permute-start(bf16[512,128]{1,0:T(8,128)(2,1)S(1)} %get-tuple-element.43.refs_0_), channel_id=1, source_target_pairs={{0,1},{1,0},{2,3},{3,2},{4,5},{5,4},{6,7},{7,6},{8,9},{9,8},{10,11... | collective-permute-start | bytes 393224 | tf_op jit(solution)/shard_map/ppermute | solution.py:507
  30.9 1.3 %collective-permute-start.7 = (bf16[512,128]{1,0:T(8,128)(2,1)S(1)}, bf16[512,128]{1,0:T(8,128)(2,1)S(1)}, u32[]{:S(2)}, u32[]{:S(2)}) collective-permute-start(bf16[512,128]{1,0:T(8,128)(2,1)S(1)} %collective-permute-done.5.refs_1_), channel_id=1, source_target_pairs={{0,1},{1,0},{2,3},{3,2},{4,5},{5,4},{6,7},{7,6},{8,9},{9,8},{10,11... | collective-permute-start | bytes 393224 | tf_op jit(solution)/shard_map/ppermute | solution.py:507
